TPU v7x, 32 devices: a whole 2x2x4 slice. The times are simulated.
32 devices in a mesh: shot: 4 (over y, x), blk: 8 (over z, core).
Axes of the slice: x: 2, y: 2, z: 4, core: 2. Of those that a mesh axis runs over, the one named last changes fastest.
Arguments:
- state_before: float32 [4, 64, 64, 128], P('shot', 'blk'), may hold values from -7 to 7
- state_now: float32 [4, 64, 64, 128], P('shot', 'blk'), may hold values from -7 to 7
- adjoint_later: float32 [4, 64, 64, 128], P('shot', 'blk'), may hold values from -7 to 7
- adjoint_now: float32 [4, 64, 64, 128], P('shot', 'blk'), may hold values from -7 to 7
- courant_sq: float32 [64, 128, 128], P('blk', 'shot'), may hold values from 0.02 to 0.3
- epsilon: float32 [64, 128, 128], P('blk', 'shot'), may hold values from 0.02 to 0.3
- tilt_angle: float32 [64, 128, 128], P('blk', 'shot'), may hold values from 0 to 1.2
- azimuth: float32 [64, 128, 128], P('blk', 'shot'), may hold values from -3.140625 to 3.140625
- aperture_anchor: int32 [4], P('shot'), may hold values from 0 to 64, as said below
- step_index: int32 [1], replicated, may hold values from 0 to 12
- wavelet: float32 [4, 16], P('shot'), may hold values from -8 to 8
- residual_traces: float32 [4, 16, 128], P('shot'), may hold values from -6 to 6
- source_x: int32 [4], P('shot'), may hold values from 0 to 63
- source_y: int32 [4], P('shot'), may hold values from 0 to 63
- source_z: int32 [4], P('shot'), may hold values from 0 to 127
- receiver_x: int32 [4, 128], P('shot'), may hold values from 0 to 63
- receiver_y: int32 [4, 128], P('shot'), may hold values from 0 to 63
- receiver_z: int32 [4, 128], P('shot'), may hold values from 0 to 127
Outputs:
- adjoint_one: float32 [4, 64, 64, 128], P('shot', 'blk')
- adjoint_zero: float32 [4, 64, 64, 128], P('shot', 'blk')
- model_grad: float32 [64, 128, 128], P('blk', 'shot')
Inputs may be any that keep to these rules, and one draw needn't show every extreme that they name: `aperture_anchor`: each value is a multiple of 32; some shot has 0 and some shot has 64.
All inputs are finite; a program needn't handle non-finite values.
Results may differ from a plain program's by a relative error of at most 0.0003.
Values sent between devices are 32-bit elements; how exact they have to be, the bound alone decides.
No kernel may reach another device: no remote copies, remote signals or barrier semaphores. Data moves between devices by JAX's collectives and lax.ppermute only.
A program may use at most 64 MiB of HBM per device.

v0:
```python
import jax
import jax.numpy as jnp
from jax import lax
from jax.sharding import PartitionSpec as P

STEPS = 4


COEF = (0.8, -0.2, 4.0 / 105.0, -1.0 / 280.0)


def padded_2(array, sides, width):
    for axis, dim in sides:
        size, length = (lax.axis_size(axis), array.shape[dim])
        up = [(i, (i + 1) % size) for i in range(size - 1)]
        down = [(j, i) for i, j in up]
        last = lax.slice_in_dim(array, length - width, length, axis=dim)
        leading = lax.slice_in_dim(array, 0, width, axis=dim)
        before = lax.ppermute(last, axis, up)
        after = lax.ppermute(leading, axis, down)
        array = jnp.concatenate([before, array, after], axis=dim)
    return array


def first_diff(padded, axis, count):
    summed = None
    for k in range(1, 5):
        upper_part = lax.slice_in_dim(padded, 4 + k, 4 + k + count, axis=axis)
        lower_part = lax.slice_in_dim(padded, 4 - k, 4 - k + count, axis=axis)
        addend = COEF[k - 1] * (upper_part - lower_part)
        summed = addend if summed is None else summed + addend
    return summed


def pad_axis(field, axis):
    widths = [(0, 0), (0, 0), (0, 0)]
    widths[axis] = (4, 4)
    return jnp.pad(field, widths)


def operate_deep(field, wide_parts, inside_rows):
    twice_eps, normal_x, normal_y, normal_z = wide_parts
    rows = field.shape[0]
    extended = padded_2(field, (("blk", 0),), 8)
    slope_x = first_diff(extended, 0, rows + 8)
    middle = extended[4 : rows + 12]
    slope_y = first_diff(pad_axis(middle, 1), 1, field.shape[1])
    slope_z = first_diff(pad_axis(middle, 2), 2, field.shape[2])
    normal_slope = normal_x * slope_x + normal_y * slope_y + normal_z * slope_z
    flux_x = jnp.where(
        inside_rows, (1.0 + twice_eps) * slope_x - twice_eps * normal_x * normal_slope, 0.0
    )
    flux_y = ((1.0 + twice_eps) * slope_y - twice_eps * normal_y * normal_slope)[4 : rows + 4]
    flux_z = ((1.0 + twice_eps) * slope_z - twice_eps * normal_z * normal_slope)[4 : rows + 4]
    result = first_diff(flux_x, 0, rows)
    result = result + first_diff(pad_axis(flux_y, 1), 1, field.shape[1])
    return result + first_diff(pad_axis(flux_z, 2), 2, field.shape[2])


def on_device(
    state_before,
    state_now,
    adjoint_later,
    adjoint_now,
    courant_sq,
    epsilon,
    tilt_angle,
    azimuth,
    aperture_anchor,
    step_index,
    wavelet,
    residual_traces,
    source_x,
    source_y,
    source_z,
    receiver_x,
    receiver_y,
    receiver_z,
):
    rows = state_now.shape[1]
    width_y = state_now.shape[2]
    depth = state_now.shape[3]
    block_index = lax.axis_index("blk")
    span_x = rows * lax.axis_size("blk")
    anchor = aperture_anchor[0]
    start_step = step_index[0]
    empty = jnp.zeros((rows, width_y, depth), jnp.float32)
    carried = (empty, empty, empty, empty)
    pieces = (
        lax.all_gather(courant_sq, "shot", axis=1, tiled=True),
        lax.all_gather(epsilon, "shot", axis=1, tiled=True),
        lax.all_gather(tilt_angle, "shot", axis=1, tiled=True),
        lax.all_gather(azimuth, "shot", axis=1, tiled=True),
    )
    count = pieces[0].shape[1]
    relative = jnp.int32(0) - anchor
    inside = (relative > -count) & (relative < width_y)
    offset = jnp.clip(relative + count, 0, width_y + count)
    placed = []
    for held, piece in zip(carried, pieces):
        spread = jnp.zeros((rows, width_y + 2 * count, depth), jnp.float32)
        spread = lax.dynamic_update_slice(spread, piece, (0, offset, 0))
        placed.append(jnp.where(inside, spread[:, count : count + width_y], 0.0))
    speed_term, eps_part, tilt_part, azimuth_part = tuple(placed)
    twice_eps = 2.0 * eps_part
    tensor_parts = (
        twice_eps,
        jnp.sin(tilt_part) * jnp.cos(azimuth_part),
        jnp.sin(tilt_part) * jnp.sin(azimuth_part),
        jnp.cos(tilt_part),
    )
    stacked = jnp.stack(tensor_parts)
    wide_stack = padded_2(stacked, (("blk", 1),), 4)
    wide_parts = (wide_stack[0], wide_stack[1], wide_stack[2], wide_stack[3])
    wide_rows = block_index * rows - 4 + lax.broadcasted_iota(jnp.int32, (rows + 8, 1, 1), 0)
    inside_rows = (wide_rows >= 0) & (wide_rows < span_x)

    def operate(field):
        return operate_deep(field, wide_parts, inside_rows)

    global_x = block_index * rows + lax.broadcasted_iota(jnp.int32, (rows, width_y, depth), 0)
    cell_y = lax.broadcasted_iota(jnp.int32, (rows, width_y, depth), 1)
    cell_z = lax.broadcasted_iota(jnp.int32, (rows, width_y, depth), 2)
    source_mask = (global_x == source_x[0]) & (cell_y == source_y[0]) & (cell_z == source_z[0])
    local_rows = receiver_x[0] - block_index * rows
    plane_index = local_rows * width_y + receiver_y[0]
    receiver_inside = (local_rows >= 0) & (local_rows < rows)
    plane_pick = (
        (
            lax.broadcasted_iota(jnp.int32, (rows * width_y, plane_index.shape[0]), 0)
            == plane_index[None, :]
        )
        & receiver_inside[None, :]
    ).astype(jnp.float32)
    depth_match = (
        lax.broadcasted_iota(jnp.int32, (plane_index.shape[0], depth), 1) == receiver_z[0][:, None]
    ).astype(jnp.float32)
    previous = state_before[0]
    current = state_now[0]
    images = []
    for t in range(STEPS):
        image = operate(current)
        images.append(image)
        if t < STEPS - 1:
            amplitude = lax.dynamic_index_in_dim(wavelet[0], start_step + t, keepdims=False)
            following = 2.0 * current - previous + speed_term * image
            following = following + jnp.where(source_mask, amplitude, 0.0)
            previous, current = (current, following)
    later = adjoint_later[0]
    present = adjoint_now[0]
    shot_grad = jnp.zeros((rows, width_y, depth), jnp.float32)
    for t in reversed(range(STEPS)):
        shot_grad = shot_grad + present * images[t]
        earlier = 2.0 * present - later + operate(speed_term * present)
        samples = lax.dynamic_index_in_dim(residual_traces[0], start_step + t, keepdims=False)
        depth_pick = depth_match * samples[:, None]
        injected = jnp.dot(
            plane_pick,
            depth_pick,
            precision=lax.Precision.HIGHEST,
            preferred_element_type=jnp.float32,
        )
        earlier = earlier + injected.reshape(rows, width_y, depth)
        later, present = (present, earlier)
    grad_slab = jnp.zeros((rows, 2 * width_y, depth), jnp.float32)
    grad_slab = lax.dynamic_update_slice(grad_slab, shot_grad, (0, anchor, 0))
    model_grad = lax.psum_scatter(grad_slab, "shot", scatter_dimension=1, tiled=True)
    return (later[None], present[None], model_grad)


def solution(mesh):
    in_specs = (
        P("shot", "blk", None, None),
        P("shot", "blk", None, None),
        P("shot", "blk", None, None),
        P("shot", "blk", None, None),
        P("blk", "shot", None),
        P("blk", "shot", None),
        P("blk", "shot", None),
        P("blk", "shot", None),
        P("shot"),
        P(),
        P("shot", None),
        P("shot", None, None),
        P("shot"),
        P("shot"),
        P("shot"),
        P("shot", None),
        P("shot", None),
        P("shot", None),
    )
    out_specs = (P("shot", "blk", None, None), P("shot", "blk", None, None), P("blk", "shot", None))
    return jax.shard_map(
        on_device, mesh=mesh, in_specs=in_specs, out_specs=out_specs, check_vma=False
    )
```

profile of v0, /device:TPU:0, one launch (start us, length us, event | category | flops | bytes accessed | tf_op | source)
XLA Modules:
  0.0 196.8 jit_solution(8157371080129240816)
XLA Ops:
  7.2 1.4 collective-permute-start.11
  8.7 3.8 %collective-permute-start.10 = (f32[8,64,128]{2,1,0:T(8,128)}, f32[8,64,128]{2,1,0:T(8,128)}, u32[]{:S(2)}, u32[]{:S(2)}) collective-permute-start(f32[8,64,128]{2,1,0:T(8,128)} %bitcast.191), channel_id=1, source_target_pairs={{0,1},{1,2},{2,3},{3,4},{4,5},{5,6},{6,7},{8,9},{9,10},{10,11},{11... | collective-permute-start | bytes 786440 | tf_op jit(solution)/shard_map/ppermute | solution.py:19
  13.1 13.1 %all_gather.15 = f32[8,128,128]{2,1,0:T(8,128)S(1)} all-gather(f32[8,32,128]{2,1,0:T(8,128)} %param.22), channel_id=1, replica_groups=mesh['shot'=4,'blk'=8] {'shot'}, dimensions={1}, use_global_device_ids=true | all-gather | bytes 655360 | tf_op jit(solution)/shard_map/all_gather | solution.py:90
  26.3 1.5 dynamic_update_slice.18
  27.8 1.3 collective-permute-start.3
  29.1 3.8 %collective-permute-start.2 = (f32[8,64,128]{2,1,0:T(8,128)S(1)}, f32[8,64,128]{2,1,0:T(8,128)}, u32[]{:S(2)}, u32[]{:S(2)}) collective-permute-start(f32[8,64,128]{2,1,0:T(8,128)S(1)} %bitcast_multiply_fusion), channel_id=1, source_target_pairs={{0,1},{1,2},{2,3},{3,4},{4,5},{5,6},{6,7},{8,9},{9,10},{10,11},{11... | collective-permute-start | bytes 786440 | tf_op jit(solution)/shard_map/ppermute | solution.py:19
  32.8 9.8 %all_gather.14 = f32[8,128,128]{2,1,0:T(8,128)S(1)} all-gather(f32[8,32,128]{2,1,0:T(8,128)S(1)} %copy-done.16), channel_id=1, replica_groups=mesh['shot'=4,'blk'=8] {'shot'}, dimensions={1}, use_global_device_ids=true | all-gather | bytes 655360 | tf_op jit(solution)/shard_map/all_gather | solution.py:93
  42.7 9.2 %all_gather.13 = f32[8,128,128]{2,1,0:T(8,128)S(1)} all-gather(f32[8,32,128]{2,1,0:T(8,128)S(1)} %copy-done.17), channel_id=1, replica_groups=mesh['shot'=4,'blk'=8] {'shot'}, dimensions={1}, use_global_device_ids=true | all-gather | bytes 655360 | tf_op jit(solution)/shard_map/all_gather | solution.py:92
  51.9 11.2 %all_gather.12 = f32[8,128,128]{2,1,0:T(8,128)} all-gather(f32[8,32,128]{2,1,0:T(8,128)S(1)} %copy-done.18), channel_id=1, replica_groups=mesh['shot'=4,'blk'=8] {'shot'}, dimensions={1}, use_global_device_ids=true | all-gather | bytes 655360 | tf_op jit(solution)/shard_map/all_gather | solution.py:91
  63.1 1.2 broadcast.140.clone.2
  64.3 3.6 %dynamic_update_slice.15 = f32[8,320,128]{2,1,0:T(8,128)} dynamic-update-slice(f32[8,320,128]{2,1,0:T(8,128)} %broadcast.140.clone.2, f32[8,128,128]{2,1,0:T(8,128)} %all_gather.12, s32[]{:T(128)} %constant.71.clone.1, s32[]{:T(128)S(6)} %min.4, s32[]{:T(128)} %constant.71.clone.1) | dynamic-update-slice | bytes 1048580 | tf_op jit(solution)/shard_map/dynamic_update_slice | solution.py:102
  67.9 1.0 fusion.514
  68.9 1.2 broadcast.140.clone
  70.1 3.5 %dynamic_update_slice.17 = f32[8,320,128]{2,1,0:T(8,128)} dynamic-update-slice(f32[8,320,128]{2,1,0:T(8,128)} %broadcast.140.clone, f32[8,128,128]{2,1,0:T(8,128)S(1)} %all_gather.14, s32[]{:T(128)} %constant.71.clone.1, s32[]{:T(128)S(6)} %min.4, s32[]{:T(128)} %constant.71.clone.1) | dynamic-update-slice | bytes 1048580 | tf_op jit(solution)/shard_map/dynamic_update_slice | solution.py:102
  73.7 1.5 dynamic_update_slice.16
  75.2 3.2 %multiply_bitcast_fusion.1 = (f32[1,8,64,128]{3,2,1,0:T(8,128)S(1)}, f32[1,8,64,128]{3,2,1,0:T(8,128)S(1)}, f32[1,8,64,128]{3,2,1,0:T(8,128)S(1)}) fusion(f32[8,320,128]{2,1,0:T(8,128)} %dynamic_update_slice.17, f32[8,320,128]{2,1,0:T(8,128)S(1)} %dynamic_update_slice.16, pred[]{:T(512)S(6)} %and.33), kind=kLoop, calls=%fused_computation.897 | loop fusion | flops 262144 | bytes 1310721 | tf_op jit(solution)/shard_map/stack | solution.py:112
  78.5 0.9 fusion.585
  79.4 1.3 collective-permute-start.1
  82.1 0.8 fusion.557
  85.0 0.6 constant_dynamic-slice_fusion
  85.6 3.1 %collective-permute-start = (f32[4,4,64,128]{3,2,1,0:T(8,128)S(1)}, f32[4,4,64,128]{3,2,1,0:T(8,128)S(1)}, u32[]{:S(2)}, u32[]{:S(2)}) collective-permute-start(f32[4,4,64,128]{3,2,1,0:T(8,128)S(1)} %get-tuple-element.78), channel_id=1, source_target_pairs={{0,1},{1,2},{2,3},{3,4},{4,5},{5,6},{6,7},{8,9},{9,10},{10,11},{11... | collective-permute-start | bytes 1572872 | tf_op jit(solution)/shard_map/ppermute | solution.py:19
  88.7 1.1 pad_maximum_fusion.6
  89.8 1.1 pad_maximum_fusion.2
  90.9 1.2 fusion.593
  92.1 1.2 fusion.589
  93.4 1.3 pad_maximum_fusion
  94.6 1.2 subtract_select_fusion.3
  95.8 1.2 subtract_select_fusion.7
  97.3 1.4 copy-done.1
  98.8 0.6 fusion.537
  99.4 1.3 collective-permute-start.5
  100.7 5.0 %collective-permute-start.4 = (f32[8,64,128]{2,1,0:T(8,128)S(1)}, f32[8,64,128]{2,1,0:T(8,128)S(1)}, u32[]{:S(2)}, u32[]{:S(2)}) collective-permute-start(f32[8,64,128]{2,1,0:T(8,128)S(1)} %get-tuple-element.42), channel_id=1, source_target_pairs={{0,1},{1,2},{2,3},{3,4},{4,5},{5,6},{6,7},{8,9},{9,10},{10,11},{11... | collective-permute-start | bytes 786440 | tf_op jit(solution)/shard_map/ppermute | solution.py:19
  105.7 1.3 fusion.516
  107.0 1.3 collective-permute-start.13
  108.3 5.2 %collective-permute-start.12 = (f32[8,64,128]{2,1,0:T(8,128)S(1)}, f32[8,64,128]{2,1,0:T(8,128)S(1)}, u32[]{:S(2)}, u32[]{:S(2)}) collective-permute-start(f32[8,64,128]{2,1,0:T(8,128)S(1)} %get-tuple-element.21), channel_id=1, source_target_pairs={{0,1},{1,2},{2,3},{3,4},{4,5},{5,6},{6,7},{8,9},{9,10},{10,11},{11... | collective-permute-start | bytes 786440 | tf_op jit(solution)/shard_map/ppermute | solution.py:19
  113.9 0.6 collective-permute-done.12
  114.8 2.4 %subtract_select_fusion.6 = (f32[16,64,128]{2,1,0:T(8,128)S(1)}, f32[16,64,128]{2,1,0:T(8,128)S(1)}, f32[16,64,128]{2,1,0:T(8,128)S(1)}, f32[16,64,128]{2,1,0:T(...) fusion(f32[16,64,128]{2,1,0:T(8,128)S(1)} %get-tuple-element.27, ...), kind=kLoop, calls=%fused_computation.482 | loop fusion | flops 8257536 | bytes 8912912 | tf_op jit(solution)/shard_map/jit(_where)/select_n | solution.py:50
  117.4 0.6 fusion.536
  118.1 1.3 collective-permute-start.7
  119.4 6.4 %collective-permute-start.6 = (f32[8,64,128]{2,1,0:T(8,128)S(1)}, f32[8,64,128]{2,1,0:T(8,128)S(1)}, u32[]{:S(2)}, u32[]{:S(2)}) collective-permute-start(f32[8,64,128]{2,1,0:T(8,128)S(1)} %get-tuple-element.36), channel_id=1, source_target_pairs={{0,1},{1,2},{2,3},{3,4},{4,5},{5,6},{6,7},{8,9},{9,10},{10,11},{11... | collective-permute-start | bytes 786440 | tf_op jit(solution)/shard_map/ppermute | solution.py:19
  125.8 1.3 select_add_fusion.1
  127.1 1.3 collective-permute-start.15
  128.4 5.0 %collective-permute-start.14 = (f32[8,64,128]{2,1,0:T(8,128)S(1)}, f32[8,64,128]{2,1,0:T(8,128)S(1)}, u32[]{:S(2)}, u32[]{:S(2)}) collective-permute-start(f32[8,64,128]{2,1,0:T(8,128)S(1)} %get-tuple-element.15), channel_id=1, source_target_pairs={{0,1},{1,2},{2,3},{3,4},{4,5},{5,6},{6,7},{8,9},{9,10},{10,11},{11... | collective-permute-start | bytes 786440 | tf_op jit(solution)/shard_map/ppermute | solution.py:19
  133.8 0.8 collective-permute-done.14
  134.8 2.4 %subtract_select_fusion.5 = (f32[16,64,128]{2,1,0:T(8,128)S(1)}, f32[16,64,128]{2,1,0:T(8,128)S(1)}, f32[16,64,128]{2,1,0:T(8,128)S(1)}, f32[16,64,128]{2,1,0:T(...) fusion(f32[16,64,128]{2,1,0:T(8,128)S(1)} %get-tuple-element.27, ...), kind=kLoop, calls=%fused_computation.480 | loop fusion | flops 8257536 | bytes 8912912 | tf_op jit(solution)/shard_map/jit(_where)/select_n | solution.py:50
  137.5 1.3 select_add_fusion
  138.8 1.3 collective-permute-start.17
  140.1 6.4 %collective-permute-start.16 = (f32[8,64,128]{2,1,0:T(8,128)S(1)}, f32[8,64,128]{2,1,0:T(8,128)S(1)}, u32[]{:S(2)}, u32[]{:S(2)}) collective-permute-start(f32[8,64,128]{2,1,0:T(8,128)S(1)} %get-tuple-element.9), channel_id=1, source_target_pairs={{0,1},{1,2},{2,3},{3,4},{4,5},{5,6},{6,7},{8,9},{9,10},{10,11},{11... | collective-permute-start | bytes 786440 | tf_op jit(solution)/shard_map/ppermute | solution.py:19
  146.6 0.3 fusion.520
  146.9 0.8 collective-permute-done.16
  148.0 1.2 subtract_select_fusion
  149.3 1.9 fusion.346
  151.2 0.7 copy-done.11
  151.9 1.3 collective-permute-start.9
  153.2 7.9 %collective-permute-start.8 = (f32[8,64,128]{2,1,0:T(8,128)S(1)}, f32[8,64,128]{2,1,0:T(8,128)}, u32[]{:S(2)}, u32[]{:S(2)}) collective-permute-start(f32[8,64,128]{2,1,0:T(8,128)S(1)} %fusion.535), channel_id=1, source_target_pairs={{0,1},{1,2},{2,3},{3,4},{4,5},{5,6},{6,7},{8,9},{9,10},{10,11},{11... | collective-permute-start | bytes 786440 | tf_op jit(solution)/shard_map/ppermute | solution.py:19
  161.0 1.1 fusion.518
  162.1 0.8 broadcast_in_dim.81
  162.9 1.8 dynamic_update_slice.19
  164.8 1.1 pad_maximum_fusion.5
  165.9 1.2 fusion.586
  167.2 1.2 subtract_select_fusion.4
  168.5 0.8 copy-done.10
  169.4 1.3 fusion.290
  170.8 19.2 %reduce-scatter.2.cloned.1.call-done = f32[8,32,128]{2,1,0:T(8,128)} async-done(((f32[8,128,128]{2,1,0:T(8,128)}), f32[8,32,128]{2,1,0:T(8,128)}) %reduce-scatter.2.cloned.1.call-update) | async-done | bytes 131088 | tf_op jit(solution)/shard_map/reduce_scatter | solution.py:167
  (88 shorter events, 3.7 us)
Async XLA Ops:
  7.2 20.6 %copy-start.6 = (f32[1,8,64,128]{3,2,1,0:T(8,128)S(1)}, f32[1,8,64,128]{3,2,1,0:T(8,128)}, u32[]{:S(2)}) copy-start(f32[1,8,64,128]{3,2,1,0:T(8,128)} %param.21) | copy-start | bytes 786436
  7.2 25.7 %copy-start.16 = (f32[8,32,128]{2,1,0:T(8,128)S(1)}, f32[8,32,128]{2,1,0:T(8,128)}, u32[]{:S(2)}) copy-start(f32[8,32,128]{2,1,0:T(8,128)} %param.25) | copy-start | bytes 393220
  7.2 182.8 %reduce-scatter.2.cloned.1.call-start = ((), (), s32[]{:S(2)}) async-start(), calls=%async_computation.1 | async-start | bytes 655360 | tf_op jit(solution)/shard_map/reduce_scatter | solution.py:167
  7.2 78.4 %collective-permute-start.11 = (f32[8,64,128]{2,1,0:T(8,128)}, f32[8,64,128]{2,1,0:T(8,128)}, u32[]{:S(2)}, u32[]{:S(2)}) collective-permute-start(f32[8,64,128]{2,1,0:T(8,128)} %bitcast.190), channel_id=1, source_target_pairs={{1,0},{2,1},{3,2},{4,3},{5,4},{6,5},{7,6},{9,8},{10,9},{11,10},{12... | collective-permute-start | bytes 786440 | tf_op jit(solution)/shard_map/ppermute | solution.py:20
  8.7 80.0 %collective-permute-start.10 = (f32[8,64,128]{2,1,0:T(8,128)}, f32[8,64,128]{2,1,0:T(8,128)}, u32[]{:S(2)}, u32[]{:S(2)}) collective-permute-start(f32[8,64,128]{2,1,0:T(8,128)} %bitcast.191), channel_id=1, source_target_pairs={{0,1},{1,2},{2,3},{3,4},{4,5},{5,6},{6,7},{8,9},{9,10},{10,11},{11... | collective-permute-start | bytes 786440 | tf_op jit(solution)/shard_map/ppermute | solution.py:19
  13.1 29.6 %copy-start.17 = (f32[8,32,128]{2,1,0:T(8,128)S(1)}, f32[8,32,128]{2,1,0:T(8,128)}, u32[]{:S(2)}) copy-start(f32[8,32,128]{2,1,0:T(8,128)} %param.24) | copy-start | bytes 393220
  26.2 25.8 %copy-start.18 = (f32[8,32,128]{2,1,0:T(8,128)S(1)}, f32[8,32,128]{2,1,0:T(8,128)}, u32[]{:S(2)}) copy-start(f32[8,32,128]{2,1,0:T(8,128)} %param.23) | copy-start | bytes 393220
  27.7 40.2 %copy-start = (f32[8,320,128]{2,1,0:T(8,128)}, f32[8,320,128]{2,1,0:T(8,128)S(1)}, u32[]{:S(2)}) copy-start(f32[8,320,128]{2,1,0:T(8,128)S(1)} %dynamic_update_slice.18) | copy-start | bytes 3932164
  27.8 62.0 %collective-permute-start.3 = (f32[8,64,128]{2,1,0:T(8,128)S(1)}, f32[8,64,128]{2,1,0:T(8,128)}, u32[]{:S(2)}, u32[]{:S(2)}) collective-permute-start(f32[8,64,128]{2,1,0:T(8,128)S(1)} %bitcast_multiply_fusion), channel_id=1, source_target_pairs={{1,0},{2,1},{3,2},{4,3},{5,4},{6,5},{7,6},{9,8},{10,9},{11,10},{12... | collective-permute-start | bytes 786440 | tf_op jit(solution)/shard_map/ppermute | solution.py:20
  29.1 60.7 %collective-permute-start.2 = (f32[8,64,128]{2,1,0:T(8,128)S(1)}, f32[8,64,128]{2,1,0:T(8,128)}, u32[]{:S(2)}, u32[]{:S(2)}) collective-permute-start(f32[8,64,128]{2,1,0:T(8,128)S(1)} %bitcast_multiply_fusion), channel_id=1, source_target_pairs={{0,1},{1,2},{2,3},{3,4},{4,5},{5,6},{6,7},{8,9},{9,10},{10,11},{11... | collective-permute-start | bytes 786440 | tf_op jit(solution)/shard_map/ppermute | solution.py:19
  78.3 3.7 %copy-start.22 = (s32[1,128]{1,0:T(1,128)S(1)}, s32[1,128]{1,0:T(1,128)}, u32[]{:S(2)}) copy-start(s32[1,128]{1,0:T(1,128)} %param.33) | copy-start | bytes 1540
  78.3 3.7 %copy-start.21 = (s32[1,128]{1,0:T(1,128)S(1)}, s32[1,128]{1,0:T(1,128)}, u32[]{:S(2)}) copy-start(s32[1,128]{1,0:T(1,128)} %param.34) | copy-start | bytes 1540
  78.4 4.6 %copy-start.19 = (s32[1,128]{1,0:T(1,128)S(1)}, s32[1,128]{1,0:T(1,128)}, u32[]{:S(2)}) copy-start(s32[1,128]{1,0:T(1,128)} %param.35) | copy-start | bytes 1540
  78.4 6.6 %copy-start.20 = (f32[1,16]{1,0:T(1,128)S(1)}, f32[1,16]{1,0:T(1,128)}, u32[]{:S(2)}) copy-start(f32[1,16]{1,0:T(1,128)} %param.28) | copy-start | bytes 196
  78.4 10.3 %copy-start.7 = (f32[1,8,64,128]{3,2,1,0:T(8,128)S(1)}, f32[1,8,64,128]{3,2,1,0:T(8,128)}, u32[]{:S(2)}) copy-start(f32[1,8,64,128]{3,2,1,0:T(8,128)} %param.19) | copy-start | bytes 786436
  79.4 14.0 %collective-permute-start.1 = (f32[4,4,64,128]{3,2,1,0:T(8,128)}, f32[4,4,64,128]{3,2,1,0:T(8,128)}, u32[]{:S(2)}, u32[]{:S(2)}) collective-permute-start(f32[4,4,64,128]{3,2,1,0:T(8,128)} %get-tuple-element.79), channel_id=1, source_target_pairs={{1,0},{2,1},{3,2},{4,3},{5,4},{6,5},{7,6},{9,8},{10,9},{11,10},{12... | collective-permute-start | bytes 1572872 | tf_op jit(solution)/shard_map/ppermute | solution.py:20
  85.6 7.8 %collective-permute-start = (f32[4,4,64,128]{3,2,1,0:T(8,128)S(1)}, f32[4,4,64,128]{3,2,1,0:T(8,128)S(1)}, u32[]{:S(2)}, u32[]{:S(2)}) collective-permute-start(f32[4,4,64,128]{3,2,1,0:T(8,128)S(1)} %get-tuple-element.78), channel_id=1, source_target_pairs={{0,1},{1,2},{2,3},{3,4},{4,5},{5,6},{6,7},{8,9},{9,10},{10,11},{11... | collective-permute-start | bytes 1572872 | tf_op jit(solution)/shard_map/ppermute | solution.py:19
  97.0 52.1 %copy-start.2 = (f32[16,64,128]{2,1,0:T(8,128)}, f32[16,64,128]{2,1,0:T(8,128)S(1)}, u32[]{:S(2)}) copy-start(f32[16,64,128]{2,1,0:T(8,128)S(1)} %get-tuple-element.59) | copy-start | bytes 1572868
  97.0 52.1 %copy-start.4 = (f32[16,64,128]{2,1,0:T(8,128)}, f32[16,64,128]{2,1,0:T(8,128)S(1)}, u32[]{:S(2)}) copy-start(f32[16,64,128]{2,1,0:T(8,128)S(1)} %get-tuple-element.60) | copy-start | bytes 1572868
  97.0 1.7 copy-start.1
  97.0 1.7 copy-start.14
  98.8 7.0 %copy-start.8 = (f32[1,8,64,128]{3,2,1,0:T(8,128)S(1)}, f32[1,8,64,128]{3,2,1,0:T(8,128)}, u32[]{:S(2)}) copy-start(f32[1,8,64,128]{3,2,1,0:T(8,128)} %param.19) | copy-start | bytes 786436
  98.8 7.0 %copy-start.15 = (f32[1,8,64,128]{3,2,1,0:T(8,128)S(1)}, f32[1,8,64,128]{3,2,1,0:T(8,128)}, u32[]{:S(2)}) copy-start(f32[1,8,64,128]{3,2,1,0:T(8,128)} %param.18) | copy-start | bytes 786436
  99.4 14.2 %collective-permute-start.5 = (f32[8,64,128]{2,1,0:T(8,128)S(1)}, f32[8,64,128]{2,1,0:T(8,128)S(1)}, u32[]{:S(2)}, u32[]{:S(2)}) collective-permute-start(f32[8,64,128]{2,1,0:T(8,128)S(1)} %get-tuple-element.42), channel_id=1, source_target_pairs={{1,0},{2,1},{3,2},{4,3},{5,4},{6,5},{7,6},{9,8},{10,9},{11,10},{12... | collective-permute-start | bytes 786440 | tf_op jit(solution)/shard_map/ppermute | solution.py:20
  100.7 12.9 %collective-permute-start.4 = (f32[8,64,128]{2,1,0:T(8,128)S(1)}, f32[8,64,128]{2,1,0:T(8,128)S(1)}, u32[]{:S(2)}, u32[]{:S(2)}) collective-permute-start(f32[8,64,128]{2,1,0:T(8,128)S(1)} %get-tuple-element.42), channel_id=1, source_target_pairs={{0,1},{1,2},{2,3},{3,4},{4,5},{5,6},{6,7},{8,9},{9,10},{10,11},{11... | collective-permute-start | bytes 786440 | tf_op jit(solution)/shard_map/ppermute | solution.py:19
  107.0 6.8 %collective-permute-start.13 = (f32[8,64,128]{2,1,0:T(8,128)S(1)}, f32[8,64,128]{2,1,0:T(8,128)S(1)}, u32[]{:S(2)}, u32[]{:S(2)}) collective-permute-start(f32[8,64,128]{2,1,0:T(8,128)S(1)} %get-tuple-element.21), channel_id=1, source_target_pairs={{1,0},{2,1},{3,2},{4,3},{5,4},{6,5},{7,6},{9,8},{10,9},{11,10},{12... | collective-permute-start | bytes 786440 | tf_op jit(solution)/shard_map/ppermute | solution.py:20
  108.3 6.2 %collective-permute-start.12 = (f32[8,64,128]{2,1,0:T(8,128)S(1)}, f32[8,64,128]{2,1,0:T(8,128)S(1)}, u32[]{:S(2)}, u32[]{:S(2)}) collective-permute-start(f32[8,64,128]{2,1,0:T(8,128)S(1)} %get-tuple-element.21), channel_id=1, source_target_pairs={{0,1},{1,2},{2,3},{3,4},{4,5},{5,6},{6,7},{8,9},{9,10},{10,11},{11... | collective-permute-start | bytes 786440 | tf_op jit(solution)/shard_map/ppermute | solution.py:19
  118.1 31.3 %copy-start.9 = (f32[8,64,128]{2,1,0:T(8,128)}, f32[8,64,128]{2,1,0:T(8,128)S(1)}, u32[]{:S(2)}) copy-start(f32[8,64,128]{2,1,0:T(8,128)S(1)} %get-tuple-element.37) | copy-start | bytes 786436
  118.1 15.4 %collective-permute-start.7 = (f32[8,64,128]{2,1,0:T(8,128)S(1)}, f32[8,64,128]{2,1,0:T(8,128)S(1)}, u32[]{:S(2)}, u32[]{:S(2)}) collective-permute-start(f32[8,64,128]{2,1,0:T(8,128)S(1)} %get-tuple-element.36), channel_id=1, source_target_pairs={{1,0},{2,1},{3,2},{4,3},{5,4},{6,5},{7,6},{9,8},{10,9},{11,10},{12... | collective-permute-start | bytes 786440 | tf_op jit(solution)/shard_map/ppermute | solution.py:20
  119.4 14.1 %collective-permute-start.6 = (f32[8,64,128]{2,1,0:T(8,128)S(1)}, f32[8,64,128]{2,1,0:T(8,128)S(1)}, u32[]{:S(2)}, u32[]{:S(2)}) collective-permute-start(f32[8,64,128]{2,1,0:T(8,128)S(1)} %get-tuple-element.36), channel_id=1, source_target_pairs={{0,1},{1,2},{2,3},{3,4},{4,5},{5,6},{6,7},{8,9},{9,10},{10,11},{11... | collective-permute-start | bytes 786440 | tf_op jit(solution)/shard_map/ppermute | solution.py:19
  127.1 6.6 %collective-permute-start.15 = (f32[8,64,128]{2,1,0:T(8,128)S(1)}, f32[8,64,128]{2,1,0:T(8,128)S(1)}, u32[]{:S(2)}, u32[]{:S(2)}) collective-permute-start(f32[8,64,128]{2,1,0:T(8,128)S(1)} %get-tuple-element.15), channel_id=1, source_target_pairs={{1,0},{2,1},{3,2},{4,3},{5,4},{6,5},{7,6},{9,8},{10,9},{11,10},{12... | collective-permute-start | bytes 786440 | tf_op jit(solution)/shard_map/ppermute | solution.py:20
  128.4 6.2 %collective-permute-start.14 = (f32[8,64,128]{2,1,0:T(8,128)S(1)}, f32[8,64,128]{2,1,0:T(8,128)S(1)}, u32[]{:S(2)}, u32[]{:S(2)}) collective-permute-start(f32[8,64,128]{2,1,0:T(8,128)S(1)} %get-tuple-element.15), channel_id=1, source_target_pairs={{0,1},{1,2},{2,3},{3,4},{4,5},{5,6},{6,7},{8,9},{9,10},{10,11},{11... | collective-permute-start | bytes 786440 | tf_op jit(solution)/shard_map/ppermute | solution.py:19
  138.8 8.1 %collective-permute-start.17 = (f32[8,64,128]{2,1,0:T(8,128)S(1)}, f32[8,64,128]{2,1,0:T(8,128)S(1)}, u32[]{:S(2)}, u32[]{:S(2)}) collective-permute-start(f32[8,64,128]{2,1,0:T(8,128)S(1)} %get-tuple-element.9), channel_id=1, source_target_pairs={{1,0},{2,1},{3,2},{4,3},{5,4},{6,5},{7,6},{9,8},{10,9},{11,10},{12... | collective-permute-start | bytes 786440 | tf_op jit(solution)/shard_map/ppermute | solution.py:20
  140.1 7.6 %collective-permute-start.16 = (f32[8,64,128]{2,1,0:T(8,128)S(1)}, f32[8,64,128]{2,1,0:T(8,128)S(1)}, u32[]{:S(2)}, u32[]{:S(2)}) collective-permute-start(f32[8,64,128]{2,1,0:T(8,128)S(1)} %get-tuple-element.9), channel_id=1, source_target_pairs={{0,1},{1,2},{2,3},{3,4},{4,5},{5,6},{6,7},{8,9},{9,10},{10,11},{11... | collective-permute-start | bytes 786440 | tf_op jit(solution)/shard_map/ppermute | solution.py:19
  151.2 0.7 copy-start.11
  151.9 12.9 %collective-permute-start.9 = (f32[8,64,128]{2,1,0:T(8,128)S(1)}, f32[8,64,128]{2,1,0:T(8,128)}, u32[]{:S(2)}, u32[]{:S(2)}) collective-permute-start(f32[8,64,128]{2,1,0:T(8,128)S(1)} %fusion.535), channel_id=1, source_target_pairs={{1,0},{2,1},{3,2},{4,3},{5,4},{6,5},{7,6},{9,8},{10,9},{11,10},{12... | collective-permute-start | bytes 786440 | tf_op jit(solution)/shard_map/ppermute | solution.py:20
  153.2 11.6 %collective-permute-start.8 = (f32[8,64,128]{2,1,0:T(8,128)S(1)}, f32[8,64,128]{2,1,0:T(8,128)}, u32[]{:S(2)}, u32[]{:S(2)}) collective-permute-start(f32[8,64,128]{2,1,0:T(8,128)S(1)} %fusion.535), channel_id=1, source_target_pairs={{0,1},{1,2},{2,3},{3,4},{4,5},{5,6},{6,7},{8,9},{9,10},{10,11},{11... | collective-permute-start | bytes 786440 | tf_op jit(solution)/shard_map/ppermute | solution.py:19
  167.1 1.2 copy-start.3
  167.1 1.2 copy-start.5
  168.3 1.0 copy-start.10
  168.3 1.0 copy-start.12
  168.4 1.1 copy-start.13
Sparse Core Ops, SparseCore 0:
  164.9 25.0 reduce-scatter.1
where the time goes:
time: 198 us; the launch traced here: 197 us
  starting transfers between devices  58.3 us (29%)
  blocking collectives  43.3 us (22%)
  other arithmetic  32.7 us (17%)
  waiting for transfers between devices  21.5 us (11%)
  local copies, waits for them, and re-layouts  20.8 us (11%)
  between operations  18.1 us (9%)
  matrix products  2.09 us (1%)
    ppermute x9, starting transfers between devices, padded_2(): before = lax.ppermute(last, axis, up)  46.5 us
    reduce_scatter x1, waiting for transfers between devices, on_device(): lax.psum_scatter(grad_slab, 'shot', scatter_dimension=1, tiled=True)  19.2 us
    all_gather x1, blocking collectives, on_device(): lax.all_gather(courant_sq, 'shot', axis=1, tiled=True)  13.1 us
    ppermute x9, starting transfers between devices, padded_2(): after = lax.ppermute(leading, axis, down)  11.7 us
    all_gather x1, blocking collectives, on_device(): lax.all_gather(epsilon, 'shot', axis=1, tiled=True)  11.2 us
    dynamic_update_slice x4, local copies, waits for them, and re-layouts, on_device(): spread = lax.dynamic_update_slice(spread, piece, (0, offset, 0))  10.1 us
    all_gather x1, blocking collectives, on_device(): lax.all_gather(azimuth, 'shot', axis=1, tiled=True)  9.84 us
    select_n x6, other arithmetic, operate_deep(): jnp.where(inside_rows, (1.0 + twice_eps) * slope_x - twice_eps * normal_x...  9.51 us
  transfers between devices with their start and end apart: 19, of which 4 were waited for; matrix products, arithmetic and copies ran while one was open for 19% of the time, Pallas kernels for 0%

commit v1 on v0

v1 whole, which is shorter than its diff:
```python
import functools

import jax
import jax.numpy as jnp
from jax import lax
from jax.experimental import pallas as pl
from jax.experimental.pallas import tpu as pltpu
from jax.sharding import PartitionSpec as P

STEPS = 4
COEF = (0.8, -0.2, 4.0 / 105.0, -1.0 / 280.0)
PAD = 8

VMEM = pl.BlockSpec(memory_space=pltpu.VMEM)
SMEM = pl.BlockSpec(memory_space=pltpu.SMEM)


def f32(*shape):
    return jax.ShapeDtypeStruct(shape, jnp.float32)


def call(body, outs, ins, scratch=(), cost=0):
    arrays = [a for a, _ in ins]
    return pl.pallas_call(
        body,
        out_shape=outs,
        in_specs=[s for _, s in ins],
        out_specs=jax.tree.map(lambda _: VMEM, outs),
        scratch_shapes=list(scratch),
        cost_estimate=pl.CostEstimate(flops=cost, bytes_accessed=1 << 20, transcendentals=0),
        compiler_params=pltpu.CompilerParams(vmem_limit_bytes=48 << 20),
    )(*arrays)


def depth_coefs(depth):
    lane = lax.broadcasted_iota(jnp.int32, (1, depth), 1)
    upper = [jnp.where(lane < depth - k, COEF[k - 1], 0.0) for k in range(1, 5)]
    lower = [jnp.where(lane >= k, COEF[k - 1], 0.0) for k in range(1, 5)]
    return upper, lower


def diff_z(tile, coefs):
    upper, lower = coefs
    depth = tile.shape[-1]
    summed = None
    for k in range(1, 5):
        term = upper[k - 1] * pltpu.roll(tile, depth - k, 1) - lower[k - 1] * pltpu.roll(tile, k, 1)
        summed = term if summed is None else summed + term
    return summed


def diff_rows(ref, row):
    summed = None
    for k in range(1, 5):
        term = COEF[k - 1] * (ref[row + k] - ref[row - k])
        summed = term if summed is None else summed + term
    return summed


def diff_y(ref, row, width):
    summed = None
    for k in range(1, 5):
        term = COEF[k - 1] * (
            ref[row, pl.ds(PAD + k, width), :] - ref[row, pl.ds(PAD - k, width), :]
        )
        summed = term if summed is None else summed + term
    return summed


def fill_field(own, partner, across, wide):
    rows, width, depth = own.shape
    odd = lax.axis_index("blk") % 2
    edge = jnp.zeros((3 * rows, PAD, depth), jnp.float32)
    wide[:, 0:PAD, :] = edge
    wide[:, PAD + width : 2 * PAD + width, :] = edge
    wide[rows : 2 * rows, PAD : PAD + width, :] = own[...]
    partner_at = jnp.where(odd == 1, 0, 2 * rows)
    across_at = jnp.where(odd == 1, 2 * rows, 0)
    wide[pl.ds(partner_at, rows), PAD : PAD + width, :] = partner[...]
    wide[pl.ds(across_at, rows), PAD : PAD + width, :] = across[...]


def apply_operator(wide, coef, flux_x, flux_y, part_z, finish):
    rows = part_z.shape[0]
    width, depth = part_z.shape[1], part_z.shape[2]
    coefs = depth_coefs(depth)
    edge = jnp.zeros((rows, PAD, depth), jnp.float32)
    flux_y[:, 0:PAD, :] = edge
    flux_y[:, PAD + width : 2 * PAD + width, :] = edge

    def slopes(i):
        slope_x = diff_rows_mid(wide, i + 4, width)
        slope_y = diff_y(wide, i + 4, width)
        slope_z = diff_z(wide[i + 4, PAD : PAD + width, :], coefs)
        along = coef[0, i] * slope_x + coef[1, i] * slope_y + coef[2, i] * slope_z
        flux_x[i] = coef[3, i] * slope_x - coef[0, i] * along
        return slope_y, slope_z, along

    def halo(i, _):
        slopes(i)
        slopes(i + rows + 4)
        return 0

    def inner(r, _):
        i = r + 4
        slope_y, slope_z, along = slopes(i)
        flux_y[r, PAD : PAD + width, :] = coef[3, i] * slope_y - coef[1, i] * along
        part_z[r] = diff_z(coef[3, i] * slope_z - coef[2, i] * along, coefs)
        return 0

    lax.fori_loop(0, 4, halo, 0)
    lax.fori_loop(0, rows, inner, 0)

    def last(r, _):
        finish(r, diff_rows(flux_x, r + 4) + diff_y(flux_y, r, width) + part_z[r])
        return 0

    lax.fori_loop(0, rows, last, 0)


def diff_rows_mid(ref, row, width):
    summed = None
    for k in range(1, 5):
        term = COEF[k - 1] * (
            ref[row + k, PAD : PAD + width, :] - ref[row - k, PAD : PAD + width, :]
        )
        summed = term if summed is None else summed + term
    return summed


def owner_kernel(speed, eps, tilt, azimuth, out):
    for r in range(speed.shape[0]):
        size = jnp.sqrt(2.0 * eps[r])
        flat = size * jnp.sin(tilt[r])
        out[0, r] = flat * jnp.cos(azimuth[r])
        out[1, r] = flat * jnp.sin(azimuth[r])
        out[2, r] = size * jnp.cos(tilt[r])
        out[3, r] = speed[r]


def prepare_kernel(step, sx, sy, sz, wavelet, rx, ry, rz, traces, src, inj):
    rows, width, depth = src.shape[1:]
    first = lax.axis_index("blk") * rows
    start = step[0]
    shape = (rows, width, depth)
    hit = (
        (lax.broadcasted_iota(jnp.int32, shape, 0) == sx[0] - first)
        & (lax.broadcasted_iota(jnp.int32, shape, 1) == sy[0])
        & (lax.broadcasted_iota(jnp.int32, shape, 2) == sz[0])
    )
    for t in range(STEPS - 1):
        src[t] = jnp.where(hit, wavelet[0, start + t], 0.0)
    receivers = rx.shape[1]
    local = rx[...] - first
    plane = jnp.where((local >= 0) & (local < rows), local * width + ry[...], -1)
    pick = (
        lax.broadcasted_iota(jnp.int32, (rows * width, receivers), 0) == plane
    ).astype(jnp.float32)
    match = lax.broadcasted_iota(jnp.int32, (depth, receivers), 0) == rz[...]
    for t in range(STEPS):
        samples = traces[0, pl.ds(start + t, 1), :]
        spread = jnp.where(match, samples, 0.0)
        added = lax.dot_general(
            pick,
            spread,
            (((1,), (1,)), ((), ())),
            precision=lax.Precision.HIGHEST,
            preferred_element_type=jnp.float32,
        )
        inj[t] = added.reshape(shape)


def window_kernel(shots, anchor, present, *refs):
    pieces = refs[:shots]
    tensor, speed, across, partner, operand = refs[shots:]
    rows, count, depth = pieces[0].shape[1:]
    parts = speed.shape[1] // count
    me = lax.axis_index("shot")
    first = anchor[0] // count
    for j in range(parts):
        place = slice(j * count, (j + 1) * count)
        slot = jnp.bitwise_xor(first + j, me)
        for k in range(shots):

            @pl.when(slot == k)
            def _():
                tensor[:, :, place, :] = pieces[k][0:3]
                speed[:, place, :] = pieces[k][3]

    odd = lax.axis_index("blk") % 2
    low = rows - 4
    across[...] = tensor[:, pl.ds(odd * low, 4)]
    partner[...] = tensor[:, pl.ds((1 - odd) * low, 4)]
    operand[...] = speed[...] * present[...]


def widen_coef(tensor, partner, across, coef):
    rows = tensor.shape[1]
    blk = lax.axis_index("blk")
    blocks = lax.axis_size("blk")
    odd = blk % 2
    coef[0:3, 4 : 4 + rows] = tensor[...]
    coef[0:3, pl.ds(jnp.where(odd == 1, 0, rows + 4), 4)] = partner[...]
    coef[0:3, pl.ds(jnp.where(odd == 1, rows + 4, 0), 4)] = across[...]
    for i in range(rows + 8):
        size = 1.0 + (coef[0, i] * coef[0, i] + coef[1, i] * coef[1, i] + coef[2, i] * coef[2, i])
        if i < 4:
            size = jnp.where(blk == 0, 0.0, size)
        if i >= rows + 4:
            size = jnp.where(blk == blocks - 1, 0.0, size)
        coef[3, i] = size


def forward_first(own, partner, across, tensor, tensor_p, tensor_a, previous, speed, src,
                  coef, image, following, wide, flux_x, flux_y, part_z):
    widen_coef(tensor, tensor_p, tensor_a, coef)
    forward(own, partner, across, coef, previous, speed, src, image, following,
            wide, flux_x, flux_y, part_z, t=0)


def forward(own, partner, across, coef, previous, speed, src, image, following,
            wide, flux_x, flux_y, part_z, t):
    fill_field(own, partner, across, wide)

    def finish(r, value):
        image[r] = value
        following[r] = 2.0 * own[r] - previous[r] + speed[r] * value + src[t, r]

    apply_operator(wide, coef, flux_x, flux_y, part_z, finish)


def backward(own, partner, across, coef, present, later, speed, inj, *rest, t):
    if t > 0:
        earlier, operand, wide, flux_x, flux_y, part_z = rest
    else:
        earlier, wide, flux_x, flux_y, part_z = rest
    fill_field(own, partner, across, wide)

    def finish(r, value):
        result = 2.0 * present[r] - later[r] + value + inj[t, r]
        earlier[r] = result
        if t > 0:
            operand[r] = speed[r] * result

    apply_operator(wide, coef, flux_x, flux_y, part_z, finish)


def forward_last(shots, anchor, own, partner, across, coef, *refs):
    adjoints = refs[:STEPS]
    images = refs[STEPS : 2 * STEPS - 1]
    out, wide, flux_x, flux_y, part_z, grad = refs[2 * STEPS - 1 :]
    count = out.shape[2]
    parts = grad.shape[1] // count
    fill_field(own, partner, across, wide)

    def finish(r, value):
        total = adjoints[STEPS - 1][r] * value
        for t in reversed(range(STEPS - 1)):
            total = total + adjoints[t][r] * images[t][r]
        grad[r] = total

    apply_operator(wide, coef, flux_x, flux_y, part_z, finish)
    me = lax.axis_index("shot")
    first = anchor[0] // count
    for k in range(shots):
        part = jnp.bitwise_xor(me, k) - first
        inside = (part >= 0) & (part < parts)
        at = pl.multiple_of(jnp.clip(part, 0, parts - 1) * count, 8)
        out[k] = jnp.where(inside, grad[:, pl.ds(at, count), :], 0.0)


def on_device(
    state_before,
    state_now,
    adjoint_later,
    adjoint_now,
    courant_sq,
    epsilon,
    tilt_angle,
    azimuth,
    aperture_anchor,
    step_index,
    wavelet,
    residual_traces,
    source_x,
    source_y,
    source_z,
    receiver_x,
    receiver_y,
    receiver_z,
):
    rows, width, depth = state_now.shape[1:]
    count = courant_sq.shape[1]
    shots = lax.axis_size("shot")
    blocks = lax.axis_size("blk")
    field = f32(rows, width, depth)
    core_pairs = [(i, i ^ 1) for i in range(blocks)]
    chip_pairs = [(i, i + 1) for i in range(1, blocks - 1, 2)]
    chip_pairs = chip_pairs + [(j, i) for i, j in chip_pairs]

    def halos(array):
        return (
            lax.ppermute(array, "blk", core_pairs),
            lax.ppermute(array, "blk", chip_pairs),
        )

    scratch = (
        pltpu.VMEM((3 * rows, width + 2 * PAD, depth), jnp.float32),
        pltpu.VMEM((rows + 8, width, depth), jnp.float32),
        pltpu.VMEM((rows, width + 2 * PAD, depth), jnp.float32),
        pltpu.VMEM((rows, width, depth), jnp.float32),
    )
    flops = 100 * (rows + 8) * width * depth

    own_piece = call(
        owner_kernel,
        f32(4, rows, count, depth),
        [(a, VMEM) for a in (courant_sq, epsilon, tilt_angle, azimuth)],
        cost=flops // 2,
    )
    pieces = [own_piece]
    for k in range(1, shots):
        pieces.append(lax.ppermute(own_piece, "shot", [(i, i ^ k) for i in range(shots)]))
    current = state_now[0]
    present = adjoint_now[0]
    now_p, now_a = halos(current)

    src, inj = call(
        prepare_kernel,
        (f32(STEPS - 1, rows, width, depth), f32(STEPS, rows, width, depth)),
        [(a, SMEM) for a in (step_index, source_x, source_y, source_z, wavelet)]
        + [(a, VMEM) for a in (receiver_x, receiver_y, receiver_z, residual_traces)],
        cost=flops,
    )
    edge = f32(3, 4, width, depth)
    tensor, speed, edge_a, edge_p, operand = call(
        functools.partial(window_kernel, shots),
        (f32(3, rows, width, depth), field, edge, edge, field),
        [(aperture_anchor, SMEM), (present, VMEM)] + [(a, VMEM) for a in pieces],
    )
    edge_a = lax.ppermute(edge_a, "blk", chip_pairs)
    edge_p = lax.ppermute(edge_p, "blk", core_pairs)
    op_p, op_a = halos(operand)

    coef, image, following = call(
        forward_first,
        (f32(4, rows + 8, width, depth), field, field),
        [
            (a, VMEM)
            for a in (current, now_p, now_a, tensor, edge_p, edge_a, state_before[0], speed, src)
        ],
        scratch,
        flops,
    )
    images = [image]
    previous, current = current, following
    adjoints = [present]
    later = adjoint_later[0]

    for t in range(STEPS - 1):
        now_p, now_a = halos(current)
        result = call(
            functools.partial(backward, t=STEPS - 1 - t),
            (field, field),
            [(a, VMEM) for a in (operand, op_p, op_a, coef, present, later, speed, inj)],
            scratch,
            flops,
        )
        later, present, operand = present, result[0], result[1]
        adjoints.append(present)
        op_p, op_a = halos(operand)
        if t < STEPS - 2:
            image, following = call(
                functools.partial(forward, t=t + 1),
                (field, field),
                [(a, VMEM) for a in (current, now_p, now_a, coef, previous, speed, src)],
                scratch,
                flops,
            )
            images.append(image)
            previous, current = current, following

    chunks = call(
        functools.partial(forward_last, shots),
        f32(shots, rows, count, depth),
        [(aperture_anchor, SMEM)]
        + [(a, VMEM) for a in (current, now_p, now_a, coef)]
        + [(a, VMEM) for a in adjoints[::-1]]
        + [(a, VMEM) for a in images],
        scratch + (pltpu.VMEM((rows, width, depth), jnp.float32),),
        flops,
    )
    received = [
        lax.ppermute(chunks[k], "shot", [(i, i ^ k) for i in range(shots)])
        for k in range(1, shots)
    ]
    (final,) = call(
        functools.partial(backward, t=0),
        (field,),
        [(a, VMEM) for a in (operand, op_p, op_a, coef, present, later, speed, inj)],
        scratch,
        flops,
    )
    model_grad = chunks[0]
    for piece in received:
        model_grad = model_grad + piece
    return (present[None], final[None], model_grad)


def solution(mesh):
    in_specs = (
        P("shot", "blk", None, None),
        P("shot", "blk", None, None),
        P("shot", "blk", None, None),
        P("shot", "blk", None, None),
        P("blk", "shot", None),
        P("blk", "shot", None),
        P("blk", "shot", None),
        P("blk", "shot", None),
        P("shot"),
        P(),
        P("shot", None),
        P("shot", None, None),
        P("shot"),
        P("shot"),
        P("shot"),
        P("shot", None),
        P("shot", None),
        P("shot", None),
    )
    out_specs = (P("shot", "blk", None, None), P("shot", "blk", None, None), P("blk", "shot", None))
    return jax.shard_map(
        on_device, mesh=mesh, in_specs=in_specs, out_specs=out_specs, check_vma=False
    )
```

time: 198 us -> 106 us (0.54)
  blocking collectives: 43.3 us -> 0 us
  Pallas kernels: 0 us -> 34.5 us
  other arithmetic: 32.7 us -> 0.69 us
  starting transfers between devices: 58.3 us -> 34.3 us
  between operations: 18.1 us -> 4.28 us
  local copies, waits for them, and re-layouts: 20.8 us -> 7.22 us
  waiting for transfers between devices: 21.5 us -> 24.1 us
  matrix products: 2.09 us -> 0 us
    all_gather x4 -> x0, blocking collectives: 43.3 us -> none  [the longest x1 13.1 us: on_device(): lax.all_gather(courant_sq, 'shot', axis=1, tiled=True)]
    pallas_call x0 -> x11, Pallas kernels: none -> 34.5 us  [call(): pl.pallas_call(body, out_shape=outs, in_specs=[s for _, s in ins], out_sp...]
    ppermute x18 -> x24, starting transfers between devices: 58.3 us -> 34.3 us  [the longest x8 19.9 us: halos(): lax.ppermute(array, 'blk', core_pairs)]
    ppermute x18 -> x24, waiting for transfers between devices: 2.25 us -> 24.1 us  [the longest x3 22.4 us: on_device(): lax.ppermute(own_piece, 'shot', [(i, i ^ k) for i in range(shots)])]
    reduce_scatter x1 -> x0, waiting for transfers between devices: 19.2 us -> none  [on_device(): lax.psum_scatter(grad_slab, 'shot', scatter_dimension=1, tiled=True)]
    dynamic_update_slice x5 -> x0, local copies, waits for them, and re-layouts: 11.9 us -> none  [the longest x4 10.1 us: on_device(): spread = lax.dynamic_update_slice(spread, piece, (0, offset, 0))]
    select_n x6 -> x0, other arithmetic: 9.51 us -> none  [operate_deep(): jnp.where(inside_rows, (1.0 + twice_eps) * slope_x - twice_eps * normal_x...]
    add x4 -> x1, other arithmetic: 5.79 us -> 0.69 us  [on_device(): model_grad = model_grad + piece]
  transfers between devices with their start and end apart: 19 -> 24, of which waited for: 4 -> 3; matrix products, arithmetic and copies ran while one was open for 19% -> 0% of each run, Pallas kernels for 0% -> 31%
where the time goes in v1:
time: 106 us; the launch traced here: 105 us
  Pallas kernels  34.5 us (33%)
  starting transfers between devices  34.3 us (32%)
  waiting for transfers between devices  24.1 us (23%)
  local copies, waits for them, and re-layouts  7.22 us (7%)
  between operations  4.28 us (4%)
    pallas_call x11, Pallas kernels, call(): pl.pallas_call(body, out_shape=outs, in_specs=[s for _, s in ins], out_sp...  34.5 us
    ppermute x3, waiting for transfers between devices, on_device(): lax.ppermute(own_piece, 'shot', [(i, i ^ k) for i in range(shots)])  22.4 us
    ppermute x8, starting transfers between devices, halos(): lax.ppermute(array, 'blk', core_pairs)  19.9 us
    unnamed x34, local copies, waits for them, and re-layouts  7.19 us
    ppermute x8, starting transfers between devices, halos(): lax.ppermute(array, 'blk', chip_pairs)  5.34 us
    ppermute x3, starting transfers between devices, on_device(): lax.ppermute(own_piece, 'shot', [(i, i ^ k) for i in range(shots)])  4.54 us
    ppermute x3, starting transfers between devices, on_device(): lax.ppermute(chunks[k], 'shot', [(i, i ^ k) for i in range(shots)])  3.55 us
  transfers between devices with their start and end apart: 24, of which 3 were waited for; matrix products, arithmetic and copies ran while one was open for 0% of the time, Pallas kernels for 31%

profile of v1, /device:TPU:0, one launch (start us, length us, event | category | flops | bytes accessed | tf_op | source)
XLA Modules:
  0.0 105.1 jit_solution(8657466746001359585)
XLA Ops:
  0.7 1.0 copy-done.8
  1.6 0.9 copy-done.9
  2.5 0.9 copy-done.10
  3.4 0.9 copy-done.11
  4.4 1.5 %shard_map.193.refs_0_ = f32[4,8,32,128]{3,2,1,0:T(8,128)S(1)} custom-call(f32[8,32,128]{2,1,0:T(8,128)S(1)} %copy-done.8, f32[8,32,128]{2,1,0:T(8,128)S(1)} %copy-done.9, f32[8,32,128]{2,1,0:T(8,128)S(1)} %copy-done.10, f32[8,32,128]{2,1,0:T(8,128)S(1)} %copy-done.11), custom_call_target="tpu_custom_call" | custom-call | flops 6553600 | bytes 1048576 | tf_op jit(solution)/shard_map/pallas_call | solution.py:24
  5.9 3.0 %collective-permute-start = (f32[4,8,32,128]{3,2,1,0:T(8,128)S(1)}, f32[4,8,32,128]{3,2,1,0:T(8,128)S(1)}, u32[]{:S(2)}, u32[]{:S(2)}) collective-permute-start(f32[4,8,32,128]{3,2,1,0:T(8,128)S(1)} %shard_map.193.refs_0_), channel_id=1, source_target_pairs={{0,8},{8,0},{16,24},{24,16},{1,9},{9,1},{17,25},{25,17},{2,10},{10... | collective-permute-start | bytes 1572872 | tf_op jit(solution)/shard_map/ppermute | solution.py:323
  8.9 1.5 %collective-permute-start.1 = (f32[4,8,32,128]{3,2,1,0:T(8,128)S(1)}, f32[4,8,32,128]{3,2,1,0:T(8,128)S(1)}, u32[]{:S(2)}, u32[]{:S(2)}) collective-permute-start(f32[4,8,32,128]{3,2,1,0:T(8,128)S(1)} %shard_map.193.refs_0_), channel_id=1, source_target_pairs={{0,16},{8,24},{16,0},{24,8},{1,17},{9,25},{17,1},{25,9},{2,18},{10... | collective-permute-start | bytes 1572872 | tf_op jit(solution)/shard_map/ppermute | solution.py:323
  10.4 0.0 collective-permute-start.2
  11.1 10.6 %collective-permute-done.refs_1_ = f32[4,8,32,128]{3,2,1,0:T(8,128)S(1)} collective-permute-done((f32[4,8,32,128]{3,2,1,0:T(8,128)S(1)}, f32[4,8,32,128]{3,2,1,0:T(8,128)S(1)}, u32[]{:S(2)}, u32[]{:S(2)}) %collective-permute-start) | collective-permute-done | bytes 524320 | tf_op jit(solution)/shard_map/ppermute | solution.py:323
  21.6 11.9 %collective-permute-done.1.refs_2_ = f32[4,8,32,128]{3,2,1,0:T(8,128)S(1)} collective-permute-done((f32[4,8,32,128]{3,2,1,0:T(8,128)S(1)}, f32[4,8,32,128]{3,2,1,0:T(8,128)S(1)}, u32[]{:S(2)}, u32[]{:S(2)}) %collective-permute-start.1) | collective-permute-done | bytes 524320 | tf_op jit(solution)/shard_map/ppermute | solution.py:323
  33.5 0.0 collective-permute-done.2.refs_3_
  33.5 0.9 copy-done.2
  34.5 0.2 shard_map.194
  34.6 0.0 copy-start.3
  34.7 0.0 copy-start.7
  34.7 0.1 collective-permute-start.7
  34.7 0.8 collective-permute-start.8
  35.6 3.0 %collective-permute-start.5 = (f32[8,64,128]{2,1,0:T(8,128)S(1)}, f32[8,64,128]{2,1,0:T(8,128)S(1)}, u32[]{:S(2)}, u32[]{:S(2)}) collective-permute-start(f32[8,64,128]{2,1,0:T(8,128)S(1)} %bitcast.24), channel_id=1, source_target_pairs={{0,1},{1,0},{2,3},{3,2},{4,5},{5,4},{6,7},{7,6},{8,9},{9,8},{10,11... | collective-permute-start | bytes 786440 | tf_op jit(solution)/shard_map/ppermute | solution.py:303
  38.6 0.7 collective-permute-start.6
  41.9 1.6 %shard_map.195 = (f32[3,8,64,128]{3,2,1,0:T(8,128)S(1)}, f32[4,8,64,128]{3,2,1,0:T(8,128)S(1)}) custom-call(s32[1]{0:T(128)S(6)} %copy.22.step, s32[1]{0:T(128)S(6)} %copy.23.sx, s32[1]{0:T(128)S(6)} %copy.24.sy, s32[1]{0:T(128)S(6)} %copy.25.sz, f32[1,16]{1,0:T(1,128)S(1)} %copy-done.13, s32[1,128]{1,0:T(1,128)S(1)} %copy-done.14, s32[1,128]{1,0:T(1,128)S(1)} %copy-done.15, ...), custom_call_target="tpu_custom_call" | custom-call | flops 13107200 | bytes 1048576 | tf_op jit(solution)/shard_map/pallas_call | solution.py:24
  43.5 3.0 %collective-permute-start.3 = (f32[8,64,128]{2,1,0:T(8,128)S(1)}, f32[8,64,128]{2,1,0:T(8,128)S(1)}, u32[]{:S(2)}, u32[]{:S(2)}) collective-permute-start(f32[8,64,128]{2,1,0:T(8,128)S(1)} %get-tuple-element.23.own), channel_id=1, source_target_pairs={{0,1},{1,0},{2,3},{3,2},{4,5},{5,4},{6,7},{7,6},{8,9},{9,8},{10,11... | collective-permute-start | bytes 786440 | tf_op jit(solution)/shard_map/ppermute | solution.py:303
  46.5 0.0 collective-permute-done.5.partner
  46.5 0.7 collective-permute-start.4
  47.1 0.0 collective-permute-done.6.across
  47.2 0.0 collective-permute-done.7.tensor_p
  47.2 0.0 collective-permute-done.8.tensor_a
  47.2 5.1 %shard_map.196 = (f32[4,16,64,128]{3,2,1,0:T(8,128)}, f32[8,64,128]{2,1,0:T(8,128)S(1)}, f32[8,64,128]{2,1,0:T(8,128)S(1)}) custom-call(f32[8,64,128]{2,1,0:T(8,128)S(1)} %bitcast.26, f32[8,64,128]{2,1,0:T(8,128)S(1)} %collective-permute-done.5.partner, f32[8,64,128]{2,1,0:T(8,128)S(1)} %collective-permute-done.6.across, ...), custom_call_target="tpu_custom_call" | custom-call | flops 13107200 | bytes 1048576 | tf_op jit(solution)/shard_map/pallas_call | solution.py:24
  52.2 2.9 %collective-permute-start.15 = (f32[8,64,128]{2,1,0:T(8,128)S(1)}, f32[8,64,128]{2,1,0:T(8,128)S(1)}, u32[]{:S(2)}, u32[]{:S(2)}) collective-permute-start(f32[8,64,128]{2,1,0:T(8,128)S(1)} %get-tuple-element.37.own.previous), channel_id=1, source_target_pairs={{0,1},{1,0},{2,3},{3,2},{4,5},{5,4},{6,7},{7,6},{8,9},{9,8},{10,11... | collective-permute-start | bytes 786440 | tf_op jit(solution)/shard_map/ppermute | solution.py:303
  55.2 0.7 collective-permute-start.16
  55.8 0.0 collective-permute-done.3.partner
  55.8 0.0 collective-permute-done.4.across
  55.9 1.6 %copy-done = f32[4,16,64,128]{3,2,1,0:T(8,128)S(1)} copy-done((f32[4,16,64,128]{3,2,1,0:T(8,128)S(1)}, f32[4,16,64,128]{3,2,1,0:T(8,128)}, u32[]{:S(2)}) %copy-start) | copy-done | bytes 2097176
  57.5 3.5 %shard_map.197 = (f32[8,64,128]{2,1,0:T(8,128)S(1)}, f32[8,64,128]{2,1,0:T(8,128)S(1)}) custom-call(f32[8,64,128]{2,1,0:T(8,128)S(1)} %get-tuple-element.23.own, f32[8,64,128]{2,1,0:T(8,128)S(1)} %collective-permute-done.3.partner, f32[8,64,128]{2,1,0:T(8,128)S(1)} %collective-permute-done.4.across, f32[4,16,64,128]{3,2,1,0:T(8,128)S(1)} %copy-done, ...), custom_call_target="tpu_custom_call" | custom-call | flops 13107200 | bytes 1048576 | tf_op jit(solution)/shard_map/pallas_call | solution.py:24
  61.0 0.7 collective-permute-start.10
  61.7 4.3 %collective-permute-start.9 = (f32[8,64,128]{2,1,0:T(8,128)S(1)}, f32[8,64,128]{2,1,0:T(8,128)S(1)}, u32[]{:S(2)}, u32[]{:S(2)}) collective-permute-start(f32[8,64,128]{2,1,0:T(8,128)S(1)} %get-tuple-element.31.own), channel_id=1, source_target_pairs={{0,1},{1,0},{2,3},{3,2},{4,5},{5,4},{6,7},{7,6},{8,9},{9,8},{10,11... | collective-permute-start | bytes 786440 | tf_op jit(solution)/shard_map/ppermute | solution.py:303
  66.0 0.0 collective-permute-done.15.partner
  66.0 3.5 %shard_map.201 = (f32[8,64,128]{2,1,0:T(8,128)S(1)}, f32[8,64,128]{2,1,0:T(8,128)S(1)}) custom-call(f32[8,64,128]{2,1,0:T(8,128)S(1)} %get-tuple-element.37.own.previous, f32[8,64,128]{2,1,0:T(8,128)S(1)} %collective-permute-done.15.partner, f32[8,64,128]{2,1,0:T(8,128)S(1)} %collective-permute-done.16.across, f32[4,16,64,128]{3,2,1,0:T(8,128)S(1)} %copy-done.1, ...), custom_call_target="tpu_custom_call" | custom-call | flops 13107200 | bytes 1048576 | tf_op jit(solution)/shard_map/pallas_call | solution.py:24
  69.5 0.1 collective-permute-start.17
  69.6 0.7 collective-permute-start.18
  70.3 0.0 collective-permute-done.10.across
  70.3 0.0 collective-permute-done.9.partner
  70.3 3.5 %shard_map.198 = (f32[8,64,128]{2,1,0:T(8,128)S(1)}, f32[8,64,128]{2,1,0:T(8,128)S(1)}) custom-call(f32[8,64,128]{2,1,0:T(8,128)S(1)} %get-tuple-element.31.own, f32[8,64,128]{2,1,0:T(8,128)S(1)} %collective-permute-done.9.partner, f32[8,64,128]{2,1,0:T(8,128)S(1)} %collective-permute-done.10.across, f32[4,16,64,128]{3,2,1,0:T(8,128)S(1)} %copy-done.1, ...), custom_call_target="tpu_custom_call" | custom-call | flops 13107200 | bytes 1048576 | tf_op jit(solution)/shard_map/pallas_call | solution.py:24
  73.8 2.2 %collective-permute-start.11 = (f32[8,64,128]{2,1,0:T(8,128)S(1)}, f32[8,64,128]{2,1,0:T(8,128)S(1)}, u32[]{:S(2)}, u32[]{:S(2)}) collective-permute-start(f32[8,64,128]{2,1,0:T(8,128)S(1)} %get-tuple-element.33.own), channel_id=1, source_target_pairs={{0,1},{1,0},{2,3},{3,2},{4,5},{5,4},{6,7},{7,6},{8,9},{9,8},{10,11... | collective-permute-start | bytes 786440 | tf_op jit(solution)/shard_map/ppermute | solution.py:303
  76.0 0.7 collective-permute-start.12
  76.7 0.0 collective-permute-done.18.across
  76.7 3.5 %shard_map.202 = (f32[8,64,128]{2,1,0:T(8,128)S(1)}, f32[8,64,128]{2,1,0:T(8,128)S(1)}) custom-call(f32[8,64,128]{2,1,0:T(8,128)S(1)} %get-tuple-element.38.own, f32[8,64,128]{2,1,0:T(8,128)S(1)} %collective-permute-done.17.partner, f32[8,64,128]{2,1,0:T(8,128)S(1)} %collective-permute-done.18.across, f32[4,16,64,128]{3,2,1,0:T(8,128)S(1)} %copy-done.1, ...), custom_call_target="tpu_custom_call" | custom-call | flops 13107200 | bytes 1048576 | tf_op jit(solution)/shard_map/pallas_call | solution.py:24
  80.2 2.7 %collective-permute-start.19 = (f32[8,64,128]{2,1,0:T(8,128)S(1)}, f32[8,64,128]{2,1,0:T(8,128)S(1)}, u32[]{:S(2)}, u32[]{:S(2)}) collective-permute-start(f32[8,64,128]{2,1,0:T(8,128)S(1)} %get-tuple-element.39.own), channel_id=1, source_target_pairs={{0,1},{1,0},{2,3},{3,2},{4,5},{5,4},{6,7},{7,6},{8,9},{9,8},{10,11... | collective-permute-start | bytes 786440 | tf_op jit(solution)/shard_map/ppermute | solution.py:303
  82.9 0.7 collective-permute-start.20
  83.6 0.0 collective-permute-done.11.partner
  83.6 4.2 %shard_map.199 = (f32[8,64,128]{2,1,0:T(8,128)}, f32[8,64,128]{2,1,0:T(8,128)S(1)}) custom-call(f32[8,64,128]{2,1,0:T(8,128)S(1)} %get-tuple-element.33.own, f32[8,64,128]{2,1,0:T(8,128)S(1)} %collective-permute-done.11.partner, f32[8,64,128]{2,1,0:T(8,128)S(1)} %collective-permute-done.12.across, f32[4,16,64,128]{3,2,1,0:T(8,128)S(1)} %copy-done.1, ...), custom_call_target="tpu_custom_call" | custom-call | flops 13107200 | bytes 1048576 | tf_op jit(solution)/shard_map/pallas_call | solution.py:24
  87.8 1.8 %collective-permute-start.13 = (f32[8,64,128]{2,1,0:T(8,128)S(1)}, f32[8,64,128]{2,1,0:T(8,128)S(1)}, u32[]{:S(2)}, u32[]{:S(2)}) collective-permute-start(f32[8,64,128]{2,1,0:T(8,128)S(1)} %get-tuple-element.36.own), channel_id=1, source_target_pairs={{0,1},{1,0},{2,3},{3,2},{4,5},{5,4},{6,7},{7,6},{8,9},{9,8},{10,11... | collective-permute-start | bytes 786440 | tf_op jit(solution)/shard_map/ppermute | solution.py:303
  89.6 0.7 collective-permute-start.14
  90.3 0.0 collective-permute-done.19.partner
  90.3 0.0 collective-permute-done.20.across
  90.3 0.0 copy-start.5
  90.3 0.9 copy-done.5
  91.3 3.7 %shard_map.203 = f32[4,8,32,128]{3,2,1,0:T(8,128)S(1)} custom-call(s32[1]{0:T(128)S(6)} %copy.21.anchor, f32[8,64,128]{2,1,0:T(8,128)S(1)} %get-tuple-element.39.own, f32[8,64,128]{2,1,0:T(8,128)S(1)} %collective-permute-done.19.partner, f32[8,64,128]{2,1,0:T(8,128)S(1)} %collective-permute-done.20.across, f32[4,16,64,128]{3,2,1,0:T(8,128)S(1)} %copy-done.1, ...), custom_call_target="tpu_custom_call" | custom-call | flops 13107200 | bytes 1048576 | tf_op jit(solution)/shard_map/pallas_call | solution.py:24
  95.0 1.3 %collective-permute-start.21 = (f32[8,32,128]{2,1,0:T(8,128)S(1)}, f32[8,32,128]{2,1,0:T(8,128)S(1)}, u32[]{:S(2)}, u32[]{:S(2)}) collective-permute-start(f32[8,32,128]{2,1,0:T(8,128)S(1)} %get-tuple-element.43), channel_id=1, source_target_pairs={{0,8},{8,0},{16,24},{24,16},{1,9},{9,1},{17,25},{25,17},{2,10},{10... | collective-permute-start | bytes 393224 | tf_op jit(solution)/shard_map/ppermute | solution.py:394
  96.3 0.8 collective-permute-start.22
  97.1 1.4 %collective-permute-start.23 = (f32[8,32,128]{2,1,0:T(8,128)S(1)}, f32[8,32,128]{2,1,0:T(8,128)S(1)}, u32[]{:S(2)}, u32[]{:S(2)}) collective-permute-start(f32[8,32,128]{2,1,0:T(8,128)S(1)} %get-tuple-element.44), channel_id=1, source_target_pairs={{0,24},{8,16},{16,8},{24,0},{1,25},{9,17},{17,9},{25,1},{2,26},{10... | collective-permute-start | bytes 393224 | tf_op jit(solution)/shard_map/ppermute | solution.py:394
  98.5 4.2 %shard_map.200 = f32[8,64,128]{2,1,0:T(8,128)} custom-call(f32[8,64,128]{2,1,0:T(8,128)S(1)} %get-tuple-element.36.own, f32[8,64,128]{2,1,0:T(8,128)S(1)} %collective-permute-done.13.partner, f32[8,64,128]{2,1,0:T(8,128)S(1)} %collective-permute-done.14.across, f32[4,16,64,128]{3,2,1,0:T(8,128)S(1)} %copy-done.1, f32[8,64,128]{2,1,0:T(8,128)S(1)} %copy-done.5, ...), custom_call_target="tpu_custom_call" | custom-call | flops 13107200 | bytes 1048576 | tf_op jit(solution)/shard_map/pallas_call | solution.py:24
  102.8 0.0 collective-permute-done.21
  102.8 1.6 %collective-permute-done.23 = f32[8,32,128]{2,1,0:T(8,128)S(1)} collective-permute-done((f32[8,32,128]{2,1,0:T(8,128)S(1)}, f32[8,32,128]{2,1,0:T(8,128)S(1)}, u32[]{:S(2)}, u32[]{:S(2)}) %collective-permute-start.23) | collective-permute-done | bytes 131104 | tf_op jit(solution)/shard_map/ppermute | solution.py:394
  104.4 0.7 fusion.2
  (31 shorter events, 0.1 us)
Async XLA Ops:
  0.6 34.9 %copy-start.4 = (f32[1,8,64,128]{3,2,1,0:T(8,128)S(1)}, f32[1,8,64,128]{3,2,1,0:T(8,128)}, u32[]{:S(2)}) copy-start(f32[1,8,64,128]{3,2,1,0:T(8,128)} %param.19) | copy-start | bytes 786436
  0.6 46.5 %copy-start.6 = (f32[1,8,64,128]{3,2,1,0:T(8,128)S(1)}, f32[1,8,64,128]{3,2,1,0:T(8,128)}, u32[]{:S(2)}) copy-start(f32[1,8,64,128]{3,2,1,0:T(8,128)} %param.18) | copy-start | bytes 786436
  0.7 1.0 copy-start.8
  1.6 0.9 copy-start.9
  2.5 0.9 copy-start.10
  3.4 0.9 copy-start.11
  4.3 37.5 %copy-start.12 = (f32[1,16,128]{2,1,0:T(8,128)S(1)}, f32[1,16,128]{2,1,0:T(8,128)}, u32[]{:S(2)}) copy-start(f32[1,16,128]{2,1,0:T(8,128)} %traces.1) | copy-start | bytes 24580
  4.3 37.5 %copy-start.13 = (f32[1,16]{1,0:T(1,128)S(1)}, f32[1,16]{1,0:T(1,128)}, u32[]{:S(2)}) copy-start(f32[1,16]{1,0:T(1,128)} %wavelet.1) | copy-start | bytes 196
  4.3 37.5 %copy-start.14 = (s32[1,128]{1,0:T(1,128)S(1)}, s32[1,128]{1,0:T(1,128)}, u32[]{:S(2)}) copy-start(s32[1,128]{1,0:T(1,128)} %rx.1) | copy-start | bytes 1540
  4.3 37.5 %copy-start.15 = (s32[1,128]{1,0:T(1,128)S(1)}, s32[1,128]{1,0:T(1,128)}, u32[]{:S(2)}) copy-start(s32[1,128]{1,0:T(1,128)} %ry.1) | copy-start | bytes 1540
  4.3 37.5 %copy-start.16 = (s32[1,128]{1,0:T(1,128)S(1)}, s32[1,128]{1,0:T(1,128)}, u32[]{:S(2)}) copy-start(s32[1,128]{1,0:T(1,128)} %rz.1) | copy-start | bytes 1540
  5.9 15.8 %collective-permute-start = (f32[4,8,32,128]{3,2,1,0:T(8,128)S(1)}, f32[4,8,32,128]{3,2,1,0:T(8,128)S(1)}, u32[]{:S(2)}, u32[]{:S(2)}) collective-permute-start(f32[4,8,32,128]{3,2,1,0:T(8,128)S(1)} %shard_map.193.refs_0_), channel_id=1, source_target_pairs={{0,8},{8,0},{16,24},{24,16},{1,9},{9,1},{17,25},{25,17},{2,10},{10... | collective-permute-start | bytes 1572872 | tf_op jit(solution)/shard_map/ppermute | solution.py:323
  8.9 24.6 %collective-permute-start.1 = (f32[4,8,32,128]{3,2,1,0:T(8,128)S(1)}, f32[4,8,32,128]{3,2,1,0:T(8,128)S(1)}, u32[]{:S(2)}, u32[]{:S(2)}) collective-permute-start(f32[4,8,32,128]{3,2,1,0:T(8,128)S(1)} %shard_map.193.refs_0_), channel_id=1, source_target_pairs={{0,16},{8,24},{16,0},{24,8},{1,17},{9,25},{17,1},{25,9},{2,18},{10... | collective-permute-start | bytes 1572872 | tf_op jit(solution)/shard_map/ppermute | solution.py:323
  10.4 23.1 %collective-permute-start.2 = (f32[4,8,32,128]{3,2,1,0:T(8,128)S(1)}, f32[4,8,32,128]{3,2,1,0:T(8,128)S(1)}, u32[]{:S(2)}, u32[]{:S(2)}) collective-permute-start(f32[4,8,32,128]{3,2,1,0:T(8,128)S(1)} %shard_map.193.refs_0_), channel_id=1, source_target_pairs={{0,24},{8,16},{16,8},{24,0},{1,25},{9,17},{17,9},{25,1},{2,26},{10... | collective-permute-start | bytes 1572872 | tf_op jit(solution)/shard_map/ppermute | solution.py:323
  33.5 1.0 copy-start.2
  34.6 21.2 %copy-start.3 = (f32[1,8,64,128]{3,2,1,0:T(8,128)S(1)}, f32[1,8,64,128]{3,2,1,0:T(8,128)}, u32[]{:S(2)}) copy-start(f32[1,8,64,128]{3,2,1,0:T(8,128)} %param.21) | copy-start | bytes 786436
  34.7 21.2 %copy-start.7 = (f32[1,8,64,128]{3,2,1,0:T(8,128)S(1)}, f32[1,8,64,128]{3,2,1,0:T(8,128)}, u32[]{:S(2)}) copy-start(f32[1,8,64,128]{3,2,1,0:T(8,128)} %param.20) | copy-start | bytes 786436
  34.7 12.5 %collective-permute-start.7 = (f32[3,4,64,128]{3,2,1,0:T(8,128)S(1)}, f32[3,4,64,128]{3,2,1,0:T(8,128)S(1)}, u32[]{:S(2)}, u32[]{:S(2)}) collective-permute-start(f32[3,4,64,128]{3,2,1,0:T(8,128)S(1)} %get-tuple-element.25), channel_id=1, source_target_pairs={{0,1},{1,0},{2,3},{3,2},{4,5},{5,4},{6,7},{7,6},{8,9},{9,8},{10,11... | collective-permute-start | bytes 1179656 | tf_op jit(solution)/shard_map/ppermute | solution.py:342
  34.7 12.4 %collective-permute-start.8 = (f32[3,4,64,128]{3,2,1,0:T(8,128)S(1)}, f32[3,4,64,128]{3,2,1,0:T(8,128)S(1)}, u32[]{:S(2)}, u32[]{:S(2)}) collective-permute-start(f32[3,4,64,128]{3,2,1,0:T(8,128)S(1)} %get-tuple-element.26), channel_id=1, source_target_pairs={{1,2},{3,4},{5,6},{2,1},{4,3},{6,5},{9,10},{11,12},{13,14},{10,9},... | collective-permute-start | bytes 1179656 | tf_op jit(solution)/shard_map/ppermute | solution.py:341
  35.6 10.9 %collective-permute-start.5 = (f32[8,64,128]{2,1,0:T(8,128)S(1)}, f32[8,64,128]{2,1,0:T(8,128)S(1)}, u32[]{:S(2)}, u32[]{:S(2)}) collective-permute-start(f32[8,64,128]{2,1,0:T(8,128)S(1)} %bitcast.24), channel_id=1, source_target_pairs={{0,1},{1,0},{2,3},{3,2},{4,5},{5,4},{6,7},{7,6},{8,9},{9,8},{10,11... | collective-permute-start | bytes 786440 | tf_op jit(solution)/shard_map/ppermute | solution.py:303
  38.6 8.6 %collective-permute-start.6 = (f32[8,64,128]{2,1,0:T(8,128)S(1)}, f32[8,64,128]{2,1,0:T(8,128)S(1)}, u32[]{:S(2)}, u32[]{:S(2)}) collective-permute-start(f32[8,64,128]{2,1,0:T(8,128)S(1)} %bitcast.25), channel_id=1, source_target_pairs={{1,2},{3,4},{5,6},{2,1},{4,3},{6,5},{9,10},{11,12},{13,14},{10,9},... | collective-permute-start | bytes 786440 | tf_op jit(solution)/shard_map/ppermute | solution.py:304
  43.5 12.4 %collective-permute-start.3 = (f32[8,64,128]{2,1,0:T(8,128)S(1)}, f32[8,64,128]{2,1,0:T(8,128)S(1)}, u32[]{:S(2)}, u32[]{:S(2)}) collective-permute-start(f32[8,64,128]{2,1,0:T(8,128)S(1)} %get-tuple-element.23.own), channel_id=1, source_target_pairs={{0,1},{1,0},{2,3},{3,2},{4,5},{5,4},{6,7},{7,6},{8,9},{9,8},{10,11... | collective-permute-start | bytes 786440 | tf_op jit(solution)/shard_map/ppermute | solution.py:303
  46.5 9.4 %collective-permute-start.4 = (f32[8,64,128]{2,1,0:T(8,128)S(1)}, f32[8,64,128]{2,1,0:T(8,128)S(1)}, u32[]{:S(2)}, u32[]{:S(2)}) collective-permute-start(f32[8,64,128]{2,1,0:T(8,128)S(1)} %get-tuple-element.23.own), channel_id=1, source_target_pairs={{1,2},{3,4},{5,6},{2,1},{4,3},{6,5},{9,10},{11,12},{13,14},{10,9},... | collective-permute-start | bytes 786440 | tf_op jit(solution)/shard_map/ppermute | solution.py:304
  52.2 13.7 %collective-permute-start.15 = (f32[8,64,128]{2,1,0:T(8,128)S(1)}, f32[8,64,128]{2,1,0:T(8,128)S(1)}, u32[]{:S(2)}, u32[]{:S(2)}) collective-permute-start(f32[8,64,128]{2,1,0:T(8,128)S(1)} %get-tuple-element.37.own.previous), channel_id=1, source_target_pairs={{0,1},{1,0},{2,3},{3,2},{4,5},{5,4},{6,7},{7,6},{8,9},{9,8},{10,11... | collective-permute-start | bytes 786440 | tf_op jit(solution)/shard_map/ppermute | solution.py:303
  55.2 10.8 %collective-permute-start.16 = (f32[8,64,128]{2,1,0:T(8,128)S(1)}, f32[8,64,128]{2,1,0:T(8,128)S(1)}, u32[]{:S(2)}, u32[]{:S(2)}) collective-permute-start(f32[8,64,128]{2,1,0:T(8,128)S(1)} %get-tuple-element.37.own.previous), channel_id=1, source_target_pairs={{1,2},{3,4},{5,6},{2,1},{4,3},{6,5},{9,10},{11,12},{13,14},{10,9},... | collective-permute-start | bytes 786440 | tf_op jit(solution)/shard_map/ppermute | solution.py:304
  55.9 1.6 %copy-start = (f32[4,16,64,128]{3,2,1,0:T(8,128)S(1)}, f32[4,16,64,128]{3,2,1,0:T(8,128)}, u32[]{:S(2)}) copy-start(f32[4,16,64,128]{3,2,1,0:T(8,128)} %get-tuple-element.29.coef) | copy-start | bytes 6291460
  57.5 8.5 %copy-start.1 = (f32[4,16,64,128]{3,2,1,0:T(8,128)S(1)}, f32[4,16,64,128]{3,2,1,0:T(8,128)}, u32[]{:S(2)}) copy-start(f32[4,16,64,128]{3,2,1,0:T(8,128)} %get-tuple-element.29.coef) | copy-start | bytes 6291460
  61.0 9.3 %collective-permute-start.10 = (f32[8,64,128]{2,1,0:T(8,128)S(1)}, f32[8,64,128]{2,1,0:T(8,128)S(1)}, u32[]{:S(2)}, u32[]{:S(2)}) collective-permute-start(f32[8,64,128]{2,1,0:T(8,128)S(1)} %get-tuple-element.31.own), channel_id=1, source_target_pairs={{1,2},{3,4},{5,6},{2,1},{4,3},{6,5},{9,10},{11,12},{13,14},{10,9},... | collective-permute-start | bytes 786440 | tf_op jit(solution)/shard_map/ppermute | solution.py:304
  61.7 8.6 %collective-permute-start.9 = (f32[8,64,128]{2,1,0:T(8,128)S(1)}, f32[8,64,128]{2,1,0:T(8,128)S(1)}, u32[]{:S(2)}, u32[]{:S(2)}) collective-permute-start(f32[8,64,128]{2,1,0:T(8,128)S(1)} %get-tuple-element.31.own), channel_id=1, source_target_pairs={{0,1},{1,0},{2,3},{3,2},{4,5},{5,4},{6,7},{7,6},{8,9},{9,8},{10,11... | collective-permute-start | bytes 786440 | tf_op jit(solution)/shard_map/ppermute | solution.py:303
  69.5 7.2 %collective-permute-start.17 = (f32[8,64,128]{2,1,0:T(8,128)S(1)}, f32[8,64,128]{2,1,0:T(8,128)S(1)}, u32[]{:S(2)}, u32[]{:S(2)}) collective-permute-start(f32[8,64,128]{2,1,0:T(8,128)S(1)} %get-tuple-element.38.own), channel_id=1, source_target_pairs={{0,1},{1,0},{2,3},{3,2},{4,5},{5,4},{6,7},{7,6},{8,9},{9,8},{10,11... | collective-permute-start | bytes 786440 | tf_op jit(solution)/shard_map/ppermute | solution.py:303
  69.6 7.1 %collective-permute-start.18 = (f32[8,64,128]{2,1,0:T(8,128)S(1)}, f32[8,64,128]{2,1,0:T(8,128)S(1)}, u32[]{:S(2)}, u32[]{:S(2)}) collective-permute-start(f32[8,64,128]{2,1,0:T(8,128)S(1)} %get-tuple-element.38.own), channel_id=1, source_target_pairs={{1,2},{3,4},{5,6},{2,1},{4,3},{6,5},{9,10},{11,12},{13,14},{10,9},... | collective-permute-start | bytes 786440 | tf_op jit(solution)/shard_map/ppermute | solution.py:304
  73.8 9.8 %collective-permute-start.11 = (f32[8,64,128]{2,1,0:T(8,128)S(1)}, f32[8,64,128]{2,1,0:T(8,128)S(1)}, u32[]{:S(2)}, u32[]{:S(2)}) collective-permute-start(f32[8,64,128]{2,1,0:T(8,128)S(1)} %get-tuple-element.33.own), channel_id=1, source_target_pairs={{0,1},{1,0},{2,3},{3,2},{4,5},{5,4},{6,7},{7,6},{8,9},{9,8},{10,11... | collective-permute-start | bytes 786440 | tf_op jit(solution)/shard_map/ppermute | solution.py:303
  76.0 7.6 %collective-permute-start.12 = (f32[8,64,128]{2,1,0:T(8,128)S(1)}, f32[8,64,128]{2,1,0:T(8,128)S(1)}, u32[]{:S(2)}, u32[]{:S(2)}) collective-permute-start(f32[8,64,128]{2,1,0:T(8,128)S(1)} %get-tuple-element.33.own), channel_id=1, source_target_pairs={{1,2},{3,4},{5,6},{2,1},{4,3},{6,5},{9,10},{11,12},{13,14},{10,9},... | collective-permute-start | bytes 786440 | tf_op jit(solution)/shard_map/ppermute | solution.py:304
  80.2 10.1 %collective-permute-start.19 = (f32[8,64,128]{2,1,0:T(8,128)S(1)}, f32[8,64,128]{2,1,0:T(8,128)S(1)}, u32[]{:S(2)}, u32[]{:S(2)}) collective-permute-start(f32[8,64,128]{2,1,0:T(8,128)S(1)} %get-tuple-element.39.own), channel_id=1, source_target_pairs={{0,1},{1,0},{2,3},{3,2},{4,5},{5,4},{6,7},{7,6},{8,9},{9,8},{10,11... | collective-permute-start | bytes 786440 | tf_op jit(solution)/shard_map/ppermute | solution.py:303
  82.9 7.4 %collective-permute-start.20 = (f32[8,64,128]{2,1,0:T(8,128)S(1)}, f32[8,64,128]{2,1,0:T(8,128)S(1)}, u32[]{:S(2)}, u32[]{:S(2)}) collective-permute-start(f32[8,64,128]{2,1,0:T(8,128)S(1)} %get-tuple-element.39.own), channel_id=1, source_target_pairs={{1,2},{3,4},{5,6},{2,1},{4,3},{6,5},{9,10},{11,12},{13,14},{10,9},... | collective-permute-start | bytes 786440 | tf_op jit(solution)/shard_map/ppermute | solution.py:304
  87.8 10.7 %collective-permute-start.13 = (f32[8,64,128]{2,1,0:T(8,128)S(1)}, f32[8,64,128]{2,1,0:T(8,128)S(1)}, u32[]{:S(2)}, u32[]{:S(2)}) collective-permute-start(f32[8,64,128]{2,1,0:T(8,128)S(1)} %get-tuple-element.36.own), channel_id=1, source_target_pairs={{0,1},{1,0},{2,3},{3,2},{4,5},{5,4},{6,7},{7,6},{8,9},{9,8},{10,11... | collective-permute-start | bytes 786440 | tf_op jit(solution)/shard_map/ppermute | solution.py:303
  89.6 8.9 %collective-permute-start.14 = (f32[8,64,128]{2,1,0:T(8,128)S(1)}, f32[8,64,128]{2,1,0:T(8,128)S(1)}, u32[]{:S(2)}, u32[]{:S(2)}) collective-permute-start(f32[8,64,128]{2,1,0:T(8,128)S(1)} %get-tuple-element.36.own), channel_id=1, source_target_pairs={{1,2},{3,4},{5,6},{2,1},{4,3},{6,5},{9,10},{11,12},{13,14},{10,9},... | collective-permute-start | bytes 786440 | tf_op jit(solution)/shard_map/ppermute | solution.py:304
  90.3 1.0 copy-start.5
  95.0 7.8 %collective-permute-start.21 = (f32[8,32,128]{2,1,0:T(8,128)S(1)}, f32[8,32,128]{2,1,0:T(8,128)S(1)}, u32[]{:S(2)}, u32[]{:S(2)}) collective-permute-start(f32[8,32,128]{2,1,0:T(8,128)S(1)} %get-tuple-element.43), channel_id=1, source_target_pairs={{0,8},{8,0},{16,24},{24,16},{1,9},{9,1},{17,25},{25,17},{2,10},{10... | collective-permute-start | bytes 393224 | tf_op jit(solution)/shard_map/ppermute | solution.py:394
  96.3 6.5 %collective-permute-start.22 = (f32[8,32,128]{2,1,0:T(8,128)S(1)}, f32[8,32,128]{2,1,0:T(8,128)S(1)}, u32[]{:S(2)}, u32[]{:S(2)}) collective-permute-start(f32[8,32,128]{2,1,0:T(8,128)S(1)} %get-tuple-element.45), channel_id=1, source_target_pairs={{0,16},{8,24},{16,0},{24,8},{1,17},{9,25},{17,1},{25,9},{2,18},{10... | collective-permute-start | bytes 393224 | tf_op jit(solution)/shard_map/ppermute | solution.py:394
  97.1 7.3 %collective-permute-start.23 = (f32[8,32,128]{2,1,0:T(8,128)S(1)}, f32[8,32,128]{2,1,0:T(8,128)S(1)}, u32[]{:S(2)}, u32[]{:S(2)}) collective-permute-start(f32[8,32,128]{2,1,0:T(8,128)S(1)} %get-tuple-element.44), channel_id=1, source_target_pairs={{0,24},{8,16},{16,8},{24,0},{1,25},{9,17},{17,9},{25,1},{2,26},{10... | collective-permute-start | bytes 393224 | tf_op jit(solution)/shard_map/ppermute | solution.py:394

commit v2 on v1

v2 whole, which is shorter than its diff:
```python
import functools

import jax
import jax.numpy as jnp
from jax import lax
from jax.experimental import pallas as pl
from jax.experimental.pallas import tpu as pltpu
from jax.sharding import PartitionSpec as P

STEPS = 4
COEF = (0.8, -0.2, 4.0 / 105.0, -1.0 / 280.0)
WHOLE = (672.0, -168.0, 32.0, -3.0)
UNIT = 1.0 / 840.0
PAD = 8

VMEM = pl.BlockSpec(memory_space=pltpu.VMEM)
SMEM = pl.BlockSpec(memory_space=pltpu.SMEM)
HBM = pl.BlockSpec(memory_space=pl.ANY)


def f32(*shape):
    return jax.ShapeDtypeStruct(shape, jnp.float32)


def call(name, body, outs, ins, scratch=(), flops=1 << 20):
    pairs = [a if isinstance(a, tuple) else (a, VMEM) for a in ins]
    return pl.pallas_call(
        body,
        name=name,
        out_shape=outs,
        in_specs=[s for _, s in pairs],
        out_specs=jax.tree.map(lambda _: VMEM, outs),
        scratch_shapes=list(scratch),
        cost_estimate=pl.CostEstimate(flops=flops, bytes_accessed=1 << 20, transcendentals=0),
        compiler_params=pltpu.CompilerParams(vmem_limit_bytes=48 << 20),
    )(*[a for a, _ in pairs])


def stencil(pick):
    summed = None
    for k in range(1, 5):
        term = COEF[k - 1] * (pick(k) - pick(-k))
        summed = term if summed is None else summed + term
    return summed


def diff_y(ref, row, width):
    return stencil(lambda k: ref[row, PAD + k : PAD + k + width, :])


def diff_z(tile, matrix):
    high = tile.astype(jnp.bfloat16)
    low = (tile - high.astype(jnp.float32)).astype(jnp.bfloat16)
    both = jnp.concatenate([high, low], axis=-1)
    return jnp.dot(both, matrix[...], preferred_element_type=jnp.float32) * UNIT


def place_halos(wide, lane, own, partner, across):
    rows, depth_rows = own.shape[0], partner.shape[0]
    blk, blocks = lax.axis_index("blk"), lax.axis_size("blk")
    odd = blk % 2
    outside = (blk == 0) | (blk == blocks - 1)
    above = depth_rows + rows
    wide[(slice(depth_rows, above), *lane)] = own[...]
    wide[(pl.ds(jnp.where(odd == 1, 0, above), depth_rows), *lane)] = partner[...]
    wide[(pl.ds(jnp.where(odd == 1, above, 0), depth_rows), *lane)] = jnp.where(
        outside, 0.0, across[...]
    )


def fill_field(own, partner, across, wide):
    rows, width, depth = own.shape
    edge = jnp.zeros((3 * rows, PAD, depth), jnp.float32)
    wide[:, 0:PAD, :] = edge
    wide[:, PAD + width : 2 * PAD + width, :] = edge
    place_halos(wide, (slice(PAD, PAD + width), slice(None)), own, partner, across)


def slopes_at(wide, i, width, matrix):
    inner = slice(PAD, PAD + width)
    return (
        stencil(lambda k: wide[i + k, inner, :]),
        diff_y(wide, i, width),
        diff_z(wide[i, inner, :], matrix),
    )


def clear_sides(flux_y, width):
    rows, _, depth = flux_y.shape
    edge = jnp.zeros((rows, PAD, depth), jnp.float32)
    flux_y[:, 0:PAD, :] = edge
    flux_y[:, PAD + width : 2 * PAD + width, :] = edge


def apply_operator(wide, coef, matrix, flux_x, flux_y, part_z, finish):
    rows, width, _ = part_z.shape
    clear_sides(flux_y, width)
    for i in range(rows + 8):
        slope_x, slope_y, slope_z = slopes_at(wide, i + 4, width, matrix)
        along = coef[0, i] * slope_x + coef[1, i] * slope_y + coef[2, i] * slope_z
        flux_x[i] = coef[3, i] * slope_x - coef[0, i] * along
        r = i - 4
        if 0 <= r < rows:
            flux_y[r, PAD : PAD + width, :] = coef[3, i] * slope_y - coef[1, i] * along
            part_z[r] = diff_z(coef[3, i] * slope_z - coef[2, i] * along, matrix)
    for r in range(rows):
        finish(r, stencil(lambda k: flux_x[r + 4 + k]) + diff_y(flux_y, r, width) + part_z[r])


def owner_kernel(eps, tilt, azimuth, out, held, sems):
    copies = [
        pltpu.make_async_copy(ref, held.at[n], sems.at[n])
        for n, ref in enumerate((eps, tilt, azimuth))
    ]
    for copy in copies:
        copy.start()
    for copy in copies:
        copy.wait()
    for r in range(out.shape[1]):
        size = jnp.sqrt(2.0 * held[0, r])
        flat = size * jnp.sin(held[1, r])
        out[0, r] = flat * jnp.cos(held[2, r])
        out[1, r] = flat * jnp.sin(held[2, r])
        out[2, r] = size * jnp.cos(held[1, r])


def prepare_kernel(shots, parts, step, anchor, sx, sy, sz, wavelet, rx, ry, rz, traces, speed,
                   own, partner, across, slope, src, inj, flags, matrix, speed_out, wide):
    rows, width, depth = src.shape[1:]
    count = speed.shape[1]
    speed_out[...] = speed[...]
    shape = matrix.shape
    offset = lax.broadcasted_iota(jnp.int32, shape, 0) % depth - lax.broadcasted_iota(
        jnp.int32, shape, 1
    )
    entries = jnp.zeros(shape, jnp.float32)
    for k in range(1, 5):
        entries = jnp.where(offset == k, WHOLE[k - 1], entries)
        entries = jnp.where(offset == -k, -WHOLE[k - 1], entries)
    matrix[...] = entries.astype(jnp.bfloat16)
    fill_field(own, partner, across, wide)
    for r in range(rows):
        slope[0, r], slope[1, r], slope[2, r] = slopes_at(wide, rows + r, width, matrix)
    me = lax.axis_index("shot")
    first_part = anchor[0] // count
    for k in range(shots):
        part = jnp.bitwise_xor(me, k) - first_part
        for j in range(parts):
            flags[k * parts + j : k * parts + j + 1, :] = jnp.full(
                (1, depth), jnp.where(part == j, 1.0, 0.0), jnp.float32
            )
    first = lax.axis_index("blk") * rows
    start = step[0]
    shape = (rows, width, depth)
    hit = (
        (lax.broadcasted_iota(jnp.int32, shape, 0) == sx[0] - first)
        & (lax.broadcasted_iota(jnp.int32, shape, 1) == sy[0])
        & (lax.broadcasted_iota(jnp.int32, shape, 2) == sz[0])
    )
    for t in range(STEPS - 1):
        src[t] = jnp.where(hit, wavelet[0, start + t], 0.0)
    receivers = rx.shape[1]
    local = rx[...] - first
    plane = jnp.where((local >= 0) & (local < rows), local * width + ry[...], -1)
    pick = (
        lax.broadcasted_iota(jnp.int32, (rows * width, receivers), 0) == plane
    ).astype(jnp.float32)
    match = lax.broadcasted_iota(jnp.int32, (depth, receivers), 0) == rz[...]
    for t in range(STEPS):
        samples = traces[0, pl.ds(start + t, 1), :]
        spread = jnp.where(match, samples, 0.0)
        added = lax.dot_general(
            pick,
            spread,
            (((1,), (1,)), ((), ())),
            precision=lax.Precision.HIGHEST,
            preferred_element_type=jnp.float32,
        )
        inj[t] = added.reshape(shape)


def window_part(pieces, flags, parts, j):
    chosen = pieces[-1][...]
    for k in reversed(range(len(pieces) - 1)):
        at = k * parts + j
        chosen = jnp.where(flags[at : at + 1, :] > 0.5, pieces[k][...], chosen)
    return chosen


def flux_kernel(shots, parts, *refs):
    pieces = refs[:shots]
    (flags, slope, matrix, tensor, flux, rest, flux_a, flux_p, edge_a, edge_p, flux_y) = refs[
        shots:
    ]
    rows, width, _ = flux.shape
    count = width // parts
    for j in range(parts):
        tensor[:, :, j * count : (j + 1) * count, :] = window_part(pieces, flags, parts, j)
    clear_sides(flux_y, width)
    for r in range(rows):
        wx, wy, wz = tensor[0, r], tensor[1, r], tensor[2, r]
        along = wx * slope[0, r] + wy * slope[1, r] + wz * slope[2, r]
        size = 1.0 + (wx * wx + wy * wy + wz * wz)
        flux[r] = size * slope[0, r] - wx * along
        flux_y[r, PAD : PAD + width, :] = size * slope[1, r] - wy * along
        rest[r] = diff_z(size * slope[2, r] - wz * along, matrix)
    for r in range(rows):
        rest[r] = rest[r] + diff_y(flux_y, r, width)
    odd = lax.axis_index("blk") % 2
    low = rows - 4
    flux_a[...] = flux[pl.ds(odd * low, 4)]
    flux_p[...] = flux[pl.ds((1 - odd) * low, 4)]
    edge_a[...] = tensor[:, pl.ds(odd * low, 4)]
    edge_p[...] = tensor[:, pl.ds((1 - odd) * low, 4)]


def speed_kernel(shots, parts, *refs):
    pieces = refs[:shots]
    flags, present, speed, operand = refs[shots:]
    count = speed.shape[1] // parts
    for j in range(parts):
        speed[:, j * count : (j + 1) * count, :] = window_part(pieces, flags, parts, j)
    operand[...] = speed[...] * present[...]


def coef_kernel(tensor, partner, across, coef):
    rows = tensor.shape[1]
    blk, blocks = lax.axis_index("blk"), lax.axis_size("blk")
    for a in range(3):
        place_halos(coef.at[a], (), tensor.at[a], partner.at[a], across.at[a])
    for i in range(rows + 8):
        size = 1.0 + (coef[0, i] * coef[0, i] + coef[1, i] * coef[1, i] + coef[2, i] * coef[2, i])
        if i < 4:
            size = jnp.where(blk == 0, 0.0, size)
        if i >= rows + 4:
            size = jnp.where(blk == blocks - 1, 0.0, size)
        coef[3, i] = size


def forward_first(flux, flux_p, flux_a, rest, own, previous, speed, src, image, following, flux_x):
    place_halos(flux_x, (), flux, flux_p, flux_a)
    for r in range(rest.shape[0]):
        value = stencil(lambda k: flux_x[r + 4 + k]) + rest[r]
        image[r] = value
        following[r] = 2.0 * own[r] - previous[r] + speed[r] * value + src[0, r]


def forward(t, own, partner, across, coef, matrix, previous, speed, src, image, following,
            wide, *scratch):
    fill_field(own, partner, across, wide)

    def finish(r, value):
        image[r] = value
        following[r] = 2.0 * own[r] - previous[r] + speed[r] * value + src[t, r]

    apply_operator(wide, coef, matrix, *scratch, finish)


def backward(t, own, partner, across, coef, matrix, present, later, inj, *refs):
    if t == 0:
        (earlier,) = refs[:1]
    elif t == 1:
        speed, lambda3, image0, image1, image2, earlier, operand, known = refs[:8]
    else:
        speed, earlier, operand = refs[:3]
    wide, flux_x, flux_y, part_z = refs[-4:]
    fill_field(own, partner, across, wide)

    def finish(r, value):
        result = 2.0 * present[r] - later[r] + value + inj[t, r]
        earlier[r] = result
        if t > 0:
            operand[r] = speed[r] * result
        if t == 1:
            known[r] = lambda3[r] * image2[r] + present[r] * image1[r] + result * image0[r]

    apply_operator(wide, coef, matrix, flux_x, flux_y, part_z, finish)


def forward_last(parts, own, partner, across, coef, matrix, known, lambda4, flags, *refs):
    *chunks, wide, flux_x, flux_y, part_z, grad = refs
    count = chunks[0].shape[1]
    fill_field(own, partner, across, wide)

    def finish(r, value):
        grad[r] = known[r] + lambda4[r] * value

    apply_operator(wide, coef, matrix, flux_x, flux_y, part_z, finish)
    for k, chunk in enumerate(chunks):
        held = jnp.zeros(chunk.shape, jnp.float32)
        for j in range(parts):
            at = k * parts + j
            held = jnp.where(
                flags[at : at + 1, :] > 0.5, grad[:, j * count : (j + 1) * count, :], held
            )
        chunk[...] = held


def on_device(
    state_before,
    state_now,
    adjoint_later,
    adjoint_now,
    courant_sq,
    epsilon,
    tilt_angle,
    azimuth,
    aperture_anchor,
    step_index,
    wavelet,
    residual_traces,
    source_x,
    source_y,
    source_z,
    receiver_x,
    receiver_y,
    receiver_z,
):
    rows, width, depth = state_now.shape[1:]
    count = courant_sq.shape[1]
    parts = width // count
    shots = lax.axis_size("shot")
    blocks = lax.axis_size("blk")
    field = f32(rows, width, depth)
    wide = (rows, width + 2 * PAD, depth)
    scratch = (
        pltpu.VMEM((3 * rows, width + 2 * PAD, depth), jnp.float32),
        pltpu.VMEM((rows + 8, width, depth), jnp.float32),
        pltpu.VMEM(wide, jnp.float32),
        pltpu.VMEM((rows, width, depth), jnp.float32),
    )
    work = 100 * (rows + 8) * width * depth

    core_pairs = [(i, i ^ 1) for i in range(blocks)]
    chip_pairs = []
    for s in range(shots):
        for b in range(blocks):
            end = b in (0, blocks - 1)
            other = (s ^ 1, b) if end else (s, b - 1 + 2 * (b % 2))
            chip_pairs.append((s * blocks + b, other[0] * blocks + other[1]))

    def to_partner(array):
        return lax.ppermute(array, "blk", core_pairs)

    def across_chips(array):
        return lax.ppermute(array, ("shot", "blk"), chip_pairs)

    def to_owners(array, k):
        return lax.ppermute(array, "shot", [(i, i ^ k) for i in range(shots)])

    current, previous = state_now[0], state_before[0]
    present, later = adjoint_now[0], adjoint_later[0]

    piece = call(
        "owner",
        owner_kernel,
        f32(3, rows, count, depth),
        [(a, HBM) for a in (epsilon, tilt_angle, azimuth)],
        (pltpu.VMEM((3, rows, count, depth), jnp.float32), pltpu.SemaphoreType.DMA((3,))),
    )
    pieces = [piece] + [to_owners(piece, k) for k in range(1, shots)]
    now_a = across_chips(current)
    now_p = to_partner(current)

    slope, src, inj, flags, matrix, speed_piece = call(
        "prepare",
        functools.partial(prepare_kernel, shots, parts),
        (
            f32(3, rows, width, depth),
            f32(STEPS - 1, rows, width, depth),
            f32(STEPS, rows, width, depth),
            f32(shots * parts, depth),
            jax.ShapeDtypeStruct((2 * depth, depth), jnp.bfloat16),
            f32(rows, count, depth),
        ),
        [
            (a, SMEM)
            for a in (step_index, aperture_anchor, source_x, source_y, source_z, wavelet)
        ]
        + [receiver_x, receiver_y, receiver_z, residual_traces, courant_sq]
        + [current, now_p, now_a],
        scratch[:1],
        work,
    )
    speed_pieces = [speed_piece] + [to_owners(speed_piece, k) for k in range(1, shots)]

    flux_edge, edge = f32(4, width, depth), f32(3, 4, width, depth)
    tensor, flux, rest, flux_a, flux_p, edge_a, edge_p = call(
        "flux",
        functools.partial(flux_kernel, shots, parts),
        (f32(3, rows, width, depth), field, field, flux_edge, flux_edge, edge, edge),
        pieces + [flags, slope, matrix],
        scratch[2:3],
        work // 3,
    )
    flux_a = across_chips(flux_a)
    flux_p = to_partner(flux_p)
    edge_a = across_chips(edge_a)
    edge_p = to_partner(edge_p)

    speed, operand = call(
        "speed",
        functools.partial(speed_kernel, shots, parts),
        (field, field),
        speed_pieces + [flags, present],
    )
    op_a = across_chips(operand)
    op_p = to_partner(operand)

    image, following = call(
        "forward0",
        forward_first,
        (field, field),
        [flux, flux_p, flux_a, rest, current, previous, speed, src],
        scratch[1:2],
        work // 4,
    )
    coef = call("coef", coef_kernel, f32(4, rows + 8, width, depth), [tensor, edge_p, edge_a])
    images = [image]
    previous, current = current, following
    adjoints = [present]
    known = None
    for t in range(STEPS - 1):
        now_a = across_chips(current)
        now_p = to_partner(current)
        back = STEPS - 1 - t
        ins = [operand, op_p, op_a, coef, matrix, present, later, inj, speed]
        outs = (field, field)
        if back == 1:
            ins = ins + [adjoints[1]] + images
            outs = (field, field, field)
        result = call(
            f"backward{t}", functools.partial(backward, back), outs, ins, scratch, work
        )
        later, present, operand = present, result[0], result[1]
        if back == 1:
            known = result[2]
        adjoints.append(present)
        op_a = across_chips(operand)
        op_p = to_partner(operand)
        if t < STEPS - 2:
            image, following = call(
                f"forward{t + 1}",
                functools.partial(forward, t + 1),
                (field, field),
                [current, now_p, now_a, coef, matrix, previous, speed, src],
                scratch,
                work,
            )
            images.append(image)
            previous, current = current, following

    chunks = call(
        "forward3",
        functools.partial(forward_last, parts),
        (f32(rows, count, depth),) * shots,
        [current, now_p, now_a, coef, matrix, known, adjoints[0], flags],
        scratch + (pltpu.VMEM((rows, width, depth), jnp.float32),),
        work,
    )
    received = [to_owners(chunks[k], k) for k in range(1, shots)]
    (final,) = call(
        "backward3",
        functools.partial(backward, 0),
        (field,),
        [operand, op_p, op_a, coef, matrix, present, later, inj],
        scratch,
        work,
    )
    model_grad = chunks[0]
    for part in received:
        model_grad = model_grad + part
    return (present[None], final[None], model_grad)


def solution(mesh):
    in_specs = (
        P("shot", "blk", None, None),
        P("shot", "blk", None, None),
        P("shot", "blk", None, None),
        P("shot", "blk", None, None),
        P("blk", "shot", None),
        P("blk", "shot", None),
        P("blk", "shot", None),
        P("blk", "shot", None),
        P("shot"),
        P(),
        P("shot", None),
        P("shot", None, None),
        P("shot"),
        P("shot"),
        P("shot"),
        P("shot", None),
        P("shot", None),
        P("shot", None),
    )
    out_specs = (P("shot", "blk", None, None), P("shot", "blk", None, None), P("blk", "shot", None))
    return jax.shard_map(
        on_device, mesh=mesh, in_specs=in_specs, out_specs=out_specs, check_vma=False
    )
```

time: 106 us -> 89.1 us (0.84)
  Pallas kernels: 34.5 us -> 15.6 us
  waiting for transfers between devices: 24.1 us -> 36.2 us
  starting transfers between devices: 34.3 us -> 24.2 us
    pallas_call x11 -> x13, Pallas kernels: 34.5 us -> 15.6 us  [call(): pl.pallas_call(body, name=name, out_shape=outs, in_specs=[s for _, s in p...]
    ppermute x24 -> x29, waiting for transfers between devices: 24.1 us -> 36.2 us  [the longest x10 26.5 us: across_chips(): return lax.ppermute(array, ('shot', 'blk'), chip_pairs)]
    ppermute x24 -> x29, starting transfers between devices: 34.3 us -> 24.2 us  [the longest x10 11.8 us: across_chips(): return lax.ppermute(array, ('shot', 'blk'), chip_pairs)]
    unnamed x34 -> x30, local copies, waits for them, and re-layouts: 7.19 us -> 7.94 us
  transfers between devices with their start and end apart: 24 -> 29, of which waited for: 3 -> 14; matrix products, arithmetic and copies ran while one was open for 0% -> 1% of each run, Pallas kernels for 31% -> 11%
where the time goes in v2:
time: 89.1 us; the launch traced here: 88.7 us
  waiting for transfers between devices  36.2 us (41%)
  starting transfers between devices  24.2 us (27%)
  Pallas kernels  15.6 us (18%)
  local copies, waits for them, and re-layouts  7.94 us (9%)
  between operations  4.08 us (5%)
    ppermute x10, waiting for transfers between devices, across_chips(): return lax.ppermute(array, ('shot', 'blk'), chip_pairs)  26.5 us
    pallas_call x13, Pallas kernels, call(): pl.pallas_call(body, name=name, out_shape=outs, in_specs=[s for _, s in p...  15.6 us
    ppermute x10, starting transfers between devices, across_chips(): return lax.ppermute(array, ('shot', 'blk'), chip_pairs)  11.8 us
    ppermute x9, starting transfers between devices, to_owners(): return lax.ppermute(array, 'shot', [(i, i ^ k) for i in range(shots)])  11.7 us
    ppermute x9, waiting for transfers between devices, to_owners(): return lax.ppermute(array, 'shot', [(i, i ^ k) for i in range(shots)])  9.66 us
    unnamed x30, local copies, waits for them, and re-layouts  7.94 us
  transfers between devices with their start and end apart: 29, of which 14 were waited for; matrix products, arithmetic and copies ran while one was open for 1% of the time, Pallas kernels for 11%

profile of v2, /device:TPU:0, one launch (start us, length us, event | category | flops | bytes accessed | tf_op | source)
XLA Modules:
  0.0 88.7 jit_solution(7613955205746091442)
XLA Ops:
  0.7 0.9 %copy-done.7 = f32[8,32,128]{2,1,0:T(8,128)S(1)} copy-done((f32[8,32,128]{2,1,0:T(8,128)S(1)}, f32[8,32,128]{2,1,0:T(8,128)}, u32[]{:S(2)}) %copy-start.7) | copy-done | bytes 131096
  1.6 0.9 %copy-done.8 = f32[8,32,128]{2,1,0:T(8,128)S(1)} copy-done((f32[8,32,128]{2,1,0:T(8,128)S(1)}, f32[8,32,128]{2,1,0:T(8,128)}, u32[]{:S(2)}) %copy-start.8) | copy-done | bytes 131096
  2.5 0.9 %copy-done.9 = f32[8,32,128]{2,1,0:T(8,128)S(1)} copy-done((f32[8,32,128]{2,1,0:T(8,128)S(1)}, f32[8,32,128]{2,1,0:T(8,128)}, u32[]{:S(2)}) %copy-start.9) | copy-done | bytes 131096
  3.4 2.0 %owner.1.refs_0_ = f32[3,8,32,128]{3,2,1,0:T(8,128)S(1)} custom-call(f32[8,32,128]{2,1,0:T(8,128)S(1)} %copy-done.7, f32[8,32,128]{2,1,0:T(8,128)S(1)} %copy-done.8, f32[8,32,128]{2,1,0:T(8,128)S(1)} %copy-done.9), custom_call_target="tpu_custom_call" | custom-call | flops 1048576 | bytes 1048576 | tf_op jit(solution)/shard_map/owner/pallas_call | solution.py:27
  5.5 3.0 %collective-permute-start.7 = (f32[3,8,32,128]{3,2,1,0:T(8,128)S(1)}, f32[3,8,32,128]{3,2,1,0:T(8,128)S(1)}, u32[]{:S(2)}, u32[]{:S(2)}) collective-permute-start(f32[3,8,32,128]{3,2,1,0:T(8,128)S(1)} %owner.1.refs_0_), channel_id=1, source_target_pairs={{0,8},{8,0},{16,24},{24,16},{1,9},{9,1},{17,25},{25,17},{2,10},{10... | collective-permute-start | bytes 1179656 | tf_op jit(solution)/shard_map/ppermute | solution.py:349
  8.5 1.5 %collective-permute-start.8 = (f32[3,8,32,128]{3,2,1,0:T(8,128)S(1)}, f32[3,8,32,128]{3,2,1,0:T(8,128)S(1)}, u32[]{:S(2)}, u32[]{:S(2)}) collective-permute-start(f32[3,8,32,128]{3,2,1,0:T(8,128)S(1)} %owner.1.refs_0_), channel_id=1, source_target_pairs={{0,16},{8,24},{16,0},{24,8},{1,17},{9,25},{17,1},{25,9},{2,18},{10... | collective-permute-start | bytes 1179656 | tf_op jit(solution)/shard_map/ppermute | solution.py:349
  10.0 0.0 collective-permute-start.9
  10.0 1.9 %collective-permute-start.1 = (f32[8,64,128]{2,1,0:T(8,128)}, f32[8,64,128]{2,1,0:T(8,128)S(1)}, u32[]{:S(2)}, u32[]{:S(2)}) collective-permute-start(f32[8,64,128]{2,1,0:T(8,128)} %bitcast.11), channel_id=1, source_target_pairs={{0,8},{1,2},{2,1},{3,4},{4,3},{5,6},{6,5},{7,15},{8,0},{9,10},{10,... | collective-permute-start | bytes 786440 | tf_op jit(solution)/shard_map/ppermute | solution.py:346
  15.2 13.7 %collective-permute-done.1.across = f32[8,64,128]{2,1,0:T(8,128)S(1)} collective-permute-done((f32[8,64,128]{2,1,0:T(8,128)}, f32[8,64,128]{2,1,0:T(8,128)S(1)}, u32[]{:S(2)}, u32[]{:S(2)}) %collective-permute-start.1) | collective-permute-done | bytes 262176 | tf_op jit(solution)/shard_map/ppermute | solution.py:346
  28.9 0.9 %copy-done.1 = f32[1,8,64,128]{3,2,1,0:T(8,128)S(1)} copy-done((f32[1,8,64,128]{3,2,1,0:T(8,128)S(1)}, f32[1,8,64,128]{3,2,1,0:T(8,128)}, u32[]{:S(2)}) %copy-start.1) | copy-done | bytes 262168
  29.8 0.9 %copy-done.6 = f32[8,32,128]{2,1,0:T(8,128)S(1)} copy-done((f32[8,32,128]{2,1,0:T(8,128)S(1)}, f32[8,32,128]{2,1,0:T(8,128)}, u32[]{:S(2)}) %copy-start.6) | copy-done | bytes 131096
  30.7 0.7 copy-done.10
  31.4 0.7 copy-done.11
  32.1 0.7 copy-done.12
  32.7 0.7 copy-done.13
  33.4 0.7 copy-done.14
  34.0 2.1 %prepare.1 = (f32[3,8,64,128]{3,2,1,0:T(8,128)S(1)}, f32[3,8,64,128]{3,2,1,0:T(8,128)S(1)}, f32[4,8,64,128]{3,2,1,0:T(8,128)S(1)}, f32[8,128]{1,0:T(8,128)S(1)},...) custom-call(s32[1]{0:T(128)S(6)} %copy.22.step, s32[1]{0:T(128)S(6)} %copy.21.anchor, s32[1]{0:T(128)S(6)} %copy.23.sx, ...), custom_call_target="tpu_custom_call" | custom-call | flops 13107200 | bytes 1048576 | tf_op jit(solution)/shard_map/prepare/pallas_call | solution.py:27
  36.2 0.5 flux.1
  36.8 0.1 collective-permute-start.10
  36.8 1.8 %collective-permute-start.2 = (f32[8,32,128]{2,1,0:T(8,128)S(1)}, f32[8,32,128]{2,1,0:T(8,128)S(1)}, u32[]{:S(2)}, u32[]{:S(2)}) collective-permute-start(f32[8,32,128]{2,1,0:T(8,128)S(1)} %get-tuple-element.35.refs_0_), channel_id=1, source_target_pairs={{0,8},{8,0},{16,24},{24,16},{1,9},{9,1},{17,25},{25,17},{2,10},{10... | collective-permute-start | bytes 393224 | tf_op jit(solution)/shard_map/ppermute | solution.py:349
  38.6 1.5 %collective-permute-start.3 = (f32[8,32,128]{2,1,0:T(8,128)S(1)}, f32[8,32,128]{2,1,0:T(8,128)S(1)}, u32[]{:S(2)}, u32[]{:S(2)}) collective-permute-start(f32[8,32,128]{2,1,0:T(8,128)S(1)} %get-tuple-element.35.refs_0_), channel_id=1, source_target_pairs={{0,16},{8,24},{16,0},{24,8},{1,17},{9,25},{17,1},{25,9},{2,18},{10... | collective-permute-start | bytes 393224 | tf_op jit(solution)/shard_map/ppermute | solution.py:349
  40.1 0.3 collective-permute-start.4
  40.4 1.7 %collective-permute-start.11 = (f32[3,4,64,128]{3,2,1,0:T(8,128)S(1)}, f32[3,4,64,128]{3,2,1,0:T(8,128)S(1)}, u32[]{:S(2)}, u32[]{:S(2)}) collective-permute-start(f32[3,4,64,128]{3,2,1,0:T(8,128)S(1)} %get-tuple-element.42), channel_id=1, source_target_pairs={{0,8},{1,2},{2,1},{3,4},{4,3},{5,6},{6,5},{7,15},{8,0},{9,10},{10,... | collective-permute-start | bytes 1179656 | tf_op jit(solution)/shard_map/ppermute | solution.py:346
  42.1 0.7 collective-permute-done.2.refs_1_
  42.8 4.2 %collective-permute-done.3.refs_2_ = f32[8,32,128]{2,1,0:T(8,128)S(1)} collective-permute-done((f32[8,32,128]{2,1,0:T(8,128)S(1)}, f32[8,32,128]{2,1,0:T(8,128)S(1)}, u32[]{:S(2)}, u32[]{:S(2)}) %collective-permute-start.3) | collective-permute-done | bytes 131104 | tf_op jit(solution)/shard_map/ppermute | solution.py:349
  47.0 0.1 speed.3
  47.1 0.1 collective-permute-start.5
  47.2 2.1 %collective-permute-start.6 = (f32[8,64,128]{2,1,0:T(8,128)S(1)}, f32[8,64,128]{2,1,0:T(8,128)S(1)}, u32[]{:S(2)}, u32[]{:S(2)}) collective-permute-start(f32[8,64,128]{2,1,0:T(8,128)S(1)} %get-tuple-element.37.own), channel_id=1, source_target_pairs={{0,8},{1,2},{2,1},{3,4},{4,3},{5,6},{6,5},{7,15},{8,0},{9,10},{10,... | collective-permute-start | bytes 786440 | tf_op jit(solution)/shard_map/ppermute | solution.py:346
  49.3 2.7 %collective-permute-done.17.flux_a = f32[4,64,128]{2,1,0:T(8,128)S(1)} collective-permute-done((f32[4,64,128]{2,1,0:T(8,128)S(1)}, f32[4,64,128]{2,1,0:T(8,128)S(1)}, u32[]{:S(2)}, u32[]{:S(2)}) %collective-permute-start.17) | collective-permute-done | bytes 131104 | tf_op jit(solution)/shard_map/ppermute | solution.py:346
  52.0 0.2 forward0.1
  52.2 0.0 copy-start.4
  52.2 0.1 collective-permute-start.18
  52.3 1.0 %collective-permute-start.19 = (f32[8,64,128]{2,1,0:T(8,128)S(1)}, f32[8,64,128]{2,1,0:T(8,128)S(1)}, u32[]{:S(2)}, u32[]{:S(2)}) collective-permute-start(f32[8,64,128]{2,1,0:T(8,128)S(1)} %get-tuple-element.55.own.previous), channel_id=1, source_target_pairs={{0,8},{1,2},{2,1},{3,4},{4,3},{5,6},{6,5},{7,15},{8,0},{9,10},{10,... | collective-permute-start | bytes 786440 | tf_op jit(solution)/shard_map/ppermute | solution.py:346
  53.4 0.3 coef.1
  53.7 1.1 %collective-permute-done.6.across = f32[8,64,128]{2,1,0:T(8,128)S(1)} collective-permute-done((f32[8,64,128]{2,1,0:T(8,128)S(1)}, f32[8,64,128]{2,1,0:T(8,128)S(1)}, u32[]{:S(2)}, u32[]{:S(2)}) %collective-permute-start.6) | collective-permute-done | bytes 262176 | tf_op jit(solution)/shard_map/ppermute | solution.py:346
  54.8 1.2 %backward0.1 = (f32[8,64,128]{2,1,0:T(8,128)S(1)}, f32[8,64,128]{2,1,0:T(8,128)S(1)}) custom-call(f32[8,64,128]{2,1,0:T(8,128)S(1)} %get-tuple-element.37.own, f32[8,64,128]{2,1,0:T(8,128)S(1)} %collective-permute-done.5.partner, f32[8,64,128]{2,1,0:T(8,128)S(1)} %collective-permute-done.6.across, f32[4,16,64,128]{3,2,1,0:T(8,128)S(1)} %coef.1, ...), custom_call_target="tpu_custom_call" | custom-call | flops 13107200 | bytes 1048576 | tf_op jit(solution)/shard_map/backward0/pallas_call | solution.py:27
  56.0 0.1 collective-permute-start.12
  56.1 1.0 %collective-permute-start.13 = (f32[8,64,128]{2,1,0:T(8,128)S(1)}, f32[8,64,128]{2,1,0:T(8,128)S(1)}, u32[]{:S(2)}, u32[]{:S(2)}) collective-permute-start(f32[8,64,128]{2,1,0:T(8,128)S(1)} %get-tuple-element.45.own), channel_id=1, source_target_pairs={{0,8},{1,2},{2,1},{3,4},{4,3},{5,6},{6,5},{7,15},{8,0},{9,10},{10,... | collective-permute-start | bytes 786440 | tf_op jit(solution)/shard_map/ppermute | solution.py:346
  57.2 1.6 %collective-permute-done.19.across = f32[8,64,128]{2,1,0:T(8,128)S(1)} collective-permute-done((f32[8,64,128]{2,1,0:T(8,128)S(1)}, f32[8,64,128]{2,1,0:T(8,128)S(1)}, u32[]{:S(2)}, u32[]{:S(2)}) %collective-permute-start.19) | collective-permute-done | bytes 262176 | tf_op jit(solution)/shard_map/ppermute | solution.py:346
  58.7 1.2 %forward1.1 = (f32[8,64,128]{2,1,0:T(8,128)S(1)}, f32[8,64,128]{2,1,0:T(8,128)S(1)}) custom-call(f32[8,64,128]{2,1,0:T(8,128)S(1)} %get-tuple-element.55.own.previous, f32[8,64,128]{2,1,0:T(8,128)S(1)} %collective-permute-done.18.partner, f32[8,64,128]{2,1,0:T(8,128)S(1)} %collective-permute-done.19.across, f32[4,16,64,128]{3,2,1,0:T(8,128)S(1)} %coef.1, ...), custom_call_target="tpu_custom_call" | custom-call | flops 13107200 | bytes 1048576 | tf_op jit(solution)/shard_map/forward1/pallas_call | solution.py:27
  60.0 0.2 collective-permute-start.20
  60.2 1.0 %collective-permute-start.21 = (f32[8,64,128]{2,1,0:T(8,128)S(1)}, f32[8,64,128]{2,1,0:T(8,128)S(1)}, u32[]{:S(2)}, u32[]{:S(2)}) collective-permute-start(f32[8,64,128]{2,1,0:T(8,128)S(1)} %get-tuple-element.57.own), channel_id=1, source_target_pairs={{0,8},{1,2},{2,1},{3,4},{4,3},{5,6},{6,5},{7,15},{8,0},{9,10},{10,... | collective-permute-start | bytes 786440 | tf_op jit(solution)/shard_map/ppermute | solution.py:346
  61.1 1.4 %collective-permute-done.13.across = f32[8,64,128]{2,1,0:T(8,128)S(1)} collective-permute-done((f32[8,64,128]{2,1,0:T(8,128)S(1)}, f32[8,64,128]{2,1,0:T(8,128)S(1)}, u32[]{:S(2)}, u32[]{:S(2)}) %collective-permute-start.13) | collective-permute-done | bytes 262176 | tf_op jit(solution)/shard_map/ppermute | solution.py:346
  62.5 1.2 %backward1.1 = (f32[8,64,128]{2,1,0:T(8,128)S(1)}, f32[8,64,128]{2,1,0:T(8,128)S(1)}) custom-call(f32[8,64,128]{2,1,0:T(8,128)S(1)} %get-tuple-element.45.own, f32[8,64,128]{2,1,0:T(8,128)S(1)} %collective-permute-done.12.partner, f32[8,64,128]{2,1,0:T(8,128)S(1)} %collective-permute-done.13.across, f32[4,16,64,128]{3,2,1,0:T(8,128)S(1)} %coef.1, ...), custom_call_target="tpu_custom_call" | custom-call | flops 13107200 | bytes 1048576 | tf_op jit(solution)/shard_map/backward1/pallas_call | solution.py:27
  63.8 0.2 collective-permute-start.14
  64.0 1.0 %collective-permute-start.15 = (f32[8,64,128]{2,1,0:T(8,128)S(1)}, f32[8,64,128]{2,1,0:T(8,128)S(1)}, u32[]{:S(2)}, u32[]{:S(2)}) collective-permute-start(f32[8,64,128]{2,1,0:T(8,128)S(1)} %get-tuple-element.47.own), channel_id=1, source_target_pairs={{0,8},{1,2},{2,1},{3,4},{4,3},{5,6},{6,5},{7,15},{8,0},{9,10},{10,... | collective-permute-start | bytes 786440 | tf_op jit(solution)/shard_map/ppermute | solution.py:346
  64.9 1.6 %collective-permute-done.21.across = f32[8,64,128]{2,1,0:T(8,128)S(1)} collective-permute-done((f32[8,64,128]{2,1,0:T(8,128)S(1)}, f32[8,64,128]{2,1,0:T(8,128)S(1)}, u32[]{:S(2)}, u32[]{:S(2)}) %collective-permute-start.21) | collective-permute-done | bytes 262176 | tf_op jit(solution)/shard_map/ppermute | solution.py:346
  66.5 1.2 %forward2.1 = (f32[8,64,128]{2,1,0:T(8,128)S(1)}, f32[8,64,128]{2,1,0:T(8,128)S(1)}) custom-call(f32[8,64,128]{2,1,0:T(8,128)S(1)} %get-tuple-element.57.own, f32[8,64,128]{2,1,0:T(8,128)S(1)} %collective-permute-done.20.partner, f32[8,64,128]{2,1,0:T(8,128)S(1)} %collective-permute-done.21.across, f32[4,16,64,128]{3,2,1,0:T(8,128)S(1)} %coef.1, ...), custom_call_target="tpu_custom_call" | custom-call | flops 13107200 | bytes 1048576 | tf_op jit(solution)/shard_map/forward2/pallas_call | solution.py:27
  67.8 0.2 collective-permute-start.24
  67.9 1.0 %collective-permute-start.25 = (f32[8,64,128]{2,1,0:T(8,128)S(1)}, f32[8,64,128]{2,1,0:T(8,128)S(1)}, u32[]{:S(2)}, u32[]{:S(2)}) collective-permute-start(f32[8,64,128]{2,1,0:T(8,128)S(1)} %get-tuple-element.61.own), channel_id=1, source_target_pairs={{0,8},{1,2},{2,1},{3,4},{4,3},{5,6},{6,5},{7,15},{8,0},{9,10},{10,... | collective-permute-start | bytes 786440 | tf_op jit(solution)/shard_map/ppermute | solution.py:346
  68.9 1.4 %collective-permute-done.15.across = f32[8,64,128]{2,1,0:T(8,128)S(1)} collective-permute-done((f32[8,64,128]{2,1,0:T(8,128)S(1)}, f32[8,64,128]{2,1,0:T(8,128)S(1)}, u32[]{:S(2)}, u32[]{:S(2)}) %collective-permute-start.15) | collective-permute-done | bytes 262176 | tf_op jit(solution)/shard_map/ppermute | solution.py:346
  70.3 2.2 %backward2.1 = (f32[8,64,128]{2,1,0:T(8,128)}, f32[8,64,128]{2,1,0:T(8,128)S(1)}, f32[8,64,128]{2,1,0:T(8,128)S(1)}) custom-call(f32[8,64,128]{2,1,0:T(8,128)S(1)} %get-tuple-element.47.own, f32[8,64,128]{2,1,0:T(8,128)S(1)} %collective-permute-done.14.partner, f32[8,64,128]{2,1,0:T(8,128)S(1)} %collective-permute-done.15.across, ...), custom_call_target="tpu_custom_call" | custom-call | flops 13107200 | bytes 1048576 | tf_op jit(solution)/shard_map/backward2/pallas_call | solution.py:27
  72.5 1.8 %collective-permute-done.25.across = f32[8,64,128]{2,1,0:T(8,128)S(1)} collective-permute-done((f32[8,64,128]{2,1,0:T(8,128)S(1)}, f32[8,64,128]{2,1,0:T(8,128)S(1)}, u32[]{:S(2)}, u32[]{:S(2)}) %collective-permute-start.25) | collective-permute-done | bytes 262176 | tf_op jit(solution)/shard_map/ppermute | solution.py:346
  74.3 1.2 %forward3.1 = (f32[8,32,128]{2,1,0:T(8,128)S(1)}, f32[8,32,128]{2,1,0:T(8,128)S(1)}, f32[8,32,128]{2,1,0:T(8,128)S(1)}, f32[8,32,128]{2,1,0:T(8,128)S(1)}) custom-call(f32[8,64,128]{2,1,0:T(8,128)S(1)} %get-tuple-element.61.own, f32[8,64,128]{2,1,0:T(8,128)S(1)} %collective-permute-done.24.partner, f32[8,64,128]{2,1,0:T(8,128)S(1)} %collective-permute-done.25.across, ...), custom_call_target="tpu_custom_call" | custom-call | flops 13107200 | bytes 1048576 | tf_op jit(solution)/shard_map/forward3/pallas_call | solution.py:27
  75.6 1.0 %collective-permute-start.26 = (f32[8,32,128]{2,1,0:T(8,128)S(1)}, f32[8,32,128]{2,1,0:T(8,128)S(1)}, u32[]{:S(2)}, u32[]{:S(2)}) collective-permute-start(f32[8,32,128]{2,1,0:T(8,128)S(1)} %get-tuple-element.64), channel_id=1, source_target_pairs={{0,8},{8,0},{16,24},{24,16},{1,9},{9,1},{17,25},{25,17},{2,10},{10... | collective-permute-start | bytes 393224 | tf_op jit(solution)/shard_map/ppermute | solution.py:349
  76.6 1.4 %collective-permute-start.27 = (f32[8,32,128]{2,1,0:T(8,128)S(1)}, f32[8,32,128]{2,1,0:T(8,128)S(1)}, u32[]{:S(2)}, u32[]{:S(2)}) collective-permute-start(f32[8,32,128]{2,1,0:T(8,128)S(1)} %get-tuple-element.65), channel_id=1, source_target_pairs={{0,16},{8,24},{16,0},{24,8},{1,17},{9,25},{17,1},{25,9},{2,18},{10... | collective-permute-start | bytes 393224 | tf_op jit(solution)/shard_map/ppermute | solution.py:349
  78.0 1.1 %collective-permute-start.28 = (f32[8,32,128]{2,1,0:T(8,128)S(1)}, f32[8,32,128]{2,1,0:T(8,128)S(1)}, u32[]{:S(2)}, u32[]{:S(2)}) collective-permute-start(f32[8,32,128]{2,1,0:T(8,128)S(1)} %get-tuple-element.66), channel_id=1, source_target_pairs={{0,24},{8,16},{16,8},{24,0},{1,25},{9,17},{17,9},{25,1},{2,26},{10... | collective-permute-start | bytes 393224 | tf_op jit(solution)/shard_map/ppermute | solution.py:349
  79.1 1.0 %collective-permute-start.23 = (f32[8,64,128]{2,1,0:T(8,128)S(1)}, f32[8,64,128]{2,1,0:T(8,128)S(1)}, u32[]{:S(2)}, u32[]{:S(2)}) collective-permute-start(f32[8,64,128]{2,1,0:T(8,128)S(1)} %get-tuple-element.60.own), channel_id=1, source_target_pairs={{0,8},{1,2},{2,1},{3,4},{4,3},{5,6},{6,5},{7,15},{8,0},{9,10},{10,... | collective-permute-start | bytes 786440 | tf_op jit(solution)/shard_map/ppermute | solution.py:346
  80.1 1.9 %collective-permute-done.26 = f32[8,32,128]{2,1,0:T(8,128)S(1)} collective-permute-done((f32[8,32,128]{2,1,0:T(8,128)S(1)}, f32[8,32,128]{2,1,0:T(8,128)S(1)}, u32[]{:S(2)}, u32[]{:S(2)}) %collective-permute-start.26) | collective-permute-done | bytes 131104 | tf_op jit(solution)/shard_map/ppermute | solution.py:349
  82.0 1.7 %collective-permute-done.27 = f32[8,32,128]{2,1,0:T(8,128)S(1)} collective-permute-done((f32[8,32,128]{2,1,0:T(8,128)S(1)}, f32[8,32,128]{2,1,0:T(8,128)S(1)}, u32[]{:S(2)}, u32[]{:S(2)}) %collective-permute-start.27) | collective-permute-done | bytes 131104 | tf_op jit(solution)/shard_map/ppermute | solution.py:349
  83.6 1.2 %collective-permute-done.28 = f32[8,32,128]{2,1,0:T(8,128)S(1)} collective-permute-done((f32[8,32,128]{2,1,0:T(8,128)S(1)}, f32[8,32,128]{2,1,0:T(8,128)S(1)}, u32[]{:S(2)}, u32[]{:S(2)}) %collective-permute-start.28) | collective-permute-done | bytes 131104 | tf_op jit(solution)/shard_map/ppermute | solution.py:349
  84.9 0.7 add_add_fusion
  85.6 1.2 %collective-permute-done.23.across = f32[8,64,128]{2,1,0:T(8,128)S(1)} collective-permute-done((f32[8,64,128]{2,1,0:T(8,128)S(1)}, f32[8,64,128]{2,1,0:T(8,128)S(1)}, u32[]{:S(2)}, u32[]{:S(2)}) %collective-permute-start.23) | collective-permute-done | bytes 262176 | tf_op jit(solution)/shard_map/ppermute | solution.py:346
  86.8 1.9 %backward3.1 = f32[8,64,128]{2,1,0:T(8,128)} custom-call(f32[8,64,128]{2,1,0:T(8,128)S(1)} %get-tuple-element.60.own, f32[8,64,128]{2,1,0:T(8,128)S(1)} %collective-permute-done.22.partner, f32[8,64,128]{2,1,0:T(8,128)S(1)} %collective-permute-done.23.across, f32[4,16,64,128]{3,2,1,0:T(8,128)S(1)} %coef.1, ...), custom_call_target="tpu_custom_call" | custom-call | flops 13107200 | bytes 1048576 | tf_op jit(solution)/shard_map/backward3/pallas_call | solution.py:27
  (38 shorter events, 0.1 us)
Async XLA Ops:
  0.6 46.4 %copy-start = (f32[1,8,64,128]{3,2,1,0:T(8,128)S(1)}, f32[1,8,64,128]{3,2,1,0:T(8,128)}, u32[]{:S(2)}) copy-start(f32[1,8,64,128]{3,2,1,0:T(8,128)} %param.21) | copy-start | bytes 786436
  0.6 0.9 %copy-start.7 = (f32[8,32,128]{2,1,0:T(8,128)S(1)}, f32[8,32,128]{2,1,0:T(8,128)}, u32[]{:S(2)}) copy-start(f32[8,32,128]{2,1,0:T(8,128)} %eps.1) | copy-start | bytes 393220
  1.6 0.9 %copy-start.8 = (f32[8,32,128]{2,1,0:T(8,128)S(1)}, f32[8,32,128]{2,1,0:T(8,128)}, u32[]{:S(2)}) copy-start(f32[8,32,128]{2,1,0:T(8,128)} %tilt.1) | copy-start | bytes 393220
  2.5 0.9 %copy-start.9 = (f32[8,32,128]{2,1,0:T(8,128)S(1)}, f32[8,32,128]{2,1,0:T(8,128)}, u32[]{:S(2)}) copy-start(f32[8,32,128]{2,1,0:T(8,128)} %azimuth.1) | copy-start | bytes 393220
  3.4 48.6 %copy-start.2 = (f32[1,8,64,128]{3,2,1,0:T(8,128)S(1)}, f32[1,8,64,128]{3,2,1,0:T(8,128)}, u32[]{:S(2)}) copy-start(f32[1,8,64,128]{3,2,1,0:T(8,128)} %param.19) | copy-start | bytes 786436
  3.4 48.6 %copy-start.3 = (f32[1,8,64,128]{3,2,1,0:T(8,128)S(1)}, f32[1,8,64,128]{3,2,1,0:T(8,128)}, u32[]{:S(2)}) copy-start(f32[1,8,64,128]{3,2,1,0:T(8,128)} %param.18) | copy-start | bytes 786436
  5.5 30.7 %collective-permute-start.7 = (f32[3,8,32,128]{3,2,1,0:T(8,128)S(1)}, f32[3,8,32,128]{3,2,1,0:T(8,128)S(1)}, u32[]{:S(2)}, u32[]{:S(2)}) collective-permute-start(f32[3,8,32,128]{3,2,1,0:T(8,128)S(1)} %owner.1.refs_0_), channel_id=1, source_target_pairs={{0,8},{8,0},{16,24},{24,16},{1,9},{9,1},{17,25},{25,17},{2,10},{10... | collective-permute-start | bytes 1179656 | tf_op jit(solution)/shard_map/ppermute | solution.py:349
  8.5 27.7 %collective-permute-start.8 = (f32[3,8,32,128]{3,2,1,0:T(8,128)S(1)}, f32[3,8,32,128]{3,2,1,0:T(8,128)S(1)}, u32[]{:S(2)}, u32[]{:S(2)}) collective-permute-start(f32[3,8,32,128]{3,2,1,0:T(8,128)S(1)} %owner.1.refs_0_), channel_id=1, source_target_pairs={{0,16},{8,24},{16,0},{24,8},{1,17},{9,25},{17,1},{25,9},{2,18},{10... | collective-permute-start | bytes 1179656 | tf_op jit(solution)/shard_map/ppermute | solution.py:349
  10.0 26.2 %collective-permute-start.9 = (f32[3,8,32,128]{3,2,1,0:T(8,128)S(1)}, f32[3,8,32,128]{3,2,1,0:T(8,128)S(1)}, u32[]{:S(2)}, u32[]{:S(2)}) collective-permute-start(f32[3,8,32,128]{3,2,1,0:T(8,128)S(1)} %owner.1.refs_0_), channel_id=1, source_target_pairs={{0,24},{8,16},{16,8},{24,0},{1,25},{9,17},{17,9},{25,1},{2,26},{10... | collective-permute-start | bytes 1179656 | tf_op jit(solution)/shard_map/ppermute | solution.py:349
  10.0 5.2 %collective-permute-start = (f32[8,64,128]{2,1,0:T(8,128)}, f32[8,64,128]{2,1,0:T(8,128)S(1)}, u32[]{:S(2)}, u32[]{:S(2)}) collective-permute-start(f32[8,64,128]{2,1,0:T(8,128)} %bitcast.10), channel_id=1, source_target_pairs={{0,1},{1,0},{2,3},{3,2},{4,5},{5,4},{6,7},{7,6},{8,9},{9,8},{10,11... | collective-permute-start | bytes 786440 | tf_op jit(solution)/shard_map/ppermute | solution.py:343
  10.0 18.9 %collective-permute-start.1 = (f32[8,64,128]{2,1,0:T(8,128)}, f32[8,64,128]{2,1,0:T(8,128)S(1)}, u32[]{:S(2)}, u32[]{:S(2)}) collective-permute-start(f32[8,64,128]{2,1,0:T(8,128)} %bitcast.11), channel_id=1, source_target_pairs={{0,8},{1,2},{2,1},{3,4},{4,3},{5,6},{6,5},{7,15},{8,0},{9,10},{10,... | collective-permute-start | bytes 786440 | tf_op jit(solution)/shard_map/ppermute | solution.py:346
  28.9 1.0 %copy-start.1 = (f32[1,8,64,128]{3,2,1,0:T(8,128)S(1)}, f32[1,8,64,128]{3,2,1,0:T(8,128)}, u32[]{:S(2)}) copy-start(f32[1,8,64,128]{3,2,1,0:T(8,128)} %param.19) | copy-start | bytes 786436
  29.8 0.9 %copy-start.6 = (f32[8,32,128]{2,1,0:T(8,128)S(1)}, f32[8,32,128]{2,1,0:T(8,128)}, u32[]{:S(2)}) copy-start(f32[8,32,128]{2,1,0:T(8,128)} %speed.2) | copy-start | bytes 393220
  30.7 0.7 copy-start.10
  31.4 0.7 copy-start.11
  32.1 0.7 copy-start.12
  32.7 0.7 copy-start.13
  33.4 0.7 copy-start.14
  36.8 15.5 %collective-permute-start.10 = (f32[3,4,64,128]{3,2,1,0:T(8,128)S(1)}, f32[3,4,64,128]{3,2,1,0:T(8,128)S(1)}, u32[]{:S(2)}, u32[]{:S(2)}) collective-permute-start(f32[3,4,64,128]{3,2,1,0:T(8,128)S(1)} %get-tuple-element.41), channel_id=1, source_target_pairs={{0,1},{1,0},{2,3},{3,2},{4,5},{5,4},{6,7},{7,6},{8,9},{9,8},{10,11... | collective-permute-start | bytes 1179656 | tf_op jit(solution)/shard_map/ppermute | solution.py:343
  36.8 6.0 %collective-permute-start.2 = (f32[8,32,128]{2,1,0:T(8,128)S(1)}, f32[8,32,128]{2,1,0:T(8,128)S(1)}, u32[]{:S(2)}, u32[]{:S(2)}) collective-permute-start(f32[8,32,128]{2,1,0:T(8,128)S(1)} %get-tuple-element.35.refs_0_), channel_id=1, source_target_pairs={{0,8},{8,0},{16,24},{24,16},{1,9},{9,1},{17,25},{25,17},{2,10},{10... | collective-permute-start | bytes 393224 | tf_op jit(solution)/shard_map/ppermute | solution.py:349
  38.6 8.4 %collective-permute-start.3 = (f32[8,32,128]{2,1,0:T(8,128)S(1)}, f32[8,32,128]{2,1,0:T(8,128)S(1)}, u32[]{:S(2)}, u32[]{:S(2)}) collective-permute-start(f32[8,32,128]{2,1,0:T(8,128)S(1)} %get-tuple-element.35.refs_0_), channel_id=1, source_target_pairs={{0,16},{8,24},{16,0},{24,8},{1,17},{9,25},{17,1},{25,9},{2,18},{10... | collective-permute-start | bytes 393224 | tf_op jit(solution)/shard_map/ppermute | solution.py:349
  40.1 6.9 %collective-permute-start.4 = (f32[8,32,128]{2,1,0:T(8,128)S(1)}, f32[8,32,128]{2,1,0:T(8,128)S(1)}, u32[]{:S(2)}, u32[]{:S(2)}) collective-permute-start(f32[8,32,128]{2,1,0:T(8,128)S(1)} %get-tuple-element.35.refs_0_), channel_id=1, source_target_pairs={{0,24},{8,16},{16,8},{24,0},{1,25},{9,17},{17,9},{25,1},{2,26},{10... | collective-permute-start | bytes 393224 | tf_op jit(solution)/shard_map/ppermute | solution.py:349
  40.4 13.0 %collective-permute-start.11 = (f32[3,4,64,128]{3,2,1,0:T(8,128)S(1)}, f32[3,4,64,128]{3,2,1,0:T(8,128)S(1)}, u32[]{:S(2)}, u32[]{:S(2)}) collective-permute-start(f32[3,4,64,128]{3,2,1,0:T(8,128)S(1)} %get-tuple-element.42), channel_id=1, source_target_pairs={{0,8},{1,2},{2,1},{3,4},{4,3},{5,6},{6,5},{7,15},{8,0},{9,10},{10,... | collective-permute-start | bytes 1179656 | tf_op jit(solution)/shard_map/ppermute | solution.py:346
  42.8 4.4 %collective-permute-start.16 = (f32[4,64,128]{2,1,0:T(8,128)S(1)}, f32[4,64,128]{2,1,0:T(8,128)S(1)}, u32[]{:S(2)}, u32[]{:S(2)}) collective-permute-start(f32[4,64,128]{2,1,0:T(8,128)S(1)} %get-tuple-element.50), channel_id=1, source_target_pairs={{0,1},{1,0},{2,3},{3,2},{4,5},{5,4},{6,7},{7,6},{8,9},{9,8},{10,11... | collective-permute-start | bytes 393224 | tf_op jit(solution)/shard_map/ppermute | solution.py:343
  47.0 5.0 %collective-permute-start.17 = (f32[4,64,128]{2,1,0:T(8,128)S(1)}, f32[4,64,128]{2,1,0:T(8,128)S(1)}, u32[]{:S(2)}, u32[]{:S(2)}) collective-permute-start(f32[4,64,128]{2,1,0:T(8,128)S(1)} %get-tuple-element.51), channel_id=1, source_target_pairs={{0,8},{1,2},{2,1},{3,4},{4,3},{5,6},{6,5},{7,15},{8,0},{9,10},{10,... | collective-permute-start | bytes 393224 | tf_op jit(solution)/shard_map/ppermute | solution.py:346
  47.1 6.5 %collective-permute-start.5 = (f32[8,64,128]{2,1,0:T(8,128)S(1)}, f32[8,64,128]{2,1,0:T(8,128)S(1)}, u32[]{:S(2)}, u32[]{:S(2)}) collective-permute-start(f32[8,64,128]{2,1,0:T(8,128)S(1)} %get-tuple-element.37.own), channel_id=1, source_target_pairs={{0,1},{1,0},{2,3},{3,2},{4,5},{5,4},{6,7},{7,6},{8,9},{9,8},{10,11... | collective-permute-start | bytes 786440 | tf_op jit(solution)/shard_map/ppermute | solution.py:343
  47.2 7.6 %collective-permute-start.6 = (f32[8,64,128]{2,1,0:T(8,128)S(1)}, f32[8,64,128]{2,1,0:T(8,128)S(1)}, u32[]{:S(2)}, u32[]{:S(2)}) collective-permute-start(f32[8,64,128]{2,1,0:T(8,128)S(1)} %get-tuple-element.37.own), channel_id=1, source_target_pairs={{0,8},{1,2},{2,1},{3,4},{4,3},{5,6},{6,5},{7,15},{8,0},{9,10},{10,... | collective-permute-start | bytes 786440 | tf_op jit(solution)/shard_map/ppermute | solution.py:346
  52.2 2.6 %copy-start.4 = (f32[1,8,64,128]{3,2,1,0:T(8,128)S(1)}, f32[1,8,64,128]{3,2,1,0:T(8,128)}, u32[]{:S(2)}) copy-start(f32[1,8,64,128]{3,2,1,0:T(8,128)} %param.20) | copy-start | bytes 786436
  52.2 4.9 %collective-permute-start.18 = (f32[8,64,128]{2,1,0:T(8,128)S(1)}, f32[8,64,128]{2,1,0:T(8,128)S(1)}, u32[]{:S(2)}, u32[]{:S(2)}) collective-permute-start(f32[8,64,128]{2,1,0:T(8,128)S(1)} %get-tuple-element.55.own.previous), channel_id=1, source_target_pairs={{0,1},{1,0},{2,3},{3,2},{4,5},{5,4},{6,7},{7,6},{8,9},{9,8},{10,11... | collective-permute-start | bytes 786440 | tf_op jit(solution)/shard_map/ppermute | solution.py:343
  52.3 6.4 %collective-permute-start.19 = (f32[8,64,128]{2,1,0:T(8,128)S(1)}, f32[8,64,128]{2,1,0:T(8,128)S(1)}, u32[]{:S(2)}, u32[]{:S(2)}) collective-permute-start(f32[8,64,128]{2,1,0:T(8,128)S(1)} %get-tuple-element.55.own.previous), channel_id=1, source_target_pairs={{0,8},{1,2},{2,1},{3,4},{4,3},{5,6},{6,5},{7,15},{8,0},{9,10},{10,... | collective-permute-start | bytes 786440 | tf_op jit(solution)/shard_map/ppermute | solution.py:346
  56.0 5.1 %collective-permute-start.12 = (f32[8,64,128]{2,1,0:T(8,128)S(1)}, f32[8,64,128]{2,1,0:T(8,128)S(1)}, u32[]{:S(2)}, u32[]{:S(2)}) collective-permute-start(f32[8,64,128]{2,1,0:T(8,128)S(1)} %get-tuple-element.45.own), channel_id=1, source_target_pairs={{0,1},{1,0},{2,3},{3,2},{4,5},{5,4},{6,7},{7,6},{8,9},{9,8},{10,11... | collective-permute-start | bytes 786440 | tf_op jit(solution)/shard_map/ppermute | solution.py:343
  56.1 6.4 %collective-permute-start.13 = (f32[8,64,128]{2,1,0:T(8,128)S(1)}, f32[8,64,128]{2,1,0:T(8,128)S(1)}, u32[]{:S(2)}, u32[]{:S(2)}) collective-permute-start(f32[8,64,128]{2,1,0:T(8,128)S(1)} %get-tuple-element.45.own), channel_id=1, source_target_pairs={{0,8},{1,2},{2,1},{3,4},{4,3},{5,6},{6,5},{7,15},{8,0},{9,10},{10,... | collective-permute-start | bytes 786440 | tf_op jit(solution)/shard_map/ppermute | solution.py:346
  60.0 5.0 %collective-permute-start.20 = (f32[8,64,128]{2,1,0:T(8,128)S(1)}, f32[8,64,128]{2,1,0:T(8,128)S(1)}, u32[]{:S(2)}, u32[]{:S(2)}) collective-permute-start(f32[8,64,128]{2,1,0:T(8,128)S(1)} %get-tuple-element.57.own), channel_id=1, source_target_pairs={{0,1},{1,0},{2,3},{3,2},{4,5},{5,4},{6,7},{7,6},{8,9},{9,8},{10,11... | collective-permute-start | bytes 786440 | tf_op jit(solution)/shard_map/ppermute | solution.py:343
  60.2 6.4 %collective-permute-start.21 = (f32[8,64,128]{2,1,0:T(8,128)S(1)}, f32[8,64,128]{2,1,0:T(8,128)S(1)}, u32[]{:S(2)}, u32[]{:S(2)}) collective-permute-start(f32[8,64,128]{2,1,0:T(8,128)S(1)} %get-tuple-element.57.own), channel_id=1, source_target_pairs={{0,8},{1,2},{2,1},{3,4},{4,3},{5,6},{6,5},{7,15},{8,0},{9,10},{10,... | collective-permute-start | bytes 786440 | tf_op jit(solution)/shard_map/ppermute | solution.py:346
  63.8 5.1 %collective-permute-start.14 = (f32[8,64,128]{2,1,0:T(8,128)S(1)}, f32[8,64,128]{2,1,0:T(8,128)S(1)}, u32[]{:S(2)}, u32[]{:S(2)}) collective-permute-start(f32[8,64,128]{2,1,0:T(8,128)S(1)} %get-tuple-element.47.own), channel_id=1, source_target_pairs={{0,1},{1,0},{2,3},{3,2},{4,5},{5,4},{6,7},{7,6},{8,9},{9,8},{10,11... | collective-permute-start | bytes 786440 | tf_op jit(solution)/shard_map/ppermute | solution.py:343
  64.0 6.4 %collective-permute-start.15 = (f32[8,64,128]{2,1,0:T(8,128)S(1)}, f32[8,64,128]{2,1,0:T(8,128)S(1)}, u32[]{:S(2)}, u32[]{:S(2)}) collective-permute-start(f32[8,64,128]{2,1,0:T(8,128)S(1)} %get-tuple-element.47.own), channel_id=1, source_target_pairs={{0,8},{1,2},{2,1},{3,4},{4,3},{5,6},{6,5},{7,15},{8,0},{9,10},{10,... | collective-permute-start | bytes 786440 | tf_op jit(solution)/shard_map/ppermute | solution.py:346
  67.8 4.8 %collective-permute-start.24 = (f32[8,64,128]{2,1,0:T(8,128)S(1)}, f32[8,64,128]{2,1,0:T(8,128)S(1)}, u32[]{:S(2)}, u32[]{:S(2)}) collective-permute-start(f32[8,64,128]{2,1,0:T(8,128)S(1)} %get-tuple-element.61.own), channel_id=1, source_target_pairs={{0,1},{1,0},{2,3},{3,2},{4,5},{5,4},{6,7},{7,6},{8,9},{9,8},{10,11... | collective-permute-start | bytes 786440 | tf_op jit(solution)/shard_map/ppermute | solution.py:343
  67.9 6.4 %collective-permute-start.25 = (f32[8,64,128]{2,1,0:T(8,128)S(1)}, f32[8,64,128]{2,1,0:T(8,128)S(1)}, u32[]{:S(2)}, u32[]{:S(2)}) collective-permute-start(f32[8,64,128]{2,1,0:T(8,128)S(1)} %get-tuple-element.61.own), channel_id=1, source_target_pairs={{0,8},{1,2},{2,1},{3,4},{4,3},{5,6},{6,5},{7,15},{8,0},{9,10},{10,... | collective-permute-start | bytes 786440 | tf_op jit(solution)/shard_map/ppermute | solution.py:346
  72.5 14.3 %copy-start.5 = (f32[8,64,128]{2,1,0:T(8,128)S(1)}, f32[8,64,128]{2,1,0:T(8,128)}, u32[]{:S(2)}) copy-start(f32[8,64,128]{2,1,0:T(8,128)} %get-tuple-element.59.present) | copy-start | bytes 786436
  75.6 6.4 %collective-permute-start.26 = (f32[8,32,128]{2,1,0:T(8,128)S(1)}, f32[8,32,128]{2,1,0:T(8,128)S(1)}, u32[]{:S(2)}, u32[]{:S(2)}) collective-permute-start(f32[8,32,128]{2,1,0:T(8,128)S(1)} %get-tuple-element.64), channel_id=1, source_target_pairs={{0,8},{8,0},{16,24},{24,16},{1,9},{9,1},{17,25},{25,17},{2,10},{10... | collective-permute-start | bytes 393224 | tf_op jit(solution)/shard_map/ppermute | solution.py:349
  76.6 7.0 %collective-permute-start.27 = (f32[8,32,128]{2,1,0:T(8,128)S(1)}, f32[8,32,128]{2,1,0:T(8,128)S(1)}, u32[]{:S(2)}, u32[]{:S(2)}) collective-permute-start(f32[8,32,128]{2,1,0:T(8,128)S(1)} %get-tuple-element.65), channel_id=1, source_target_pairs={{0,16},{8,24},{16,0},{24,8},{1,17},{9,25},{17,1},{25,9},{2,18},{10... | collective-permute-start | bytes 393224 | tf_op jit(solution)/shard_map/ppermute | solution.py:349
  78.0 6.8 %collective-permute-start.28 = (f32[8,32,128]{2,1,0:T(8,128)S(1)}, f32[8,32,128]{2,1,0:T(8,128)S(1)}, u32[]{:S(2)}, u32[]{:S(2)}) collective-permute-start(f32[8,32,128]{2,1,0:T(8,128)S(1)} %get-tuple-element.66), channel_id=1, source_target_pairs={{0,24},{8,16},{16,8},{24,0},{1,25},{9,17},{17,9},{25,1},{2,26},{10... | collective-permute-start | bytes 393224 | tf_op jit(solution)/shard_map/ppermute | solution.py:349
  79.1 6.4 %collective-permute-start.22 = (f32[8,64,128]{2,1,0:T(8,128)S(1)}, f32[8,64,128]{2,1,0:T(8,128)S(1)}, u32[]{:S(2)}, u32[]{:S(2)}) collective-permute-start(f32[8,64,128]{2,1,0:T(8,128)S(1)} %get-tuple-element.60.own), channel_id=1, source_target_pairs={{0,1},{1,0},{2,3},{3,2},{4,5},{5,4},{6,7},{7,6},{8,9},{9,8},{10,11... | collective-permute-start | bytes 786440 | tf_op jit(solution)/shard_map/ppermute | solution.py:343
  79.1 7.7 %collective-permute-start.23 = (f32[8,64,128]{2,1,0:T(8,128)S(1)}, f32[8,64,128]{2,1,0:T(8,128)S(1)}, u32[]{:S(2)}, u32[]{:S(2)}) collective-permute-start(f32[8,64,128]{2,1,0:T(8,128)S(1)} %get-tuple-element.60.own), channel_id=1, source_target_pairs={{0,8},{1,2},{2,1},{3,4},{4,3},{5,6},{6,5},{7,15},{8,0},{9,10},{10,... | collective-permute-start | bytes 786440 | tf_op jit(solution)/shard_map/ppermute | solution.py:346

commit v3 on v2

--- a/solution.py
+++ b/solution.py
@@ -15,7 +15,7 @@
 
 VMEM = pl.BlockSpec(memory_space=pltpu.VMEM)
 SMEM = pl.BlockSpec(memory_space=pltpu.SMEM)
-HBM = pl.BlockSpec(memory_space=pl.ANY)
+HBM = pl.BlockSpec(memory_space=pltpu.HBM)
 
 
 def f32(*shape):
@@ -107,28 +107,52 @@
         finish(r, stencil(lambda k: flux_x[r + 4 + k]) + diff_y(flux_y, r, width) + part_z[r])
 
 
-def owner_kernel(eps, tilt, azimuth, out, held, sems):
+def sin_cos(angle):
+    square = angle * angle
+    sine, cosine = 0.0, 1.0 / 479001600.0
+    for factor in (-39916800.0, 362880.0, -5040.0, 120.0, -6.0, 1.0):
+        sine = sine * square + 1.0 / factor
+    for factor in (-3628800.0, 40320.0, -720.0, 24.0, -2.0, 1.0):
+        cosine = cosine * square + 1.0 / factor
+    return angle * sine, cosine
+
+
+def owner_kernel(eps, tilt, azimuth, anchor, wx, wy, wz, first, held, held_anchor, sems):
+    rows, count, _ = wx.shape
     copies = [
         pltpu.make_async_copy(ref, held.at[n], sems.at[n])
         for n, ref in enumerate((eps, tilt, azimuth))
     ]
+    copies.append(pltpu.make_async_copy(anchor, held_anchor, sems.at[3]))
     for copy in copies:
         copy.start()
     for copy in copies:
         copy.wait()
-    for r in range(out.shape[1]):
+    for r in range(rows):
         size = jnp.sqrt(2.0 * held[0, r])
-        flat = size * jnp.sin(held[1, r])
-        out[0, r] = flat * jnp.cos(held[2, r])
-        out[1, r] = flat * jnp.sin(held[2, r])
-        out[2, r] = size * jnp.cos(held[1, r])
-
-
-def prepare_kernel(shots, parts, step, anchor, sx, sy, sz, wavelet, rx, ry, rz, traces, speed,
-                   own, partner, across, slope, src, inj, flags, matrix, speed_out, wide):
+        sin_tilt, cos_tilt = sin_cos(held[1, r])
+        sin_half, cos_half = sin_cos(0.5 * held[2, r])
+        flat = size * sin_tilt
+        wx[r] = flat * (1.0 - 2.0 * sin_half * sin_half)
+        wy[r] = flat * (2.0 * sin_half * cos_half)
+        wz[r] = size * cos_tilt
+    first[...] = jnp.full(first.shape, (held_anchor[0] // count).astype(jnp.float32))
+
+
+def prepare_kernel(shots, parts, step, anchor, sx, sy, sz, wavelet, rx, ry, rz, traces,
+                   own, partner, across, slope, src, inj, flags, matrix,
+                   wide, scalars, wave, receiver, samples_held, sems):
     rows, width, depth = src.shape[1:]
-    count = speed.shape[1]
-    speed_out[...] = speed[...]
+    copies = [
+        pltpu.make_async_copy(ref, scalars[n], sems.at[n])
+        for n, ref in enumerate((step, anchor, sx, sy, sz))
+    ]
+    copies.append(pltpu.make_async_copy(wavelet, wave, sems.at[5]))
+    for n, ref in enumerate((rx, ry, rz)):
+        copies.append(pltpu.make_async_copy(ref, receiver[n], sems.at[6 + n]))
+    copies.append(pltpu.make_async_copy(traces, samples_held, sems.at[9]))
+    for copy in copies:
+        copy.start()
     shape = matrix.shape
     offset = lax.broadcasted_iota(jnp.int32, shape, 0) % depth - lax.broadcasted_iota(
         jnp.int32, shape, 1
@@ -139,10 +163,12 @@
         entries = jnp.where(offset == -k, -WHOLE[k - 1], entries)
     matrix[...] = entries.astype(jnp.bfloat16)
     fill_field(own, partner, across, wide)
-    for r in range(rows):
-        slope[0, r], slope[1, r], slope[2, r] = slopes_at(wide, rows + r, width, matrix)
+    for i in range(rows + 8):
+        slope[0, i], slope[1, i], slope[2, i] = slopes_at(wide, i + 4, width, matrix)
+    for copy in copies:
+        copy.wait()
     me = lax.axis_index("shot")
-    first_part = anchor[0] // count
+    first_part = scalars[1][0] // (width // parts)
     for k in range(shots):
         part = jnp.bitwise_xor(me, k) - first_part
         for j in range(parts):
@@ -150,24 +176,26 @@
                 (1, depth), jnp.where(part == j, 1.0, 0.0), jnp.float32
             )
     first = lax.axis_index("blk") * rows
-    start = step[0]
+    start = scalars[0][0]
     shape = (rows, width, depth)
     hit = (
-        (lax.broadcasted_iota(jnp.int32, shape, 0) == sx[0] - first)
-        & (lax.broadcasted_iota(jnp.int32, shape, 1) == sy[0])
-        & (lax.broadcasted_iota(jnp.int32, shape, 2) == sz[0])
-    )
+        (lax.broadcasted_iota(jnp.int32, shape, 0) == scalars[2][0] - first)
+        & (lax.broadcasted_iota(jnp.int32, shape, 1) == scalars[3][0])
+        & (lax.broadcasted_iota(jnp.int32, shape, 2) == scalars[4][0])
+    )
+    moment = lax.broadcasted_iota(jnp.int32, wave.shape, 1)
     for t in range(STEPS - 1):
-        src[t] = jnp.where(hit, wavelet[0, start + t], 0.0)
+        value = jnp.sum(jnp.where(moment == start + t, wave[...], 0.0), axis=1, keepdims=True)
+        src[t] = jnp.where(hit, value, 0.0)
     receivers = rx.shape[1]
-    local = rx[...] - first
-    plane = jnp.where((local >= 0) & (local < rows), local * width + ry[...], -1)
+    local = receiver[0][...] - first
+    plane = jnp.where((local >= 0) & (local < rows), local * width + receiver[1][...], -1)
     pick = (
         lax.broadcasted_iota(jnp.int32, (rows * width, receivers), 0) == plane
     ).astype(jnp.float32)
-    match = lax.broadcasted_iota(jnp.int32, (depth, receivers), 0) == rz[...]
+    match = lax.broadcasted_iota(jnp.int32, (depth, receivers), 0) == receiver[2][...]
     for t in range(STEPS):
-        samples = traces[0, pl.ds(start + t, 1), :]
+        samples = samples_held[0, pl.ds(start + t, 1), :]
         spread = jnp.where(match, samples, 0.0)
         added = lax.dot_general(
             pick,
@@ -179,6 +207,15 @@
         inj[t] = added.reshape(shape)
 
 
+def relay_kernel(parts, first, own, received, *refs):
+    out = refs[-1] if len(refs) < 3 else refs[-2]
+    part = lax.axis_index("shot").astype(jnp.float32) - first[0:1, :]
+    inside = (part > -0.5) & (part < parts - 0.5)
+    out[...] = jnp.where(inside, own[...], received[...])
+    if len(refs) >= 3:
+        refs[-1][...] = refs[0][...]
+
+
 def window_part(pieces, flags, parts, j):
     chosen = pieces[-1][...]
     for k in reversed(range(len(pieces) - 1)):
@@ -187,59 +224,76 @@
     return chosen
 
 
-def flux_kernel(shots, parts, *refs):
-    pieces = refs[:shots]
-    (flags, slope, matrix, tensor, flux, rest, flux_a, flux_p, edge_a, edge_p, flux_y) = refs[
-        shots:
-    ]
+def edge_rows(field, out_a, out_p):
+    odd = lax.axis_index("blk") % 2
+    low = field.shape[0] - 4
+    out_a[...] = field[pl.ds(odd * low, 4)]
+    out_p[...] = field[pl.ds((1 - odd) * low, 4)]
+
+
+def window_kernel(slots, parts, *refs):
+    held = max(slots) + 1
+    flags, tensor, edge_a, edge_p = refs[2 * held :]
+    count = tensor.shape[2] // parts
+    for a in range(2):
+        pieces = [refs[a * held + slot] for slot in slots]
+        for j in range(parts):
+            tensor[a, :, j * count : (j + 1) * count, :] = window_part(pieces, flags, parts, j)
+        edge_rows(tensor.at[a], edge_a.at[a], edge_p.at[a])
+
+
+def flux_kernel(slots, parts, *refs):
+    held = max(slots) + 1
+    pieces = [refs[slot] for slot in slots]
+    flags, tensor, slope, matrix, _, last, flux, rest, edge_a, edge_p, flux_y = refs[held:]
     rows, width, _ = flux.shape
     count = width // parts
     for j in range(parts):
-        tensor[:, :, j * count : (j + 1) * count, :] = window_part(pieces, flags, parts, j)
+        last[:, j * count : (j + 1) * count, :] = window_part(pieces, flags, parts, j)
+    edge_rows(last, edge_a, edge_p)
     clear_sides(flux_y, width)
     for r in range(rows):
-        wx, wy, wz = tensor[0, r], tensor[1, r], tensor[2, r]
-        along = wx * slope[0, r] + wy * slope[1, r] + wz * slope[2, r]
+        wx, wy, wz = tensor[0, r], tensor[1, r], last[r]
+        along = wx * slope[0, r + 4] + wy * slope[1, r + 4] + wz * slope[2, r + 4]
         size = 1.0 + (wx * wx + wy * wy + wz * wz)
-        flux[r] = size * slope[0, r] - wx * along
-        flux_y[r, PAD : PAD + width, :] = size * slope[1, r] - wy * along
-        rest[r] = diff_z(size * slope[2, r] - wz * along, matrix)
+        flux[r] = size * slope[0, r + 4] - wx * along
+        flux_y[r, PAD : PAD + width, :] = size * slope[1, r + 4] - wy * along
+        rest[r] = diff_z(size * slope[2, r + 4] - wz * along, matrix)
     for r in range(rows):
         rest[r] = rest[r] + diff_y(flux_y, r, width)
-    odd = lax.axis_index("blk") % 2
-    low = rows - 4
-    flux_a[...] = flux[pl.ds(odd * low, 4)]
-    flux_p[...] = flux[pl.ds((1 - odd) * low, 4)]
-    edge_a[...] = tensor[:, pl.ds(odd * low, 4)]
-    edge_p[...] = tensor[:, pl.ds((1 - odd) * low, 4)]
-
-
-def speed_kernel(shots, parts, *refs):
-    pieces = refs[:shots]
-    flags, present, speed, operand = refs[shots:]
+
+
+def speed_kernel(slots, parts, *refs):
+    held = max(slots) + 1
+    pieces = [refs[slot] for slot in slots]
+    flags, present, speed, operand = refs[held:]
     count = speed.shape[1] // parts
     for j in range(parts):
         speed[:, j * count : (j + 1) * count, :] = window_part(pieces, flags, parts, j)
     operand[...] = speed[...] * present[...]
 
 
-def coef_kernel(tensor, partner, across, coef):
-    rows = tensor.shape[1]
+def forward_first(tensor, tensor_p, tensor_a, last, last_p, last_a, slope, flux, rest,
+                  own, previous, speed, src, image, following, coef, flux_x):
+    rows = rest.shape[0]
     blk, blocks = lax.axis_index("blk"), lax.axis_size("blk")
-    for a in range(3):
-        place_halos(coef.at[a], (), tensor.at[a], partner.at[a], across.at[a])
+    for a in range(2):
+        place_halos(coef.at[a], (), tensor.at[a], tensor_p.at[a], tensor_a.at[a])
+    place_halos(coef.at[2], (), last, last_p, last_a)
     for i in range(rows + 8):
-        size = 1.0 + (coef[0, i] * coef[0, i] + coef[1, i] * coef[1, i] + coef[2, i] * coef[2, i])
+        wx, wy, wz = coef[0, i], coef[1, i], coef[2, i]
+        size = 1.0 + (wx * wx + wy * wy + wz * wz)
         if i < 4:
             size = jnp.where(blk == 0, 0.0, size)
         if i >= rows + 4:
             size = jnp.where(blk == blocks - 1, 0.0, size)
         coef[3, i] = size
-
-
-def forward_first(flux, flux_p, flux_a, rest, own, previous, speed, src, image, following, flux_x):
-    place_halos(flux_x, (), flux, flux_p, flux_a)
-    for r in range(rest.shape[0]):
+        if 4 <= i < rows + 4:
+            flux_x[i] = flux[i - 4]
+        else:
+            along = wx * slope[0, i] + wy * slope[1, i] + wz * slope[2, i]
+            flux_x[i] = size * slope[0, i] - wx * along
+    for r in range(rows):
         value = stencil(lambda k: flux_x[r + 4 + k]) + rest[r]
         image[r] = value
         following[r] = 2.0 * own[r] - previous[r] + speed[r] * value + src[0, r]
@@ -258,7 +312,8 @@
 
 def backward(t, own, partner, across, coef, matrix, present, later, inj, *refs):
     if t == 0:
-        (earlier,) = refs[:1]
+        earlier, copied = refs[:2]
+        copied[...] = present[...]
     elif t == 1:
         speed, lambda3, image0, image1, image2, earlier, operand, known = refs[:8]
     else:
@@ -294,6 +349,14 @@
                 flags[at : at + 1, :] > 0.5, grad[:, j * count : (j + 1) * count, :], held
             )
         chunk[...] = held
+
+
+def total_kernel(*refs):
+    out = refs[-1]
+    total = refs[0][...]
+    for ref in refs[1:-2]:
+        total = total + ref[...]
+    out[...] = total
 
 
 def on_device(
@@ -351,71 +414,120 @@
     current, previous = state_now[0], state_before[0]
     present, later = adjoint_now[0], adjoint_later[0]
 
-    piece = call(
+    wx, wy, wz, first = call(
         "owner",
         owner_kernel,
-        f32(3, rows, count, depth),
-        [(a, HBM) for a in (epsilon, tilt_angle, azimuth)],
-        (pltpu.VMEM((3, rows, count, depth), jnp.float32), pltpu.SemaphoreType.DMA((3,))),
-    )
-    pieces = [piece] + [to_owners(piece, k) for k in range(1, shots)]
-    now_a = across_chips(current)
-    now_p = to_partner(current)
-
-    slope, src, inj, flags, matrix, speed_piece = call(
-        "prepare",
-        functools.partial(prepare_kernel, shots, parts),
+        (f32(rows, count, depth),) * 3 + (f32(8, depth),),
+        [(a, HBM) for a in (epsilon, tilt_angle, azimuth, aperture_anchor)],
         (
-            f32(3, rows, width, depth),
-            f32(STEPS - 1, rows, width, depth),
-            f32(STEPS, rows, width, depth),
-            f32(shots * parts, depth),
-            jax.ShapeDtypeStruct((2 * depth, depth), jnp.bfloat16),
-            f32(rows, count, depth),
+            pltpu.VMEM((3, rows, count, depth), jnp.float32),
+            pltpu.SMEM((1,), jnp.int32),
+            pltpu.SemaphoreType.DMA((4,)),
         ),
-        [
-            (a, SMEM)
-            for a in (step_index, aperture_anchor, source_x, source_y, source_z, wavelet)
-        ]
-        + [receiver_x, receiver_y, receiver_z, residual_traces, courant_sq]
-        + [current, now_p, now_a],
-        scratch[:1],
-        work,
-    )
-    speed_pieces = [speed_piece] + [to_owners(speed_piece, k) for k in range(1, shots)]
-
-    flux_edge, edge = f32(4, width, depth), f32(3, 4, width, depth)
-    tensor, flux, rest, flux_a, flux_p, edge_a, edge_p = call(
+    )
+    model = [wx, wy, wz, courant_sq]
+    piece = f32(rows, count, depth)
+
+    def prepare():
+        now_a = across_chips(current)
+        now_p = to_partner(current)
+        return call(
+            "prepare",
+            functools.partial(prepare_kernel, shots, parts),
+            (
+                f32(3, rows + 8, width, depth),
+                f32(STEPS - 1, rows, width, depth),
+                f32(STEPS, rows, width, depth),
+                f32(shots * parts, depth),
+                jax.ShapeDtypeStruct((2 * depth, depth), jnp.bfloat16),
+            ),
+            [
+                (a, HBM)
+                for a in (step_index, aperture_anchor, source_x, source_y, source_z, wavelet)
+                + (receiver_x, receiver_y, receiver_z, residual_traces)
+            ]
+            + [current, now_p, now_a],
+            (
+                scratch[0],
+                [pltpu.SMEM((1,), jnp.int32)] * 5,
+                pltpu.VMEM(wavelet.shape, jnp.float32),
+                [pltpu.VMEM(receiver_x.shape, jnp.int32)] * 3,
+                pltpu.VMEM(residual_traces.shape, jnp.float32),
+                pltpu.SemaphoreType.DMA((10,)),
+            ),
+            work,
+        )
+
+    if shots == 4 and parts == 2:
+        slots = (0, 1, 2, 1)
+        relay = functools.partial(relay_kernel, parts)
+        first = to_owners(first, 1)
+        over_y = [to_owners(wx, 2), to_owners(wy, 2)]
+        over_x = []
+        going = model[2:]
+        for n in range(4):
+            if n < 2:
+                sent, going_on = call(
+                    f"relay{n}",
+                    relay,
+                    (piece, piece),
+                    [first, model[n], over_y[n], going[n]],
+                )
+                over_y.append(to_owners(going_on, 2))
+            else:
+                (sent,) = call(
+                    f"relay{n}",
+                    relay,
+                    (piece,),
+                    [first, model[n], over_y[n], (over_x[n - 2], HBM)],
+                )
+            over_x.append(to_owners(sent, 1))
+        gathered = [[model[n], over_x[n], over_y[n]] for n in range(4)]
+        after = sent
+    else:
+        slots = tuple(range(shots))
+        gathered = [[a] + [to_owners(a, k) for k in range(1, shots)] for a in model]
+        after = wx
+    slope, src, inj, flags, matrix = prepare()
+
+    edge = f32(4, width, depth)
+    tensor, edge_a, edge_p = call(
+        "window",
+        functools.partial(window_kernel, slots, parts),
+        (f32(2, rows, width, depth), f32(2, 4, width, depth), f32(2, 4, width, depth)),
+        gathered[0] + gathered[1] + [flags],
+    )
+    edge_a = across_chips(edge_a)
+    edge_p = to_partner(edge_p)
+    last, flux, rest, last_a, last_p = call(
         "flux",
-        functools.partial(flux_kernel, shots, parts),
-        (f32(3, rows, width, depth), field, field, flux_edge, flux_edge, edge, edge),
-        pieces + [flags, slope, matrix],
+        functools.partial(flux_kernel, slots, parts),
+        (field, field, field, edge, edge),
+        gathered[2] + [flags, tensor, slope, matrix, (after, HBM)],
         scratch[2:3],
         work // 3,
     )
-    flux_a = across_chips(flux_a)
-    flux_p = to_partner(flux_p)
-    edge_a = across_chips(edge_a)
-    edge_p = to_partner(edge_p)
+    last_a = across_chips(last_a)
+    last_p = to_partner(last_p)
 
     speed, operand = call(
         "speed",
-        functools.partial(speed_kernel, shots, parts),
+        functools.partial(speed_kernel, slots, parts),
         (field, field),
-        speed_pieces + [flags, present],
+        gathered[3] + [flags, present],
     )
     op_a = across_chips(operand)
     op_p = to_partner(operand)
 
-    image, following = call(
+    image, following, coef = call(
         "forward0",
         forward_first,
-        (field, field),
-        [flux, flux_p, flux_a, rest, current, previous, speed, src],
+        (field, field, f32(4, rows + 8, width, depth)),
+        [tensor, edge_p, edge_a, last, last_p, last_a, slope, flux, rest]
+        + [current, previous, speed, src],
         scratch[1:2],
         work // 4,
     )
-    coef = call("coef", coef_kernel, f32(4, rows + 8, width, depth), [tensor, edge_p, edge_a])
     images = [image]
     previous, current = current, following
     adjoints = [present]
@@ -459,18 +571,16 @@
         work,
     )
     received = [to_owners(chunks[k], k) for k in range(1, shots)]
-    (final,) = call(
+    final, copied = call(
         "backward3",
         functools.partial(backward, 0),
-        (field,),
+        (field, field),
         [operand, op_p, op_a, coef, matrix, present, later, inj],
         scratch,
         work,
     )
-    model_grad = chunks[0]
-    for part in received:
-        model_grad = model_grad + part
-    return (present[None], final[None], model_grad)
+    model_grad = call("total", total_kernel, piece, [chunks[0]] + received + [(final, HBM)])
+    return (copied[None], final[None], model_grad)
 
 
 def solution(mesh):

time: 89.1 us -> 79.6 us (0.89)
  waiting for transfers between devices: 36.2 us -> 21.7 us
  starting transfers between devices: 24.2 us -> 28.4 us
  Pallas kernels: 15.6 us -> 17.8 us
    ppermute x10, waiting for transfers between devices: 26.5 us -> 15.4 us  [across_chips(): return lax.ppermute(array, ('shot', 'blk'), chip_pairs)]
    ppermute x9 -> x12, starting transfers between devices: 11.7 us -> 17.7 us  [to_owners(): return lax.ppermute(array, 'shot', [(i, i ^ k) for i in range(shots)])]
    ppermute x10, starting transfers between devices: 11.8 us -> 7.77 us  [across_chips(): return lax.ppermute(array, ('shot', 'blk'), chip_pairs)]
    ppermute x9 -> x12, waiting for transfers between devices: 9.66 us -> 6.27 us  [to_owners(): return lax.ppermute(array, 'shot', [(i, i ^ k) for i in range(shots)])]
    pallas_call x13 -> x18, Pallas kernels: 15.6 us -> 17.8 us  [call(): pl.pallas_call(body, name=name, out_shape=outs, in_specs=[s for _, s in p...]
    ppermute x10, starting transfers between devices: 0.82 us -> 2.96 us  [to_partner(): return lax.ppermute(array, 'blk', core_pairs)]
    unnamed x30 -> x38, local copies, waits for them, and re-layouts: 7.94 us -> 7.1 us
  transfers between devices with their start and end apart: 29 -> 32, of which waited for: 14 -> 11; matrix products, arithmetic and copies ran while one was open for 1% -> 0% of each run, Pallas kernels for 11% -> 20%
where the time goes in v3:
time: 79.6 us; the launch traced here: 79.3 us
  starting transfers between devices  28.4 us (36%)
  waiting for transfers between devices  21.7 us (27%)
  Pallas kernels  17.8 us (22%)
  local copies, waits for them, and re-layouts  7.1 us (9%)
  between operations  4.19 us (5%)
    pallas_call x18, Pallas kernels, call(): pl.pallas_call(body, name=name, out_shape=outs, in_specs=[s for _, s in p...  17.8 us
    ppermute x12, starting transfers between devices, to_owners(): return lax.ppermute(array, 'shot', [(i, i ^ k) for i in range(shots)])  17.7 us
    ppermute x10, waiting for transfers between devices, across_chips(): return lax.ppermute(array, ('shot', 'blk'), chip_pairs)  15.4 us
    ppermute x10, starting transfers between devices, across_chips(): return lax.ppermute(array, ('shot', 'blk'), chip_pairs)  7.77 us
    unnamed x38, local copies, waits for them, and re-layouts  7.1 us
    ppermute x12, waiting for transfers between devices, to_owners(): return lax.ppermute(array, 'shot', [(i, i ^ k) for i in range(shots)])  6.27 us
    ppermute x10, starting transfers between devices, to_partner(): return lax.ppermute(array, 'blk', core_pairs)  2.96 us
  transfers between devices with their start and end apart: 32, of which 11 were waited for; matrix products, arithmetic and copies ran while one was open for 0% of the time, Pallas kernels for 20%

profile of v3, /device:TPU:0, one launch (start us, length us, event | category | flops | bytes accessed | tf_op | source)
XLA Modules:
  0.0 79.3 jit_solution(13187227558581930716)
XLA Ops:
  0.6 0.0 copy-start.4
  1.3 0.9 %copy-done.11 = f32[8,32,128]{2,1,0:T(8,128)S(1)} copy-done((f32[8,32,128]{2,1,0:T(8,128)S(1)}, f32[8,32,128]{2,1,0:T(8,128)}, u32[]{:S(2)}) %copy-start.11) | copy-done | bytes 131096
  2.2 0.9 %copy-done.12 = f32[8,32,128]{2,1,0:T(8,128)S(1)} copy-done((f32[8,32,128]{2,1,0:T(8,128)S(1)}, f32[8,32,128]{2,1,0:T(8,128)}, u32[]{:S(2)}) %copy-start.12) | copy-done | bytes 131096
  3.1 0.9 %copy-done.13 = f32[8,32,128]{2,1,0:T(8,128)S(1)} copy-done((f32[8,32,128]{2,1,0:T(8,128)S(1)}, f32[8,32,128]{2,1,0:T(8,128)}, u32[]{:S(2)}) %copy-start.13) | copy-done | bytes 131096
  4.1 1.4 %owner.1 = (f32[8,32,128]{2,1,0:T(8,128)S(1)}, f32[8,32,128]{2,1,0:T(8,128)S(1)}, f32[8,32,128]{2,1,0:T(8,128)S(1)}, f32[8,128]{1,0:T(8,128)S(1)}) custom-call(f32[8,32,128]{2,1,0:T(8,128)S(1)} %copy-done.11, f32[8,32,128]{2,1,0:T(8,128)S(1)} %copy-done.12, f32[8,32,128]{2,1,0:T(8,128)S(1)} %copy-done.13, s32[1]{0:T(128)S(6)} %copy.21.anchor), custom_call_target="tpu_custom_call" | custom-call | flops 1048576 | bytes 1048576 | tf_op jit(solution)/shard_map/owner/pallas_call | solution.py:27
  5.5 3.0 %collective-permute-start.9 = (f32[8,32,128]{2,1,0:T(8,128)S(1)}, f32[8,32,128]{2,1,0:T(8,128)S(1)}, u32[]{:S(2)}, u32[]{:S(2)}) collective-permute-start(f32[8,32,128]{2,1,0:T(8,128)S(1)} %get-tuple-element.52.own.refs_0_), channel_id=1, source_target_pairs={{0,16},{8,24},{16,0},{24,8},{1,17},{9,25},{17,1},{25,9},{2,18},{10... | collective-permute-start | bytes 393224 | tf_op jit(solution)/shard_map/ppermute | solution.py:412
  8.5 1.5 %collective-permute-start = (f32[8,128]{1,0:T(8,128)S(1)}, f32[8,128]{1,0:T(8,128)S(1)}, u32[]{:S(2)}, u32[]{:S(2)}) collective-permute-start(f32[8,128]{1,0:T(8,128)S(1)} %get-tuple-element.46), channel_id=1, source_target_pairs={{0,8},{8,0},{16,24},{24,16},{1,9},{9,1},{17,25},{25,17},{2,10},{10... | collective-permute-start | bytes 12296 | tf_op jit(solution)/shard_map/ppermute | solution.py:412
  10.0 0.5 collective-permute-start.1
  10.5 1.6 %collective-permute-done.first = f32[8,128]{1,0:T(8,128)S(1)} collective-permute-done((f32[8,128]{1,0:T(8,128)S(1)}, f32[8,128]{1,0:T(8,128)S(1)}, u32[]{:S(2)}, u32[]{:S(2)}) %collective-permute-start) | collective-permute-done | bytes 4128 | tf_op jit(solution)/shard_map/ppermute | solution.py:412
  12.1 0.3 collective-permute-done.9.received.refs_2_
  12.4 2.5 %collective-permute-start.10 = (f32[8,32,128]{2,1,0:T(8,128)S(1)}, f32[8,32,128]{2,1,0:T(8,128)S(1)}, u32[]{:S(2)}, u32[]{:S(2)}) collective-permute-start(f32[8,32,128]{2,1,0:T(8,128)S(1)} %get-tuple-element.54), channel_id=1, source_target_pairs={{0,8},{8,0},{16,24},{24,16},{1,9},{9,1},{17,25},{25,17},{2,10},{10... | collective-permute-start | bytes 393224 | tf_op jit(solution)/shard_map/ppermute | solution.py:412
  15.0 0.2 collective-permute-start.6
  15.1 1.9 %collective-permute-start.13 = (f32[8,32,128]{2,1,0:T(8,128)S(1)}, f32[8,32,128]{2,1,0:T(8,128)S(1)}, u32[]{:S(2)}, u32[]{:S(2)}) collective-permute-start(f32[8,32,128]{2,1,0:T(8,128)S(1)} %get-tuple-element.58), channel_id=1, source_target_pairs={{0,16},{8,24},{16,0},{24,8},{1,17},{9,25},{17,1},{25,9},{2,18},{10... | collective-permute-start | bytes 393224 | tf_op jit(solution)/shard_map/ppermute | solution.py:412
  17.0 0.9 %copy-done.5 = f32[8,32,128]{2,1,0:T(8,128)S(1)} copy-done((f32[8,32,128]{2,1,0:T(8,128)S(1)}, f32[8,32,128]{2,1,0:T(8,128)}, u32[]{:S(2)}) %copy-start.5) | copy-done | bytes 131096
  18.0 1.6 %collective-permute-start.3 = (f32[8,32,128]{2,1,0:T(8,128)S(1)}, f32[8,32,128]{2,1,0:T(8,128)S(1)}, u32[]{:S(2)}, u32[]{:S(2)}) collective-permute-start(f32[8,32,128]{2,1,0:T(8,128)S(1)} %get-tuple-element.49), channel_id=1, source_target_pairs={{0,8},{8,0},{16,24},{24,16},{1,9},{9,1},{17,25},{25,17},{2,10},{10... | collective-permute-start | bytes 393224 | tf_op jit(solution)/shard_map/ppermute | solution.py:412
  19.5 0.5 collective-permute-start.2
  20.0 0.9 %collective-permute-done.13.received.refs_2_ = f32[8,32,128]{2,1,0:T(8,128)S(1)} collective-permute-done((f32[8,32,128]{2,1,0:T(8,128)S(1)}, f32[8,32,128]{2,1,0:T(8,128)S(1)}, u32[]{:S(2)}, u32[]{:S(2)}) %collective-permute-start.13) | collective-permute-done | bytes 131104 | tf_op jit(solution)/shard_map/ppermute | solution.py:412
  21.0 1.5 %collective-permute-start.14 = (f32[8,32,128]{2,1,0:T(8,128)S(1)}, f32[8,32,128]{2,1,0:T(8,128)S(1)}, u32[]{:S(2)}, u32[]{:S(2)}) collective-permute-start(f32[8,32,128]{2,1,0:T(8,128)S(1)} %relay2.1), channel_id=1, source_target_pairs={{0,8},{8,0},{16,24},{24,16},{1,9},{9,1},{17,25},{25,17},{2,10},{10... | collective-permute-start | bytes 393224 | tf_op jit(solution)/shard_map/ppermute | solution.py:412
  25.1 0.0 copy-start.6
  25.1 0.9 %copy-done.6 = f32[8,32,128]{2,1,0:T(8,128)S(1)} copy-done((f32[8,32,128]{2,1,0:T(8,128)S(1)}, f32[8,32,128]{2,1,0:T(8,128)}, u32[]{:S(2)}) %copy-start.6) | copy-done | bytes 131096
  26.0 1.2 %collective-permute-start.4 = (f32[8,32,128]{2,1,0:T(8,128)S(1)}, f32[8,32,128]{2,1,0:T(8,128)S(1)}, u32[]{:S(2)}, u32[]{:S(2)}) collective-permute-start(f32[8,32,128]{2,1,0:T(8,128)S(1)} %relay3.1.refs_7_), channel_id=1, source_target_pairs={{0,8},{8,0},{16,24},{24,16},{1,9},{9,1},{17,25},{25,17},{2,10},{10... | collective-permute-start | bytes 393224 | tf_op jit(solution)/shard_map/ppermute | solution.py:412
  27.3 2.1 %prepare.1 = (f32[3,16,64,128]{3,2,1,0:T(8,128)S(1)}, f32[3,8,64,128]{3,2,1,0:T(8,128)S(1)}, f32[4,8,64,128]{3,2,1,0:T(8,128)S(1)}, f32[8,128]{1,0:T(8,128)S(1)}, bf16[256,128]{1,0:T(8,128)(2,1)S(1)}) custom-call(s32[1]{0:T(128)S(6)} %copy.22.step, s32[1]{0:T(128)S(6)} %copy.21.anchor, s32[1]{0:T(128)S(6)} %copy.23.sx, s32[1]{0:T(128)S(6)} %copy.24.sy, ...), custom_call_target="tpu_custom_call" | custom-call | flops 13107200 | bytes 1048576 | tf_op jit(solution)/shard_map/prepare/pallas_call | solution.py:27
  29.4 0.2 window.1
  29.6 0.4 flux.1
  30.0 0.1 collective-permute-start.15
  30.1 0.5 collective-permute-start.11
  30.6 0.9 %collective-permute-start.12 = (f32[2,4,64,128]{3,2,1,0:T(8,128)S(1)}, f32[2,4,64,128]{3,2,1,0:T(8,128)S(1)}, u32[]{:S(2)}, u32[]{:S(2)}) collective-permute-start(f32[2,4,64,128]{3,2,1,0:T(8,128)S(1)} %get-tuple-element.57), channel_id=1, source_target_pairs={{0,8},{1,2},{2,1},{3,4},{4,3},{5,6},{6,5},{7,15},{8,0},{9,10},{10,... | collective-permute-start | bytes 786440 | tf_op jit(solution)/shard_map/ppermute | solution.py:409
  31.5 0.1 speed.1
  31.6 1.1 %collective-permute-start.7 = (f32[8,64,128]{2,1,0:T(8,128)S(1)}, f32[8,64,128]{2,1,0:T(8,128)S(1)}, u32[]{:S(2)}, u32[]{:S(2)}) collective-permute-start(f32[8,64,128]{2,1,0:T(8,128)S(1)} %get-tuple-element.51.own), channel_id=1, source_target_pairs={{0,1},{1,0},{2,3},{3,2},{4,5},{5,4},{6,7},{7,6},{8,9},{9,8},{10,11... | collective-permute-start | bytes 786440 | tf_op jit(solution)/shard_map/ppermute | solution.py:406
  32.7 0.3 collective-permute-start.8
  33.0 1.8 %collective-permute-start.16 = (f32[4,64,128]{2,1,0:T(8,128)S(1)}, f32[4,64,128]{2,1,0:T(8,128)S(1)}, u32[]{:S(2)}, u32[]{:S(2)}) collective-permute-start(f32[4,64,128]{2,1,0:T(8,128)S(1)} %get-tuple-element.63), channel_id=1, source_target_pairs={{0,8},{1,2},{2,1},{3,4},{4,3},{5,6},{6,5},{7,15},{8,0},{9,10},{10,... | collective-permute-start | bytes 393224 | tf_op jit(solution)/shard_map/ppermute | solution.py:409
  34.8 6.4 %collective-permute-done.16.last_a = f32[4,64,128]{2,1,0:T(8,128)S(1)} collective-permute-done((f32[4,64,128]{2,1,0:T(8,128)S(1)}, f32[4,64,128]{2,1,0:T(8,128)S(1)}, u32[]{:S(2)}, u32[]{:S(2)}) %collective-permute-start.16) | collective-permute-done | bytes 131104 | tf_op jit(solution)/shard_map/ppermute | solution.py:409
  41.2 1.7 %forward0.1 = (f32[8,64,128]{2,1,0:T(8,128)S(1)}, f32[8,64,128]{2,1,0:T(8,128)S(1)}, f32[4,16,64,128]{3,2,1,0:T(8,128)}) custom-call(f32[2,8,64,128]{3,2,1,0:T(8,128)S(1)} %get-tuple-element.55.refs_4_.tensor, f32[2,4,64,128]{3,2,1,0:T(8,128)S(1)} %collective-permute-done.11.tensor_p, f32[2,4,64,128]{3,2,1,0:T(8,128)S(1)} %collective-permute-done.12.tensor_a, ...), custom_call_target="tpu_custom_call" | custom-call | flops 3276800 | bytes 1048576 | tf_op jit(solution)/shard_map/forward0/pallas_call | solution.py:27
  42.9 0.9 %collective-permute-start.22 = (f32[8,64,128]{2,1,0:T(8,128)S(1)}, f32[8,64,128]{2,1,0:T(8,128)S(1)}, u32[]{:S(2)}, u32[]{:S(2)}) collective-permute-start(f32[8,64,128]{2,1,0:T(8,128)S(1)} %get-tuple-element.75.own.previous), channel_id=1, source_target_pairs={{0,8},{1,2},{2,1},{3,4},{4,3},{5,6},{6,5},{7,15},{8,0},{9,10},{10,... | collective-permute-start | bytes 786440 | tf_op jit(solution)/shard_map/ppermute | solution.py:409
  43.8 1.6 %copy-done = f32[4,16,64,128]{3,2,1,0:T(8,128)S(1)} copy-done((f32[4,16,64,128]{3,2,1,0:T(8,128)S(1)}, f32[4,16,64,128]{3,2,1,0:T(8,128)}, u32[]{:S(2)}) %copy-start) | copy-done | bytes 2097176
  45.4 1.2 %backward0.1 = (f32[8,64,128]{2,1,0:T(8,128)S(1)}, f32[8,64,128]{2,1,0:T(8,128)S(1)}) custom-call(f32[8,64,128]{2,1,0:T(8,128)S(1)} %get-tuple-element.51.own, f32[8,64,128]{2,1,0:T(8,128)S(1)} %collective-permute-done.7.partner, f32[8,64,128]{2,1,0:T(8,128)S(1)} %collective-permute-done.8.across, f32[4,16,64,128]{3,2,1,0:T(8,128)S(1)} %copy-done, ...), custom_call_target="tpu_custom_call" | custom-call | flops 13107200 | bytes 1048576 | tf_op jit(solution)/shard_map/backward0/pallas_call | solution.py:27
  46.6 0.7 collective-permute-start.17
  47.3 0.6 collective-permute-start.18
  47.9 1.4 %collective-permute-done.22.across = f32[8,64,128]{2,1,0:T(8,128)S(1)} collective-permute-done((f32[8,64,128]{2,1,0:T(8,128)S(1)}, f32[8,64,128]{2,1,0:T(8,128)S(1)}, u32[]{:S(2)}, u32[]{:S(2)}) %collective-permute-start.22) | collective-permute-done | bytes 262176 | tf_op jit(solution)/shard_map/ppermute | solution.py:409
  49.2 1.2 %forward1.1 = (f32[8,64,128]{2,1,0:T(8,128)S(1)}, f32[8,64,128]{2,1,0:T(8,128)S(1)}) custom-call(f32[8,64,128]{2,1,0:T(8,128)S(1)} %get-tuple-element.75.own.previous, f32[8,64,128]{2,1,0:T(8,128)S(1)} %collective-permute-done.21.partner, f32[8,64,128]{2,1,0:T(8,128)S(1)} %collective-permute-done.22.across, f32[4,16,64,128]{3,2,1,0:T(8,128)S(1)} %copy-done.1, ...), custom_call_target="tpu_custom_call" | custom-call | flops 13107200 | bytes 1048576 | tf_op jit(solution)/shard_map/forward1/pallas_call | solution.py:27
  50.5 0.2 collective-permute-start.23
  50.7 0.9 %collective-permute-start.24 = (f32[8,64,128]{2,1,0:T(8,128)S(1)}, f32[8,64,128]{2,1,0:T(8,128)S(1)}, u32[]{:S(2)}, u32[]{:S(2)}) collective-permute-start(f32[8,64,128]{2,1,0:T(8,128)S(1)} %get-tuple-element.77.own), channel_id=1, source_target_pairs={{0,8},{1,2},{2,1},{3,4},{4,3},{5,6},{6,5},{7,15},{8,0},{9,10},{10,... | collective-permute-start | bytes 786440 | tf_op jit(solution)/shard_map/ppermute | solution.py:409
  51.6 2.1 %collective-permute-done.18.across = f32[8,64,128]{2,1,0:T(8,128)S(1)} collective-permute-done((f32[8,64,128]{2,1,0:T(8,128)S(1)}, f32[8,64,128]{2,1,0:T(8,128)S(1)}, u32[]{:S(2)}, u32[]{:S(2)}) %collective-permute-start.18) | collective-permute-done | bytes 262176 | tf_op jit(solution)/shard_map/ppermute | solution.py:409
  53.7 1.2 %backward1.1 = (f32[8,64,128]{2,1,0:T(8,128)S(1)}, f32[8,64,128]{2,1,0:T(8,128)S(1)}) custom-call(f32[8,64,128]{2,1,0:T(8,128)S(1)} %get-tuple-element.70.own, f32[8,64,128]{2,1,0:T(8,128)S(1)} %collective-permute-done.17.partner, f32[8,64,128]{2,1,0:T(8,128)S(1)} %collective-permute-done.18.across, f32[4,16,64,128]{3,2,1,0:T(8,128)S(1)} %copy-done.1, ...), custom_call_target="tpu_custom_call" | custom-call | flops 13107200 | bytes 1048576 | tf_op jit(solution)/shard_map/backward1/pallas_call | solution.py:27
  54.9 0.1 collective-permute-start.19
  55.0 0.7 collective-permute-start.20
  55.7 1.4 %collective-permute-done.24.across = f32[8,64,128]{2,1,0:T(8,128)S(1)} collective-permute-done((f32[8,64,128]{2,1,0:T(8,128)S(1)}, f32[8,64,128]{2,1,0:T(8,128)S(1)}, u32[]{:S(2)}, u32[]{:S(2)}) %collective-permute-start.24) | collective-permute-done | bytes 262176 | tf_op jit(solution)/shard_map/ppermute | solution.py:409
  57.0 1.2 %forward2.1 = (f32[8,64,128]{2,1,0:T(8,128)S(1)}, f32[8,64,128]{2,1,0:T(8,128)S(1)}) custom-call(f32[8,64,128]{2,1,0:T(8,128)S(1)} %get-tuple-element.77.own, f32[8,64,128]{2,1,0:T(8,128)S(1)} %collective-permute-done.23.partner, f32[8,64,128]{2,1,0:T(8,128)S(1)} %collective-permute-done.24.across, f32[4,16,64,128]{3,2,1,0:T(8,128)S(1)} %copy-done.1, ...), custom_call_target="tpu_custom_call" | custom-call | flops 13107200 | bytes 1048576 | tf_op jit(solution)/shard_map/forward2/pallas_call | solution.py:27
  58.3 0.2 collective-permute-start.27
  58.4 0.9 %collective-permute-start.28 = (f32[8,64,128]{2,1,0:T(8,128)S(1)}, f32[8,64,128]{2,1,0:T(8,128)S(1)}, u32[]{:S(2)}, u32[]{:S(2)}) collective-permute-start(f32[8,64,128]{2,1,0:T(8,128)S(1)} %get-tuple-element.83.own), channel_id=1, source_target_pairs={{0,8},{1,2},{2,1},{3,4},{4,3},{5,6},{6,5},{7,15},{8,0},{9,10},{10,... | collective-permute-start | bytes 786440 | tf_op jit(solution)/shard_map/ppermute | solution.py:409
  59.4 2.0 %collective-permute-done.20.across = f32[8,64,128]{2,1,0:T(8,128)S(1)} collective-permute-done((f32[8,64,128]{2,1,0:T(8,128)S(1)}, f32[8,64,128]{2,1,0:T(8,128)S(1)}, u32[]{:S(2)}, u32[]{:S(2)}) %collective-permute-start.20) | collective-permute-done | bytes 262176 | tf_op jit(solution)/shard_map/ppermute | solution.py:409
  61.4 3.0 %backward2.1 = (f32[8,64,128]{2,1,0:T(8,128)S(1)}, f32[8,64,128]{2,1,0:T(8,128)S(1)}, f32[8,64,128]{2,1,0:T(8,128)S(1)}) custom-call(f32[8,64,128]{2,1,0:T(8,128)S(1)} %get-tuple-element.72.own, f32[8,64,128]{2,1,0:T(8,128)S(1)} %collective-permute-done.19.partner, f32[8,64,128]{2,1,0:T(8,128)S(1)} %collective-permute-done.20.across, ...), custom_call_target="tpu_custom_call" | custom-call | flops 13107200 | bytes 1048576 | tf_op jit(solution)/shard_map/backward2/pallas_call | solution.py:27
  64.5 0.2 collective-permute-start.25
  64.6 0.6 collective-permute-start.26
  65.3 1.2 %forward3.1 = (f32[8,32,128]{2,1,0:T(8,128)S(1)}, f32[8,32,128]{2,1,0:T(8,128)S(1)}, f32[8,32,128]{2,1,0:T(8,128)S(1)}, f32[8,32,128]{2,1,0:T(8,128)S(1)}) custom-call(f32[8,64,128]{2,1,0:T(8,128)S(1)} %get-tuple-element.83.own, f32[8,64,128]{2,1,0:T(8,128)S(1)} %collective-permute-done.27.partner, f32[8,64,128]{2,1,0:T(8,128)S(1)} %collective-permute-done.28.across, ...), custom_call_target="tpu_custom_call" | custom-call | flops 13107200 | bytes 1048576 | tf_op jit(solution)/shard_map/forward3/pallas_call | solution.py:27
  66.5 1.5 %collective-permute-start.29 = (f32[8,32,128]{2,1,0:T(8,128)S(1)}, f32[8,32,128]{2,1,0:T(8,128)S(1)}, u32[]{:S(2)}, u32[]{:S(2)}) collective-permute-start(f32[8,32,128]{2,1,0:T(8,128)S(1)} %get-tuple-element.86), channel_id=1, source_target_pairs={{0,8},{8,0},{16,24},{24,16},{1,9},{9,1},{17,25},{25,17},{2,10},{10... | collective-permute-start | bytes 393224 | tf_op jit(solution)/shard_map/ppermute | solution.py:412
  68.0 1.6 %collective-permute-start.30 = (f32[8,32,128]{2,1,0:T(8,128)S(1)}, f32[8,32,128]{2,1,0:T(8,128)S(1)}, u32[]{:S(2)}, u32[]{:S(2)}) collective-permute-start(f32[8,32,128]{2,1,0:T(8,128)S(1)} %get-tuple-element.87), channel_id=1, source_target_pairs={{0,16},{8,24},{16,0},{24,8},{1,17},{9,25},{17,1},{25,9},{2,18},{10... | collective-permute-start | bytes 393224 | tf_op jit(solution)/shard_map/ppermute | solution.py:412
  69.5 0.5 collective-permute-start.31
  70.1 2.2 %collective-permute-done.26.across = f32[8,64,128]{2,1,0:T(8,128)S(1)} collective-permute-done((f32[8,64,128]{2,1,0:T(8,128)S(1)}, f32[8,64,128]{2,1,0:T(8,128)S(1)}, u32[]{:S(2)}, u32[]{:S(2)}) %collective-permute-start.26) | collective-permute-done | bytes 262176 | tf_op jit(solution)/shard_map/ppermute | solution.py:409
  72.2 2.0 %backward3.1 = (f32[8,64,128]{2,1,0:T(8,128)}, f32[8,64,128]{2,1,0:T(8,128)}) custom-call(f32[8,64,128]{2,1,0:T(8,128)S(1)} %get-tuple-element.79.own, f32[8,64,128]{2,1,0:T(8,128)S(1)} %collective-permute-done.25.partner, f32[8,64,128]{2,1,0:T(8,128)S(1)} %collective-permute-done.26.across, f32[4,16,64,128]{3,2,1,0:T(8,128)S(1)} %copy-done.2, ...), custom_call_target="tpu_custom_call" | custom-call | flops 13107200 | bytes 1048576 | tf_op jit(solution)/shard_map/backward3/pallas_call | solution.py:27
  74.2 0.8 %collective-permute-done.29.refs_1_ = f32[8,32,128]{2,1,0:T(8,128)S(1)} collective-permute-done((f32[8,32,128]{2,1,0:T(8,128)S(1)}, f32[8,32,128]{2,1,0:T(8,128)S(1)}, u32[]{:S(2)}, u32[]{:S(2)}) %collective-permute-start.29) | collective-permute-done | bytes 131104 | tf_op jit(solution)/shard_map/ppermute | solution.py:412
  75.1 2.6 %collective-permute-done.31.refs_3_ = f32[8,32,128]{2,1,0:T(8,128)S(1)} collective-permute-done((f32[8,32,128]{2,1,0:T(8,128)S(1)}, f32[8,32,128]{2,1,0:T(8,128)S(1)}, u32[]{:S(2)}, u32[]{:S(2)}) %collective-permute-start.31) | collective-permute-done | bytes 131104 | tf_op jit(solution)/shard_map/ppermute | solution.py:412
  77.6 0.9 %copy-done.10 = f32[8,64,128]{2,1,0:T(8,128)S(1)} copy-done((f32[8,64,128]{2,1,0:T(8,128)S(1)}, f32[8,64,128]{2,1,0:T(8,128)}, u32[]{:S(2)}) %copy-start.10) | copy-done | bytes 262168
  78.6 0.7 total.1
  (56 shorter events, 0.3 us)
Async XLA Ops:
  0.6 26.6 %copy-start.4 = (f32[1,8,64,128]{3,2,1,0:T(8,128)S(1)}, f32[1,8,64,128]{3,2,1,0:T(8,128)}, u32[]{:S(2)}) copy-start(f32[1,8,64,128]{3,2,1,0:T(8,128)} %param.19) | copy-start | bytes 786436
  1.3 0.9 %copy-start.11 = (f32[8,32,128]{2,1,0:T(8,128)S(1)}, f32[8,32,128]{2,1,0:T(8,128)}, u32[]{:S(2)}) copy-start(f32[8,32,128]{2,1,0:T(8,128)} %eps.1) | copy-start | bytes 393220
  2.2 0.9 %copy-start.12 = (f32[8,32,128]{2,1,0:T(8,128)S(1)}, f32[8,32,128]{2,1,0:T(8,128)}, u32[]{:S(2)}) copy-start(f32[8,32,128]{2,1,0:T(8,128)} %tilt.1) | copy-start | bytes 393220
  3.1 0.9 %copy-start.13 = (f32[8,32,128]{2,1,0:T(8,128)S(1)}, f32[8,32,128]{2,1,0:T(8,128)}, u32[]{:S(2)}) copy-start(f32[8,32,128]{2,1,0:T(8,128)} %azimuth.1) | copy-start | bytes 393220
  4.0 23.2 %copy-start.14 = (f32[1,16,128]{2,1,0:T(8,128)S(1)}, f32[1,16,128]{2,1,0:T(8,128)}, u32[]{:S(2)}) copy-start(f32[1,16,128]{2,1,0:T(8,128)} %traces.1) | copy-start | bytes 24580
  4.1 23.2 %copy-start.15 = (f32[1,16]{1,0:T(1,128)S(1)}, f32[1,16]{1,0:T(1,128)}, u32[]{:S(2)}) copy-start(f32[1,16]{1,0:T(1,128)} %wavelet.1) | copy-start | bytes 196
  4.1 23.2 %copy-start.16 = (s32[1,128]{1,0:T(1,128)S(1)}, s32[1,128]{1,0:T(1,128)}, u32[]{:S(2)}) copy-start(s32[1,128]{1,0:T(1,128)} %rx.1) | copy-start | bytes 1540
  4.1 23.2 %copy-start.17 = (s32[1,128]{1,0:T(1,128)S(1)}, s32[1,128]{1,0:T(1,128)}, u32[]{:S(2)}) copy-start(s32[1,128]{1,0:T(1,128)} %ry.1) | copy-start | bytes 1540
  4.1 23.2 %copy-start.18 = (s32[1,128]{1,0:T(1,128)S(1)}, s32[1,128]{1,0:T(1,128)}, u32[]{:S(2)}) copy-start(s32[1,128]{1,0:T(1,128)} %rz.1) | copy-start | bytes 1540
  5.5 6.9 %collective-permute-start.9 = (f32[8,32,128]{2,1,0:T(8,128)S(1)}, f32[8,32,128]{2,1,0:T(8,128)S(1)}, u32[]{:S(2)}, u32[]{:S(2)}) collective-permute-start(f32[8,32,128]{2,1,0:T(8,128)S(1)} %get-tuple-element.52.own.refs_0_), channel_id=1, source_target_pairs={{0,16},{8,24},{16,0},{24,8},{1,17},{9,25},{17,1},{25,9},{2,18},{10... | collective-permute-start | bytes 393224 | tf_op jit(solution)/shard_map/ppermute | solution.py:412
  8.5 3.6 %collective-permute-start = (f32[8,128]{1,0:T(8,128)S(1)}, f32[8,128]{1,0:T(8,128)S(1)}, u32[]{:S(2)}, u32[]{:S(2)}) collective-permute-start(f32[8,128]{1,0:T(8,128)S(1)} %get-tuple-element.46), channel_id=1, source_target_pairs={{0,8},{8,0},{16,24},{24,16},{1,9},{9,1},{17,25},{25,17},{2,10},{10... | collective-permute-start | bytes 12296 | tf_op jit(solution)/shard_map/ppermute | solution.py:412
  10.0 7.0 %collective-permute-start.1 = (f32[8,32,128]{2,1,0:T(8,128)S(1)}, f32[8,32,128]{2,1,0:T(8,128)S(1)}, u32[]{:S(2)}, u32[]{:S(2)}) collective-permute-start(f32[8,32,128]{2,1,0:T(8,128)S(1)} %get-tuple-element.47.own.refs_3_), channel_id=1, source_target_pairs={{0,16},{8,24},{16,0},{24,8},{1,17},{9,25},{17,1},{25,9},{2,18},{10... | collective-permute-start | bytes 393224 | tf_op jit(solution)/shard_map/ppermute | solution.py:412
  12.4 7.1 %collective-permute-start.10 = (f32[8,32,128]{2,1,0:T(8,128)S(1)}, f32[8,32,128]{2,1,0:T(8,128)S(1)}, u32[]{:S(2)}, u32[]{:S(2)}) collective-permute-start(f32[8,32,128]{2,1,0:T(8,128)S(1)} %get-tuple-element.54), channel_id=1, source_target_pairs={{0,8},{8,0},{16,24},{24,16},{1,9},{9,1},{17,25},{25,17},{2,10},{10... | collective-permute-start | bytes 393224 | tf_op jit(solution)/shard_map/ppermute | solution.py:412
  15.0 12.2 %collective-permute-start.5 = (f32[8,64,128]{2,1,0:T(8,128)}, f32[8,64,128]{2,1,0:T(8,128)S(1)}, u32[]{:S(2)}, u32[]{:S(2)}) collective-permute-start(f32[8,64,128]{2,1,0:T(8,128)} %bitcast.10), channel_id=1, source_target_pairs={{0,1},{1,0},{2,3},{3,2},{4,5},{5,4},{6,7},{7,6},{8,9},{9,8},{10,11... | collective-permute-start | bytes 786440 | tf_op jit(solution)/shard_map/ppermute | solution.py:406
  15.0 12.2 %collective-permute-start.6 = (f32[8,64,128]{2,1,0:T(8,128)}, f32[8,64,128]{2,1,0:T(8,128)S(1)}, u32[]{:S(2)}, u32[]{:S(2)}) collective-permute-start(f32[8,64,128]{2,1,0:T(8,128)} %bitcast.11), channel_id=1, source_target_pairs={{0,8},{1,2},{2,1},{3,4},{4,3},{5,6},{6,5},{7,15},{8,0},{9,10},{10,... | collective-permute-start | bytes 786440 | tf_op jit(solution)/shard_map/ppermute | solution.py:409
  15.1 5.9 %collective-permute-start.13 = (f32[8,32,128]{2,1,0:T(8,128)S(1)}, f32[8,32,128]{2,1,0:T(8,128)S(1)}, u32[]{:S(2)}, u32[]{:S(2)}) collective-permute-start(f32[8,32,128]{2,1,0:T(8,128)S(1)} %get-tuple-element.58), channel_id=1, source_target_pairs={{0,16},{8,24},{16,0},{24,8},{1,17},{9,25},{17,1},{25,9},{2,18},{10... | collective-permute-start | bytes 393224 | tf_op jit(solution)/shard_map/ppermute | solution.py:412
  17.0 0.9 %copy-start.5 = (f32[8,32,128]{2,1,0:T(8,128)S(1)}, f32[8,32,128]{2,1,0:T(8,128)}, u32[]{:S(2)}) copy-start(f32[8,32,128]{2,1,0:T(8,128)} %refs_0_.3) | copy-start | bytes 393220
  18.0 7.1 %collective-permute-start.3 = (f32[8,32,128]{2,1,0:T(8,128)S(1)}, f32[8,32,128]{2,1,0:T(8,128)S(1)}, u32[]{:S(2)}, u32[]{:S(2)}) collective-permute-start(f32[8,32,128]{2,1,0:T(8,128)S(1)} %get-tuple-element.49), channel_id=1, source_target_pairs={{0,8},{8,0},{16,24},{24,16},{1,9},{9,1},{17,25},{25,17},{2,10},{10... | collective-permute-start | bytes 393224 | tf_op jit(solution)/shard_map/ppermute | solution.py:412
  19.5 5.5 %collective-permute-start.2 = (f32[8,32,128]{2,1,0:T(8,128)S(1)}, f32[8,32,128]{2,1,0:T(8,128)S(1)}, u32[]{:S(2)}, u32[]{:S(2)}) collective-permute-start(f32[8,32,128]{2,1,0:T(8,128)S(1)} %get-tuple-element.48), channel_id=1, source_target_pairs={{0,16},{8,24},{16,0},{24,8},{1,17},{9,25},{17,1},{25,9},{2,18},{10... | collective-permute-start | bytes 393224 | tf_op jit(solution)/shard_map/ppermute | solution.py:412
  21.0 8.6 %collective-permute-start.14 = (f32[8,32,128]{2,1,0:T(8,128)S(1)}, f32[8,32,128]{2,1,0:T(8,128)S(1)}, u32[]{:S(2)}, u32[]{:S(2)}) collective-permute-start(f32[8,32,128]{2,1,0:T(8,128)S(1)} %relay2.1), channel_id=1, source_target_pairs={{0,8},{8,0},{16,24},{24,16},{1,9},{9,1},{17,25},{25,17},{2,10},{10... | collective-permute-start | bytes 393224 | tf_op jit(solution)/shard_map/ppermute | solution.py:412
  25.1 0.9 %copy-start.6 = (f32[8,32,128]{2,1,0:T(8,128)S(1)}, f32[8,32,128]{2,1,0:T(8,128)}, u32[]{:S(2)}) copy-start(f32[8,32,128]{2,1,0:T(8,128)} %refs_0_.3) | copy-start | bytes 393220
  26.0 5.5 %copy-start.3 = (f32[1,8,64,128]{3,2,1,0:T(8,128)S(1)}, f32[1,8,64,128]{3,2,1,0:T(8,128)}, u32[]{:S(2)}) copy-start(f32[1,8,64,128]{3,2,1,0:T(8,128)} %param.21) | copy-start | bytes 786436
  26.0 5.5 %copy-start.7 = (f32[8,32,128]{2,1,0:T(8,128)S(1)}, f32[8,32,128]{2,1,0:T(8,128)}, u32[]{:S(2)}) copy-start(f32[8,32,128]{2,1,0:T(8,128)} %refs_0_.3) | copy-start | bytes 393220
  26.0 5.5 %collective-permute-start.4 = (f32[8,32,128]{2,1,0:T(8,128)S(1)}, f32[8,32,128]{2,1,0:T(8,128)S(1)}, u32[]{:S(2)}, u32[]{:S(2)}) collective-permute-start(f32[8,32,128]{2,1,0:T(8,128)S(1)} %relay3.1.refs_7_), channel_id=1, source_target_pairs={{0,8},{8,0},{16,24},{24,16},{1,9},{9,1},{17,25},{25,17},{2,10},{10... | collective-permute-start | bytes 393224 | tf_op jit(solution)/shard_map/ppermute | solution.py:412
  29.4 11.8 %copy-start.8 = (f32[1,8,64,128]{3,2,1,0:T(8,128)S(1)}, f32[1,8,64,128]{3,2,1,0:T(8,128)}, u32[]{:S(2)}) copy-start(f32[1,8,64,128]{3,2,1,0:T(8,128)} %param.18) | copy-start | bytes 786436
  30.0 3.0 %collective-permute-start.15 = (f32[4,64,128]{2,1,0:T(8,128)S(1)}, f32[4,64,128]{2,1,0:T(8,128)S(1)}, u32[]{:S(2)}, u32[]{:S(2)}) collective-permute-start(f32[4,64,128]{2,1,0:T(8,128)S(1)} %get-tuple-element.62), channel_id=1, source_target_pairs={{0,1},{1,0},{2,3},{3,2},{4,5},{5,4},{6,7},{7,6},{8,9},{9,8},{10,11... | collective-permute-start | bytes 393224 | tf_op jit(solution)/shard_map/ppermute | solution.py:406
  30.1 11.1 %collective-permute-start.11 = (f32[2,4,64,128]{3,2,1,0:T(8,128)S(1)}, f32[2,4,64,128]{3,2,1,0:T(8,128)S(1)}, u32[]{:S(2)}, u32[]{:S(2)}) collective-permute-start(f32[2,4,64,128]{3,2,1,0:T(8,128)S(1)} %get-tuple-element.56), channel_id=1, source_target_pairs={{0,1},{1,0},{2,3},{3,2},{4,5},{5,4},{6,7},{7,6},{8,9},{9,8},{10,11... | collective-permute-start | bytes 786440 | tf_op jit(solution)/shard_map/ppermute | solution.py:406
  30.6 10.6 %collective-permute-start.12 = (f32[2,4,64,128]{3,2,1,0:T(8,128)S(1)}, f32[2,4,64,128]{3,2,1,0:T(8,128)S(1)}, u32[]{:S(2)}, u32[]{:S(2)}) collective-permute-start(f32[2,4,64,128]{3,2,1,0:T(8,128)S(1)} %get-tuple-element.57), channel_id=1, source_target_pairs={{0,8},{1,2},{2,1},{3,4},{4,3},{5,6},{6,5},{7,15},{8,0},{9,10},{10,... | collective-permute-start | bytes 786440 | tf_op jit(solution)/shard_map/ppermute | solution.py:409
  31.6 12.2 %collective-permute-start.7 = (f32[8,64,128]{2,1,0:T(8,128)S(1)}, f32[8,64,128]{2,1,0:T(8,128)S(1)}, u32[]{:S(2)}, u32[]{:S(2)}) collective-permute-start(f32[8,64,128]{2,1,0:T(8,128)S(1)} %get-tuple-element.51.own), channel_id=1, source_target_pairs={{0,1},{1,0},{2,3},{3,2},{4,5},{5,4},{6,7},{7,6},{8,9},{9,8},{10,11... | collective-permute-start | bytes 786440 | tf_op jit(solution)/shard_map/ppermute | solution.py:406
  32.7 11.1 %collective-permute-start.8 = (f32[8,64,128]{2,1,0:T(8,128)S(1)}, f32[8,64,128]{2,1,0:T(8,128)S(1)}, u32[]{:S(2)}, u32[]{:S(2)}) collective-permute-start(f32[8,64,128]{2,1,0:T(8,128)S(1)} %get-tuple-element.51.own), channel_id=1, source_target_pairs={{0,8},{1,2},{2,1},{3,4},{4,3},{5,6},{6,5},{7,15},{8,0},{9,10},{10,... | collective-permute-start | bytes 786440 | tf_op jit(solution)/shard_map/ppermute | solution.py:409
  33.0 8.2 %collective-permute-start.16 = (f32[4,64,128]{2,1,0:T(8,128)S(1)}, f32[4,64,128]{2,1,0:T(8,128)S(1)}, u32[]{:S(2)}, u32[]{:S(2)}) collective-permute-start(f32[4,64,128]{2,1,0:T(8,128)S(1)} %get-tuple-element.63), channel_id=1, source_target_pairs={{0,8},{1,2},{2,1},{3,4},{4,3},{5,6},{6,5},{7,15},{8,0},{9,10},{10,... | collective-permute-start | bytes 393224 | tf_op jit(solution)/shard_map/ppermute | solution.py:409
  41.2 2.6 %copy-start.9 = (f32[1,8,64,128]{3,2,1,0:T(8,128)S(1)}, f32[1,8,64,128]{3,2,1,0:T(8,128)}, u32[]{:S(2)}) copy-start(f32[1,8,64,128]{3,2,1,0:T(8,128)} %param.20) | copy-start | bytes 786436
  42.9 5.0 %collective-permute-start.21 = (f32[8,64,128]{2,1,0:T(8,128)S(1)}, f32[8,64,128]{2,1,0:T(8,128)S(1)}, u32[]{:S(2)}, u32[]{:S(2)}) collective-permute-start(f32[8,64,128]{2,1,0:T(8,128)S(1)} %get-tuple-element.75.own.previous), channel_id=1, source_target_pairs={{0,1},{1,0},{2,3},{3,2},{4,5},{5,4},{6,7},{7,6},{8,9},{9,8},{10,11... | collective-permute-start | bytes 786440 | tf_op jit(solution)/shard_map/ppermute | solution.py:406
  42.9 6.4 %collective-permute-start.22 = (f32[8,64,128]{2,1,0:T(8,128)S(1)}, f32[8,64,128]{2,1,0:T(8,128)S(1)}, u32[]{:S(2)}, u32[]{:S(2)}) collective-permute-start(f32[8,64,128]{2,1,0:T(8,128)S(1)} %get-tuple-element.75.own.previous), channel_id=1, source_target_pairs={{0,8},{1,2},{2,1},{3,4},{4,3},{5,6},{6,5},{7,15},{8,0},{9,10},{10,... | collective-permute-start | bytes 786440 | tf_op jit(solution)/shard_map/ppermute | solution.py:409
  43.8 1.6 %copy-start = (f32[4,16,64,128]{3,2,1,0:T(8,128)S(1)}, f32[4,16,64,128]{3,2,1,0:T(8,128)}, u32[]{:S(2)}) copy-start(f32[4,16,64,128]{3,2,1,0:T(8,128)} %get-tuple-element.68.coef) | copy-start | bytes 6291460
  45.4 3.8 %copy-start.1 = (f32[4,16,64,128]{3,2,1,0:T(8,128)S(1)}, f32[4,16,64,128]{3,2,1,0:T(8,128)}, u32[]{:S(2)}) copy-start(f32[4,16,64,128]{3,2,1,0:T(8,128)} %get-tuple-element.68.coef) | copy-start | bytes 6291460
  46.6 4.9 %collective-permute-start.17 = (f32[8,64,128]{2,1,0:T(8,128)S(1)}, f32[8,64,128]{2,1,0:T(8,128)S(1)}, u32[]{:S(2)}, u32[]{:S(2)}) collective-permute-start(f32[8,64,128]{2,1,0:T(8,128)S(1)} %get-tuple-element.70.own), channel_id=1, source_target_pairs={{0,1},{1,0},{2,3},{3,2},{4,5},{5,4},{6,7},{7,6},{8,9},{9,8},{10,11... | collective-permute-start | bytes 786440 | tf_op jit(solution)/shard_map/ppermute | solution.py:406
  47.3 6.4 %collective-permute-start.18 = (f32[8,64,128]{2,1,0:T(8,128)S(1)}, f32[8,64,128]{2,1,0:T(8,128)S(1)}, u32[]{:S(2)}, u32[]{:S(2)}) collective-permute-start(f32[8,64,128]{2,1,0:T(8,128)S(1)} %get-tuple-element.70.own), channel_id=1, source_target_pairs={{0,8},{1,2},{2,1},{3,4},{4,3},{5,6},{6,5},{7,15},{8,0},{9,10},{10,... | collective-permute-start | bytes 786440 | tf_op jit(solution)/shard_map/ppermute | solution.py:409
  50.5 5.2 %collective-permute-start.23 = (f32[8,64,128]{2,1,0:T(8,128)S(1)}, f32[8,64,128]{2,1,0:T(8,128)S(1)}, u32[]{:S(2)}, u32[]{:S(2)}) collective-permute-start(f32[8,64,128]{2,1,0:T(8,128)S(1)} %get-tuple-element.77.own), channel_id=1, source_target_pairs={{0,1},{1,0},{2,3},{3,2},{4,5},{5,4},{6,7},{7,6},{8,9},{9,8},{10,11... | collective-permute-start | bytes 786440 | tf_op jit(solution)/shard_map/ppermute | solution.py:406
  50.7 6.4 %collective-permute-start.24 = (f32[8,64,128]{2,1,0:T(8,128)S(1)}, f32[8,64,128]{2,1,0:T(8,128)S(1)}, u32[]{:S(2)}, u32[]{:S(2)}) collective-permute-start(f32[8,64,128]{2,1,0:T(8,128)S(1)} %get-tuple-element.77.own), channel_id=1, source_target_pairs={{0,8},{1,2},{2,1},{3,4},{4,3},{5,6},{6,5},{7,15},{8,0},{9,10},{10,... | collective-permute-start | bytes 786440 | tf_op jit(solution)/shard_map/ppermute | solution.py:409
  54.9 4.5 %collective-permute-start.19 = (f32[8,64,128]{2,1,0:T(8,128)S(1)}, f32[8,64,128]{2,1,0:T(8,128)S(1)}, u32[]{:S(2)}, u32[]{:S(2)}) collective-permute-start(f32[8,64,128]{2,1,0:T(8,128)S(1)} %get-tuple-element.72.own), channel_id=1, source_target_pairs={{0,1},{1,0},{2,3},{3,2},{4,5},{5,4},{6,7},{7,6},{8,9},{9,8},{10,11... | collective-permute-start | bytes 786440 | tf_op jit(solution)/shard_map/ppermute | solution.py:406
  55.0 6.4 %collective-permute-start.20 = (f32[8,64,128]{2,1,0:T(8,128)S(1)}, f32[8,64,128]{2,1,0:T(8,128)S(1)}, u32[]{:S(2)}, u32[]{:S(2)}) collective-permute-start(f32[8,64,128]{2,1,0:T(8,128)S(1)} %get-tuple-element.72.own), channel_id=1, source_target_pairs={{0,8},{1,2},{2,1},{3,4},{4,3},{5,6},{6,5},{7,15},{8,0},{9,10},{10,... | collective-permute-start | bytes 786440 | tf_op jit(solution)/shard_map/ppermute | solution.py:409
  58.3 7.0 %collective-permute-start.27 = (f32[8,64,128]{2,1,0:T(8,128)S(1)}, f32[8,64,128]{2,1,0:T(8,128)S(1)}, u32[]{:S(2)}, u32[]{:S(2)}) collective-permute-start(f32[8,64,128]{2,1,0:T(8,128)S(1)} %get-tuple-element.83.own), channel_id=1, source_target_pairs={{0,1},{1,0},{2,3},{3,2},{4,5},{5,4},{6,7},{7,6},{8,9},{9,8},{10,11... | collective-permute-start | bytes 786440 | tf_op jit(solution)/shard_map/ppermute | solution.py:406
  58.4 6.8 %collective-permute-start.28 = (f32[8,64,128]{2,1,0:T(8,128)S(1)}, f32[8,64,128]{2,1,0:T(8,128)S(1)}, u32[]{:S(2)}, u32[]{:S(2)}) collective-permute-start(f32[8,64,128]{2,1,0:T(8,128)S(1)} %get-tuple-element.83.own), channel_id=1, source_target_pairs={{0,8},{1,2},{2,1},{3,4},{4,3},{5,6},{6,5},{7,15},{8,0},{9,10},{10,... | collective-permute-start | bytes 786440 | tf_op jit(solution)/shard_map/ppermute | solution.py:409
  61.4 3.8 %copy-start.2 = (f32[4,16,64,128]{3,2,1,0:T(8,128)S(1)}, f32[4,16,64,128]{3,2,1,0:T(8,128)}, u32[]{:S(2)}) copy-start(f32[4,16,64,128]{3,2,1,0:T(8,128)} %get-tuple-element.68.coef) | copy-start | bytes 6291460
  64.5 5.6 %collective-permute-start.25 = (f32[8,64,128]{2,1,0:T(8,128)S(1)}, f32[8,64,128]{2,1,0:T(8,128)S(1)}, u32[]{:S(2)}, u32[]{:S(2)}) collective-permute-start(f32[8,64,128]{2,1,0:T(8,128)S(1)} %get-tuple-element.79.own), channel_id=1, source_target_pairs={{0,1},{1,0},{2,3},{3,2},{4,5},{5,4},{6,7},{7,6},{8,9},{9,8},{10,11... | collective-permute-start | bytes 786440 | tf_op jit(solution)/shard_map/ppermute | solution.py:406
  64.6 7.6 %collective-permute-start.26 = (f32[8,64,128]{2,1,0:T(8,128)S(1)}, f32[8,64,128]{2,1,0:T(8,128)S(1)}, u32[]{:S(2)}, u32[]{:S(2)}) collective-permute-start(f32[8,64,128]{2,1,0:T(8,128)S(1)} %get-tuple-element.79.own), channel_id=1, source_target_pairs={{0,8},{1,2},{2,1},{3,4},{4,3},{5,6},{6,5},{7,15},{8,0},{9,10},{10,... | collective-permute-start | bytes 786440 | tf_op jit(solution)/shard_map/ppermute | solution.py:409
  66.5 8.5 %collective-permute-start.29 = (f32[8,32,128]{2,1,0:T(8,128)S(1)}, f32[8,32,128]{2,1,0:T(8,128)S(1)}, u32[]{:S(2)}, u32[]{:S(2)}) collective-permute-start(f32[8,32,128]{2,1,0:T(8,128)S(1)} %get-tuple-element.86), channel_id=1, source_target_pairs={{0,8},{8,0},{16,24},{24,16},{1,9},{9,1},{17,25},{25,17},{2,10},{10... | collective-permute-start | bytes 393224 | tf_op jit(solution)/shard_map/ppermute | solution.py:412
  68.0 7.1 %collective-permute-start.30 = (f32[8,32,128]{2,1,0:T(8,128)S(1)}, f32[8,32,128]{2,1,0:T(8,128)S(1)}, u32[]{:S(2)}, u32[]{:S(2)}) collective-permute-start(f32[8,32,128]{2,1,0:T(8,128)S(1)} %get-tuple-element.87), channel_id=1, source_target_pairs={{0,16},{8,24},{16,0},{24,8},{1,17},{9,25},{17,1},{25,9},{2,18},{10... | collective-permute-start | bytes 393224 | tf_op jit(solution)/shard_map/ppermute | solution.py:412
  69.5 8.1 %collective-permute-start.31 = (f32[8,32,128]{2,1,0:T(8,128)S(1)}, f32[8,32,128]{2,1,0:T(8,128)S(1)}, u32[]{:S(2)}, u32[]{:S(2)}) collective-permute-start(f32[8,32,128]{2,1,0:T(8,128)S(1)} %get-tuple-element.88), channel_id=1, source_target_pairs={{0,24},{8,16},{16,8},{24,0},{1,25},{9,17},{17,9},{25,1},{2,26},{10... | collective-permute-start | bytes 393224 | tf_op jit(solution)/shard_map/ppermute | solution.py:412
  77.6 1.0 %copy-start.10 = (f32[8,64,128]{2,1,0:T(8,128)S(1)}, f32[8,64,128]{2,1,0:T(8,128)}, u32[]{:S(2)}) copy-start(f32[8,64,128]{2,1,0:T(8,128)} %get-tuple-element.82.refs_4_) | copy-start | bytes 786436

commit v4 on v2

v4 whole, which is shorter than its diff:
```python
import functools

import jax
import jax.numpy as jnp
from jax import lax
from jax.experimental import pallas as pl
from jax.experimental.pallas import tpu as pltpu
from jax.sharding import PartitionSpec as P

STEPS = 4
COEF = (0.8, -0.2, 4.0 / 105.0, -1.0 / 280.0)
WHOLE = (672.0, -168.0, 32.0, -3.0)
UNIT = 1.0 / 840.0
PAD = 8

VMEM = pl.BlockSpec(memory_space=pltpu.VMEM)
SMEM = pl.BlockSpec(memory_space=pltpu.SMEM)
HBM = pl.BlockSpec(memory_space=pltpu.HBM)


def f32(*shape):
    return jax.ShapeDtypeStruct(shape, jnp.float32)


def call(name, body, outs, ins, scratch=(), flops=1 << 20, moved=1 << 20):
    pairs = [a if isinstance(a, tuple) else (a, VMEM) for a in ins]
    return pl.pallas_call(
        body,
        name=name,
        out_shape=outs,
        in_specs=[s for _, s in pairs],
        out_specs=jax.tree.map(lambda _: VMEM, outs),
        scratch_shapes=list(scratch),
        cost_estimate=pl.CostEstimate(flops=flops, bytes_accessed=moved, transcendentals=0),
        compiler_params=pltpu.CompilerParams(vmem_limit_bytes=16 << 20),
    )(*[a for a, _ in pairs])


def stencil(pick):
    summed = None
    for k in range(1, 5):
        term = COEF[k - 1] * (pick(k) - pick(-k))
        summed = term if summed is None else summed + term
    return summed


def diff_y(ref, row, width):
    return stencil(lambda k: ref[row, PAD + k : PAD + k + width, :])


def diff_z(tile, matrix):
    high = tile.astype(jnp.bfloat16)
    low = (tile - high.astype(jnp.float32)).astype(jnp.bfloat16)
    both = jnp.concatenate([high, low], axis=-1)
    return jnp.dot(both, matrix[...], preferred_element_type=jnp.float32) * UNIT


def place_halos(wide, lane, own, partner, across):
    rows, halo = own.shape[0], sum(ref.shape[0] for ref in partner)
    blk, blocks = lax.axis_index("blk"), lax.axis_size("blk")
    odd = blk % 2
    outside = (blk == 0) | (blk == blocks - 1)
    above = halo + rows
    wide[(slice(halo, above), *lane)] = own[...]
    partner_at = jnp.where(odd == 1, 0, above)
    across_at = jnp.where(odd == 1, above, 0)
    for ref_p, ref_a in zip(partner, across):
        part = ref_p.shape[0]
        wide[(pl.ds(partner_at, part), *lane)] = ref_p[...]
        wide[(pl.ds(across_at, part), *lane)] = jnp.where(outside, 0.0, ref_a[...])
        partner_at, across_at = partner_at + part, across_at + part


def fill_field(own, partner, across, wide):
    rows, width, depth = own.shape
    edge = jnp.zeros((3 * rows, PAD, depth), jnp.float32)
    wide[:, 0:PAD, :] = edge
    wide[:, PAD + width : 2 * PAD + width, :] = edge
    place_halos(wide, (slice(PAD, PAD + width), slice(None)), own, (partner,), (across,))


def slopes_at(wide, i, width, matrix):
    inner = slice(PAD, PAD + width)
    return (
        stencil(lambda k: wide[i + k, inner, :]),
        diff_y(wide, i, width),
        diff_z(wide[i, inner, :], matrix),
    )


def clear_sides(flux_y, width):
    rows, _, depth = flux_y.shape
    edge = jnp.zeros((rows, PAD, depth), jnp.float32)
    flux_y[:, 0:PAD, :] = edge
    flux_y[:, PAD + width : 2 * PAD + width, :] = edge


def apply_operator(wide, coef, matrix, flux_x, flux_y, part_z, finish):
    rows, width, _ = part_z.shape
    clear_sides(flux_y, width)
    for i in range(rows + 8):
        slope_x, slope_y, slope_z = slopes_at(wide, i + 4, width, matrix)
        along = coef[0, i] * slope_x + coef[1, i] * slope_y + coef[2, i] * slope_z
        flux_x[i] = coef[3, i] * slope_x - coef[0, i] * along
        r = i - 4
        if 0 <= r < rows:
            flux_y[r, PAD : PAD + width, :] = coef[3, i] * slope_y - coef[1, i] * along
            part_z[r] = diff_z(coef[3, i] * slope_z - coef[2, i] * along, matrix)
    for r in range(rows):
        finish(r, stencil(lambda k: flux_x[r + 4 + k]) + diff_y(flux_y, r, width) + part_z[r])


def sin_cos(angle):
    square = angle * angle
    sine, cosine = 0.0, 1.0 / 479001600.0
    for factor in (-39916800.0, 362880.0, -5040.0, 120.0, -6.0, 1.0):
        sine = sine * square + 1.0 / factor
    for factor in (-3628800.0, 40320.0, -720.0, 24.0, -2.0, 1.0):
        cosine = cosine * square + 1.0 / factor
    return angle * sine, cosine


def owner_kernel(eps, tilt, azimuth, speed, state, wx, wy, wz, out, current, held, sems):
    rows = wx.shape[0]
    copies = [
        pltpu.make_async_copy(ref, to, sems.at[n])
        for n, (ref, to) in enumerate(
            (
                (eps, held.at[0]),
                (tilt, held.at[1]),
                (azimuth, held.at[2]),
                (speed, out),
                (state.at[0], current),
            )
        )
    ]
    for copy in copies:
        copy.start()
    for copy in copies[:3]:
        copy.wait()
    for r in range(rows):
        size = jnp.sqrt(2.0 * held[0, r])
        sin_tilt, cos_tilt = sin_cos(held[1, r])
        sin_half, cos_half = sin_cos(0.5 * held[2, r])
        flat = size * sin_tilt
        wx[r] = flat * (1.0 - 2.0 * sin_half * sin_half)
        wy[r] = flat * (2.0 * sin_half * cos_half)
        wz[r] = size * cos_tilt
    for copy in copies[3:]:
        copy.wait()


def first_kernel(anchor, wz, first, wz_first):
    rows, count, depth = wz.shape
    number = jnp.full((count, depth), (anchor[0] // count).astype(jnp.float32))
    first[...] = number[0:8]
    wz_first[0:rows] = wz[...]
    wz_first[rows] = number


def prepare_kernel(shots, parts, first, own, partner, across, slope, flags, matrix, wide):
    rows, width, depth = own.shape
    shape = matrix.shape
    offset = lax.broadcasted_iota(jnp.int32, shape, 0) % depth - lax.broadcasted_iota(
        jnp.int32, shape, 1
    )
    entries = jnp.zeros(shape, jnp.float32)
    for k in range(1, 5):
        entries = jnp.where(offset == k, WHOLE[k - 1], entries)
        entries = jnp.where(offset == -k, -WHOLE[k - 1], entries)
    matrix[...] = entries.astype(jnp.bfloat16)
    me = lax.axis_index("shot")
    for k in range(shots):
        part = jnp.bitwise_xor(me, k).astype(jnp.float32) - first[0:1, :]
        for j in range(parts):
            flags[k * parts + j : k * parts + j + 1, :] = jnp.where(
                jnp.abs(part - j) < 0.5, 1.0, 0.0
            )
    fill_field(own, partner, across, wide)
    for i in range(rows + 8):
        slope[0, i], slope[1, i], slope[2, i] = slopes_at(wide, i + 4, width, matrix)


def inject_kernel(numbers, wavelet, rx, ry, rz, traces, src, inj,
                  scalars, wave, receiver, samples_held, sems):
    rows, width, depth = src.shape[1:]
    copies = [
        pltpu.make_async_copy(numbers, scalars, sems.at[0]),
        pltpu.make_async_copy(wavelet, wave, sems.at[1]),
        pltpu.make_async_copy(traces, samples_held, sems.at[2]),
    ]
    for n, ref in enumerate((rx, ry, rz)):
        copies.append(pltpu.make_async_copy(ref, receiver[n], sems.at[3 + n]))
    for copy in copies:
        copy.start()
    for copy in copies:
        copy.wait()
    first = lax.axis_index("blk") * rows
    start = scalars[0]
    shape = (rows, width, depth)
    hit = (
        (lax.broadcasted_iota(jnp.int32, shape, 0) == scalars[1] - first)
        & (lax.broadcasted_iota(jnp.int32, shape, 1) == scalars[2])
        & (lax.broadcasted_iota(jnp.int32, shape, 2) == scalars[3])
    )
    moment = lax.broadcasted_iota(jnp.int32, wave.shape, 1)
    for t in range(STEPS - 1):
        value = jnp.sum(jnp.where(moment == start + t, wave[...], 0.0), axis=1, keepdims=True)
        src[t] = jnp.where(hit, value, 0.0)
    receivers = rx.shape[1]
    local = receiver[0][...] - first
    plane = jnp.where((local >= 0) & (local < rows), local * width + receiver[1][...], -1)
    pick = (
        lax.broadcasted_iota(jnp.int32, (rows * width, receivers), 0) == plane
    ).astype(jnp.float32)
    match = lax.broadcasted_iota(jnp.int32, (depth, receivers), 0) == receiver[2][...]
    for t in range(STEPS):
        samples = samples_held[0, pl.ds(start + t, 1), :]
        spread = jnp.where(match, samples, 0.0)
        added = lax.dot_general(
            pick,
            spread,
            (((1,), (1,)), ((), ())),
            precision=lax.Precision.HIGHEST,
            preferred_element_type=jnp.float32,
        )
        inj[t] = added.reshape(shape)


def relay_kernel(parts, wz_first, own, received, *refs):
    out = refs[-1]
    first = wz_first[wz_first.shape[0] - 1, 0:1, :]
    part = lax.axis_index("shot").astype(jnp.float32) - first
    inside = (part > -0.5) & (part < parts - 0.5)
    out[...] = jnp.where(inside, own[...], received[...])


def pair_kernel(own, received, out):
    out[0] = own[...]
    out[1] = received[0 : own.shape[0]]


def window_part(pieces, flags, parts, j):
    chosen = pieces[-1][...]
    for k in reversed(range(len(pieces) - 1)):
        at = k * parts + j
        chosen = jnp.where(flags[at : at + 1, :] > 0.5, pieces[k][...], chosen)
    return chosen


def piece_refs(refs, places):
    return [refs[i] if at is None else refs[i].at[at] for i, at in places]


def flux_kernel(places, parts, flags, slope, matrix, *refs):
    tensor, flux, rest, edge_a0, edge_a1, edge_p0, edge_p1, flux_y = refs[-8:]
    rows, width, _ = flux.shape
    count = width // parts
    for a in range(3):
        pieces = piece_refs(refs, places[a])
        for j in range(parts):
            tensor[a, :, j * count : (j + 1) * count, :] = window_part(pieces, flags, parts, j)
    odd = lax.axis_index("blk") % 2
    low = rows - 4
    for n, (out_a, out_p) in enumerate(((edge_a0, edge_p0), (edge_a1, edge_p1))):
        out_a[...] = tensor[:, pl.ds(odd * low + 2 * n, 2)]
        out_p[...] = tensor[:, pl.ds((1 - odd) * low + 2 * n, 2)]
    clear_sides(flux_y, width)
    for r in range(rows):
        wx, wy, wz = tensor[0, r], tensor[1, r], tensor[2, r]
        along = wx * slope[0, r + 4] + wy * slope[1, r + 4] + wz * slope[2, r + 4]
        size = 1.0 + (wx * wx + wy * wy + wz * wz)
        flux[r] = size * slope[0, r + 4] - wx * along
        flux_y[r, PAD : PAD + width, :] = size * slope[1, r + 4] - wy * along
        rest[r] = diff_z(size * slope[2, r + 4] - wz * along, matrix)
    for r in range(rows):
        rest[r] = rest[r] + diff_y(flux_y, r, width)


def speed_kernel(places, parts, flags, present, *refs):
    speed, operand = refs[-2:]
    pieces = piece_refs(refs, places)
    count = speed.shape[1] // parts
    for j in range(parts):
        speed[:, j * count : (j + 1) * count, :] = window_part(pieces, flags, parts, j)
    operand[...] = speed[...] * present[...]


def forward_first(tensor, edge_p0, edge_p1, edge_a0, edge_a1, slope, flux, rest, own, previous,
                  speed, src, image, following, coef, flux_x):
    rows = rest.shape[0]
    blk, blocks = lax.axis_index("blk"), lax.axis_size("blk")
    for a in range(3):
        place_halos(coef.at[a], (), tensor.at[a], (edge_p0.at[a], edge_p1.at[a]),
                    (edge_a0.at[a], edge_a1.at[a]))
    for i in range(rows + 8):
        wx, wy, wz = coef[0, i], coef[1, i], coef[2, i]
        size = 1.0 + (wx * wx + wy * wy + wz * wz)
        if i < 4:
            size = jnp.where(blk == 0, 0.0, size)
        if i >= rows + 4:
            size = jnp.where(blk == blocks - 1, 0.0, size)
        coef[3, i] = size
        if 4 <= i < rows + 4:
            flux_x[i] = flux[i - 4]
        else:
            along = wx * slope[0, i] + wy * slope[1, i] + wz * slope[2, i]
            flux_x[i] = size * slope[0, i] - wx * along
    for r in range(rows):
        value = stencil(lambda k: flux_x[r + 4 + k]) + rest[r]
        image[r] = value
        following[r] = 2.0 * own[r] - previous[r] + speed[r] * value + src[0, r]


def forward(t, own, partner, across, coef, matrix, previous, speed, src, image, following,
            wide, *scratch):
    fill_field(own, partner, across, wide)

    def finish(r, value):
        image[r] = value
        following[r] = 2.0 * own[r] - previous[r] + speed[r] * value + src[t, r]

    apply_operator(wide, coef, matrix, *scratch, finish)


def backward(t, own, partner, across, coef, matrix, present, later, inj, *refs):
    if t == 0:
        earlier, copied, done = refs[:3]
        copied[...] = present[...]
        done[...] = jnp.zeros(done.shape, jnp.float32)
    elif t == 1:
        speed, lambda3, image0, image1, image2, earlier, operand, known = refs[:8]
    else:
        speed, earlier, operand = refs[:3]
    wide, flux_x, flux_y, part_z = refs[-4:]
    fill_field(own, partner, across, wide)

    def finish(r, value):
        result = 2.0 * present[r] - later[r] + value + inj[t, r]
        earlier[r] = result
        if t > 0:
            operand[r] = speed[r] * result
        if t == 1:
            known[r] = lambda3[r] * image2[r] + present[r] * image1[r] + result * image0[r]

    apply_operator(wide, coef, matrix, flux_x, flux_y, part_z, finish)


def forward_last(parts, own, partner, across, coef, matrix, known, lambda4, flags, *refs):
    *chunks, wide, flux_x, flux_y, part_z, grad = refs
    count = chunks[0].shape[1]
    fill_field(own, partner, across, wide)

    def finish(r, value):
        grad[r] = known[r] + lambda4[r] * value

    apply_operator(wide, coef, matrix, flux_x, flux_y, part_z, finish)
    for k, chunk in enumerate(chunks):
        held = jnp.zeros(chunk.shape, jnp.float32)
        for j in range(parts):
            at = k * parts + j
            held = jnp.where(
                flags[at : at + 1, :] > 0.5, grad[:, j * count : (j + 1) * count, :], held
            )
        chunk[...] = held


def total_kernel(*refs):
    out = refs[-1]
    total = refs[0][...]
    for ref in refs[1:-2]:
        total = total + ref[...]
    out[...] = total


def on_device(
    state_before,
    state_now,
    adjoint_later,
    adjoint_now,
    courant_sq,
    epsilon,
    tilt_angle,
    azimuth,
    aperture_anchor,
    step_index,
    wavelet,
    residual_traces,
    source_x,
    source_y,
    source_z,
    receiver_x,
    receiver_y,
    receiver_z,
):
    rows, width, depth = state_now.shape[1:]
    count = courant_sq.shape[1]
    parts = width // count
    shots = lax.axis_size("shot")
    blocks = lax.axis_size("blk")
    field, piece = f32(rows, width, depth), f32(rows, count, depth)
    wide = (rows, width + 2 * PAD, depth)
    scratch = (
        pltpu.VMEM((3 * rows, width + 2 * PAD, depth), jnp.float32),
        pltpu.VMEM((rows + 8, width, depth), jnp.float32),
        pltpu.VMEM(wide, jnp.float32),
        pltpu.VMEM((rows, width, depth), jnp.float32),
    )
    work = 100 * (rows + 8) * width * depth

    core_pairs = [(i, i ^ 1) for i in range(blocks)]
    chip_pairs = []
    for s in range(shots):
        for b in range(blocks):
            end = b in (0, blocks - 1)
            other = (s ^ 1, b) if end else (s, b - 1 + 2 * (b % 2))
            chip_pairs.append((s * blocks + b, other[0] * blocks + other[1]))

    def to_partner(array):
        return lax.ppermute(array, "blk", core_pairs)

    def across_chips(array):
        return lax.ppermute(array, ("shot", "blk"), chip_pairs)

    def halos(array):
        return to_partner(array), across_chips(array)

    def in_hbm(array):
        return pltpu.with_memory_space_constraint(array, pltpu.HBM), HBM

    def to_owners(array, k):
        return lax.ppermute(array, "shot", [(i, i ^ k) for i in range(shots)])

    previous = state_before[0]
    present, later = adjoint_now[0], adjoint_later[0]

    wx, wy, wz, speed, current = call(
        "owner",
        owner_kernel,
        (piece,) * 4 + (field,),
        [in_hbm(a) for a in (epsilon, tilt_angle, azimuth, courant_sq, state_now)],
        (
            pltpu.VMEM((3, rows, count, depth), jnp.float32),
            pltpu.SemaphoreType.DMA((5,)),
        ),
    )
    first, wz_first = call(
        "first",
        first_kernel,
        (f32(8, depth), f32(rows + 1, count, depth)),
        [(aperture_anchor, SMEM), wz],
    )

    if shots == 4 and parts == 2:
        relay = functools.partial(relay_kernel, parts)
        wx_y = to_owners(wx, 2)
        wz_x = to_owners(wz_first, 1)
        wy_y = to_owners(wy, 2)
        speed_x = to_owners(speed, 1)
        wx_sent = call("relay_wx", relay, piece, [wz_x, wx, wx_y])
        wx_x = to_owners(wx_sent, 1)
        both = f32(2, rows, count, depth)
        wz_y = to_owners(call("pair_wz", pair_kernel, both, [wz, wz_x]), 2)
        wy_sent = call("relay_wy", relay, piece, [wz_x, wy, wy_y, speed_x, wx_sent])
        wy_x = to_owners(wy_sent, 1)
        speed_y = to_owners(call("pair_speed", pair_kernel, both, [speed, speed_x]), 2)
        pieces = [wx, wx_x, wx_y, wy, wy_x, wy_y, wz, wz_x, wz_y]
        places = [
            [(0, None), (1, None), (2, None), (1, None)],
            [(3, None), (4, None), (5, None), (4, None)],
            [(6, None), (7, slice(0, rows)), (8, 0), (8, 1)],
        ]
        speed_pieces = [speed, speed_x, speed_y]
        speed_places = [(0, None), (1, None), (2, 0), (2, 1)]
    else:
        pieces, places = [], []
        for array in (wx, wy, wz):
            places.append([(len(pieces) + k, None) for k in range(shots)])
            pieces = pieces + [array] + [to_owners(array, k) for k in range(1, shots)]
        speed_places = places[0]
        speed_pieces = [speed] + [to_owners(speed, k) for k in range(1, shots)]

    now_p, now_a = halos(current)
    slope, flags, matrix = call(
        "prepare",
        functools.partial(prepare_kernel, shots, parts),
        (
            f32(3, rows + 8, width, depth),
            f32(shots * parts, depth),
            jax.ShapeDtypeStruct((2 * depth, depth), jnp.bfloat16),
        ),
        [first, current, now_p, now_a],
        scratch[:1],
    )
    edge = f32(3, 2, width, depth)
    tensor, flux, rest, *edges = call(
        "flux",
        functools.partial(flux_kernel, places, parts),
        (f32(3, rows, width, depth), field, field, edge, edge, edge, edge),
        [flags, slope, matrix] + pieces,
        scratch[2:3],
        work // 3,
    )
    edges_a = [across_chips(a) for a in edges[:2]]
    edges_p = [to_partner(a) for a in edges[2:]]

    speed, operand = call(
        "speed",
        functools.partial(speed_kernel, speed_places, parts),
        (field, field),
        [flags, present] + speed_pieces,
    )
    op_p, op_a = halos(operand)

    numbers = jnp.concatenate([step_index, source_x, source_y, source_z])
    src, inj = call(
        "inject",
        inject_kernel,
        (f32(STEPS - 1, rows, width, depth), f32(STEPS, rows, width, depth)),
        [
            in_hbm(a)
            for a in (numbers, wavelet, receiver_x, receiver_y, receiver_z, residual_traces)
        ],
        (
            pltpu.SMEM((4,), jnp.int32),
            pltpu.VMEM(wavelet.shape, jnp.float32),
            [pltpu.VMEM(receiver_x.shape, jnp.int32)] * 3,
            pltpu.VMEM(residual_traces.shape, jnp.float32),
            pltpu.SemaphoreType.DMA((6,)),
        ),
        1 << 28,
        1,
    )
    image, following, coef = call(
        "forward0",
        forward_first,
        (field, field, f32(4, rows + 8, width, depth)),
        [tensor, *edges_p, *edges_a, slope, flux, rest]
        + [current, previous, speed, src],
        scratch[1:2],
        work // 4,
    )
    images = [image]
    previous, current = current, following
    adjoints = [present]
    known = None
    for t in range(STEPS - 1):
        now_p, now_a = halos(current)
        back = STEPS - 1 - t
        ins = [operand, op_p, op_a, coef, matrix, present, later, inj, speed]
        outs = (field, field)
        if back == 1:
            ins = ins + [adjoints[1]] + images
            outs = (field, field, field)
        result = call(
            f"backward{t}", functools.partial(backward, back), outs, ins, scratch, work
        )
        later, present, operand = present, result[0], result[1]
        if back == 1:
            known = result[2]
        adjoints.append(present)
        op_p, op_a = halos(operand)
        if t < STEPS - 2:
            image, following = call(
                f"forward{t + 1}",
                functools.partial(forward, t + 1),
                (field, field),
                [current, now_p, now_a, coef, matrix, previous, speed, src],
                scratch,
                work,
            )
            images.append(image)
            previous, current = current, following

    chunks = call(
        "forward3",
        functools.partial(forward_last, parts),
        (f32(rows, count, depth),) * shots,
        [current, now_p, now_a, coef, matrix, known, adjoints[0], flags],
        scratch + (pltpu.VMEM((rows, width, depth), jnp.float32),),
        work,
    )
    received = [to_owners(chunks[k], k) for k in range(1, shots)]
    final, copied, done = call(
        "backward3",
        functools.partial(backward, 0),
        (field, field, f32(8, depth)),
        [operand, op_p, op_a, coef, matrix, present, later, inj],
        scratch,
        work,
    )
    model_grad = call("total", total_kernel, piece, [chunks[0]] + received + [done])
    return (copied[None], final[None], model_grad)


def solution(mesh):
    in_specs = (
        P("shot", "blk", None, None),
        P("shot", "blk", None, None),
        P("shot", "blk", None, None),
        P("shot", "blk", None, None),
        P("blk", "shot", None),
        P("blk", "shot", None),
        P("blk", "shot", None),
        P("blk", "shot", None),
        P("shot"),
        P(),
        P("shot", None),
        P("shot", None, None),
        P("shot"),
        P("shot"),
        P("shot"),
        P("shot", None),
        P("shot", None),
        P("shot", None),
    )
    out_specs = (P("shot", "blk", None, None), P("shot", "blk", None, None), P("blk", "shot", None))
    return jax.shard_map(
        on_device, mesh=mesh, in_specs=in_specs, out_specs=out_specs, check_vma=False
    )
```

time: 89.1 us -> 67.1 us (0.75)
  waiting for transfers between devices: 36.2 us -> 17.6 us
  local copies, waits for them, and re-layouts: 7.94 us -> 0.02 us
  starting transfers between devices: 24.2 us -> 29.2 us
    ppermute x10, waiting for transfers between devices: 26.5 us -> 7.48 us  [across_chips(): return lax.ppermute(array, ('shot', 'blk'), chip_pairs)]
    unnamed x30 -> x6, local copies, waits for them, and re-layouts: 7.94 us -> 0.02 us
    ppermute x9 -> x11, starting transfers between devices: 11.7 us -> 15.7 us  [to_owners(): return lax.ppermute(array, 'shot', [(i, i ^ k) for i in range(shots)])]
    ppermute x10, starting transfers between devices: 0.82 us -> 3.09 us  [to_partner(): return lax.ppermute(array, 'blk', core_pairs)]
    ppermute x10, starting transfers between devices: 11.8 us -> 10.4 us  [across_chips(): return lax.ppermute(array, ('shot', 'blk'), chip_pairs)]
    ppermute x9 -> x11, waiting for transfers between devices: 9.66 us -> 10.1 us  [to_owners(): return lax.ppermute(array, 'shot', [(i, i ^ k) for i in range(shots)])]
    pallas_call x13 -> x19, Pallas kernels: 15.6 us -> 15.4 us  [call(): pl.pallas_call(body, name=name, out_shape=outs, in_specs=[s for _, s in p...]
  transfers between devices with their start and end apart: 29 -> 31, of which waited for: 14 -> 12; matrix products, arithmetic and copies ran while one was open for 1% -> 1% of each run, Pallas kernels for 11% -> 20%
where the time goes in v4:
time: 67.1 us; the launch traced here: 66.9 us
  starting transfers between devices  29.2 us (44%)
  waiting for transfers between devices  17.6 us (26%)
  Pallas kernels  15.4 us (23%)
  between operations  4.1 us (6%)
    ppermute x11, starting transfers between devices, to_owners(): return lax.ppermute(array, 'shot', [(i, i ^ k) for i in range(shots)])  15.7 us
    pallas_call x19, Pallas kernels, call(): pl.pallas_call(body, name=name, out_shape=outs, in_specs=[s for _, s in p...  15.4 us
    ppermute x10, starting transfers between devices, across_chips(): return lax.ppermute(array, ('shot', 'blk'), chip_pairs)  10.4 us
    ppermute x11, waiting for transfers between devices, to_owners(): return lax.ppermute(array, 'shot', [(i, i ^ k) for i in range(shots)])  10.1 us
    ppermute x10, waiting for transfers between devices, across_chips(): return lax.ppermute(array, ('shot', 'blk'), chip_pairs)  7.48 us
    ppermute x10, starting transfers between devices, to_partner(): return lax.ppermute(array, 'blk', core_pairs)  3.09 us
  transfers between devices with their start and end apart: 31, of which 12 were waited for; matrix products, arithmetic and copies ran while one was open for 1% of the time, Pallas kernels for 20%

profile of v4, /device:TPU:0, one launch (start us, length us, event | category | flops | bytes accessed | tf_op | source)
XLA Modules:
  0.0 66.9 jit_solution(10306141477742934186)
XLA Ops:
  1.3 1.4 %owner.1 = (f32[8,32,128]{2,1,0:T(8,128)S(1)}, f32[8,32,128]{2,1,0:T(8,128)S(1)}, f32[8,32,128]{2,1,0:T(8,128)S(1)}, f32[8,32,128]{2,1,0:T(8,128)S(1)}, f32[8,64,128]{2,1,0:T(8,128)S(1)}) custom-call(f32[8,32,128]{2,1,0:T(8,128)} %eps.1, f32[8,32,128]{2,1,0:T(8,128)} %tilt.1, f32[8,32,128]{2,1,0:T(8,128)} %azimuth.1, f32[8,32,128]{2,1,0:T(8,128)} %speed.2, ...), custom_call_target="tpu_custom_call" | custom-call | flops 1048576 | bytes 1048576 | tf_op jit(solution)/shard_map/owner/pallas_call | solution.py:27
  2.7 3.0 %collective-permute-start.6 = (f32[9,32,128]{2,1,0:T(8,128)S(1)}, f32[9,32,128]{2,1,0:T(8,128)S(1)}, u32[]{:S(2)}, u32[]{:S(2)}) collective-permute-start(f32[9,32,128]{2,1,0:T(8,128)S(1)} %get-tuple-element.54), channel_id=1, source_target_pairs={{0,8},{8,0},{16,24},{24,16},{1,9},{9,1},{17,25},{25,17},{2,10},{10... | collective-permute-start | bytes 442376 | tf_op jit(solution)/shard_map/ppermute | solution.py:432
  5.7 1.5 %collective-permute-start.7 = (f32[8,32,128]{2,1,0:T(8,128)S(1)}, f32[8,32,128]{2,1,0:T(8,128)S(1)}, u32[]{:S(2)}, u32[]{:S(2)}) collective-permute-start(f32[8,32,128]{2,1,0:T(8,128)S(1)} %get-tuple-element.53.own.refs_0_), channel_id=1, source_target_pairs={{0,16},{8,24},{16,0},{24,8},{1,17},{9,25},{17,1},{25,9},{2,18},{10... | collective-permute-start | bytes 393224 | tf_op jit(solution)/shard_map/ppermute | solution.py:432
  7.2 0.5 collective-permute-start.1
  7.8 1.5 %collective-permute-start.2 = (f32[8,32,128]{2,1,0:T(8,128)S(1)}, f32[8,32,128]{2,1,0:T(8,128)S(1)}, u32[]{:S(2)}, u32[]{:S(2)}) collective-permute-start(f32[8,32,128]{2,1,0:T(8,128)S(1)} %get-tuple-element.49.own.refs_0_), channel_id=1, source_target_pairs={{0,8},{8,0},{16,24},{24,16},{1,9},{9,1},{17,25},{25,17},{2,10},{10... | collective-permute-start | bytes 393224 | tf_op jit(solution)/shard_map/ppermute | solution.py:432
  9.2 0.3 collective-permute-done.6.wz_first.received.refs_7_
  9.5 1.8 %collective-permute-start.9 = (f32[8,32,128]{2,1,0:T(8,128)S(1)}, f32[8,32,128]{2,1,0:T(8,128)S(1)}, u32[]{:S(2)}, u32[]{:S(2)}) collective-permute-start(f32[8,32,128]{2,1,0:T(8,128)S(1)} %get-tuple-element.55.own.refs_3_), channel_id=1, source_target_pairs={{0,16},{8,24},{16,0},{24,8},{1,17},{9,25},{17,1},{25,9},{2,18},{10... | collective-permute-start | bytes 393224 | tf_op jit(solution)/shard_map/ppermute | solution.py:432
  11.3 0.0 collective-permute-done.7.received.refs_2_
  11.3 0.8 %collective-permute-start.11 = (f32[2,8,32,128]{3,2,1,0:T(8,128)S(1)}, f32[2,8,32,128]{3,2,1,0:T(8,128)S(1)}, u32[]{:S(2)}, u32[]{:S(2)}) collective-permute-start(f32[2,8,32,128]{3,2,1,0:T(8,128)S(1)} %pair_wz.1), channel_id=1, source_target_pairs={{0,16},{8,24},{16,0},{24,8},{1,17},{9,25},{17,1},{25,9},{2,18},{10... | collective-permute-start | bytes 786440 | tf_op jit(solution)/shard_map/ppermute | solution.py:432
  12.2 4.2 %collective-permute-done.2.received.refs_1_.refs_0_ = f32[8,32,128]{2,1,0:T(8,128)S(1)} collective-permute-done((f32[8,32,128]{2,1,0:T(8,128)S(1)}, f32[8,32,128]{2,1,0:T(8,128)S(1)}, u32[]{:S(2)}, u32[]{:S(2)}) %collective-permute-start.2) | collective-permute-done | bytes 131104 | tf_op jit(solution)/shard_map/ppermute | solution.py:432
  16.4 0.0 collective-permute-done.9.received.refs_5_
  16.4 0.0 copy-start
  16.4 1.4 %collective-permute-start.10 = (f32[8,32,128]{2,1,0:T(8,128)S(1)}, f32[8,32,128]{2,1,0:T(8,128)S(1)}, u32[]{:S(2)}, u32[]{:S(2)}) collective-permute-start(f32[8,32,128]{2,1,0:T(8,128)S(1)} %relay_wy.1), channel_id=1, source_target_pairs={{0,8},{8,0},{16,24},{24,16},{1,9},{9,1},{17,25},{25,17},{2,10},{10... | collective-permute-start | bytes 393224 | tf_op jit(solution)/shard_map/ppermute | solution.py:432
  17.8 0.7 %collective-permute-start.8 = (f32[8,32,128]{2,1,0:T(8,128)S(1)}, f32[8,32,128]{2,1,0:T(8,128)S(1)}, u32[]{:S(2)}, u32[]{:S(2)}) collective-permute-start(f32[8,32,128]{2,1,0:T(8,128)S(1)} %relay_wx.1.refs_1_), channel_id=1, source_target_pairs={{0,8},{8,0},{16,24},{24,16},{1,9},{9,1},{17,25},{25,17},{2,10},{10... | collective-permute-start | bytes 393224 | tf_op jit(solution)/shard_map/ppermute | solution.py:432
  18.6 0.0 collective-permute-done.partner
  18.6 1.4 %collective-permute-start.3 = (f32[2,8,32,128]{3,2,1,0:T(8,128)S(1)}, f32[2,8,32,128]{3,2,1,0:T(8,128)S(1)}, u32[]{:S(2)}, u32[]{:S(2)}) collective-permute-start(f32[2,8,32,128]{3,2,1,0:T(8,128)S(1)} %pair_speed.1), channel_id=1, source_target_pairs={{0,16},{8,24},{16,0},{24,8},{1,17},{9,25},{17,1},{25,9},{2,18},{10... | collective-permute-start | bytes 786440 | tf_op jit(solution)/shard_map/ppermute | solution.py:432
  20.0 0.0 collective-permute-done.1.across
  20.0 0.9 %prepare.1 = (f32[3,16,64,128]{3,2,1,0:T(8,128)S(1)}, f32[8,128]{1,0:T(8,128)S(1)}, bf16[256,128]{1,0:T(8,128)(2,1)S(1)}) custom-call(f32[8,128]{1,0:T(8,128)S(1)} %get-tuple-element.46.first, f32[8,64,128]{2,1,0:T(8,128)S(1)} %get-tuple-element.47.own.previous, f32[8,64,128]{2,1,0:T(8,128)S(1)} %collective-permute-done.partner, ...), custom_call_target="tpu_custom_call" | custom-call | flops 1048576 | bytes 1048576 | tf_op jit(solution)/shard_map/prepare/pallas_call | solution.py:27
  20.8 0.6 collective-permute-done.10.refs_4_
  21.5 1.4 %collective-permute-done.8.refs_1_ = f32[8,32,128]{2,1,0:T(8,128)S(1)} collective-permute-done((f32[8,32,128]{2,1,0:T(8,128)S(1)}, f32[8,32,128]{2,1,0:T(8,128)S(1)}, u32[]{:S(2)}, u32[]{:S(2)}) %collective-permute-start.8) | collective-permute-done | bytes 131104 | tf_op jit(solution)/shard_map/ppermute | solution.py:432
  22.9 0.0 collective-permute-done.11.refs_8_
  22.9 0.5 flux.1
  23.4 0.1 collective-permute-start.12
  23.5 0.5 collective-permute-start.13
  24.0 1.3 %collective-permute-start.14 = (f32[3,2,64,128]{3,2,1,0:T(8,128)S(1)}, f32[3,2,64,128]{3,2,1,0:T(8,128)S(1)}, u32[]{:S(2)}, u32[]{:S(2)}) collective-permute-start(f32[3,2,64,128]{3,2,1,0:T(8,128)S(1)} %get-tuple-element.59), channel_id=1, source_target_pairs={{0,8},{1,2},{2,1},{3,4},{4,3},{5,6},{6,5},{7,15},{8,0},{9,10},{10,... | collective-permute-start | bytes 589832 | tf_op jit(solution)/shard_map/ppermute | solution.py:423
  25.3 0.7 %collective-permute-start.15 = (f32[3,2,64,128]{3,2,1,0:T(8,128)S(1)}, f32[3,2,64,128]{3,2,1,0:T(8,128)S(1)}, u32[]{:S(2)}, u32[]{:S(2)}) collective-permute-start(f32[3,2,64,128]{3,2,1,0:T(8,128)S(1)} %get-tuple-element.60), channel_id=1, source_target_pairs={{0,8},{1,2},{2,1},{3,4},{4,3},{5,6},{6,5},{7,15},{8,0},{9,10},{10,... | collective-permute-start | bytes 589832 | tf_op jit(solution)/shard_map/ppermute | solution.py:423
  28.6 0.1 speed.3
  28.7 0.1 collective-permute-start.4
  28.8 1.4 %collective-permute-start.5 = (f32[8,64,128]{2,1,0:T(8,128)S(1)}, f32[8,64,128]{2,1,0:T(8,128)S(1)}, u32[]{:S(2)}, u32[]{:S(2)}) collective-permute-start(f32[8,64,128]{2,1,0:T(8,128)S(1)} %get-tuple-element.50.own), channel_id=1, source_target_pairs={{0,8},{1,2},{2,1},{3,4},{4,3},{5,6},{6,5},{7,15},{8,0},{9,10},{10,... | collective-permute-start | bytes 786440 | tf_op jit(solution)/shard_map/ppermute | solution.py:423
  30.2 0.6 pad_add_fusion.numbers
  30.8 1.8 %inject.1 = (f32[3,8,64,128]{3,2,1,0:T(8,128)S(1)}, f32[4,8,64,128]{3,2,1,0:T(8,128)S(1)}) custom-call(s32[4]{0:T(128)} %pad_add_fusion.numbers, f32[1,16]{1,0:T(1,128)} %wavelet.1, s32[1,128]{1,0:T(1,128)} %rx.1, s32[1,128]{1,0:T(1,128)} %ry.1, s32[1,128]{1,0:T(1,128)} %rz.1, f32[1,16,128]{2,1,0:T(8,128)} %traces.1), custom_call_target="tpu_custom_call" | custom-call | flops 268435456 | bytes 1 | tf_op jit(solution)/shard_map/inject/pallas_call | solution.py:27
  32.6 0.0 copy-start.2
  32.6 0.5 forward0.1
  33.1 0.1 collective-permute-start.20
  33.2 1.4 %collective-permute-start.21 = (f32[8,64,128]{2,1,0:T(8,128)S(1)}, f32[8,64,128]{2,1,0:T(8,128)S(1)}, u32[]{:S(2)}, u32[]{:S(2)}) collective-permute-start(f32[8,64,128]{2,1,0:T(8,128)S(1)} %get-tuple-element.72.own.previous), channel_id=1, source_target_pairs={{0,8},{1,2},{2,1},{3,4},{4,3},{5,6},{6,5},{7,15},{8,0},{9,10},{10,... | collective-permute-start | bytes 786440 | tf_op jit(solution)/shard_map/ppermute | solution.py:423
  34.6 0.6 collective-permute-done.5.across
  35.2 1.2 %backward0.1 = (f32[8,64,128]{2,1,0:T(8,128)S(1)}, f32[8,64,128]{2,1,0:T(8,128)S(1)}) custom-call(f32[8,64,128]{2,1,0:T(8,128)S(1)} %get-tuple-element.50.own, f32[8,64,128]{2,1,0:T(8,128)S(1)} %collective-permute-done.4.partner, f32[8,64,128]{2,1,0:T(8,128)S(1)} %collective-permute-done.5.across, f32[4,16,64,128]{3,2,1,0:T(8,128)S(1)} %get-tuple-element.65.coef, ...), custom_call_target="tpu_custom_call" | custom-call | flops 13107200 | bytes 1048576 | tf_op jit(solution)/shard_map/backward0/pallas_call | solution.py:27
  36.5 1.2 %collective-permute-start.16 = (f32[8,64,128]{2,1,0:T(8,128)S(1)}, f32[8,64,128]{2,1,0:T(8,128)S(1)}, u32[]{:S(2)}, u32[]{:S(2)}) collective-permute-start(f32[8,64,128]{2,1,0:T(8,128)S(1)} %get-tuple-element.67.own), channel_id=1, source_target_pairs={{0,1},{1,0},{2,3},{3,2},{4,5},{5,4},{6,7},{7,6},{8,9},{9,8},{10,11... | collective-permute-start | bytes 786440 | tf_op jit(solution)/shard_map/ppermute | solution.py:420
  37.7 1.0 %collective-permute-start.17 = (f32[8,64,128]{2,1,0:T(8,128)S(1)}, f32[8,64,128]{2,1,0:T(8,128)S(1)}, u32[]{:S(2)}, u32[]{:S(2)}) collective-permute-start(f32[8,64,128]{2,1,0:T(8,128)S(1)} %get-tuple-element.67.own), channel_id=1, source_target_pairs={{0,8},{1,2},{2,1},{3,4},{4,3},{5,6},{6,5},{7,15},{8,0},{9,10},{10,... | collective-permute-start | bytes 786440 | tf_op jit(solution)/shard_map/ppermute | solution.py:423
  38.7 1.0 %collective-permute-done.21.across = f32[8,64,128]{2,1,0:T(8,128)S(1)} collective-permute-done((f32[8,64,128]{2,1,0:T(8,128)S(1)}, f32[8,64,128]{2,1,0:T(8,128)S(1)}, u32[]{:S(2)}, u32[]{:S(2)}) %collective-permute-start.21) | collective-permute-done | bytes 262176 | tf_op jit(solution)/shard_map/ppermute | solution.py:423
  39.7 1.2 %forward1.1 = (f32[8,64,128]{2,1,0:T(8,128)S(1)}, f32[8,64,128]{2,1,0:T(8,128)S(1)}) custom-call(f32[8,64,128]{2,1,0:T(8,128)S(1)} %get-tuple-element.72.own.previous, f32[8,64,128]{2,1,0:T(8,128)S(1)} %collective-permute-done.20.partner, f32[8,64,128]{2,1,0:T(8,128)S(1)} %collective-permute-done.21.across, f32[4,16,64,128]{3,2,1,0:T(8,128)S(1)} %get-tuple-element.65.coef, ...), custom_call_target="tpu_custom_call" | custom-call | flops 13107200 | bytes 1048576 | tf_op jit(solution)/shard_map/forward1/pallas_call | solution.py:27
  40.9 0.8 %collective-permute-start.22 = (f32[8,64,128]{2,1,0:T(8,128)S(1)}, f32[8,64,128]{2,1,0:T(8,128)S(1)}, u32[]{:S(2)}, u32[]{:S(2)}) collective-permute-start(f32[8,64,128]{2,1,0:T(8,128)S(1)} %get-tuple-element.74.own), channel_id=1, source_target_pairs={{0,1},{1,0},{2,3},{3,2},{4,5},{5,4},{6,7},{7,6},{8,9},{9,8},{10,11... | collective-permute-start | bytes 786440 | tf_op jit(solution)/shard_map/ppermute | solution.py:420
  41.7 1.0 %collective-permute-start.23 = (f32[8,64,128]{2,1,0:T(8,128)S(1)}, f32[8,64,128]{2,1,0:T(8,128)S(1)}, u32[]{:S(2)}, u32[]{:S(2)}) collective-permute-start(f32[8,64,128]{2,1,0:T(8,128)S(1)} %get-tuple-element.74.own), channel_id=1, source_target_pairs={{0,8},{1,2},{2,1},{3,4},{4,3},{5,6},{6,5},{7,15},{8,0},{9,10},{10,... | collective-permute-start | bytes 786440 | tf_op jit(solution)/shard_map/ppermute | solution.py:423
  42.7 1.4 %collective-permute-done.17.across = f32[8,64,128]{2,1,0:T(8,128)S(1)} collective-permute-done((f32[8,64,128]{2,1,0:T(8,128)S(1)}, f32[8,64,128]{2,1,0:T(8,128)S(1)}, u32[]{:S(2)}, u32[]{:S(2)}) %collective-permute-start.17) | collective-permute-done | bytes 262176 | tf_op jit(solution)/shard_map/ppermute | solution.py:423
  44.1 1.2 %backward1.1 = (f32[8,64,128]{2,1,0:T(8,128)S(1)}, f32[8,64,128]{2,1,0:T(8,128)S(1)}) custom-call(f32[8,64,128]{2,1,0:T(8,128)S(1)} %get-tuple-element.67.own, f32[8,64,128]{2,1,0:T(8,128)S(1)} %collective-permute-done.16.partner, f32[8,64,128]{2,1,0:T(8,128)S(1)} %collective-permute-done.17.across, f32[4,16,64,128]{3,2,1,0:T(8,128)S(1)} %get-tuple-element.65.coef, ...), custom_call_target="tpu_custom_call" | custom-call | flops 13107200 | bytes 1048576 | tf_op jit(solution)/shard_map/backward1/pallas_call | solution.py:27
  45.3 0.1 collective-permute-start.18
  45.4 1.0 %collective-permute-start.19 = (f32[8,64,128]{2,1,0:T(8,128)S(1)}, f32[8,64,128]{2,1,0:T(8,128)S(1)}, u32[]{:S(2)}, u32[]{:S(2)}) collective-permute-start(f32[8,64,128]{2,1,0:T(8,128)S(1)} %get-tuple-element.69.own), channel_id=1, source_target_pairs={{0,8},{1,2},{2,1},{3,4},{4,3},{5,6},{6,5},{7,15},{8,0},{9,10},{10,... | collective-permute-start | bytes 786440 | tf_op jit(solution)/shard_map/ppermute | solution.py:423
  46.4 1.7 %collective-permute-done.23.across = f32[8,64,128]{2,1,0:T(8,128)S(1)} collective-permute-done((f32[8,64,128]{2,1,0:T(8,128)S(1)}, f32[8,64,128]{2,1,0:T(8,128)S(1)}, u32[]{:S(2)}, u32[]{:S(2)}) %collective-permute-start.23) | collective-permute-done | bytes 262176 | tf_op jit(solution)/shard_map/ppermute | solution.py:423
  48.1 1.2 %forward2.1 = (f32[8,64,128]{2,1,0:T(8,128)S(1)}, f32[8,64,128]{2,1,0:T(8,128)S(1)}) custom-call(f32[8,64,128]{2,1,0:T(8,128)S(1)} %get-tuple-element.74.own, f32[8,64,128]{2,1,0:T(8,128)S(1)} %collective-permute-done.22.partner, f32[8,64,128]{2,1,0:T(8,128)S(1)} %collective-permute-done.23.across, f32[4,16,64,128]{3,2,1,0:T(8,128)S(1)} %get-tuple-element.65.coef, ...), custom_call_target="tpu_custom_call" | custom-call | flops 13107200 | bytes 1048576 | tf_op jit(solution)/shard_map/forward2/pallas_call | solution.py:27
  49.3 0.1 collective-permute-start.26
  49.4 1.0 %collective-permute-start.27 = (f32[8,64,128]{2,1,0:T(8,128)S(1)}, f32[8,64,128]{2,1,0:T(8,128)S(1)}, u32[]{:S(2)}, u32[]{:S(2)}) collective-permute-start(f32[8,64,128]{2,1,0:T(8,128)S(1)} %get-tuple-element.80.own), channel_id=1, source_target_pairs={{0,8},{1,2},{2,1},{3,4},{4,3},{5,6},{6,5},{7,15},{8,0},{9,10},{10,... | collective-permute-start | bytes 786440 | tf_op jit(solution)/shard_map/ppermute | solution.py:423
  50.4 1.4 %collective-permute-done.19.across = f32[8,64,128]{2,1,0:T(8,128)S(1)} collective-permute-done((f32[8,64,128]{2,1,0:T(8,128)S(1)}, f32[8,64,128]{2,1,0:T(8,128)S(1)}, u32[]{:S(2)}, u32[]{:S(2)}) %collective-permute-start.19) | collective-permute-done | bytes 262176 | tf_op jit(solution)/shard_map/ppermute | solution.py:423
  51.8 1.3 %backward2.1 = (f32[8,64,128]{2,1,0:T(8,128)S(1)}, f32[8,64,128]{2,1,0:T(8,128)S(1)}, f32[8,64,128]{2,1,0:T(8,128)S(1)}) custom-call(f32[8,64,128]{2,1,0:T(8,128)S(1)} %get-tuple-element.69.own, f32[8,64,128]{2,1,0:T(8,128)S(1)} %collective-permute-done.18.partner, f32[8,64,128]{2,1,0:T(8,128)S(1)} %collective-permute-done.19.across, ...), custom_call_target="tpu_custom_call" | custom-call | flops 13107200 | bytes 1048576 | tf_op jit(solution)/shard_map/backward2/pallas_call | solution.py:27
  53.1 0.2 collective-permute-start.24
  53.3 1.1 %collective-permute-start.25 = (f32[8,64,128]{2,1,0:T(8,128)S(1)}, f32[8,64,128]{2,1,0:T(8,128)S(1)}, u32[]{:S(2)}, u32[]{:S(2)}) collective-permute-start(f32[8,64,128]{2,1,0:T(8,128)S(1)} %get-tuple-element.76.own), channel_id=1, source_target_pairs={{0,8},{1,2},{2,1},{3,4},{4,3},{5,6},{6,5},{7,15},{8,0},{9,10},{10,... | collective-permute-start | bytes 786440 | tf_op jit(solution)/shard_map/ppermute | solution.py:423
  54.4 1.4 %collective-permute-done.27.across = f32[8,64,128]{2,1,0:T(8,128)S(1)} collective-permute-done((f32[8,64,128]{2,1,0:T(8,128)S(1)}, f32[8,64,128]{2,1,0:T(8,128)S(1)}, u32[]{:S(2)}, u32[]{:S(2)}) %collective-permute-start.27) | collective-permute-done | bytes 262176 | tf_op jit(solution)/shard_map/ppermute | solution.py:423
  55.8 1.3 %forward3.1 = (f32[8,32,128]{2,1,0:T(8,128)S(1)}, f32[8,32,128]{2,1,0:T(8,128)S(1)}, f32[8,32,128]{2,1,0:T(8,128)S(1)}, f32[8,32,128]{2,1,0:T(8,128)S(1)}) custom-call(f32[8,64,128]{2,1,0:T(8,128)S(1)} %get-tuple-element.80.own, f32[8,64,128]{2,1,0:T(8,128)S(1)} %collective-permute-done.26.partner, f32[8,64,128]{2,1,0:T(8,128)S(1)} %collective-permute-done.27.across, ...), custom_call_target="tpu_custom_call" | custom-call | flops 13107200 | bytes 1048576 | tf_op jit(solution)/shard_map/forward3/pallas_call | solution.py:27
  57.1 1.0 %collective-permute-start.28 = (f32[8,32,128]{2,1,0:T(8,128)S(1)}, f32[8,32,128]{2,1,0:T(8,128)S(1)}, u32[]{:S(2)}, u32[]{:S(2)}) collective-permute-start(f32[8,32,128]{2,1,0:T(8,128)S(1)} %get-tuple-element.83), channel_id=1, source_target_pairs={{0,8},{8,0},{16,24},{24,16},{1,9},{9,1},{17,25},{25,17},{2,10},{10... | collective-permute-start | bytes 393224 | tf_op jit(solution)/shard_map/ppermute | solution.py:432
  58.1 1.5 %collective-permute-start.29 = (f32[8,32,128]{2,1,0:T(8,128)S(1)}, f32[8,32,128]{2,1,0:T(8,128)S(1)}, u32[]{:S(2)}, u32[]{:S(2)}) collective-permute-start(f32[8,32,128]{2,1,0:T(8,128)S(1)} %get-tuple-element.84), channel_id=1, source_target_pairs={{0,16},{8,24},{16,0},{24,8},{1,17},{9,25},{17,1},{25,9},{2,18},{10... | collective-permute-start | bytes 393224 | tf_op jit(solution)/shard_map/ppermute | solution.py:432
  59.7 1.0 %collective-permute-start.30 = (f32[8,32,128]{2,1,0:T(8,128)S(1)}, f32[8,32,128]{2,1,0:T(8,128)S(1)}, u32[]{:S(2)}, u32[]{:S(2)}) collective-permute-start(f32[8,32,128]{2,1,0:T(8,128)S(1)} %get-tuple-element.85), channel_id=1, source_target_pairs={{0,24},{8,16},{16,8},{24,0},{1,25},{9,17},{17,9},{25,1},{2,26},{10... | collective-permute-start | bytes 393224 | tf_op jit(solution)/shard_map/ppermute | solution.py:432
  60.7 2.0 %backward3.1 = (f32[8,64,128]{2,1,0:T(8,128)}, f32[8,64,128]{2,1,0:T(8,128)}, f32[8,128]{1,0:T(8,128)S(1)}) custom-call(f32[8,64,128]{2,1,0:T(8,128)S(1)} %get-tuple-element.76.own, f32[8,64,128]{2,1,0:T(8,128)S(1)} %collective-permute-done.24.partner, f32[8,64,128]{2,1,0:T(8,128)S(1)} %collective-permute-done.25.across, ...), custom_call_target="tpu_custom_call" | custom-call | flops 13107200 | bytes 1048576 | tf_op jit(solution)/shard_map/backward3/pallas_call | solution.py:27
  62.6 0.9 %collective-permute-done.28.refs_1_ = f32[8,32,128]{2,1,0:T(8,128)S(1)} collective-permute-done((f32[8,32,128]{2,1,0:T(8,128)S(1)}, f32[8,32,128]{2,1,0:T(8,128)S(1)}, u32[]{:S(2)}, u32[]{:S(2)}) %collective-permute-start.28) | collective-permute-done | bytes 131104 | tf_op jit(solution)/shard_map/ppermute | solution.py:432
  63.5 2.7 %collective-permute-done.29.refs_2_ = f32[8,32,128]{2,1,0:T(8,128)S(1)} collective-permute-done((f32[8,32,128]{2,1,0:T(8,128)S(1)}, f32[8,32,128]{2,1,0:T(8,128)S(1)}, u32[]{:S(2)}, u32[]{:S(2)}) %collective-permute-start.29) | collective-permute-done | bytes 131104 | tf_op jit(solution)/shard_map/ppermute | solution.py:432
  66.2 0.7 %total.1 = f32[8,32,128]{2,1,0:T(8,128)} custom-call(f32[8,32,128]{2,1,0:T(8,128)S(1)} %get-tuple-element.82.refs_0_, f32[8,32,128]{2,1,0:T(8,128)S(1)} %collective-permute-done.28.refs_1_, f32[8,32,128]{2,1,0:T(8,128)S(1)} %collective-permute-done.29.refs_2_, f32[8,32,128]{2,1,0:T(8,128)S(1)} %collective-permute-done.30.refs_3_, ...), custom_call_target="tpu_custom_call" | custom-call | flops 1048576 | bytes 1048576 | tf_op jit(solution)/shard_map/total/pallas_call | solution.py:27
  (24 shorter events, 0.1 us)
Async XLA Ops:
  2.7 6.9 %collective-permute-start.6 = (f32[9,32,128]{2,1,0:T(8,128)S(1)}, f32[9,32,128]{2,1,0:T(8,128)S(1)}, u32[]{:S(2)}, u32[]{:S(2)}) collective-permute-start(f32[9,32,128]{2,1,0:T(8,128)S(1)} %get-tuple-element.54), channel_id=1, source_target_pairs={{0,8},{8,0},{16,24},{24,16},{1,9},{9,1},{17,25},{25,17},{2,10},{10... | collective-permute-start | bytes 442376 | tf_op jit(solution)/shard_map/ppermute | solution.py:432
  5.7 5.6 %collective-permute-start.7 = (f32[8,32,128]{2,1,0:T(8,128)S(1)}, f32[8,32,128]{2,1,0:T(8,128)S(1)}, u32[]{:S(2)}, u32[]{:S(2)}) collective-permute-start(f32[8,32,128]{2,1,0:T(8,128)S(1)} %get-tuple-element.53.own.refs_0_), channel_id=1, source_target_pairs={{0,16},{8,24},{16,0},{24,8},{1,17},{9,25},{17,1},{25,9},{2,18},{10... | collective-permute-start | bytes 393224 | tf_op jit(solution)/shard_map/ppermute | solution.py:432
  7.2 11.3 %collective-permute-start = (f32[8,64,128]{2,1,0:T(8,128)S(1)}, f32[8,64,128]{2,1,0:T(8,128)S(1)}, u32[]{:S(2)}, u32[]{:S(2)}) collective-permute-start(f32[8,64,128]{2,1,0:T(8,128)S(1)} %get-tuple-element.47.own.previous), channel_id=1, source_target_pairs={{0,1},{1,0},{2,3},{3,2},{4,5},{5,4},{6,7},{7,6},{8,9},{9,8},{10,11... | collective-permute-start | bytes 786440 | tf_op jit(solution)/shard_map/ppermute | solution.py:420
  7.2 12.8 %collective-permute-start.1 = (f32[8,64,128]{2,1,0:T(8,128)S(1)}, f32[8,64,128]{2,1,0:T(8,128)S(1)}, u32[]{:S(2)}, u32[]{:S(2)}) collective-permute-start(f32[8,64,128]{2,1,0:T(8,128)S(1)} %get-tuple-element.47.own.previous), channel_id=1, source_target_pairs={{0,8},{1,2},{2,1},{3,4},{4,3},{5,6},{6,5},{7,15},{8,0},{9,10},{10,... | collective-permute-start | bytes 786440 | tf_op jit(solution)/shard_map/ppermute | solution.py:423
  7.8 8.6 %collective-permute-start.2 = (f32[8,32,128]{2,1,0:T(8,128)S(1)}, f32[8,32,128]{2,1,0:T(8,128)S(1)}, u32[]{:S(2)}, u32[]{:S(2)}) collective-permute-start(f32[8,32,128]{2,1,0:T(8,128)S(1)} %get-tuple-element.49.own.refs_0_), channel_id=1, source_target_pairs={{0,8},{8,0},{16,24},{24,16},{1,9},{9,1},{17,25},{25,17},{2,10},{10... | collective-permute-start | bytes 393224 | tf_op jit(solution)/shard_map/ppermute | solution.py:432
  9.5 6.9 %collective-permute-start.9 = (f32[8,32,128]{2,1,0:T(8,128)S(1)}, f32[8,32,128]{2,1,0:T(8,128)S(1)}, u32[]{:S(2)}, u32[]{:S(2)}) collective-permute-start(f32[8,32,128]{2,1,0:T(8,128)S(1)} %get-tuple-element.55.own.refs_3_), channel_id=1, source_target_pairs={{0,16},{8,24},{16,0},{24,8},{1,17},{9,25},{17,1},{25,9},{2,18},{10... | collective-permute-start | bytes 393224 | tf_op jit(solution)/shard_map/ppermute | solution.py:432
  11.3 11.5 %collective-permute-start.11 = (f32[2,8,32,128]{3,2,1,0:T(8,128)S(1)}, f32[2,8,32,128]{3,2,1,0:T(8,128)S(1)}, u32[]{:S(2)}, u32[]{:S(2)}) collective-permute-start(f32[2,8,32,128]{3,2,1,0:T(8,128)S(1)} %pair_wz.1), channel_id=1, source_target_pairs={{0,16},{8,24},{16,0},{24,8},{1,17},{9,25},{17,1},{25,9},{2,18},{10... | collective-permute-start | bytes 786440 | tf_op jit(solution)/shard_map/ppermute | solution.py:432
  16.4 12.2 %copy-start = (f32[1,8,64,128]{3,2,1,0:T(8,128)S(1)}, f32[1,8,64,128]{3,2,1,0:T(8,128)}, u32[]{:S(2)}) copy-start(f32[1,8,64,128]{3,2,1,0:T(8,128)} %param.21) | copy-start | bytes 786436
  16.4 5.0 %collective-permute-start.10 = (f32[8,32,128]{2,1,0:T(8,128)S(1)}, f32[8,32,128]{2,1,0:T(8,128)S(1)}, u32[]{:S(2)}, u32[]{:S(2)}) collective-permute-start(f32[8,32,128]{2,1,0:T(8,128)S(1)} %relay_wy.1), channel_id=1, source_target_pairs={{0,8},{8,0},{16,24},{24,16},{1,9},{9,1},{17,25},{25,17},{2,10},{10... | collective-permute-start | bytes 393224 | tf_op jit(solution)/shard_map/ppermute | solution.py:432
  17.8 5.1 %collective-permute-start.8 = (f32[8,32,128]{2,1,0:T(8,128)S(1)}, f32[8,32,128]{2,1,0:T(8,128)S(1)}, u32[]{:S(2)}, u32[]{:S(2)}) collective-permute-start(f32[8,32,128]{2,1,0:T(8,128)S(1)} %relay_wx.1.refs_1_), channel_id=1, source_target_pairs={{0,8},{8,0},{16,24},{24,16},{1,9},{9,1},{17,25},{25,17},{2,10},{10... | collective-permute-start | bytes 393224 | tf_op jit(solution)/shard_map/ppermute | solution.py:432
  18.6 10.0 %collective-permute-start.3 = (f32[2,8,32,128]{3,2,1,0:T(8,128)S(1)}, f32[2,8,32,128]{3,2,1,0:T(8,128)S(1)}, u32[]{:S(2)}, u32[]{:S(2)}) collective-permute-start(f32[2,8,32,128]{3,2,1,0:T(8,128)S(1)} %pair_speed.1), channel_id=1, source_target_pairs={{0,16},{8,24},{16,0},{24,8},{1,17},{9,25},{17,1},{25,9},{2,18},{10... | collective-permute-start | bytes 786440 | tf_op jit(solution)/shard_map/ppermute | solution.py:432
  22.9 9.7 %copy-start.1 = (f32[1,8,64,128]{3,2,1,0:T(8,128)S(1)}, f32[1,8,64,128]{3,2,1,0:T(8,128)}, u32[]{:S(2)}) copy-start(f32[1,8,64,128]{3,2,1,0:T(8,128)} %param.18) | copy-start | bytes 786436
  23.4 5.4 %collective-permute-start.12 = (f32[3,2,64,128]{3,2,1,0:T(8,128)S(1)}, f32[3,2,64,128]{3,2,1,0:T(8,128)S(1)}, u32[]{:S(2)}, u32[]{:S(2)}) collective-permute-start(f32[3,2,64,128]{3,2,1,0:T(8,128)S(1)} %get-tuple-element.57), channel_id=1, source_target_pairs={{0,1},{1,0},{2,3},{3,2},{4,5},{5,4},{6,7},{7,6},{8,9},{9,8},{10,11... | collective-permute-start | bytes 589832 | tf_op jit(solution)/shard_map/ppermute | solution.py:420
  23.5 9.1 %collective-permute-start.13 = (f32[3,2,64,128]{3,2,1,0:T(8,128)S(1)}, f32[3,2,64,128]{3,2,1,0:T(8,128)S(1)}, u32[]{:S(2)}, u32[]{:S(2)}) collective-permute-start(f32[3,2,64,128]{3,2,1,0:T(8,128)S(1)} %get-tuple-element.58), channel_id=1, source_target_pairs={{0,1},{1,0},{2,3},{3,2},{4,5},{5,4},{6,7},{7,6},{8,9},{9,8},{10,11... | collective-permute-start | bytes 589832 | tf_op jit(solution)/shard_map/ppermute | solution.py:420
  24.0 8.6 %collective-permute-start.14 = (f32[3,2,64,128]{3,2,1,0:T(8,128)S(1)}, f32[3,2,64,128]{3,2,1,0:T(8,128)S(1)}, u32[]{:S(2)}, u32[]{:S(2)}) collective-permute-start(f32[3,2,64,128]{3,2,1,0:T(8,128)S(1)} %get-tuple-element.59), channel_id=1, source_target_pairs={{0,8},{1,2},{2,1},{3,4},{4,3},{5,6},{6,5},{7,15},{8,0},{9,10},{10,... | collective-permute-start | bytes 589832 | tf_op jit(solution)/shard_map/ppermute | solution.py:423
  25.3 7.3 %collective-permute-start.15 = (f32[3,2,64,128]{3,2,1,0:T(8,128)S(1)}, f32[3,2,64,128]{3,2,1,0:T(8,128)S(1)}, u32[]{:S(2)}, u32[]{:S(2)}) collective-permute-start(f32[3,2,64,128]{3,2,1,0:T(8,128)S(1)} %get-tuple-element.60), channel_id=1, source_target_pairs={{0,8},{1,2},{2,1},{3,4},{4,3},{5,6},{6,5},{7,15},{8,0},{9,10},{10,... | collective-permute-start | bytes 589832 | tf_op jit(solution)/shard_map/ppermute | solution.py:423
  28.7 5.9 %collective-permute-start.4 = (f32[8,64,128]{2,1,0:T(8,128)S(1)}, f32[8,64,128]{2,1,0:T(8,128)S(1)}, u32[]{:S(2)}, u32[]{:S(2)}) collective-permute-start(f32[8,64,128]{2,1,0:T(8,128)S(1)} %get-tuple-element.50.own), channel_id=1, source_target_pairs={{0,1},{1,0},{2,3},{3,2},{4,5},{5,4},{6,7},{7,6},{8,9},{9,8},{10,11... | collective-permute-start | bytes 786440 | tf_op jit(solution)/shard_map/ppermute | solution.py:420
  28.8 6.4 %collective-permute-start.5 = (f32[8,64,128]{2,1,0:T(8,128)S(1)}, f32[8,64,128]{2,1,0:T(8,128)S(1)}, u32[]{:S(2)}, u32[]{:S(2)}) collective-permute-start(f32[8,64,128]{2,1,0:T(8,128)S(1)} %get-tuple-element.50.own), channel_id=1, source_target_pairs={{0,8},{1,2},{2,1},{3,4},{4,3},{5,6},{6,5},{7,15},{8,0},{9,10},{10,... | collective-permute-start | bytes 786440 | tf_op jit(solution)/shard_map/ppermute | solution.py:423
  32.6 2.6 %copy-start.2 = (f32[1,8,64,128]{3,2,1,0:T(8,128)S(1)}, f32[1,8,64,128]{3,2,1,0:T(8,128)}, u32[]{:S(2)}) copy-start(f32[1,8,64,128]{3,2,1,0:T(8,128)} %param.20) | copy-start | bytes 786436
  33.1 5.5 %collective-permute-start.20 = (f32[8,64,128]{2,1,0:T(8,128)S(1)}, f32[8,64,128]{2,1,0:T(8,128)S(1)}, u32[]{:S(2)}, u32[]{:S(2)}) collective-permute-start(f32[8,64,128]{2,1,0:T(8,128)S(1)} %get-tuple-element.72.own.previous), channel_id=1, source_target_pairs={{0,1},{1,0},{2,3},{3,2},{4,5},{5,4},{6,7},{7,6},{8,9},{9,8},{10,11... | collective-permute-start | bytes 786440 | tf_op jit(solution)/shard_map/ppermute | solution.py:420
  33.2 6.4 %collective-permute-start.21 = (f32[8,64,128]{2,1,0:T(8,128)S(1)}, f32[8,64,128]{2,1,0:T(8,128)S(1)}, u32[]{:S(2)}, u32[]{:S(2)}) collective-permute-start(f32[8,64,128]{2,1,0:T(8,128)S(1)} %get-tuple-element.72.own.previous), channel_id=1, source_target_pairs={{0,8},{1,2},{2,1},{3,4},{4,3},{5,6},{6,5},{7,15},{8,0},{9,10},{10,... | collective-permute-start | bytes 786440 | tf_op jit(solution)/shard_map/ppermute | solution.py:423
  36.5 6.2 %collective-permute-start.16 = (f32[8,64,128]{2,1,0:T(8,128)S(1)}, f32[8,64,128]{2,1,0:T(8,128)S(1)}, u32[]{:S(2)}, u32[]{:S(2)}) collective-permute-start(f32[8,64,128]{2,1,0:T(8,128)S(1)} %get-tuple-element.67.own), channel_id=1, source_target_pairs={{0,1},{1,0},{2,3},{3,2},{4,5},{5,4},{6,7},{7,6},{8,9},{9,8},{10,11... | collective-permute-start | bytes 786440 | tf_op jit(solution)/shard_map/ppermute | solution.py:420
  37.7 6.4 %collective-permute-start.17 = (f32[8,64,128]{2,1,0:T(8,128)S(1)}, f32[8,64,128]{2,1,0:T(8,128)S(1)}, u32[]{:S(2)}, u32[]{:S(2)}) collective-permute-start(f32[8,64,128]{2,1,0:T(8,128)S(1)} %get-tuple-element.67.own), channel_id=1, source_target_pairs={{0,8},{1,2},{2,1},{3,4},{4,3},{5,6},{6,5},{7,15},{8,0},{9,10},{10,... | collective-permute-start | bytes 786440 | tf_op jit(solution)/shard_map/ppermute | solution.py:423
  40.9 5.5 %collective-permute-start.22 = (f32[8,64,128]{2,1,0:T(8,128)S(1)}, f32[8,64,128]{2,1,0:T(8,128)S(1)}, u32[]{:S(2)}, u32[]{:S(2)}) collective-permute-start(f32[8,64,128]{2,1,0:T(8,128)S(1)} %get-tuple-element.74.own), channel_id=1, source_target_pairs={{0,1},{1,0},{2,3},{3,2},{4,5},{5,4},{6,7},{7,6},{8,9},{9,8},{10,11... | collective-permute-start | bytes 786440 | tf_op jit(solution)/shard_map/ppermute | solution.py:420
  41.7 6.4 %collective-permute-start.23 = (f32[8,64,128]{2,1,0:T(8,128)S(1)}, f32[8,64,128]{2,1,0:T(8,128)S(1)}, u32[]{:S(2)}, u32[]{:S(2)}) collective-permute-start(f32[8,64,128]{2,1,0:T(8,128)S(1)} %get-tuple-element.74.own), channel_id=1, source_target_pairs={{0,8},{1,2},{2,1},{3,4},{4,3},{5,6},{6,5},{7,15},{8,0},{9,10},{10,... | collective-permute-start | bytes 786440 | tf_op jit(solution)/shard_map/ppermute | solution.py:423
  45.3 5.1 %collective-permute-start.18 = (f32[8,64,128]{2,1,0:T(8,128)S(1)}, f32[8,64,128]{2,1,0:T(8,128)S(1)}, u32[]{:S(2)}, u32[]{:S(2)}) collective-permute-start(f32[8,64,128]{2,1,0:T(8,128)S(1)} %get-tuple-element.69.own), channel_id=1, source_target_pairs={{0,1},{1,0},{2,3},{3,2},{4,5},{5,4},{6,7},{7,6},{8,9},{9,8},{10,11... | collective-permute-start | bytes 786440 | tf_op jit(solution)/shard_map/ppermute | solution.py:420
  45.4 6.4 %collective-permute-start.19 = (f32[8,64,128]{2,1,0:T(8,128)S(1)}, f32[8,64,128]{2,1,0:T(8,128)S(1)}, u32[]{:S(2)}, u32[]{:S(2)}) collective-permute-start(f32[8,64,128]{2,1,0:T(8,128)S(1)} %get-tuple-element.69.own), channel_id=1, source_target_pairs={{0,8},{1,2},{2,1},{3,4},{4,3},{5,6},{6,5},{7,15},{8,0},{9,10},{10,... | collective-permute-start | bytes 786440 | tf_op jit(solution)/shard_map/ppermute | solution.py:423
  49.3 5.1 %collective-permute-start.26 = (f32[8,64,128]{2,1,0:T(8,128)S(1)}, f32[8,64,128]{2,1,0:T(8,128)S(1)}, u32[]{:S(2)}, u32[]{:S(2)}) collective-permute-start(f32[8,64,128]{2,1,0:T(8,128)S(1)} %get-tuple-element.80.own), channel_id=1, source_target_pairs={{0,1},{1,0},{2,3},{3,2},{4,5},{5,4},{6,7},{7,6},{8,9},{9,8},{10,11... | collective-permute-start | bytes 786440 | tf_op jit(solution)/shard_map/ppermute | solution.py:420
  49.4 6.4 %collective-permute-start.27 = (f32[8,64,128]{2,1,0:T(8,128)S(1)}, f32[8,64,128]{2,1,0:T(8,128)S(1)}, u32[]{:S(2)}, u32[]{:S(2)}) collective-permute-start(f32[8,64,128]{2,1,0:T(8,128)S(1)} %get-tuple-element.80.own), channel_id=1, source_target_pairs={{0,8},{1,2},{2,1},{3,4},{4,3},{5,6},{6,5},{7,15},{8,0},{9,10},{10,... | collective-permute-start | bytes 786440 | tf_op jit(solution)/shard_map/ppermute | solution.py:423
  53.1 7.5 %collective-permute-start.24 = (f32[8,64,128]{2,1,0:T(8,128)S(1)}, f32[8,64,128]{2,1,0:T(8,128)S(1)}, u32[]{:S(2)}, u32[]{:S(2)}) collective-permute-start(f32[8,64,128]{2,1,0:T(8,128)S(1)} %get-tuple-element.76.own), channel_id=1, source_target_pairs={{0,1},{1,0},{2,3},{3,2},{4,5},{5,4},{6,7},{7,6},{8,9},{9,8},{10,11... | collective-permute-start | bytes 786440 | tf_op jit(solution)/shard_map/ppermute | solution.py:420
  53.3 7.4 %collective-permute-start.25 = (f32[8,64,128]{2,1,0:T(8,128)S(1)}, f32[8,64,128]{2,1,0:T(8,128)S(1)}, u32[]{:S(2)}, u32[]{:S(2)}) collective-permute-start(f32[8,64,128]{2,1,0:T(8,128)S(1)} %get-tuple-element.76.own), channel_id=1, source_target_pairs={{0,8},{1,2},{2,1},{3,4},{4,3},{5,6},{6,5},{7,15},{8,0},{9,10},{10,... | collective-permute-start | bytes 786440 | tf_op jit(solution)/shard_map/ppermute | solution.py:423
  57.1 6.4 %collective-permute-start.28 = (f32[8,32,128]{2,1,0:T(8,128)S(1)}, f32[8,32,128]{2,1,0:T(8,128)S(1)}, u32[]{:S(2)}, u32[]{:S(2)}) collective-permute-start(f32[8,32,128]{2,1,0:T(8,128)S(1)} %get-tuple-element.83), channel_id=1, source_target_pairs={{0,8},{8,0},{16,24},{24,16},{1,9},{9,1},{17,25},{25,17},{2,10},{10... | collective-permute-start | bytes 393224 | tf_op jit(solution)/shard_map/ppermute | solution.py:432
  58.1 8.0 %collective-permute-start.29 = (f32[8,32,128]{2,1,0:T(8,128)S(1)}, f32[8,32,128]{2,1,0:T(8,128)S(1)}, u32[]{:S(2)}, u32[]{:S(2)}) collective-permute-start(f32[8,32,128]{2,1,0:T(8,128)S(1)} %get-tuple-element.84), channel_id=1, source_target_pairs={{0,16},{8,24},{16,0},{24,8},{1,17},{9,25},{17,1},{25,9},{2,18},{10... | collective-permute-start | bytes 393224 | tf_op jit(solution)/shard_map/ppermute | solution.py:432
  59.7 6.5 %collective-permute-start.30 = (f32[8,32,128]{2,1,0:T(8,128)S(1)}, f32[8,32,128]{2,1,0:T(8,128)S(1)}, u32[]{:S(2)}, u32[]{:S(2)}) collective-permute-start(f32[8,32,128]{2,1,0:T(8,128)S(1)} %get-tuple-element.85), channel_id=1, source_target_pairs={{0,24},{8,16},{16,8},{24,0},{1,25},{9,17},{17,9},{25,1},{2,26},{10... | collective-permute-start | bytes 393224 | tf_op jit(solution)/shard_map/ppermute | solution.py:432

commit v5 on v4

v5 whole, which is shorter than its diff:
```python
import functools

import jax
import jax.numpy as jnp
from jax import lax
from jax.experimental import pallas as pl
from jax.experimental.pallas import tpu as pltpu
from jax.sharding import PartitionSpec as P

STEPS = 4
COEF = (0.8, -0.2, 4.0 / 105.0, -1.0 / 280.0)
WHOLE = (672.0, -168.0, 32.0, -3.0)
UNIT = 1.0 / 840.0

VMEM = pl.BlockSpec(memory_space=pltpu.VMEM)
SMEM = pl.BlockSpec(memory_space=pltpu.SMEM)
HBM = pl.BlockSpec(memory_space=pltpu.HBM)


def f32(*shape):
    return jax.ShapeDtypeStruct(shape, jnp.float32)


def call(name, body, outs, ins, scratch=(), flops=1 << 20, moved=1 << 20):
    pairs = [a if isinstance(a, tuple) else (a, VMEM) for a in ins]
    return pl.pallas_call(
        body,
        name=name,
        out_shape=outs,
        in_specs=[s for _, s in pairs],
        out_specs=jax.tree.map(lambda _: VMEM, outs),
        scratch_shapes=list(scratch),
        cost_estimate=pl.CostEstimate(flops=flops, bytes_accessed=moved, transcendentals=0),
        compiler_params=pltpu.CompilerParams(vmem_limit_bytes=16 << 20),
    )(*[a for a, _ in pairs])


def stencil(pick):
    summed = None
    for k in range(1, 5):
        term = COEF[k - 1] * (pick(k) - pick(-k))
        summed = term if summed is None else summed + term
    return summed


def halves(tile):
    high = tile.astype(jnp.bfloat16)
    return high, (tile - high.astype(jnp.float32)).astype(jnp.bfloat16)


def diff_z(tile, matrix):
    return jnp.dot(
        jnp.concatenate(halves(tile), axis=1), matrix[...], preferred_element_type=jnp.float32
    )


def diff_y(tile, matrix):
    return jnp.dot(
        matrix[...], jnp.concatenate(halves(tile), axis=0), preferred_element_type=jnp.float32
    )


def diff_matrix(size, along, shape):
    row = lax.broadcasted_iota(jnp.int32, shape, 0) % size
    column = lax.broadcasted_iota(jnp.int32, shape, 1) % size
    offset = row - column if along == 0 else column - row
    entries = jnp.zeros(shape, jnp.float32)
    for k in range(1, 5):
        entries = jnp.where(offset == k, WHOLE[k - 1], entries)
        entries = jnp.where(offset == -k, -WHOLE[k - 1], entries)
    return entries.astype(jnp.bfloat16)


def place_halos(wide, own, partner, across):
    rows, halo = own.shape[0], sum(ref.shape[0] for ref in partner)
    blk, blocks = lax.axis_index("blk"), lax.axis_size("blk")
    odd = blk % 2
    outside = (blk == 0) | (blk == blocks - 1)
    above = halo + rows
    wide[halo:above] = own[...]
    partner_at = jnp.where(odd == 1, 0, above)
    across_at = jnp.where(odd == 1, above, 0)
    for ref_p, ref_a in zip(partner, across):
        part = ref_p.shape[0]
        wide[pl.ds(partner_at, part)] = ref_p[...]
        wide[pl.ds(across_at, part)] = jnp.where(outside, 0.0, ref_a[...])
        partner_at, across_at = partner_at + part, across_at + part


def slopes_yz(wide, first, out_y, out_z, matrix_y, matrix_z):
    for i in range(out_z.shape[0]):
        out_z[i] = diff_z(wide[first + i] * UNIT, matrix_z)
    for i in range(out_y.shape[0]):
        out_y[i] = diff_y(wide[first + i] * UNIT, matrix_y)


def apply_operator(halos, coef, matrix_y, matrix_z, scratch, finish):
    wide, flux_x, all_y, all_z, part = scratch
    rows = part.shape[0]
    own, partner, across = halos
    place_halos(wide, own, (partner,), (across,))
    slopes_yz(wide, 4, all_y, all_z, matrix_y, matrix_z)
    for i in range(rows + 8):
        slope_x = stencil(lambda k: wide[i + 4 + k])
        slope_y, slope_z = all_y[i], all_z[i]
        along = coef[0, i] * slope_x + coef[1, i] * slope_y + coef[2, i] * slope_z
        flux_x[i] = coef[3, i] * slope_x - coef[0, i] * along
        if 4 <= i < rows + 4:
            part[i - 4] = UNIT * (
                diff_z(coef[3, i] * slope_z - coef[2, i] * along, matrix_z)
                + diff_y(coef[3, i] * slope_y - coef[1, i] * along, matrix_y)
            )
    for r in range(rows):
        finish(r, stencil(lambda k: flux_x[r + 4 + k]) + part[r])


def sin_cos(angle):
    square = angle * angle
    sine, cosine = 0.0, 1.0 / 479001600.0
    for factor in (-39916800.0, 362880.0, -5040.0, 120.0, -6.0, 1.0):
        sine = sine * square + 1.0 / factor
    for factor in (-3628800.0, 40320.0, -720.0, 24.0, -2.0, 1.0):
        cosine = cosine * square + 1.0 / factor
    return angle * sine, cosine


def owner_kernel(eps, tilt, azimuth, speed, state, wx, wy, wz, out, current, held, sems):
    rows = wx.shape[0]
    copies = [
        pltpu.make_async_copy(ref, to, sems.at[n])
        for n, (ref, to) in enumerate(
            (
                (eps, held.at[0]),
                (tilt, held.at[1]),
                (azimuth, held.at[2]),
                (speed, out),
                (state.at[0], current),
            )
        )
    ]
    for copy in copies:
        copy.start()
    for copy in copies[:3]:
        copy.wait()
    for r in range(rows):
        size = jnp.sqrt(2.0 * held[0, r])
        sin_tilt, cos_tilt = sin_cos(held[1, r])
        sin_half, cos_half = sin_cos(0.5 * held[2, r])
        flat = size * sin_tilt
        wx[r] = flat * (1.0 - 2.0 * sin_half * sin_half)
        wy[r] = flat * (2.0 * sin_half * cos_half)
        wz[r] = size * cos_tilt
    for copy in copies[3:]:
        copy.wait()


def first_kernel(anchor, wz, first, wz_first):
    rows, count, depth = wz.shape
    number = (anchor[...].reshape(1, 1) // count).astype(jnp.float32)
    number = jnp.broadcast_to(number, (count, depth))
    first[...] = number[0:8]
    wz_first[0:rows] = wz[...]
    wz_first[rows] = number


def prepare_kernel(shots, parts, first, own, partner, across, *refs):
    slope, flags, matrix_y, matrix_z, wide = refs[-5:]
    rows, width, depth = own.shape
    matrix_y[...] = diff_matrix(width, 1, matrix_y.shape)
    matrix_z[...] = diff_matrix(depth, 0, matrix_z.shape)
    me = lax.axis_index("shot")
    for k in range(shots):
        part = jnp.bitwise_xor(me, k).astype(jnp.float32) - first[0:1, :]
        for j in range(parts):
            flags[k * parts + j : k * parts + j + 1, :] = jnp.where(
                jnp.abs(part - j) < 0.5, 1.0, 0.0
            )
    place_halos(wide, own, (partner,), (across,))
    slopes_yz(wide, 4, slope.at[1], slope.at[2], matrix_y, matrix_z)
    for i in range(rows + 8):
        slope[0, i] = stencil(lambda k: wide[i + 4 + k])


def inject_kernel(step, sx, sy, sz, wavelet, rx, ry, rz, traces, src, inj):
    rows, width, depth = src.shape[1:]
    start, sx, sy, sz = (ref[...].reshape(1, 1) for ref in (step, sx, sy, sz))
    first = lax.axis_index("blk") * rows
    shape = (rows, width, depth)
    plane = (width, depth)
    here = (lax.broadcasted_iota(jnp.int32, plane, 0) == sy) & (
        lax.broadcasted_iota(jnp.int32, plane, 1) == sz
    )
    moment = lax.broadcasted_iota(jnp.int32, wavelet.shape, 1)
    for t in range(STEPS - 1):
        chosen = jnp.where(moment == start + t, wavelet[...], 0.0)
        value = jnp.sum(chosen, axis=1, keepdims=True)
        for r in range(rows):
            src[t, r] = jnp.where(here & (sx == first + r), value, 0.0)
    receivers = rx.shape[1]
    local = rx[...] - first
    cell = jnp.where((local >= 0) & (local < rows), local * width + ry[...], -1)
    pick = (
        lax.broadcasted_iota(jnp.int32, (rows * width, receivers), 0) == cell
    ).astype(jnp.float32)
    match = lax.broadcasted_iota(jnp.int32, (depth, receivers), 0) == rz[...]
    moment = lax.broadcasted_iota(jnp.int32, traces.shape[1:], 0)
    for t in range(STEPS):
        chosen = jnp.where(moment == start + t, traces[0], 0.0)
        samples = jnp.sum(chosen, axis=0, keepdims=True)
        spread = jnp.where(match, samples, 0.0)
        added = lax.dot_general(
            pick,
            spread,
            (((1,), (1,)), ((), ())),
            precision=lax.Precision.HIGHEST,
            preferred_element_type=jnp.float32,
        )
        inj[t] = added.reshape(shape)


def relay_kernel(parts, wz_first, own, received, *refs):
    out = refs[-1]
    first = wz_first[wz_first.shape[0] - 1, 0:1, :]
    part = lax.axis_index("shot").astype(jnp.float32) - first
    inside = (part > -0.5) & (part < parts - 0.5)
    out[...] = jnp.where(inside, own[...], received[...])


def pair_kernel(own, received, out):
    out[0] = own[...]
    out[1] = received[0 : own.shape[0]]


def window_part(pieces, flags, parts, j):
    chosen = pieces[-1][...]
    for k in reversed(range(len(pieces) - 1)):
        at = k * parts + j
        chosen = jnp.where(flags[at : at + 1, :] > 0.5, pieces[k][...], chosen)
    return chosen


def piece_refs(refs, places):
    return [refs[i] if at is None else refs[i].at[at] for i, at in places]


def flux_kernel(places, parts, flags, slope, matrix_y, matrix_z, *refs):
    tensor, flux, rest, edge_a0, edge_a1, edge_p0, edge_p1 = refs[-7:]
    rows, width, _ = flux.shape
    count = width // parts
    for a in range(3):
        pieces = piece_refs(refs, places[a])
        for j in range(parts):
            tensor[a, :, j * count : (j + 1) * count, :] = window_part(pieces, flags, parts, j)
    odd = lax.axis_index("blk") % 2
    low = rows - 4
    for n, (out_a, out_p) in enumerate(((edge_a0, edge_p0), (edge_a1, edge_p1))):
        out_a[...] = tensor[:, pl.ds(odd * low + 2 * n, 2)]
        out_p[...] = tensor[:, pl.ds((1 - odd) * low + 2 * n, 2)]
    for r in range(rows):
        wx, wy, wz = tensor[0, r], tensor[1, r], tensor[2, r]
        along = wx * slope[0, r + 4] + wy * slope[1, r + 4] + wz * slope[2, r + 4]
        size = 1.0 + (wx * wx + wy * wy + wz * wz)
        flux[r] = size * slope[0, r + 4] - wx * along
        rest[r] = UNIT * (
            diff_z(size * slope[2, r + 4] - wz * along, matrix_z)
            + diff_y(size * slope[1, r + 4] - wy * along, matrix_y)
        )


def speed_kernel(places, parts, flags, present, *refs):
    speed, operand = refs[-2:]
    pieces = piece_refs(refs, places)
    count = speed.shape[1] // parts
    for j in range(parts):
        speed[:, j * count : (j + 1) * count, :] = window_part(pieces, flags, parts, j)
    operand[...] = speed[...] * present[...]


def forward_first(tensor, edge_p0, edge_p1, edge_a0, edge_a1, slope, flux, rest, own, previous, speed, src,
                  image, following, coef, flux_x):
    rows = rest.shape[0]
    blk, blocks = lax.axis_index("blk"), lax.axis_size("blk")
    for a in range(3):
        place_halos(coef.at[a], tensor.at[a], (edge_p0.at[a], edge_p1.at[a]),
                    (edge_a0.at[a], edge_a1.at[a]))
    for i in range(rows + 8):
        wx, wy, wz = coef[0, i], coef[1, i], coef[2, i]
        size = 1.0 + (wx * wx + wy * wy + wz * wz)
        if i < 4:
            size = jnp.where(blk == 0, 0.0, size)
        if i >= rows + 4:
            size = jnp.where(blk == blocks - 1, 0.0, size)
        coef[3, i] = size
        if 4 <= i < rows + 4:
            flux_x[i] = flux[i - 4]
        else:
            along = wx * slope[0, i] + wy * slope[1, i] + wz * slope[2, i]
            flux_x[i] = size * slope[0, i] - wx * along
    for r in range(rows):
        value = stencil(lambda k: flux_x[r + 4 + k]) + rest[r]
        image[r] = value
        following[r] = 2.0 * own[r] - previous[r] + speed[r] * value + src[0, r]


def forward(t, own, across, partner, coef, matrix_y, matrix_z, previous, speed, src,
            image, following, *scratch):
    def finish(r, value):
        image[r] = value
        following[r] = 2.0 * own[r] - previous[r] + speed[r] * value + src[t, r]

    apply_operator((own, partner, across), coef, matrix_y, matrix_z, scratch, finish)


def backward(t, own, across, partner, coef, matrix_y, matrix_z, present, later, inj, *refs):
    refs, scratch = refs[:-5], refs[-5:]
    if t == 0:
        earlier, copied, done = refs
        copied[...] = present[...]
        done[...] = jnp.zeros(done.shape, jnp.float32)
    elif t == 1:
        speed, lambda3, image0, image1, image2, earlier, operand, known = refs
    else:
        speed, earlier, operand = refs

    def finish(r, value):
        result = 2.0 * present[r] - later[r] + value + inj[t, r]
        earlier[r] = result
        if t > 0:
            operand[r] = speed[r] * result
        if t == 1:
            known[r] = lambda3[r] * image2[r] + present[r] * image1[r] + result * image0[r]

    apply_operator((own, partner, across), coef, matrix_y, matrix_z, scratch, finish)


def forward_last(parts, own, across, partner, coef, matrix_y, matrix_z, known, lambda4, flags,
                 *refs):
    chunks, scratch, grad = refs[:-6], refs[-6:-1], refs[-1]
    count = chunks[0].shape[1]

    def finish(r, value):
        grad[r] = known[r] + lambda4[r] * value

    apply_operator((own, partner, across), coef, matrix_y, matrix_z, scratch, finish)
    for k, chunk in enumerate(chunks):
        held = jnp.zeros(chunk.shape, jnp.float32)
        for j in range(parts):
            at = k * parts + j
            held = jnp.where(
                flags[at : at + 1, :] > 0.5, grad[:, j * count : (j + 1) * count, :], held
            )
        chunk[...] = held


def total_kernel(*refs):
    out = refs[-1]
    total = refs[0][...]
    for ref in refs[1:-2]:
        total = total + ref[...]
    out[...] = total


def on_device(
    state_before,
    state_now,
    adjoint_later,
    adjoint_now,
    courant_sq,
    epsilon,
    tilt_angle,
    azimuth,
    aperture_anchor,
    step_index,
    wavelet,
    residual_traces,
    source_x,
    source_y,
    source_z,
    receiver_x,
    receiver_y,
    receiver_z,
):
    rows, width, depth = state_now.shape[1:]
    count = courant_sq.shape[1]
    parts = width // count
    shots = lax.axis_size("shot")
    blocks = lax.axis_size("blk")
    field, piece = f32(rows, width, depth), f32(rows, count, depth)
    extended = pltpu.VMEM((rows + 8, width, depth), jnp.float32)
    wide = pltpu.VMEM((3 * rows, width, depth), jnp.float32)
    own_rows = pltpu.VMEM((rows, width, depth), jnp.float32)
    scratch = (wide, extended, extended, extended, own_rows)
    work = 100 * (rows + 8) * width * depth

    core_pairs = [(i, i ^ 1) for i in range(blocks)]
    def chip_pairs(hop):
        pairs = []
        for s in range(shots):
            for b in range(blocks):
                end = b in (0, blocks - 1)
                other = (s ^ hop, b) if end else (s, b - 1 + 2 * (b % 2))
                pairs.append((s * blocks + b, other[0] * blocks + other[1]))
        return pairs

    def to_partner(array, name):
        with jax.named_scope(f"{name}_to_core"):
            return lax.ppermute(array, "blk", core_pairs)

    def across_chips(array, name, hop=2):
        with jax.named_scope(f"{name}_to_chip"):
            return lax.ppermute(array, ("shot", "blk"), chip_pairs(hop))

    def halos(array, name):
        return to_partner(array, name), across_chips(array, name)

    def in_hbm(array):
        return pltpu.with_memory_space_constraint(array, pltpu.HBM), HBM

    def to_owners(array, k, name):
        with jax.named_scope(f"{name}_to_{k}"):
            return lax.ppermute(array, "shot", [(i, i ^ k) for i in range(shots)])

    previous = state_before[0]
    present, later = adjoint_now[0], adjoint_later[0]

    wx, wy, wz, speed, current = call(
        "owner",
        owner_kernel,
        (piece,) * 4 + (field,),
        [in_hbm(a) for a in (epsilon, tilt_angle, azimuth, courant_sq, state_now)],
        (
            pltpu.VMEM((3, rows, count, depth), jnp.float32),
            pltpu.SemaphoreType.DMA((5,)),
        ),
    )
    first, wz_first = call(
        "first",
        first_kernel,
        (f32(8, depth), f32(rows + 1, count, depth)),
        [aperture_anchor, wz],
    )

    if shots == 4 and parts == 2:
        relay = functools.partial(relay_kernel, parts)
        wx_y = to_owners(wx, 2, "wx")
        wz_x = to_owners(wz_first, 1, "wz")
        wy_y = to_owners(wy, 2, "wy")
        wx_sent = call("relay_wx", relay, piece, [wz_x, wx, wx_y])
        wx_x = to_owners(wx_sent, 1, "wx")
        both = f32(2, rows, count, depth)
        wz_y = to_owners(call("pair_wz", pair_kernel, both, [wz, wz_x]), 2, "wz")
        wy_sent = call("relay_wy", relay, piece, [wz_x, wy, wy_y, wx_sent])
        wy_x = to_owners(wy_sent, 1, "wy")
        speed_x = to_owners(speed, 1, "speed")
        speed_y = to_owners(call("pair_speed", pair_kernel, both, [speed, speed_x]), 2, "speed")
        before = [wx_x, speed_x]
        pieces = [wx, wx_x, wx_y, wy, wy_x, wy_y, wz, wz_x, wz_y]
        places = [
            [(0, None), (1, None), (2, None), (1, None)],
            [(3, None), (4, None), (5, None), (4, None)],
            [(6, None), (7, slice(0, rows)), (8, 0), (8, 1)],
        ]
        speed_pieces = [speed, speed_x, speed_y]
        speed_places = [(0, None), (1, None), (2, 0), (2, 1)]
    else:
        pieces, places, before = [], [], []
        for array in (wx, wy, wz):
            places.append([(len(pieces) + k, None) for k in range(shots)])
            pieces = pieces + [array] + [to_owners(array, k, "w") for k in range(1, shots)]
        speed_places = places[0]
        speed_pieces = [speed] + [to_owners(speed, k, "speed") for k in range(1, shots)]

    src, inj = call(
        "inject",
        inject_kernel,
        (f32(STEPS - 1, rows, width, depth), f32(STEPS, rows, width, depth)),
        [step_index, source_x, source_y, source_z, wavelet, receiver_x, receiver_y, receiver_z]
        + [residual_traces],
    )
    now_p, now_a = to_partner(current, "state"), across_chips(current, "state", 1)
    slope, flags, matrix_y, matrix_z = call(
        "prepare",
        functools.partial(prepare_kernel, shots, parts),
        (
            f32(3, rows + 8, width, depth),
            f32(shots * parts, depth),
            jax.ShapeDtypeStruct((width, 2 * width), jnp.bfloat16),
            jax.ShapeDtypeStruct((2 * depth, depth), jnp.bfloat16),
        ),
        [first, current, now_p, now_a, src] + before,
        [wide],
    )
    edge = f32(3, 2, width, depth)
    tensor, flux, rest, *edges = call(
        "flux",
        functools.partial(flux_kernel, places, parts),
        (f32(3, rows, width, depth), field, field) + (edge,) * 4,
        [flags, slope, matrix_y, matrix_z] + pieces,
        flops=work // 3,
    )
    edges_a = [across_chips(a, "edge") for a in edges[:2]]
    edges_p = [to_partner(a, "edge") for a in edges[2:]]
    speed, operand = call(
        "speed",
        functools.partial(speed_kernel, speed_places, parts),
        (field, field),
        [flags, present] + speed_pieces,
    )
    op_p, op_a = halos(operand, "adjoint")

    image, following, coef = call(
        "forward0",
        forward_first,
        (field, field, f32(4, rows + 8, width, depth)),
        [tensor, *edges_p, *edges_a, slope, flux, rest]
        + [current, previous, speed, src],
        [extended],
        work // 4,
    )
    images = [image]
    previous, current = current, following
    adjoints = [present]
    known = None
    for t in range(STEPS - 1):
        now_p, now_a = halos(current, "state")
        back = STEPS - 1 - t
        ins = [operand, op_a, op_p, coef, matrix_y, matrix_z, present, later, inj, speed]
        outs = (field, field)
        if back == 1:
            ins = ins + [adjoints[1]] + images
            outs = (field, field, field)
        result = call(
            f"backward{t}", functools.partial(backward, back), outs, ins, scratch, work
        )
        later, present, operand = present, result[0], result[1]
        if back == 1:
            known = result[2]
        adjoints.append(present)
        op_p, op_a = halos(operand, "adjoint")
        if t < STEPS - 2:
            image, following = call(
                f"forward{t + 1}",
                functools.partial(forward, t + 1),
                (field, field),
                [current, now_a, now_p, coef, matrix_y, matrix_z, previous, speed, src],
                scratch,
                work,
            )
            images.append(image)
            previous, current = current, following

    chunks = call(
        "forward3",
        functools.partial(forward_last, parts),
        (piece,) * shots,
        [current, now_a, now_p, coef, matrix_y, matrix_z, known, adjoints[0], flags],
        scratch + (own_rows,),
        work,
    )
    received = [to_owners(chunks[k], k, "grad") for k in range(1, shots)]
    final, copied, done = call(
        "backward3",
        functools.partial(backward, 0),
        (field, field, f32(8, depth)),
        [operand, op_a, op_p, coef, matrix_y, matrix_z, present, later, inj],
        scratch,
        work,
    )
    model_grad = call("total", total_kernel, piece, [chunks[0]] + received + [done])
    return (copied[None], final[None], model_grad)


def solution(mesh):
    in_specs = (
        P("shot", "blk", None, None),
        P("shot", "blk", None, None),
        P("shot", "blk", None, None),
        P("shot", "blk", None, None),
        P("blk", "shot", None),
        P("blk", "shot", None),
        P("blk", "shot", None),
        P("blk", "shot", None),
        P("shot"),
        P(),
        P("shot", None),
        P("shot", None, None),
        P("shot"),
        P("shot"),
        P("shot"),
        P("shot", None),
        P("shot", None),
        P("shot", None),
    )
    out_specs = (P("shot", "blk", None, None), P("shot", "blk", None, None), P("blk", "shot", None))
    return jax.shard_map(
        on_device, mesh=mesh, in_specs=in_specs, out_specs=out_specs, check_vma=False
    )
```

time: 67.1 us -> 64.4 us (0.960)
  starting transfers between devices: 29.2 us -> 20 us
  waiting for transfers between devices: 17.6 us -> 26.8 us
  Pallas kernels: 15.4 us -> 13.1 us
    ppermute x10, waiting for transfers between devices: 7.48 us -> 20.6 us  [across_chips(): return lax.ppermute(array, ('shot', 'blk'), chip_pairs(hop))]
    ppermute x10, starting transfers between devices: 10.4 us -> 3.22 us  [across_chips(): return lax.ppermute(array, ('shot', 'blk'), chip_pairs(hop))]
    ppermute x11, waiting for transfers between devices: 10.1 us -> 6.2 us  [to_owners(): return lax.ppermute(array, 'shot', [(i, i ^ k) for i in range(shots)])]
    pallas_call x19, Pallas kernels: 15.4 us -> 13.1 us  [call(): pl.pallas_call(body, name=name, out_shape=outs, in_specs=[s for _, s in p...]
    ppermute x10, starting transfers between devices: 3.09 us -> 1.12 us  [to_partner(): return lax.ppermute(array, 'blk', core_pairs)]
  transfers between devices with their start and end apart: 31 -> 31, of which waited for: 12 -> 13; matrix products, arithmetic and copies ran while one was open for 1% -> 0% of each run, Pallas kernels for 20% -> 17%
where the time goes in v5:
time: 64.4 us; the launch traced here: 64.2 us
  waiting for transfers between devices  26.8 us (42%)
  starting transfers between devices  20 us (31%)
  Pallas kernels  13.1 us (20%)
  between operations  4.22 us (7%)
    ppermute x10, waiting for transfers between devices, across_chips(): return lax.ppermute(array, ('shot', 'blk'), chip_pairs(hop))  20.6 us
    ppermute x11, starting transfers between devices, to_owners(): return lax.ppermute(array, 'shot', [(i, i ^ k) for i in range(shots)])  15.6 us
    pallas_call x19, Pallas kernels, call(): pl.pallas_call(body, name=name, out_shape=outs, in_specs=[s for _, s in p...  13.1 us
    ppermute x11, waiting for transfers between devices, to_owners(): return lax.ppermute(array, 'shot', [(i, i ^ k) for i in range(shots)])  6.2 us
    ppermute x10, starting transfers between devices, across_chips(): return lax.ppermute(array, ('shot', 'blk'), chip_pairs(hop))  3.22 us
  transfers between devices with their start and end apart: 31, of which 13 were waited for; matrix products, arithmetic and copies ran while one was open for 0% of the time, Pallas kernels for 17%

profile of v5, /device:TPU:0, one launch (start us, length us, event | category | flops | bytes accessed | tf_op | source)
XLA Modules:
  0.0 64.2 jit_solution(14440361582585126309)
XLA Ops:
  1.4 1.4 %owner.1 = (f32[8,32,128]{2,1,0:T(8,128)S(1)}, f32[8,32,128]{2,1,0:T(8,128)S(1)}, f32[8,32,128]{2,1,0:T(8,128)S(1)}, f32[8,32,128]{2,1,0:T(8,128)S(1)}, f32[8,64,128]{2,1,0:T(8,128)S(1)}) custom-call(f32[8,32,128]{2,1,0:T(8,128)} %eps.1, f32[8,32,128]{2,1,0:T(8,128)} %tilt.1, f32[8,32,128]{2,1,0:T(8,128)} %azimuth.1, f32[8,32,128]{2,1,0:T(8,128)} %speed.2, ...), custom_call_target="tpu_custom_call" | custom-call | flops 1048576 | bytes 1048576 | tf_op jit(solution)/shard_map/owner/pallas_call | solution.py:26
  2.8 0.1 first.1
  2.8 2.9 %collective-permute-start.2 = (f32[9,32,128]{2,1,0:T(8,128)S(1)}, f32[9,32,128]{2,1,0:T(8,128)S(1)}, u32[]{:S(2)}, u32[]{:S(2)}) collective-permute-start(f32[9,32,128]{2,1,0:T(8,128)S(1)} %get-tuple-element.50), channel_id=1, source_target_pairs={{0,8},{8,0},{16,24},{24,16},{1,9},{9,1},{17,25},{25,17},{2,10},{10... | collective-permute-start | bytes 442376 | tf_op jit(solution)/shard_map/wz_to_1/ppermute | solution.py:421
  5.8 1.5 %collective-permute-start.3 = (f32[8,32,128]{2,1,0:T(8,128)S(1)}, f32[8,32,128]{2,1,0:T(8,128)S(1)}, u32[]{:S(2)}, u32[]{:S(2)}) collective-permute-start(f32[8,32,128]{2,1,0:T(8,128)S(1)} %get-tuple-element.51.own.refs_0_), channel_id=1, source_target_pairs={{0,16},{8,24},{16,0},{24,8},{1,17},{9,25},{17,1},{25,9},{2,18},{10... | collective-permute-start | bytes 393224 | tf_op jit(solution)/shard_map/wx_to_2/ppermute | solution.py:421
  7.3 0.5 collective-permute-start.1
  7.8 0.1 collective-permute-start.9
  7.9 1.7 %collective-permute-done.2.wz_first.received.refs_7_ = f32[9,32,128]{2,1,0:T(8,128)S(1)} collective-permute-done((f32[9,32,128]{2,1,0:T(8,128)S(1)}, f32[9,32,128]{2,1,0:T(8,128)S(1)}, u32[]{:S(2)}, u32[]{:S(2)}) %collective-permute-start.2) | collective-permute-done | bytes 147488 | tf_op jit(solution)/shard_map/wz_to_1/ppermute | solution.py:421
  9.6 1.7 %collective-permute-start.5 = (f32[8,32,128]{2,1,0:T(8,128)S(1)}, f32[8,32,128]{2,1,0:T(8,128)S(1)}, u32[]{:S(2)}, u32[]{:S(2)}) collective-permute-start(f32[8,32,128]{2,1,0:T(8,128)S(1)} %get-tuple-element.52.own.refs_0_), channel_id=1, source_target_pairs={{0,8},{8,0},{16,24},{24,16},{1,9},{9,1},{17,25},{25,17},{2,10},{10... | collective-permute-start | bytes 393224 | tf_op jit(solution)/shard_map/speed_to_1/ppermute | solution.py:421
  11.4 0.0 collective-permute-done.3.received.refs_2_
  11.4 1.6 %collective-permute-start.11 = (f32[2,8,32,128]{3,2,1,0:T(8,128)S(1)}, f32[2,8,32,128]{3,2,1,0:T(8,128)S(1)}, u32[]{:S(2)}, u32[]{:S(2)}) collective-permute-start(f32[2,8,32,128]{3,2,1,0:T(8,128)S(1)} %pair_wz.1), channel_id=1, source_target_pairs={{0,16},{8,24},{16,0},{24,8},{1,17},{9,25},{17,1},{25,9},{2,18},{10... | collective-permute-start | bytes 786440 | tf_op jit(solution)/shard_map/wz_to_2/ppermute | solution.py:421
  13.0 1.0 %collective-permute-done.9.received.refs_5_ = f32[8,32,128]{2,1,0:T(8,128)S(1)} collective-permute-done((f32[8,32,128]{2,1,0:T(8,128)S(1)}, f32[8,32,128]{2,1,0:T(8,128)S(1)}, u32[]{:S(2)}, u32[]{:S(2)}) %collective-permute-start.9) | collective-permute-done | bytes 131104 | tf_op jit(solution)/shard_map/wy_to_2/ppermute | solution.py:421
  14.0 1.6 %collective-permute-start.4 = (f32[8,32,128]{2,1,0:T(8,128)S(1)}, f32[8,32,128]{2,1,0:T(8,128)S(1)}, u32[]{:S(2)}, u32[]{:S(2)}) collective-permute-start(f32[8,32,128]{2,1,0:T(8,128)S(1)} %relay_wx.1.refs_0_), channel_id=1, source_target_pairs={{0,8},{8,0},{16,24},{24,16},{1,9},{9,1},{17,25},{25,17},{2,10},{10... | collective-permute-start | bytes 393224 | tf_op jit(solution)/shard_map/wx_to_1/ppermute | solution.py:421
  15.7 0.8 %collective-permute-done.5.refs_2_.received.refs_1_ = f32[8,32,128]{2,1,0:T(8,128)S(1)} collective-permute-done((f32[8,32,128]{2,1,0:T(8,128)S(1)}, f32[8,32,128]{2,1,0:T(8,128)S(1)}, u32[]{:S(2)}, u32[]{:S(2)}) %collective-permute-start.5) | collective-permute-done | bytes 131104 | tf_op jit(solution)/shard_map/speed_to_1/ppermute | solution.py:421
  16.5 0.5 collective-permute-start.10
  17.0 0.0 collective-permute-done.partner
  17.1 2.1 %collective-permute-start.6 = (f32[2,8,32,128]{3,2,1,0:T(8,128)S(1)}, f32[2,8,32,128]{3,2,1,0:T(8,128)S(1)}, u32[]{:S(2)}, u32[]{:S(2)}) collective-permute-start(f32[2,8,32,128]{3,2,1,0:T(8,128)S(1)} %pair_speed.1), channel_id=1, source_target_pairs={{0,16},{8,24},{16,0},{24,8},{1,17},{9,25},{17,1},{25,9},{2,18},{10... | collective-permute-start | bytes 786440 | tf_op jit(solution)/shard_map/speed_to_2/ppermute | solution.py:421
  21.8 1.1 %inject.1 = (f32[3,8,64,128]{3,2,1,0:T(8,128)S(1)}, f32[4,8,64,128]{3,2,1,0:T(8,128)S(1)}) custom-call(s32[1]{0:T(128)S(6)} %copy.22.step, s32[1]{0:T(128)S(6)} %copy.23.sx, s32[1]{0:T(128)S(6)} %copy.24.sy, s32[1]{0:T(128)S(6)} %copy.25.sz, f32[1,16]{1,0:T(1,128)S(1)} %copy-done.4, s32[1,128]{1,0:T(1,128)S(1)} %copy-done.5, s32[1,128]{1,0:T(1,128)S(1)} %copy-done.6, ...), custom_call_target="tpu_custom_call" | custom-call | flops 1048576 | bytes 1048576 | tf_op jit(solution)/shard_map/inject/pallas_call | solution.py:26
  22.9 0.0 copy-start
  22.9 0.8 %prepare.1 = (f32[3,16,64,128]{3,2,1,0:T(8,128)S(1)}, f32[8,128]{1,0:T(8,128)S(1)}, bf16[64,128]{1,0:T(8,128)(2,1)S(1)}, bf16[256,128]{1,0:T(8,128)(2,1)S(1)}) custom-call(f32[8,128]{1,0:T(8,128)S(1)} %get-tuple-element.47.first, f32[8,64,128]{2,1,0:T(8,128)S(1)} %get-tuple-element.48.own.previous, f32[8,64,128]{2,1,0:T(8,128)S(1)} %collective-permute-done.partner, ...), custom_call_target="tpu_custom_call" | custom-call | flops 1048576 | bytes 1048576 | tf_op jit(solution)/shard_map/prepare/pallas_call | solution.py:26
  23.7 0.0 copy-start.1
  23.8 0.0 collective-permute-done.10.refs_4_
  23.8 0.6 flux.1
  24.3 0.1 collective-permute-start.12
  24.4 0.5 collective-permute-start.13
  24.9 0.0 collective-permute-start.14
  24.9 2.0 %collective-permute-start.15 = (f32[3,2,64,128]{3,2,1,0:T(8,128)S(1)}, f32[3,2,64,128]{3,2,1,0:T(8,128)S(1)}, u32[]{:S(2)}, u32[]{:S(2)}) collective-permute-start(f32[3,2,64,128]{3,2,1,0:T(8,128)S(1)} %get-tuple-element.63), channel_id=1, source_target_pairs={{0,16},{1,2},{2,1},{3,4},{4,3},{5,6},{6,5},{7,23},{8,24},{9,10},{1... | collective-permute-start | bytes 589832 | tf_op jit(solution)/shard_map/edge_to_chip/ppermute | solution.py:411
  26.9 0.0 collective-permute-done.6.refs_2_
  26.9 0.1 speed.3
  27.0 0.1 collective-permute-start.7
  27.2 0.2 collective-permute-start.8
  27.4 3.2 %collective-permute-done.14.edge_a0 = f32[3,2,64,128]{3,2,1,0:T(8,128)S(1)} collective-permute-done((f32[3,2,64,128]{3,2,1,0:T(8,128)S(1)}, f32[3,2,64,128]{3,2,1,0:T(8,128)S(1)}, u32[]{:S(2)}, u32[]{:S(2)}) %collective-permute-start.14) | collective-permute-done | bytes 196640 | tf_op jit(solution)/shard_map/edge_to_chip/ppermute | solution.py:411
  30.6 2.1 %collective-permute-done.15.edge_a1 = f32[3,2,64,128]{3,2,1,0:T(8,128)S(1)} collective-permute-done((f32[3,2,64,128]{3,2,1,0:T(8,128)S(1)}, f32[3,2,64,128]{3,2,1,0:T(8,128)S(1)}, u32[]{:S(2)}, u32[]{:S(2)}) %collective-permute-start.15) | collective-permute-done | bytes 196640 | tf_op jit(solution)/shard_map/edge_to_chip/ppermute | solution.py:411
  32.7 0.5 forward0.1
  33.2 0.1 collective-permute-start.20
  33.3 0.1 collective-permute-start.21
  33.4 2.1 %collective-permute-done.7.across = f32[8,64,128]{2,1,0:T(8,128)S(1)} collective-permute-done((f32[8,64,128]{2,1,0:T(8,128)S(1)}, f32[8,64,128]{2,1,0:T(8,128)S(1)}, u32[]{:S(2)}, u32[]{:S(2)}) %collective-permute-start.7) | collective-permute-done | bytes 262176 | tf_op jit(solution)/shard_map/adjoint_to_chip/ppermute | solution.py:411
  35.5 1.0 %backward0.1 = (f32[8,64,128]{2,1,0:T(8,128)S(1)}, f32[8,64,128]{2,1,0:T(8,128)S(1)}) custom-call(f32[8,64,128]{2,1,0:T(8,128)S(1)} %get-tuple-element.54.own, f32[8,64,128]{2,1,0:T(8,128)S(1)} %collective-permute-done.7.across, f32[8,64,128]{2,1,0:T(8,128)S(1)} %collective-permute-done.8.partner, f32[4,16,64,128]{3,2,1,0:T(8,128)S(1)} %get-tuple-element.67.coef, ...), custom_call_target="tpu_custom_call" | custom-call | flops 13107200 | bytes 1048576 | tf_op jit(solution)/shard_map/backward0/pallas_call | solution.py:26
  36.5 0.1 collective-permute-start.16
  36.6 0.1 collective-permute-start.17
  36.7 3.0 %collective-permute-done.20.across = f32[8,64,128]{2,1,0:T(8,128)S(1)} collective-permute-done((f32[8,64,128]{2,1,0:T(8,128)S(1)}, f32[8,64,128]{2,1,0:T(8,128)S(1)}, u32[]{:S(2)}, u32[]{:S(2)}) %collective-permute-start.20) | collective-permute-done | bytes 262176 | tf_op jit(solution)/shard_map/state_to_chip/ppermute | solution.py:411
  39.7 1.0 %forward1.1 = (f32[8,64,128]{2,1,0:T(8,128)S(1)}, f32[8,64,128]{2,1,0:T(8,128)S(1)}) custom-call(f32[8,64,128]{2,1,0:T(8,128)S(1)} %get-tuple-element.74.own.previous, f32[8,64,128]{2,1,0:T(8,128)S(1)} %collective-permute-done.20.across, f32[8,64,128]{2,1,0:T(8,128)S(1)} %collective-permute-done.21.partner, f32[4,16,64,128]{3,2,1,0:T(8,128)S(1)} %get-tuple-element.67.coef, ...), custom_call_target="tpu_custom_call" | custom-call | flops 13107200 | bytes 1048576 | tf_op jit(solution)/shard_map/forward1/pallas_call | solution.py:26
  40.7 0.1 collective-permute-start.22
  40.8 0.1 collective-permute-start.23
  40.8 2.1 %collective-permute-done.16.across = f32[8,64,128]{2,1,0:T(8,128)S(1)} collective-permute-done((f32[8,64,128]{2,1,0:T(8,128)S(1)}, f32[8,64,128]{2,1,0:T(8,128)S(1)}, u32[]{:S(2)}, u32[]{:S(2)}) %collective-permute-start.16) | collective-permute-done | bytes 262176 | tf_op jit(solution)/shard_map/adjoint_to_chip/ppermute | solution.py:411
  42.9 1.0 %backward1.1 = (f32[8,64,128]{2,1,0:T(8,128)S(1)}, f32[8,64,128]{2,1,0:T(8,128)S(1)}) custom-call(f32[8,64,128]{2,1,0:T(8,128)S(1)} %get-tuple-element.69.own, f32[8,64,128]{2,1,0:T(8,128)S(1)} %collective-permute-done.16.across, f32[8,64,128]{2,1,0:T(8,128)S(1)} %collective-permute-done.17.partner, f32[4,16,64,128]{3,2,1,0:T(8,128)S(1)} %get-tuple-element.67.coef, ...), custom_call_target="tpu_custom_call" | custom-call | flops 13107200 | bytes 1048576 | tf_op jit(solution)/shard_map/backward1/pallas_call | solution.py:26
  43.9 0.1 collective-permute-start.18
  44.0 0.1 collective-permute-start.19
  44.1 3.0 %collective-permute-done.22.across = f32[8,64,128]{2,1,0:T(8,128)S(1)} collective-permute-done((f32[8,64,128]{2,1,0:T(8,128)S(1)}, f32[8,64,128]{2,1,0:T(8,128)S(1)}, u32[]{:S(2)}, u32[]{:S(2)}) %collective-permute-start.22) | collective-permute-done | bytes 262176 | tf_op jit(solution)/shard_map/state_to_chip/ppermute | solution.py:411
  47.1 1.0 %forward2.1 = (f32[8,64,128]{2,1,0:T(8,128)S(1)}, f32[8,64,128]{2,1,0:T(8,128)S(1)}) custom-call(f32[8,64,128]{2,1,0:T(8,128)S(1)} %get-tuple-element.76.own, f32[8,64,128]{2,1,0:T(8,128)S(1)} %collective-permute-done.22.across, f32[8,64,128]{2,1,0:T(8,128)S(1)} %collective-permute-done.23.partner, f32[4,16,64,128]{3,2,1,0:T(8,128)S(1)} %get-tuple-element.67.coef, ...), custom_call_target="tpu_custom_call" | custom-call | flops 13107200 | bytes 1048576 | tf_op jit(solution)/shard_map/forward2/pallas_call | solution.py:26
  48.1 0.1 collective-permute-start.26
  48.2 0.1 collective-permute-start.27
  48.3 2.1 %collective-permute-done.18.across = f32[8,64,128]{2,1,0:T(8,128)S(1)} collective-permute-done((f32[8,64,128]{2,1,0:T(8,128)S(1)}, f32[8,64,128]{2,1,0:T(8,128)S(1)}, u32[]{:S(2)}, u32[]{:S(2)}) %collective-permute-start.18) | collective-permute-done | bytes 262176 | tf_op jit(solution)/shard_map/adjoint_to_chip/ppermute | solution.py:411
  50.4 1.1 %backward2.1 = (f32[8,64,128]{2,1,0:T(8,128)S(1)}, f32[8,64,128]{2,1,0:T(8,128)S(1)}, f32[8,64,128]{2,1,0:T(8,128)S(1)}) custom-call(f32[8,64,128]{2,1,0:T(8,128)S(1)} %get-tuple-element.71.own, f32[8,64,128]{2,1,0:T(8,128)S(1)} %collective-permute-done.18.across, f32[8,64,128]{2,1,0:T(8,128)S(1)} %collective-permute-done.19.partner, ...), custom_call_target="tpu_custom_call" | custom-call | flops 13107200 | bytes 1048576 | tf_op jit(solution)/shard_map/backward2/pallas_call | solution.py:26
  51.5 0.1 collective-permute-start.24
  51.5 0.1 collective-permute-start.25
  51.6 2.9 %collective-permute-done.26.across = f32[8,64,128]{2,1,0:T(8,128)S(1)} collective-permute-done((f32[8,64,128]{2,1,0:T(8,128)S(1)}, f32[8,64,128]{2,1,0:T(8,128)S(1)}, u32[]{:S(2)}, u32[]{:S(2)}) %collective-permute-start.26) | collective-permute-done | bytes 262176 | tf_op jit(solution)/shard_map/state_to_chip/ppermute | solution.py:411
  54.6 1.0 %forward3.1 = (f32[8,32,128]{2,1,0:T(8,128)S(1)}, f32[8,32,128]{2,1,0:T(8,128)S(1)}, f32[8,32,128]{2,1,0:T(8,128)S(1)}, f32[8,32,128]{2,1,0:T(8,128)S(1)}) custom-call(f32[8,64,128]{2,1,0:T(8,128)S(1)} %get-tuple-element.82.own, f32[8,64,128]{2,1,0:T(8,128)S(1)} %collective-permute-done.26.across, f32[8,64,128]{2,1,0:T(8,128)S(1)} %collective-permute-done.27.partner, ...), custom_call_target="tpu_custom_call" | custom-call | flops 13107200 | bytes 1048576 | tf_op jit(solution)/shard_map/forward3/pallas_call | solution.py:26
  55.6 0.1 collective-permute-start.28
  55.6 1.5 %collective-permute-start.29 = (f32[8,32,128]{2,1,0:T(8,128)S(1)}, f32[8,32,128]{2,1,0:T(8,128)S(1)}, u32[]{:S(2)}, u32[]{:S(2)}) collective-permute-start(f32[8,32,128]{2,1,0:T(8,128)S(1)} %get-tuple-element.86), channel_id=1, source_target_pairs={{0,16},{8,24},{16,0},{24,8},{1,17},{9,25},{17,1},{25,9},{2,18},{10... | collective-permute-start | bytes 393224 | tf_op jit(solution)/shard_map/grad_to_2/ppermute | solution.py:421
  57.1 2.0 %collective-permute-start.30 = (f32[8,32,128]{2,1,0:T(8,128)S(1)}, f32[8,32,128]{2,1,0:T(8,128)S(1)}, u32[]{:S(2)}, u32[]{:S(2)}) collective-permute-start(f32[8,32,128]{2,1,0:T(8,128)S(1)} %get-tuple-element.87), channel_id=1, source_target_pairs={{0,24},{8,16},{16,8},{24,0},{1,25},{9,17},{17,9},{25,1},{2,26},{10... | collective-permute-start | bytes 393224 | tf_op jit(solution)/shard_map/grad_to_3/ppermute | solution.py:421
  59.1 1.7 %backward3.1 = (f32[8,64,128]{2,1,0:T(8,128)}, f32[8,64,128]{2,1,0:T(8,128)}, f32[8,128]{1,0:T(8,128)S(1)}) custom-call(f32[8,64,128]{2,1,0:T(8,128)S(1)} %get-tuple-element.78.own, f32[8,64,128]{2,1,0:T(8,128)S(1)} %collective-permute-done.24.across, f32[8,64,128]{2,1,0:T(8,128)S(1)} %collective-permute-done.25.partner, ...), custom_call_target="tpu_custom_call" | custom-call | flops 13107200 | bytes 1048576 | tf_op jit(solution)/shard_map/backward3/pallas_call | solution.py:26
  60.8 0.5 collective-permute-done.28.refs_1_
  61.4 2.1 %collective-permute-done.29.refs_2_ = f32[8,32,128]{2,1,0:T(8,128)S(1)} collective-permute-done((f32[8,32,128]{2,1,0:T(8,128)S(1)}, f32[8,32,128]{2,1,0:T(8,128)S(1)}, u32[]{:S(2)}, u32[]{:S(2)}) %collective-permute-start.29) | collective-permute-done | bytes 131104 | tf_op jit(solution)/shard_map/grad_to_2/ppermute | solution.py:421
  63.5 0.7 %total.1 = f32[8,32,128]{2,1,0:T(8,128)} custom-call(f32[8,32,128]{2,1,0:T(8,128)S(1)} %get-tuple-element.84.refs_0_, f32[8,32,128]{2,1,0:T(8,128)S(1)} %collective-permute-done.28.refs_1_, f32[8,32,128]{2,1,0:T(8,128)S(1)} %collective-permute-done.29.refs_2_, f32[8,32,128]{2,1,0:T(8,128)S(1)} %collective-permute-done.30.refs_3_, ...), custom_call_target="tpu_custom_call" | custom-call | flops 1048576 | bytes 1048576 | tf_op jit(solution)/shard_map/total/pallas_call | solution.py:26
  (33 shorter events, 0.2 us)
Async XLA Ops:
  0.6 21.1 %copy-start.4 = (f32[1,16]{1,0:T(1,128)S(1)}, f32[1,16]{1,0:T(1,128)}, u32[]{:S(2)}) copy-start(f32[1,16]{1,0:T(1,128)} %wavelet.1) | copy-start | bytes 196
  0.6 21.1 %copy-start.3 = (f32[1,16,128]{2,1,0:T(8,128)S(1)}, f32[1,16,128]{2,1,0:T(8,128)}, u32[]{:S(2)}) copy-start(f32[1,16,128]{2,1,0:T(8,128)} %traces.1) | copy-start | bytes 24580
  0.7 21.1 %copy-start.5 = (s32[1,128]{1,0:T(1,128)S(1)}, s32[1,128]{1,0:T(1,128)}, u32[]{:S(2)}) copy-start(s32[1,128]{1,0:T(1,128)} %rx.1) | copy-start | bytes 1540
  0.7 21.1 %copy-start.6 = (s32[1,128]{1,0:T(1,128)S(1)}, s32[1,128]{1,0:T(1,128)}, u32[]{:S(2)}) copy-start(s32[1,128]{1,0:T(1,128)} %ry.1) | copy-start | bytes 1540
  0.7 21.1 %copy-start.7 = (s32[1,128]{1,0:T(1,128)S(1)}, s32[1,128]{1,0:T(1,128)}, u32[]{:S(2)}) copy-start(s32[1,128]{1,0:T(1,128)} %rz.1) | copy-start | bytes 1540
  2.8 6.8 %collective-permute-start.2 = (f32[9,32,128]{2,1,0:T(8,128)S(1)}, f32[9,32,128]{2,1,0:T(8,128)S(1)}, u32[]{:S(2)}, u32[]{:S(2)}) collective-permute-start(f32[9,32,128]{2,1,0:T(8,128)S(1)} %get-tuple-element.50), channel_id=1, source_target_pairs={{0,8},{8,0},{16,24},{24,16},{1,9},{9,1},{17,25},{25,17},{2,10},{10... | collective-permute-start | bytes 442376 | tf_op jit(solution)/shard_map/wz_to_1/ppermute | solution.py:421
  5.8 5.6 %collective-permute-start.3 = (f32[8,32,128]{2,1,0:T(8,128)S(1)}, f32[8,32,128]{2,1,0:T(8,128)S(1)}, u32[]{:S(2)}, u32[]{:S(2)}) collective-permute-start(f32[8,32,128]{2,1,0:T(8,128)S(1)} %get-tuple-element.51.own.refs_0_), channel_id=1, source_target_pairs={{0,16},{8,24},{16,0},{24,8},{1,17},{9,25},{17,1},{25,9},{2,18},{10... | collective-permute-start | bytes 393224 | tf_op jit(solution)/shard_map/wx_to_2/ppermute | solution.py:421
  7.3 9.7 %collective-permute-start = (f32[8,64,128]{2,1,0:T(8,128)S(1)}, f32[8,64,128]{2,1,0:T(8,128)S(1)}, u32[]{:S(2)}, u32[]{:S(2)}) collective-permute-start(f32[8,64,128]{2,1,0:T(8,128)S(1)} %get-tuple-element.48.own.previous), channel_id=1, source_target_pairs={{0,1},{1,0},{2,3},{3,2},{4,5},{5,4},{6,7},{7,6},{8,9},{9,8},{10,11... | collective-permute-start | bytes 786440 | tf_op jit(solution)/shard_map/state_to_core/ppermute | solution.py:407
  7.3 15.6 %collective-permute-start.1 = (f32[8,64,128]{2,1,0:T(8,128)S(1)}, f32[8,64,128]{2,1,0:T(8,128)S(1)}, u32[]{:S(2)}, u32[]{:S(2)}) collective-permute-start(f32[8,64,128]{2,1,0:T(8,128)S(1)} %get-tuple-element.48.own.previous), channel_id=1, source_target_pairs={{0,8},{1,2},{2,1},{3,4},{4,3},{5,6},{6,5},{7,15},{8,0},{9,10},{10,... | collective-permute-start | bytes 786440 | tf_op jit(solution)/shard_map/state_to_chip/ppermute | solution.py:411
  7.8 6.2 %collective-permute-start.9 = (f32[8,32,128]{2,1,0:T(8,128)S(1)}, f32[8,32,128]{2,1,0:T(8,128)S(1)}, u32[]{:S(2)}, u32[]{:S(2)}) collective-permute-start(f32[8,32,128]{2,1,0:T(8,128)S(1)} %get-tuple-element.58.own.refs_3_), channel_id=1, source_target_pairs={{0,16},{8,24},{16,0},{24,8},{1,17},{9,25},{17,1},{25,9},{2,18},{10... | collective-permute-start | bytes 393224 | tf_op jit(solution)/shard_map/wy_to_2/ppermute | solution.py:421
  9.6 6.9 %collective-permute-start.5 = (f32[8,32,128]{2,1,0:T(8,128)S(1)}, f32[8,32,128]{2,1,0:T(8,128)S(1)}, u32[]{:S(2)}, u32[]{:S(2)}) collective-permute-start(f32[8,32,128]{2,1,0:T(8,128)S(1)} %get-tuple-element.52.own.refs_0_), channel_id=1, source_target_pairs={{0,8},{8,0},{16,24},{24,16},{1,9},{9,1},{17,25},{25,17},{2,10},{10... | collective-permute-start | bytes 393224 | tf_op jit(solution)/shard_map/speed_to_1/ppermute | solution.py:421
  11.4 12.4 %collective-permute-start.11 = (f32[2,8,32,128]{3,2,1,0:T(8,128)S(1)}, f32[2,8,32,128]{3,2,1,0:T(8,128)S(1)}, u32[]{:S(2)}, u32[]{:S(2)}) collective-permute-start(f32[2,8,32,128]{3,2,1,0:T(8,128)S(1)} %pair_wz.1), channel_id=1, source_target_pairs={{0,16},{8,24},{16,0},{24,8},{1,17},{9,25},{17,1},{25,9},{2,18},{10... | collective-permute-start | bytes 786440 | tf_op jit(solution)/shard_map/wz_to_2/ppermute | solution.py:421
  14.0 8.9 %collective-permute-start.4 = (f32[8,32,128]{2,1,0:T(8,128)S(1)}, f32[8,32,128]{2,1,0:T(8,128)S(1)}, u32[]{:S(2)}, u32[]{:S(2)}) collective-permute-start(f32[8,32,128]{2,1,0:T(8,128)S(1)} %relay_wx.1.refs_0_), channel_id=1, source_target_pairs={{0,8},{8,0},{16,24},{24,16},{1,9},{9,1},{17,25},{25,17},{2,10},{10... | collective-permute-start | bytes 393224 | tf_op jit(solution)/shard_map/wx_to_1/ppermute | solution.py:421
  16.5 7.3 %collective-permute-start.10 = (f32[8,32,128]{2,1,0:T(8,128)S(1)}, f32[8,32,128]{2,1,0:T(8,128)S(1)}, u32[]{:S(2)}, u32[]{:S(2)}) collective-permute-start(f32[8,32,128]{2,1,0:T(8,128)S(1)} %relay_wy.1), channel_id=1, source_target_pairs={{0,8},{8,0},{16,24},{24,16},{1,9},{9,1},{17,25},{25,17},{2,10},{10... | collective-permute-start | bytes 393224 | tf_op jit(solution)/shard_map/wy_to_1/ppermute | solution.py:421
  17.1 9.9 %collective-permute-start.6 = (f32[2,8,32,128]{3,2,1,0:T(8,128)S(1)}, f32[2,8,32,128]{3,2,1,0:T(8,128)S(1)}, u32[]{:S(2)}, u32[]{:S(2)}) collective-permute-start(f32[2,8,32,128]{3,2,1,0:T(8,128)S(1)} %pair_speed.1), channel_id=1, source_target_pairs={{0,16},{8,24},{16,0},{24,8},{1,17},{9,25},{17,1},{25,9},{2,18},{10... | collective-permute-start | bytes 786440 | tf_op jit(solution)/shard_map/speed_to_2/ppermute | solution.py:421
  22.9 4.0 %copy-start = (f32[1,8,64,128]{3,2,1,0:T(8,128)S(1)}, f32[1,8,64,128]{3,2,1,0:T(8,128)}, u32[]{:S(2)}) copy-start(f32[1,8,64,128]{3,2,1,0:T(8,128)} %param.21) | copy-start | bytes 786436
  23.7 9.0 %copy-start.1 = (f32[1,8,64,128]{3,2,1,0:T(8,128)S(1)}, f32[1,8,64,128]{3,2,1,0:T(8,128)}, u32[]{:S(2)}) copy-start(f32[1,8,64,128]{3,2,1,0:T(8,128)} %param.18) | copy-start | bytes 786436
  24.3 2.8 %collective-permute-start.12 = (f32[3,2,64,128]{3,2,1,0:T(8,128)S(1)}, f32[3,2,64,128]{3,2,1,0:T(8,128)S(1)}, u32[]{:S(2)}, u32[]{:S(2)}) collective-permute-start(f32[3,2,64,128]{3,2,1,0:T(8,128)S(1)} %get-tuple-element.60), channel_id=1, source_target_pairs={{0,1},{1,0},{2,3},{3,2},{4,5},{5,4},{6,7},{7,6},{8,9},{9,8},{10,11... | collective-permute-start | bytes 589832 | tf_op jit(solution)/shard_map/edge_to_core/ppermute | solution.py:407
  24.4 3.0 %collective-permute-start.13 = (f32[3,2,64,128]{3,2,1,0:T(8,128)S(1)}, f32[3,2,64,128]{3,2,1,0:T(8,128)S(1)}, u32[]{:S(2)}, u32[]{:S(2)}) collective-permute-start(f32[3,2,64,128]{3,2,1,0:T(8,128)S(1)} %get-tuple-element.61), channel_id=1, source_target_pairs={{0,1},{1,0},{2,3},{3,2},{4,5},{5,4},{6,7},{7,6},{8,9},{9,8},{10,11... | collective-permute-start | bytes 589832 | tf_op jit(solution)/shard_map/edge_to_core/ppermute | solution.py:407
  24.9 5.7 %collective-permute-start.14 = (f32[3,2,64,128]{3,2,1,0:T(8,128)S(1)}, f32[3,2,64,128]{3,2,1,0:T(8,128)S(1)}, u32[]{:S(2)}, u32[]{:S(2)}) collective-permute-start(f32[3,2,64,128]{3,2,1,0:T(8,128)S(1)} %get-tuple-element.62), channel_id=1, source_target_pairs={{0,16},{1,2},{2,1},{3,4},{4,3},{5,6},{6,5},{7,23},{8,24},{9,10},{1... | collective-permute-start | bytes 589832 | tf_op jit(solution)/shard_map/edge_to_chip/ppermute | solution.py:411
  24.9 7.7 %collective-permute-start.15 = (f32[3,2,64,128]{3,2,1,0:T(8,128)S(1)}, f32[3,2,64,128]{3,2,1,0:T(8,128)S(1)}, u32[]{:S(2)}, u32[]{:S(2)}) collective-permute-start(f32[3,2,64,128]{3,2,1,0:T(8,128)S(1)} %get-tuple-element.63), channel_id=1, source_target_pairs={{0,16},{1,2},{2,1},{3,4},{4,3},{5,6},{6,5},{7,23},{8,24},{9,10},{1... | collective-permute-start | bytes 589832 | tf_op jit(solution)/shard_map/edge_to_chip/ppermute | solution.py:411
  27.0 8.5 %collective-permute-start.7 = (f32[8,64,128]{2,1,0:T(8,128)S(1)}, f32[8,64,128]{2,1,0:T(8,128)S(1)}, u32[]{:S(2)}, u32[]{:S(2)}) collective-permute-start(f32[8,64,128]{2,1,0:T(8,128)S(1)} %get-tuple-element.54.own), channel_id=1, source_target_pairs={{0,16},{1,2},{2,1},{3,4},{4,3},{5,6},{6,5},{7,23},{8,24},{9,10},{1... | collective-permute-start | bytes 786440 | tf_op jit(solution)/shard_map/adjoint_to_chip/ppermute | solution.py:411
  27.2 8.3 %collective-permute-start.8 = (f32[8,64,128]{2,1,0:T(8,128)S(1)}, f32[8,64,128]{2,1,0:T(8,128)S(1)}, u32[]{:S(2)}, u32[]{:S(2)}) collective-permute-start(f32[8,64,128]{2,1,0:T(8,128)S(1)} %get-tuple-element.54.own), channel_id=1, source_target_pairs={{0,1},{1,0},{2,3},{3,2},{4,5},{5,4},{6,7},{7,6},{8,9},{9,8},{10,11... | collective-permute-start | bytes 786440 | tf_op jit(solution)/shard_map/adjoint_to_core/ppermute | solution.py:407
  32.7 2.8 %copy-start.2 = (f32[1,8,64,128]{3,2,1,0:T(8,128)S(1)}, f32[1,8,64,128]{3,2,1,0:T(8,128)}, u32[]{:S(2)}) copy-start(f32[1,8,64,128]{3,2,1,0:T(8,128)} %param.20) | copy-start | bytes 786436
  33.2 6.4 %collective-permute-start.20 = (f32[8,64,128]{2,1,0:T(8,128)S(1)}, f32[8,64,128]{2,1,0:T(8,128)S(1)}, u32[]{:S(2)}, u32[]{:S(2)}) collective-permute-start(f32[8,64,128]{2,1,0:T(8,128)S(1)} %get-tuple-element.74.own.previous), channel_id=1, source_target_pairs={{0,16},{1,2},{2,1},{3,4},{4,3},{5,6},{6,5},{7,23},{8,24},{9,10},{1... | collective-permute-start | bytes 786440 | tf_op jit(solution)/shard_map/state_to_chip/ppermute | solution.py:411
  33.3 6.3 %collective-permute-start.21 = (f32[8,64,128]{2,1,0:T(8,128)S(1)}, f32[8,64,128]{2,1,0:T(8,128)S(1)}, u32[]{:S(2)}, u32[]{:S(2)}) collective-permute-start(f32[8,64,128]{2,1,0:T(8,128)S(1)} %get-tuple-element.74.own.previous), channel_id=1, source_target_pairs={{0,1},{1,0},{2,3},{3,2},{4,5},{5,4},{6,7},{7,6},{8,9},{9,8},{10,11... | collective-permute-start | bytes 786440 | tf_op jit(solution)/shard_map/state_to_core/ppermute | solution.py:407
  36.5 6.4 %collective-permute-start.16 = (f32[8,64,128]{2,1,0:T(8,128)S(1)}, f32[8,64,128]{2,1,0:T(8,128)S(1)}, u32[]{:S(2)}, u32[]{:S(2)}) collective-permute-start(f32[8,64,128]{2,1,0:T(8,128)S(1)} %get-tuple-element.69.own), channel_id=1, source_target_pairs={{0,16},{1,2},{2,1},{3,4},{4,3},{5,6},{6,5},{7,23},{8,24},{9,10},{1... | collective-permute-start | bytes 786440 | tf_op jit(solution)/shard_map/adjoint_to_chip/ppermute | solution.py:411
  36.6 6.3 %collective-permute-start.17 = (f32[8,64,128]{2,1,0:T(8,128)S(1)}, f32[8,64,128]{2,1,0:T(8,128)S(1)}, u32[]{:S(2)}, u32[]{:S(2)}) collective-permute-start(f32[8,64,128]{2,1,0:T(8,128)S(1)} %get-tuple-element.69.own), channel_id=1, source_target_pairs={{0,1},{1,0},{2,3},{3,2},{4,5},{5,4},{6,7},{7,6},{8,9},{9,8},{10,11... | collective-permute-start | bytes 786440 | tf_op jit(solution)/shard_map/adjoint_to_core/ppermute | solution.py:407
  40.7 6.4 %collective-permute-start.22 = (f32[8,64,128]{2,1,0:T(8,128)S(1)}, f32[8,64,128]{2,1,0:T(8,128)S(1)}, u32[]{:S(2)}, u32[]{:S(2)}) collective-permute-start(f32[8,64,128]{2,1,0:T(8,128)S(1)} %get-tuple-element.76.own), channel_id=1, source_target_pairs={{0,16},{1,2},{2,1},{3,4},{4,3},{5,6},{6,5},{7,23},{8,24},{9,10},{1... | collective-permute-start | bytes 786440 | tf_op jit(solution)/shard_map/state_to_chip/ppermute | solution.py:411
  40.8 6.3 %collective-permute-start.23 = (f32[8,64,128]{2,1,0:T(8,128)S(1)}, f32[8,64,128]{2,1,0:T(8,128)S(1)}, u32[]{:S(2)}, u32[]{:S(2)}) collective-permute-start(f32[8,64,128]{2,1,0:T(8,128)S(1)} %get-tuple-element.76.own), channel_id=1, source_target_pairs={{0,1},{1,0},{2,3},{3,2},{4,5},{5,4},{6,7},{7,6},{8,9},{9,8},{10,11... | collective-permute-start | bytes 786440 | tf_op jit(solution)/shard_map/state_to_core/ppermute | solution.py:407
  43.9 6.4 %collective-permute-start.18 = (f32[8,64,128]{2,1,0:T(8,128)S(1)}, f32[8,64,128]{2,1,0:T(8,128)S(1)}, u32[]{:S(2)}, u32[]{:S(2)}) collective-permute-start(f32[8,64,128]{2,1,0:T(8,128)S(1)} %get-tuple-element.71.own), channel_id=1, source_target_pairs={{0,16},{1,2},{2,1},{3,4},{4,3},{5,6},{6,5},{7,23},{8,24},{9,10},{1... | collective-permute-start | bytes 786440 | tf_op jit(solution)/shard_map/adjoint_to_chip/ppermute | solution.py:411
  44.0 6.3 %collective-permute-start.19 = (f32[8,64,128]{2,1,0:T(8,128)S(1)}, f32[8,64,128]{2,1,0:T(8,128)S(1)}, u32[]{:S(2)}, u32[]{:S(2)}) collective-permute-start(f32[8,64,128]{2,1,0:T(8,128)S(1)} %get-tuple-element.71.own), channel_id=1, source_target_pairs={{0,1},{1,0},{2,3},{3,2},{4,5},{5,4},{6,7},{7,6},{8,9},{9,8},{10,11... | collective-permute-start | bytes 786440 | tf_op jit(solution)/shard_map/adjoint_to_core/ppermute | solution.py:407
  48.1 6.4 %collective-permute-start.26 = (f32[8,64,128]{2,1,0:T(8,128)S(1)}, f32[8,64,128]{2,1,0:T(8,128)S(1)}, u32[]{:S(2)}, u32[]{:S(2)}) collective-permute-start(f32[8,64,128]{2,1,0:T(8,128)S(1)} %get-tuple-element.82.own), channel_id=1, source_target_pairs={{0,16},{1,2},{2,1},{3,4},{4,3},{5,6},{6,5},{7,23},{8,24},{9,10},{1... | collective-permute-start | bytes 786440 | tf_op jit(solution)/shard_map/state_to_chip/ppermute | solution.py:411
  48.2 6.3 %collective-permute-start.27 = (f32[8,64,128]{2,1,0:T(8,128)S(1)}, f32[8,64,128]{2,1,0:T(8,128)S(1)}, u32[]{:S(2)}, u32[]{:S(2)}) collective-permute-start(f32[8,64,128]{2,1,0:T(8,128)S(1)} %get-tuple-element.82.own), channel_id=1, source_target_pairs={{0,1},{1,0},{2,3},{3,2},{4,5},{5,4},{6,7},{7,6},{8,9},{9,8},{10,11... | collective-permute-start | bytes 786440 | tf_op jit(solution)/shard_map/state_to_core/ppermute | solution.py:407
  51.5 7.7 %collective-permute-start.24 = (f32[8,64,128]{2,1,0:T(8,128)S(1)}, f32[8,64,128]{2,1,0:T(8,128)S(1)}, u32[]{:S(2)}, u32[]{:S(2)}) collective-permute-start(f32[8,64,128]{2,1,0:T(8,128)S(1)} %get-tuple-element.78.own), channel_id=1, source_target_pairs={{0,16},{1,2},{2,1},{3,4},{4,3},{5,6},{6,5},{7,23},{8,24},{9,10},{1... | collective-permute-start | bytes 786440 | tf_op jit(solution)/shard_map/adjoint_to_chip/ppermute | solution.py:411
  51.5 7.6 %collective-permute-start.25 = (f32[8,64,128]{2,1,0:T(8,128)S(1)}, f32[8,64,128]{2,1,0:T(8,128)S(1)}, u32[]{:S(2)}, u32[]{:S(2)}) collective-permute-start(f32[8,64,128]{2,1,0:T(8,128)S(1)} %get-tuple-element.78.own), channel_id=1, source_target_pairs={{0,1},{1,0},{2,3},{3,2},{4,5},{5,4},{6,7},{7,6},{8,9},{9,8},{10,11... | collective-permute-start | bytes 786440 | tf_op jit(solution)/shard_map/adjoint_to_core/ppermute | solution.py:407
  55.6 5.8 %collective-permute-start.28 = (f32[8,32,128]{2,1,0:T(8,128)S(1)}, f32[8,32,128]{2,1,0:T(8,128)S(1)}, u32[]{:S(2)}, u32[]{:S(2)}) collective-permute-start(f32[8,32,128]{2,1,0:T(8,128)S(1)} %get-tuple-element.85), channel_id=1, source_target_pairs={{0,8},{8,0},{16,24},{24,16},{1,9},{9,1},{17,25},{25,17},{2,10},{10... | collective-permute-start | bytes 393224 | tf_op jit(solution)/shard_map/grad_to_1/ppermute | solution.py:421
  55.6 7.9 %collective-permute-start.29 = (f32[8,32,128]{2,1,0:T(8,128)S(1)}, f32[8,32,128]{2,1,0:T(8,128)S(1)}, u32[]{:S(2)}, u32[]{:S(2)}) collective-permute-start(f32[8,32,128]{2,1,0:T(8,128)S(1)} %get-tuple-element.86), channel_id=1, source_target_pairs={{0,16},{8,24},{16,0},{24,8},{1,17},{9,25},{17,1},{25,9},{2,18},{10... | collective-permute-start | bytes 393224 | tf_op jit(solution)/shard_map/grad_to_2/ppermute | solution.py:421
  57.1 6.4 %collective-permute-start.30 = (f32[8,32,128]{2,1,0:T(8,128)S(1)}, f32[8,32,128]{2,1,0:T(8,128)S(1)}, u32[]{:S(2)}, u32[]{:S(2)}) collective-permute-start(f32[8,32,128]{2,1,0:T(8,128)S(1)} %get-tuple-element.87), channel_id=1, source_target_pairs={{0,24},{8,16},{16,8},{24,0},{1,25},{9,17},{17,9},{25,1},{2,26},{10... | collective-permute-start | bytes 393224 | tf_op jit(solution)/shard_map/grad_to_3/ppermute | solution.py:421

commit v6 on v5

--- a/solution.py
+++ b/solution.py
@@ -470,13 +470,6 @@
         speed_places = places[0]
         speed_pieces = [speed] + [to_owners(speed, k, "speed") for k in range(1, shots)]
 
-    src, inj = call(
-        "inject",
-        inject_kernel,
-        (f32(STEPS - 1, rows, width, depth), f32(STEPS, rows, width, depth)),
-        [step_index, source_x, source_y, source_z, wavelet, receiver_x, receiver_y, receiver_z]
-        + [residual_traces],
-    )
     now_p, now_a = to_partner(current, "state"), across_chips(current, "state", 1)
     slope, flags, matrix_y, matrix_z = call(
         "prepare",
@@ -487,7 +480,7 @@
             jax.ShapeDtypeStruct((width, 2 * width), jnp.bfloat16),
             jax.ShapeDtypeStruct((2 * depth, depth), jnp.bfloat16),
         ),
-        [first, current, now_p, now_a, src] + before,
+        [first, current, now_p, now_a] + before,
         [wide],
     )
     edge = f32(3, 2, width, depth)
@@ -500,6 +493,14 @@
     )
     edges_a = [across_chips(a, "edge") for a in edges[:2]]
     edges_p = [to_partner(a, "edge") for a in edges[2:]]
+    src, inj = call(
+        "inject",
+        inject_kernel,
+        (f32(STEPS - 1, rows, width, depth), f32(STEPS, rows, width, depth)),
+        [step_index, source_x, source_y, source_z, wavelet, receiver_x, receiver_y, receiver_z]
+        + [residual_traces],
+    )
+
     speed, operand = call(
         "speed",
         functools.partial(speed_kernel, speed_places, parts),

time: 64.4 us -> 63 us (0.978)
  waiting for transfers between devices: 26.8 us -> 19.4 us
  starting transfers between devices: 20 us -> 26.2 us
    ppermute x10, waiting for transfers between devices: 20.6 us -> 10.6 us  [across_chips(): return lax.ppermute(array, ('shot', 'blk'), chip_pairs(hop))]
    ppermute x10, starting transfers between devices: 3.22 us -> 8.06 us  [across_chips(): return lax.ppermute(array, ('shot', 'blk'), chip_pairs(hop))]
    ppermute x11, waiting for transfers between devices: 6.2 us -> 8.72 us  [to_owners(): return lax.ppermute(array, 'shot', [(i, i ^ k) for i in range(shots)])]
    ppermute x10, starting transfers between devices: 1.12 us -> 2.54 us  [to_partner(): return lax.ppermute(array, 'blk', core_pairs)]
  transfers between devices with their start and end apart: 31 -> 31, of which waited for: 13 -> 14; matrix products, arithmetic and copies ran while one was open for 0% -> 0% of each run, Pallas kernels for 17% -> 17%
where the time goes in v6:
time: 63 us; the launch traced here: 62.9 us
  starting transfers between devices  26.2 us (42%)
  waiting for transfers between devices  19.4 us (31%)
  Pallas kernels  13.1 us (21%)
  between operations  4.12 us (7%)
    ppermute x11, starting transfers between devices, to_owners(): return lax.ppermute(array, 'shot', [(i, i ^ k) for i in range(shots)])  15.6 us
    pallas_call x19, Pallas kernels, call(): pl.pallas_call(body, name=name, out_shape=outs, in_specs=[s for _, s in p...  13.1 us
    ppermute x10, waiting for transfers between devices, across_chips(): return lax.ppermute(array, ('shot', 'blk'), chip_pairs(hop))  10.6 us
    ppermute x11, waiting for transfers between devices, to_owners(): return lax.ppermute(array, 'shot', [(i, i ^ k) for i in range(shots)])  8.72 us
    ppermute x10, starting transfers between devices, across_chips(): return lax.ppermute(array, ('shot', 'blk'), chip_pairs(hop))  8.06 us
    ppermute x10, starting transfers between devices, to_partner(): return lax.ppermute(array, 'blk', core_pairs)  2.54 us
  transfers between devices with their start and end apart: 31, of which 14 were waited for; matrix products, arithmetic and copies ran while one was open for 0% of the time, Pallas kernels for 17%

profile of v6, /device:TPU:0, one launch (start us, length us, event | category | flops | bytes accessed | tf_op | source)
XLA Modules:
  0.0 62.9 jit_solution(5233979890715448657)
XLA Ops:
  1.3 1.4 %owner.1 = (f32[8,32,128]{2,1,0:T(8,128)S(1)}, f32[8,32,128]{2,1,0:T(8,128)S(1)}, f32[8,32,128]{2,1,0:T(8,128)S(1)}, f32[8,32,128]{2,1,0:T(8,128)S(1)}, f32[8,64,128]{2,1,0:T(8,128)S(1)}) custom-call(f32[8,32,128]{2,1,0:T(8,128)} %eps.1, f32[8,32,128]{2,1,0:T(8,128)} %tilt.1, f32[8,32,128]{2,1,0:T(8,128)} %azimuth.1, f32[8,32,128]{2,1,0:T(8,128)} %speed.2, ...), custom_call_target="tpu_custom_call" | custom-call | flops 1048576 | bytes 1048576 | tf_op jit(solution)/shard_map/owner/pallas_call | solution.py:26
  2.7 0.1 first.1
  2.8 2.9 %collective-permute-start.2 = (f32[9,32,128]{2,1,0:T(8,128)S(1)}, f32[9,32,128]{2,1,0:T(8,128)S(1)}, u32[]{:S(2)}, u32[]{:S(2)}) collective-permute-start(f32[9,32,128]{2,1,0:T(8,128)S(1)} %get-tuple-element.49), channel_id=1, source_target_pairs={{0,8},{8,0},{16,24},{24,16},{1,9},{9,1},{17,25},{25,17},{2,10},{10... | collective-permute-start | bytes 442376 | tf_op jit(solution)/shard_map/wz_to_1/ppermute | solution.py:421
  5.7 1.5 %collective-permute-start.3 = (f32[8,32,128]{2,1,0:T(8,128)S(1)}, f32[8,32,128]{2,1,0:T(8,128)S(1)}, u32[]{:S(2)}, u32[]{:S(2)}) collective-permute-start(f32[8,32,128]{2,1,0:T(8,128)S(1)} %get-tuple-element.50.own.refs_0_), channel_id=1, source_target_pairs={{0,16},{8,24},{16,0},{24,8},{1,17},{9,25},{17,1},{25,9},{2,18},{10... | collective-permute-start | bytes 393224 | tf_op jit(solution)/shard_map/wx_to_2/ppermute | solution.py:421
  7.2 0.0 collective-permute-start
  7.2 0.5 collective-permute-start.1
  7.8 0.1 collective-permute-start.9
  7.8 1.7 %collective-permute-done.2.wz_first.received.refs_7_ = f32[9,32,128]{2,1,0:T(8,128)S(1)} collective-permute-done((f32[9,32,128]{2,1,0:T(8,128)S(1)}, f32[9,32,128]{2,1,0:T(8,128)S(1)}, u32[]{:S(2)}, u32[]{:S(2)}) %collective-permute-start.2) | collective-permute-done | bytes 147488 | tf_op jit(solution)/shard_map/wz_to_1/ppermute | solution.py:421
  9.5 1.7 %collective-permute-start.5 = (f32[8,32,128]{2,1,0:T(8,128)S(1)}, f32[8,32,128]{2,1,0:T(8,128)S(1)}, u32[]{:S(2)}, u32[]{:S(2)}) collective-permute-start(f32[8,32,128]{2,1,0:T(8,128)S(1)} %get-tuple-element.51.own.refs_0_), channel_id=1, source_target_pairs={{0,8},{8,0},{16,24},{24,16},{1,9},{9,1},{17,25},{25,17},{2,10},{10... | collective-permute-start | bytes 393224 | tf_op jit(solution)/shard_map/speed_to_1/ppermute | solution.py:421
  11.3 0.0 collective-permute-done.3.received.refs_2_
  11.3 1.6 %collective-permute-start.11 = (f32[2,8,32,128]{3,2,1,0:T(8,128)S(1)}, f32[2,8,32,128]{3,2,1,0:T(8,128)S(1)}, u32[]{:S(2)}, u32[]{:S(2)}) collective-permute-start(f32[2,8,32,128]{3,2,1,0:T(8,128)S(1)} %pair_wz.1), channel_id=1, source_target_pairs={{0,16},{8,24},{16,0},{24,8},{1,17},{9,25},{17,1},{25,9},{2,18},{10... | collective-permute-start | bytes 786440 | tf_op jit(solution)/shard_map/wz_to_2/ppermute | solution.py:421
  12.9 1.0 %collective-permute-done.9.received.refs_5_ = f32[8,32,128]{2,1,0:T(8,128)S(1)} collective-permute-done((f32[8,32,128]{2,1,0:T(8,128)S(1)}, f32[8,32,128]{2,1,0:T(8,128)S(1)}, u32[]{:S(2)}, u32[]{:S(2)}) %collective-permute-start.9) | collective-permute-done | bytes 131104 | tf_op jit(solution)/shard_map/wy_to_2/ppermute | solution.py:421
  13.9 1.6 %collective-permute-start.4 = (f32[8,32,128]{2,1,0:T(8,128)S(1)}, f32[8,32,128]{2,1,0:T(8,128)S(1)}, u32[]{:S(2)}, u32[]{:S(2)}) collective-permute-start(f32[8,32,128]{2,1,0:T(8,128)S(1)} %relay_wx.1.refs_0_), channel_id=1, source_target_pairs={{0,8},{8,0},{16,24},{24,16},{1,9},{9,1},{17,25},{25,17},{2,10},{10... | collective-permute-start | bytes 393224 | tf_op jit(solution)/shard_map/wx_to_1/ppermute | solution.py:421
  15.6 0.8 %collective-permute-done.5.refs_1_.received = f32[8,32,128]{2,1,0:T(8,128)S(1)} collective-permute-done((f32[8,32,128]{2,1,0:T(8,128)S(1)}, f32[8,32,128]{2,1,0:T(8,128)S(1)}, u32[]{:S(2)}, u32[]{:S(2)}) %collective-permute-start.5) | collective-permute-done | bytes 131104 | tf_op jit(solution)/shard_map/speed_to_1/ppermute | solution.py:421
  16.4 0.5 collective-permute-start.10
  17.0 0.0 copy-start
  17.0 2.1 %collective-permute-start.6 = (f32[2,8,32,128]{3,2,1,0:T(8,128)S(1)}, f32[2,8,32,128]{3,2,1,0:T(8,128)S(1)}, u32[]{:S(2)}, u32[]{:S(2)}) collective-permute-start(f32[2,8,32,128]{3,2,1,0:T(8,128)S(1)} %pair_speed.1), channel_id=1, source_target_pairs={{0,16},{8,24},{16,0},{24,8},{1,17},{9,25},{17,1},{25,9},{2,18},{10... | collective-permute-start | bytes 786440 | tf_op jit(solution)/shard_map/speed_to_2/ppermute | solution.py:421
  19.0 1.2 %collective-permute-done.4.refs_0_.refs_1_ = f32[8,32,128]{2,1,0:T(8,128)S(1)} collective-permute-done((f32[8,32,128]{2,1,0:T(8,128)S(1)}, f32[8,32,128]{2,1,0:T(8,128)S(1)}, u32[]{:S(2)}, u32[]{:S(2)}) %collective-permute-start.4) | collective-permute-done | bytes 131104 | tf_op jit(solution)/shard_map/wx_to_1/ppermute | solution.py:421
  20.3 0.8 %prepare.1 = (f32[3,16,64,128]{3,2,1,0:T(8,128)S(1)}, f32[8,128]{1,0:T(8,128)S(1)}, bf16[64,128]{1,0:T(8,128)(2,1)S(1)}, bf16[256,128]{1,0:T(8,128)(2,1)S(1)}) custom-call(f32[8,128]{1,0:T(8,128)S(1)} %get-tuple-element.47.first, f32[8,64,128]{2,1,0:T(8,128)S(1)} %get-tuple-element.48.own.previous, f32[8,64,128]{2,1,0:T(8,128)S(1)} %collective-permute-done.partner, ...), custom_call_target="tpu_custom_call" | custom-call | flops 1048576 | bytes 1048576 | tf_op jit(solution)/shard_map/prepare/pallas_call | solution.py:26
  21.1 0.0 copy-start.4
  21.1 0.0 copy-start.5
  21.1 0.0 copy-start.6
  21.1 0.0 copy-start.7
  21.1 0.0 copy-start.1
  21.1 1.3 %collective-permute-done.10.refs_4_ = f32[8,32,128]{2,1,0:T(8,128)S(1)} collective-permute-done((f32[8,32,128]{2,1,0:T(8,128)S(1)}, f32[8,32,128]{2,1,0:T(8,128)S(1)}, u32[]{:S(2)}, u32[]{:S(2)}) %collective-permute-start.10) | collective-permute-done | bytes 131104 | tf_op jit(solution)/shard_map/wy_to_1/ppermute | solution.py:421
  22.5 0.6 flux.1
  23.0 0.1 collective-permute-start.12
  23.1 0.5 collective-permute-start.13
  23.6 0.7 %collective-permute-start.14 = (f32[3,2,64,128]{3,2,1,0:T(8,128)S(1)}, f32[3,2,64,128]{3,2,1,0:T(8,128)S(1)}, u32[]{:S(2)}, u32[]{:S(2)}) collective-permute-start(f32[3,2,64,128]{3,2,1,0:T(8,128)S(1)} %get-tuple-element.61), channel_id=1, source_target_pairs={{0,16},{1,2},{2,1},{3,4},{4,3},{5,6},{6,5},{7,23},{8,24},{9,10},{1... | collective-permute-start | bytes 589832 | tf_op jit(solution)/shard_map/edge_to_chip/ppermute | solution.py:411
  24.3 1.3 %collective-permute-start.15 = (f32[3,2,64,128]{3,2,1,0:T(8,128)S(1)}, f32[3,2,64,128]{3,2,1,0:T(8,128)S(1)}, u32[]{:S(2)}, u32[]{:S(2)}) collective-permute-start(f32[3,2,64,128]{3,2,1,0:T(8,128)S(1)} %get-tuple-element.62), channel_id=1, source_target_pairs={{0,16},{1,2},{2,1},{3,4},{4,3},{5,6},{6,5},{7,23},{8,24},{9,10},{1... | collective-permute-start | bytes 589832 | tf_op jit(solution)/shard_map/edge_to_chip/ppermute | solution.py:411
  25.6 0.1 speed.3
  25.7 0.8 %collective-permute-start.7 = (f32[8,64,128]{2,1,0:T(8,128)S(1)}, f32[8,64,128]{2,1,0:T(8,128)S(1)}, u32[]{:S(2)}, u32[]{:S(2)}) collective-permute-start(f32[8,64,128]{2,1,0:T(8,128)S(1)} %get-tuple-element.53.own), channel_id=1, source_target_pairs={{0,16},{1,2},{2,1},{3,4},{4,3},{5,6},{6,5},{7,23},{8,24},{9,10},{1... | collective-permute-start | bytes 786440 | tf_op jit(solution)/shard_map/adjoint_to_chip/ppermute | solution.py:411
  26.5 0.7 %collective-permute-start.8 = (f32[8,64,128]{2,1,0:T(8,128)S(1)}, f32[8,64,128]{2,1,0:T(8,128)S(1)}, u32[]{:S(2)}, u32[]{:S(2)}) collective-permute-start(f32[8,64,128]{2,1,0:T(8,128)S(1)} %get-tuple-element.53.own), channel_id=1, source_target_pairs={{0,1},{1,0},{2,3},{3,2},{4,5},{5,4},{6,7},{7,6},{8,9},{9,8},{10,11... | collective-permute-start | bytes 786440 | tf_op jit(solution)/shard_map/adjoint_to_core/ppermute | solution.py:407
  29.9 1.1 %inject.1 = (f32[3,8,64,128]{3,2,1,0:T(8,128)S(1)}, f32[4,8,64,128]{3,2,1,0:T(8,128)S(1)}) custom-call(s32[1]{0:T(128)S(6)} %copy.22.step, s32[1]{0:T(128)S(6)} %copy.23.sx, s32[1]{0:T(128)S(6)} %copy.24.sy, s32[1]{0:T(128)S(6)} %copy.25.sz, f32[1,16]{1,0:T(1,128)S(1)} %copy-done.4, s32[1,128]{1,0:T(1,128)S(1)} %copy-done.5, s32[1,128]{1,0:T(1,128)S(1)} %copy-done.6, ...), custom_call_target="tpu_custom_call" | custom-call | flops 1048576 | bytes 1048576 | tf_op jit(solution)/shard_map/inject/pallas_call | solution.py:26
  31.1 0.3 collective-permute-done.15.edge_a1
  31.4 0.5 forward0.1
  31.9 0.8 %collective-permute-start.20 = (f32[8,64,128]{2,1,0:T(8,128)S(1)}, f32[8,64,128]{2,1,0:T(8,128)S(1)}, u32[]{:S(2)}, u32[]{:S(2)}) collective-permute-start(f32[8,64,128]{2,1,0:T(8,128)S(1)} %get-tuple-element.74.own.previous), channel_id=1, source_target_pairs={{0,16},{1,2},{2,1},{3,4},{4,3},{5,6},{6,5},{7,23},{8,24},{9,10},{1... | collective-permute-start | bytes 786440 | tf_op jit(solution)/shard_map/state_to_chip/ppermute | solution.py:411
  32.7 0.7 %collective-permute-start.21 = (f32[8,64,128]{2,1,0:T(8,128)S(1)}, f32[8,64,128]{2,1,0:T(8,128)S(1)}, u32[]{:S(2)}, u32[]{:S(2)}) collective-permute-start(f32[8,64,128]{2,1,0:T(8,128)S(1)} %get-tuple-element.74.own.previous), channel_id=1, source_target_pairs={{0,1},{1,0},{2,3},{3,2},{4,5},{5,4},{6,7},{7,6},{8,9},{9,8},{10,11... | collective-permute-start | bytes 786440 | tf_op jit(solution)/shard_map/state_to_core/ppermute | solution.py:407
  33.4 0.8 %collective-permute-done.7.across = f32[8,64,128]{2,1,0:T(8,128)S(1)} collective-permute-done((f32[8,64,128]{2,1,0:T(8,128)S(1)}, f32[8,64,128]{2,1,0:T(8,128)S(1)}, u32[]{:S(2)}, u32[]{:S(2)}) %collective-permute-start.7) | collective-permute-done | bytes 262176 | tf_op jit(solution)/shard_map/adjoint_to_chip/ppermute | solution.py:411
  34.2 1.0 %backward0.1 = (f32[8,64,128]{2,1,0:T(8,128)S(1)}, f32[8,64,128]{2,1,0:T(8,128)S(1)}) custom-call(f32[8,64,128]{2,1,0:T(8,128)S(1)} %get-tuple-element.53.own, f32[8,64,128]{2,1,0:T(8,128)S(1)} %collective-permute-done.7.across, f32[8,64,128]{2,1,0:T(8,128)S(1)} %collective-permute-done.8.partner, f32[4,16,64,128]{3,2,1,0:T(8,128)S(1)} %get-tuple-element.67.coef, ...), custom_call_target="tpu_custom_call" | custom-call | flops 13107200 | bytes 1048576 | tf_op jit(solution)/shard_map/backward0/pallas_call | solution.py:26
  35.2 0.8 %collective-permute-start.16 = (f32[8,64,128]{2,1,0:T(8,128)S(1)}, f32[8,64,128]{2,1,0:T(8,128)S(1)}, u32[]{:S(2)}, u32[]{:S(2)}) collective-permute-start(f32[8,64,128]{2,1,0:T(8,128)S(1)} %get-tuple-element.69.own), channel_id=1, source_target_pairs={{0,16},{1,2},{2,1},{3,4},{4,3},{5,6},{6,5},{7,23},{8,24},{9,10},{1... | collective-permute-start | bytes 786440 | tf_op jit(solution)/shard_map/adjoint_to_chip/ppermute | solution.py:411
  36.0 0.4 collective-permute-start.17
  36.4 1.9 %collective-permute-done.20.across = f32[8,64,128]{2,1,0:T(8,128)S(1)} collective-permute-done((f32[8,64,128]{2,1,0:T(8,128)S(1)}, f32[8,64,128]{2,1,0:T(8,128)S(1)}, u32[]{:S(2)}, u32[]{:S(2)}) %collective-permute-start.20) | collective-permute-done | bytes 262176 | tf_op jit(solution)/shard_map/state_to_chip/ppermute | solution.py:411
  38.3 1.0 %forward1.1 = (f32[8,64,128]{2,1,0:T(8,128)S(1)}, f32[8,64,128]{2,1,0:T(8,128)S(1)}) custom-call(f32[8,64,128]{2,1,0:T(8,128)S(1)} %get-tuple-element.74.own.previous, f32[8,64,128]{2,1,0:T(8,128)S(1)} %collective-permute-done.20.across, f32[8,64,128]{2,1,0:T(8,128)S(1)} %collective-permute-done.21.partner, f32[4,16,64,128]{3,2,1,0:T(8,128)S(1)} %get-tuple-element.67.coef, ...), custom_call_target="tpu_custom_call" | custom-call | flops 13107200 | bytes 1048576 | tf_op jit(solution)/shard_map/forward1/pallas_call | solution.py:26
  39.3 0.8 %collective-permute-start.22 = (f32[8,64,128]{2,1,0:T(8,128)S(1)}, f32[8,64,128]{2,1,0:T(8,128)S(1)}, u32[]{:S(2)}, u32[]{:S(2)}) collective-permute-start(f32[8,64,128]{2,1,0:T(8,128)S(1)} %get-tuple-element.76.own), channel_id=1, source_target_pairs={{0,16},{1,2},{2,1},{3,4},{4,3},{5,6},{6,5},{7,23},{8,24},{9,10},{1... | collective-permute-start | bytes 786440 | tf_op jit(solution)/shard_map/state_to_chip/ppermute | solution.py:411
  40.1 0.1 collective-permute-start.23
  40.2 1.4 %collective-permute-done.16.across = f32[8,64,128]{2,1,0:T(8,128)S(1)} collective-permute-done((f32[8,64,128]{2,1,0:T(8,128)S(1)}, f32[8,64,128]{2,1,0:T(8,128)S(1)}, u32[]{:S(2)}, u32[]{:S(2)}) %collective-permute-start.16) | collective-permute-done | bytes 262176 | tf_op jit(solution)/shard_map/adjoint_to_chip/ppermute | solution.py:411
  41.6 1.0 %backward1.1 = (f32[8,64,128]{2,1,0:T(8,128)S(1)}, f32[8,64,128]{2,1,0:T(8,128)S(1)}) custom-call(f32[8,64,128]{2,1,0:T(8,128)S(1)} %get-tuple-element.69.own, f32[8,64,128]{2,1,0:T(8,128)S(1)} %collective-permute-done.16.across, f32[8,64,128]{2,1,0:T(8,128)S(1)} %collective-permute-done.17.partner, f32[4,16,64,128]{3,2,1,0:T(8,128)S(1)} %get-tuple-element.67.coef, ...), custom_call_target="tpu_custom_call" | custom-call | flops 13107200 | bytes 1048576 | tf_op jit(solution)/shard_map/backward1/pallas_call | solution.py:26
  42.6 0.8 %collective-permute-start.18 = (f32[8,64,128]{2,1,0:T(8,128)S(1)}, f32[8,64,128]{2,1,0:T(8,128)S(1)}, u32[]{:S(2)}, u32[]{:S(2)}) collective-permute-start(f32[8,64,128]{2,1,0:T(8,128)S(1)} %get-tuple-element.71.own), channel_id=1, source_target_pairs={{0,16},{1,2},{2,1},{3,4},{4,3},{5,6},{6,5},{7,23},{8,24},{9,10},{1... | collective-permute-start | bytes 786440 | tf_op jit(solution)/shard_map/adjoint_to_chip/ppermute | solution.py:411
  43.4 2.4 %collective-permute-done.22.across = f32[8,64,128]{2,1,0:T(8,128)S(1)} collective-permute-done((f32[8,64,128]{2,1,0:T(8,128)S(1)}, f32[8,64,128]{2,1,0:T(8,128)S(1)}, u32[]{:S(2)}, u32[]{:S(2)}) %collective-permute-start.22) | collective-permute-done | bytes 262176 | tf_op jit(solution)/shard_map/state_to_chip/ppermute | solution.py:411
  45.8 1.0 %forward2.1 = (f32[8,64,128]{2,1,0:T(8,128)S(1)}, f32[8,64,128]{2,1,0:T(8,128)S(1)}) custom-call(f32[8,64,128]{2,1,0:T(8,128)S(1)} %get-tuple-element.76.own, f32[8,64,128]{2,1,0:T(8,128)S(1)} %collective-permute-done.22.across, f32[8,64,128]{2,1,0:T(8,128)S(1)} %collective-permute-done.23.partner, f32[4,16,64,128]{3,2,1,0:T(8,128)S(1)} %get-tuple-element.67.coef, ...), custom_call_target="tpu_custom_call" | custom-call | flops 13107200 | bytes 1048576 | tf_op jit(solution)/shard_map/forward2/pallas_call | solution.py:26
  46.8 0.8 %collective-permute-start.26 = (f32[8,64,128]{2,1,0:T(8,128)S(1)}, f32[8,64,128]{2,1,0:T(8,128)S(1)}, u32[]{:S(2)}, u32[]{:S(2)}) collective-permute-start(f32[8,64,128]{2,1,0:T(8,128)S(1)} %get-tuple-element.82.own), channel_id=1, source_target_pairs={{0,16},{1,2},{2,1},{3,4},{4,3},{5,6},{6,5},{7,23},{8,24},{9,10},{1... | collective-permute-start | bytes 786440 | tf_op jit(solution)/shard_map/state_to_chip/ppermute | solution.py:411
  47.6 1.5 %collective-permute-done.18.across = f32[8,64,128]{2,1,0:T(8,128)S(1)} collective-permute-done((f32[8,64,128]{2,1,0:T(8,128)S(1)}, f32[8,64,128]{2,1,0:T(8,128)S(1)}, u32[]{:S(2)}, u32[]{:S(2)}) %collective-permute-start.18) | collective-permute-done | bytes 262176 | tf_op jit(solution)/shard_map/adjoint_to_chip/ppermute | solution.py:411
  49.1 1.0 %backward2.1 = (f32[8,64,128]{2,1,0:T(8,128)S(1)}, f32[8,64,128]{2,1,0:T(8,128)S(1)}, f32[8,64,128]{2,1,0:T(8,128)S(1)}) custom-call(f32[8,64,128]{2,1,0:T(8,128)S(1)} %get-tuple-element.71.own, f32[8,64,128]{2,1,0:T(8,128)S(1)} %collective-permute-done.18.across, f32[8,64,128]{2,1,0:T(8,128)S(1)} %collective-permute-done.19.partner, ...), custom_call_target="tpu_custom_call" | custom-call | flops 13107200 | bytes 1048576 | tf_op jit(solution)/shard_map/backward2/pallas_call | solution.py:26
  50.1 0.8 %collective-permute-start.24 = (f32[8,64,128]{2,1,0:T(8,128)S(1)}, f32[8,64,128]{2,1,0:T(8,128)S(1)}, u32[]{:S(2)}, u32[]{:S(2)}) collective-permute-start(f32[8,64,128]{2,1,0:T(8,128)S(1)} %get-tuple-element.78.own), channel_id=1, source_target_pairs={{0,16},{1,2},{2,1},{3,4},{4,3},{5,6},{6,5},{7,23},{8,24},{9,10},{1... | collective-permute-start | bytes 786440 | tf_op jit(solution)/shard_map/adjoint_to_chip/ppermute | solution.py:411
  50.9 2.3 %collective-permute-done.26.across = f32[8,64,128]{2,1,0:T(8,128)S(1)} collective-permute-done((f32[8,64,128]{2,1,0:T(8,128)S(1)}, f32[8,64,128]{2,1,0:T(8,128)S(1)}, u32[]{:S(2)}, u32[]{:S(2)}) %collective-permute-start.26) | collective-permute-done | bytes 262176 | tf_op jit(solution)/shard_map/state_to_chip/ppermute | solution.py:411
  53.2 1.0 %forward3.1 = (f32[8,32,128]{2,1,0:T(8,128)S(1)}, f32[8,32,128]{2,1,0:T(8,128)S(1)}, f32[8,32,128]{2,1,0:T(8,128)S(1)}, f32[8,32,128]{2,1,0:T(8,128)S(1)}) custom-call(f32[8,64,128]{2,1,0:T(8,128)S(1)} %get-tuple-element.82.own, f32[8,64,128]{2,1,0:T(8,128)S(1)} %collective-permute-done.26.across, f32[8,64,128]{2,1,0:T(8,128)S(1)} %collective-permute-done.27.partner, ...), custom_call_target="tpu_custom_call" | custom-call | flops 13107200 | bytes 1048576 | tf_op jit(solution)/shard_map/forward3/pallas_call | solution.py:26
  54.2 0.5 collective-permute-start.28
  54.7 1.1 %collective-permute-start.29 = (f32[8,32,128]{2,1,0:T(8,128)S(1)}, f32[8,32,128]{2,1,0:T(8,128)S(1)}, u32[]{:S(2)}, u32[]{:S(2)}) collective-permute-start(f32[8,32,128]{2,1,0:T(8,128)S(1)} %get-tuple-element.86), channel_id=1, source_target_pairs={{0,16},{8,24},{16,0},{24,8},{1,17},{9,25},{17,1},{25,9},{2,18},{10... | collective-permute-start | bytes 393224 | tf_op jit(solution)/shard_map/grad_to_2/ppermute | solution.py:421
  55.9 1.9 %collective-permute-start.30 = (f32[8,32,128]{2,1,0:T(8,128)S(1)}, f32[8,32,128]{2,1,0:T(8,128)S(1)}, u32[]{:S(2)}, u32[]{:S(2)}) collective-permute-start(f32[8,32,128]{2,1,0:T(8,128)S(1)} %get-tuple-element.87), channel_id=1, source_target_pairs={{0,24},{8,16},{16,8},{24,0},{1,25},{9,17},{17,9},{25,1},{2,26},{10... | collective-permute-start | bytes 393224 | tf_op jit(solution)/shard_map/grad_to_3/ppermute | solution.py:421
  57.8 1.7 %backward3.1 = (f32[8,64,128]{2,1,0:T(8,128)}, f32[8,64,128]{2,1,0:T(8,128)}, f32[8,128]{1,0:T(8,128)S(1)}) custom-call(f32[8,64,128]{2,1,0:T(8,128)S(1)} %get-tuple-element.78.own, f32[8,64,128]{2,1,0:T(8,128)S(1)} %collective-permute-done.24.across, f32[8,64,128]{2,1,0:T(8,128)S(1)} %collective-permute-done.25.partner, ...), custom_call_target="tpu_custom_call" | custom-call | flops 13107200 | bytes 1048576 | tf_op jit(solution)/shard_map/backward3/pallas_call | solution.py:26
  59.5 0.6 collective-permute-done.28.refs_1_
  60.1 2.1 %collective-permute-done.29.refs_2_ = f32[8,32,128]{2,1,0:T(8,128)S(1)} collective-permute-done((f32[8,32,128]{2,1,0:T(8,128)S(1)}, f32[8,32,128]{2,1,0:T(8,128)S(1)}, u32[]{:S(2)}, u32[]{:S(2)}) %collective-permute-start.29) | collective-permute-done | bytes 131104 | tf_op jit(solution)/shard_map/grad_to_2/ppermute | solution.py:421
  62.2 0.7 %total.1 = f32[8,32,128]{2,1,0:T(8,128)} custom-call(f32[8,32,128]{2,1,0:T(8,128)S(1)} %get-tuple-element.84.refs_0_, f32[8,32,128]{2,1,0:T(8,128)S(1)} %collective-permute-done.28.refs_1_, f32[8,32,128]{2,1,0:T(8,128)S(1)} %collective-permute-done.29.refs_2_, f32[8,32,128]{2,1,0:T(8,128)S(1)} %collective-permute-done.30.refs_3_, ...), custom_call_target="tpu_custom_call" | custom-call | flops 1048576 | bytes 1048576 | tf_op jit(solution)/shard_map/total/pallas_call | solution.py:26
  (33 shorter events, 0.2 us)
Async XLA Ops:
  2.8 6.8 %collective-permute-start.2 = (f32[9,32,128]{2,1,0:T(8,128)S(1)}, f32[9,32,128]{2,1,0:T(8,128)S(1)}, u32[]{:S(2)}, u32[]{:S(2)}) collective-permute-start(f32[9,32,128]{2,1,0:T(8,128)S(1)} %get-tuple-element.49), channel_id=1, source_target_pairs={{0,8},{8,0},{16,24},{24,16},{1,9},{9,1},{17,25},{25,17},{2,10},{10... | collective-permute-start | bytes 442376 | tf_op jit(solution)/shard_map/wz_to_1/ppermute | solution.py:421
  5.7 5.6 %collective-permute-start.3 = (f32[8,32,128]{2,1,0:T(8,128)S(1)}, f32[8,32,128]{2,1,0:T(8,128)S(1)}, u32[]{:S(2)}, u32[]{:S(2)}) collective-permute-start(f32[8,32,128]{2,1,0:T(8,128)S(1)} %get-tuple-element.50.own.refs_0_), channel_id=1, source_target_pairs={{0,16},{8,24},{16,0},{24,8},{1,17},{9,25},{17,1},{25,9},{2,18},{10... | collective-permute-start | bytes 393224 | tf_op jit(solution)/shard_map/wx_to_2/ppermute | solution.py:421
  7.2 9.8 %collective-permute-start = (f32[8,64,128]{2,1,0:T(8,128)S(1)}, f32[8,64,128]{2,1,0:T(8,128)S(1)}, u32[]{:S(2)}, u32[]{:S(2)}) collective-permute-start(f32[8,64,128]{2,1,0:T(8,128)S(1)} %get-tuple-element.48.own.previous), channel_id=1, source_target_pairs={{0,1},{1,0},{2,3},{3,2},{4,5},{5,4},{6,7},{7,6},{8,9},{9,8},{10,11... | collective-permute-start | bytes 786440 | tf_op jit(solution)/shard_map/state_to_core/ppermute | solution.py:407
  7.2 11.8 %collective-permute-start.1 = (f32[8,64,128]{2,1,0:T(8,128)S(1)}, f32[8,64,128]{2,1,0:T(8,128)S(1)}, u32[]{:S(2)}, u32[]{:S(2)}) collective-permute-start(f32[8,64,128]{2,1,0:T(8,128)S(1)} %get-tuple-element.48.own.previous), channel_id=1, source_target_pairs={{0,8},{1,2},{2,1},{3,4},{4,3},{5,6},{6,5},{7,15},{8,0},{9,10},{10,... | collective-permute-start | bytes 786440 | tf_op jit(solution)/shard_map/state_to_chip/ppermute | solution.py:411
  7.8 6.2 %collective-permute-start.9 = (f32[8,32,128]{2,1,0:T(8,128)S(1)}, f32[8,32,128]{2,1,0:T(8,128)S(1)}, u32[]{:S(2)}, u32[]{:S(2)}) collective-permute-start(f32[8,32,128]{2,1,0:T(8,128)S(1)} %get-tuple-element.57.own.refs_3_), channel_id=1, source_target_pairs={{0,16},{8,24},{16,0},{24,8},{1,17},{9,25},{17,1},{25,9},{2,18},{10... | collective-permute-start | bytes 393224 | tf_op jit(solution)/shard_map/wy_to_2/ppermute | solution.py:421
  9.5 6.9 %collective-permute-start.5 = (f32[8,32,128]{2,1,0:T(8,128)S(1)}, f32[8,32,128]{2,1,0:T(8,128)S(1)}, u32[]{:S(2)}, u32[]{:S(2)}) collective-permute-start(f32[8,32,128]{2,1,0:T(8,128)S(1)} %get-tuple-element.51.own.refs_0_), channel_id=1, source_target_pairs={{0,8},{8,0},{16,24},{24,16},{1,9},{9,1},{17,25},{25,17},{2,10},{10... | collective-permute-start | bytes 393224 | tf_op jit(solution)/shard_map/speed_to_1/ppermute | solution.py:421
  11.3 11.1 %collective-permute-start.11 = (f32[2,8,32,128]{3,2,1,0:T(8,128)S(1)}, f32[2,8,32,128]{3,2,1,0:T(8,128)S(1)}, u32[]{:S(2)}, u32[]{:S(2)}) collective-permute-start(f32[2,8,32,128]{3,2,1,0:T(8,128)S(1)} %pair_wz.1), channel_id=1, source_target_pairs={{0,16},{8,24},{16,0},{24,8},{1,17},{9,25},{17,1},{25,9},{2,18},{10... | collective-permute-start | bytes 786440 | tf_op jit(solution)/shard_map/wz_to_2/ppermute | solution.py:421
  13.9 6.3 %collective-permute-start.4 = (f32[8,32,128]{2,1,0:T(8,128)S(1)}, f32[8,32,128]{2,1,0:T(8,128)S(1)}, u32[]{:S(2)}, u32[]{:S(2)}) collective-permute-start(f32[8,32,128]{2,1,0:T(8,128)S(1)} %relay_wx.1.refs_0_), channel_id=1, source_target_pairs={{0,8},{8,0},{16,24},{24,16},{1,9},{9,1},{17,25},{25,17},{2,10},{10... | collective-permute-start | bytes 393224 | tf_op jit(solution)/shard_map/wx_to_1/ppermute | solution.py:421
  16.4 6.1 %collective-permute-start.10 = (f32[8,32,128]{2,1,0:T(8,128)S(1)}, f32[8,32,128]{2,1,0:T(8,128)S(1)}, u32[]{:S(2)}, u32[]{:S(2)}) collective-permute-start(f32[8,32,128]{2,1,0:T(8,128)S(1)} %relay_wy.1), channel_id=1, source_target_pairs={{0,8},{8,0},{16,24},{24,16},{1,9},{9,1},{17,25},{25,17},{2,10},{10... | collective-permute-start | bytes 393224 | tf_op jit(solution)/shard_map/wy_to_1/ppermute | solution.py:421
  17.0 8.7 %copy-start = (f32[1,8,64,128]{3,2,1,0:T(8,128)S(1)}, f32[1,8,64,128]{3,2,1,0:T(8,128)}, u32[]{:S(2)}) copy-start(f32[1,8,64,128]{3,2,1,0:T(8,128)} %param.21) | copy-start | bytes 786436
  17.0 8.6 %collective-permute-start.6 = (f32[2,8,32,128]{3,2,1,0:T(8,128)S(1)}, f32[2,8,32,128]{3,2,1,0:T(8,128)S(1)}, u32[]{:S(2)}, u32[]{:S(2)}) collective-permute-start(f32[2,8,32,128]{3,2,1,0:T(8,128)S(1)} %pair_speed.1), channel_id=1, source_target_pairs={{0,16},{8,24},{16,0},{24,8},{1,17},{9,25},{17,1},{25,9},{2,18},{10... | collective-permute-start | bytes 786440 | tf_op jit(solution)/shard_map/speed_to_2/ppermute | solution.py:421
  21.1 8.8 %copy-start.3 = (f32[1,16,128]{2,1,0:T(8,128)S(1)}, f32[1,16,128]{2,1,0:T(8,128)}, u32[]{:S(2)}) copy-start(f32[1,16,128]{2,1,0:T(8,128)} %traces.1) | copy-start | bytes 24580
  21.1 8.8 %copy-start.4 = (f32[1,16]{1,0:T(1,128)S(1)}, f32[1,16]{1,0:T(1,128)}, u32[]{:S(2)}) copy-start(f32[1,16]{1,0:T(1,128)} %wavelet.1) | copy-start | bytes 196
  21.1 8.8 %copy-start.5 = (s32[1,128]{1,0:T(1,128)S(1)}, s32[1,128]{1,0:T(1,128)}, u32[]{:S(2)}) copy-start(s32[1,128]{1,0:T(1,128)} %rx.1) | copy-start | bytes 1540
  21.1 8.8 %copy-start.6 = (s32[1,128]{1,0:T(1,128)S(1)}, s32[1,128]{1,0:T(1,128)}, u32[]{:S(2)}) copy-start(s32[1,128]{1,0:T(1,128)} %ry.1) | copy-start | bytes 1540
  21.1 8.8 %copy-start.7 = (s32[1,128]{1,0:T(1,128)S(1)}, s32[1,128]{1,0:T(1,128)}, u32[]{:S(2)}) copy-start(s32[1,128]{1,0:T(1,128)} %rz.1) | copy-start | bytes 1540
  21.1 10.3 %copy-start.1 = (f32[1,8,64,128]{3,2,1,0:T(8,128)S(1)}, f32[1,8,64,128]{3,2,1,0:T(8,128)}, u32[]{:S(2)}) copy-start(f32[1,8,64,128]{3,2,1,0:T(8,128)} %param.18) | copy-start | bytes 786436
  23.0 3.5 %collective-permute-start.12 = (f32[3,2,64,128]{3,2,1,0:T(8,128)S(1)}, f32[3,2,64,128]{3,2,1,0:T(8,128)S(1)}, u32[]{:S(2)}, u32[]{:S(2)}) collective-permute-start(f32[3,2,64,128]{3,2,1,0:T(8,128)S(1)} %get-tuple-element.59), channel_id=1, source_target_pairs={{0,1},{1,0},{2,3},{3,2},{4,5},{5,4},{6,7},{7,6},{8,9},{9,8},{10,11... | collective-permute-start | bytes 589832 | tf_op jit(solution)/shard_map/edge_to_core/ppermute | solution.py:407
  23.1 7.9 %collective-permute-start.13 = (f32[3,2,64,128]{3,2,1,0:T(8,128)S(1)}, f32[3,2,64,128]{3,2,1,0:T(8,128)S(1)}, u32[]{:S(2)}, u32[]{:S(2)}) collective-permute-start(f32[3,2,64,128]{3,2,1,0:T(8,128)S(1)} %get-tuple-element.60), channel_id=1, source_target_pairs={{0,1},{1,0},{2,3},{3,2},{4,5},{5,4},{6,7},{7,6},{8,9},{9,8},{10,11... | collective-permute-start | bytes 589832 | tf_op jit(solution)/shard_map/edge_to_core/ppermute | solution.py:407
  23.6 7.4 %collective-permute-start.14 = (f32[3,2,64,128]{3,2,1,0:T(8,128)S(1)}, f32[3,2,64,128]{3,2,1,0:T(8,128)S(1)}, u32[]{:S(2)}, u32[]{:S(2)}) collective-permute-start(f32[3,2,64,128]{3,2,1,0:T(8,128)S(1)} %get-tuple-element.61), channel_id=1, source_target_pairs={{0,16},{1,2},{2,1},{3,4},{4,3},{5,6},{6,5},{7,23},{8,24},{9,10},{1... | collective-permute-start | bytes 589832 | tf_op jit(solution)/shard_map/edge_to_chip/ppermute | solution.py:411
  24.3 7.1 %collective-permute-start.15 = (f32[3,2,64,128]{3,2,1,0:T(8,128)S(1)}, f32[3,2,64,128]{3,2,1,0:T(8,128)S(1)}, u32[]{:S(2)}, u32[]{:S(2)}) collective-permute-start(f32[3,2,64,128]{3,2,1,0:T(8,128)S(1)} %get-tuple-element.62), channel_id=1, source_target_pairs={{0,16},{1,2},{2,1},{3,4},{4,3},{5,6},{6,5},{7,23},{8,24},{9,10},{1... | collective-permute-start | bytes 589832 | tf_op jit(solution)/shard_map/edge_to_chip/ppermute | solution.py:411
  25.7 8.5 %collective-permute-start.7 = (f32[8,64,128]{2,1,0:T(8,128)S(1)}, f32[8,64,128]{2,1,0:T(8,128)S(1)}, u32[]{:S(2)}, u32[]{:S(2)}) collective-permute-start(f32[8,64,128]{2,1,0:T(8,128)S(1)} %get-tuple-element.53.own), channel_id=1, source_target_pairs={{0,16},{1,2},{2,1},{3,4},{4,3},{5,6},{6,5},{7,23},{8,24},{9,10},{1... | collective-permute-start | bytes 786440 | tf_op jit(solution)/shard_map/adjoint_to_chip/ppermute | solution.py:411
  26.5 7.7 %collective-permute-start.8 = (f32[8,64,128]{2,1,0:T(8,128)S(1)}, f32[8,64,128]{2,1,0:T(8,128)S(1)}, u32[]{:S(2)}, u32[]{:S(2)}) collective-permute-start(f32[8,64,128]{2,1,0:T(8,128)S(1)} %get-tuple-element.53.own), channel_id=1, source_target_pairs={{0,1},{1,0},{2,3},{3,2},{4,5},{5,4},{6,7},{7,6},{8,9},{9,8},{10,11... | collective-permute-start | bytes 786440 | tf_op jit(solution)/shard_map/adjoint_to_core/ppermute | solution.py:407
  31.4 2.8 %copy-start.2 = (f32[1,8,64,128]{3,2,1,0:T(8,128)S(1)}, f32[1,8,64,128]{3,2,1,0:T(8,128)}, u32[]{:S(2)}) copy-start(f32[1,8,64,128]{3,2,1,0:T(8,128)} %param.20) | copy-start | bytes 786436
  31.9 6.4 %collective-permute-start.20 = (f32[8,64,128]{2,1,0:T(8,128)S(1)}, f32[8,64,128]{2,1,0:T(8,128)S(1)}, u32[]{:S(2)}, u32[]{:S(2)}) collective-permute-start(f32[8,64,128]{2,1,0:T(8,128)S(1)} %get-tuple-element.74.own.previous), channel_id=1, source_target_pairs={{0,16},{1,2},{2,1},{3,4},{4,3},{5,6},{6,5},{7,23},{8,24},{9,10},{1... | collective-permute-start | bytes 786440 | tf_op jit(solution)/shard_map/state_to_chip/ppermute | solution.py:411
  32.7 5.7 %collective-permute-start.21 = (f32[8,64,128]{2,1,0:T(8,128)S(1)}, f32[8,64,128]{2,1,0:T(8,128)S(1)}, u32[]{:S(2)}, u32[]{:S(2)}) collective-permute-start(f32[8,64,128]{2,1,0:T(8,128)S(1)} %get-tuple-element.74.own.previous), channel_id=1, source_target_pairs={{0,1},{1,0},{2,3},{3,2},{4,5},{5,4},{6,7},{7,6},{8,9},{9,8},{10,11... | collective-permute-start | bytes 786440 | tf_op jit(solution)/shard_map/state_to_core/ppermute | solution.py:407
  35.2 6.4 %collective-permute-start.16 = (f32[8,64,128]{2,1,0:T(8,128)S(1)}, f32[8,64,128]{2,1,0:T(8,128)S(1)}, u32[]{:S(2)}, u32[]{:S(2)}) collective-permute-start(f32[8,64,128]{2,1,0:T(8,128)S(1)} %get-tuple-element.69.own), channel_id=1, source_target_pairs={{0,16},{1,2},{2,1},{3,4},{4,3},{5,6},{6,5},{7,23},{8,24},{9,10},{1... | collective-permute-start | bytes 786440 | tf_op jit(solution)/shard_map/adjoint_to_chip/ppermute | solution.py:411
  36.0 5.7 %collective-permute-start.17 = (f32[8,64,128]{2,1,0:T(8,128)S(1)}, f32[8,64,128]{2,1,0:T(8,128)S(1)}, u32[]{:S(2)}, u32[]{:S(2)}) collective-permute-start(f32[8,64,128]{2,1,0:T(8,128)S(1)} %get-tuple-element.69.own), channel_id=1, source_target_pairs={{0,1},{1,0},{2,3},{3,2},{4,5},{5,4},{6,7},{7,6},{8,9},{9,8},{10,11... | collective-permute-start | bytes 786440 | tf_op jit(solution)/shard_map/adjoint_to_core/ppermute | solution.py:407
  39.3 6.4 %collective-permute-start.22 = (f32[8,64,128]{2,1,0:T(8,128)S(1)}, f32[8,64,128]{2,1,0:T(8,128)S(1)}, u32[]{:S(2)}, u32[]{:S(2)}) collective-permute-start(f32[8,64,128]{2,1,0:T(8,128)S(1)} %get-tuple-element.76.own), channel_id=1, source_target_pairs={{0,16},{1,2},{2,1},{3,4},{4,3},{5,6},{6,5},{7,23},{8,24},{9,10},{1... | collective-permute-start | bytes 786440 | tf_op jit(solution)/shard_map/state_to_chip/ppermute | solution.py:411
  40.1 5.7 %collective-permute-start.23 = (f32[8,64,128]{2,1,0:T(8,128)S(1)}, f32[8,64,128]{2,1,0:T(8,128)S(1)}, u32[]{:S(2)}, u32[]{:S(2)}) collective-permute-start(f32[8,64,128]{2,1,0:T(8,128)S(1)} %get-tuple-element.76.own), channel_id=1, source_target_pairs={{0,1},{1,0},{2,3},{3,2},{4,5},{5,4},{6,7},{7,6},{8,9},{9,8},{10,11... | collective-permute-start | bytes 786440 | tf_op jit(solution)/shard_map/state_to_core/ppermute | solution.py:407
  42.6 6.4 %collective-permute-start.18 = (f32[8,64,128]{2,1,0:T(8,128)S(1)}, f32[8,64,128]{2,1,0:T(8,128)S(1)}, u32[]{:S(2)}, u32[]{:S(2)}) collective-permute-start(f32[8,64,128]{2,1,0:T(8,128)S(1)} %get-tuple-element.71.own), channel_id=1, source_target_pairs={{0,16},{1,2},{2,1},{3,4},{4,3},{5,6},{6,5},{7,23},{8,24},{9,10},{1... | collective-permute-start | bytes 786440 | tf_op jit(solution)/shard_map/adjoint_to_chip/ppermute | solution.py:411
  43.4 5.7 %collective-permute-start.19 = (f32[8,64,128]{2,1,0:T(8,128)S(1)}, f32[8,64,128]{2,1,0:T(8,128)S(1)}, u32[]{:S(2)}, u32[]{:S(2)}) collective-permute-start(f32[8,64,128]{2,1,0:T(8,128)S(1)} %get-tuple-element.71.own), channel_id=1, source_target_pairs={{0,1},{1,0},{2,3},{3,2},{4,5},{5,4},{6,7},{7,6},{8,9},{9,8},{10,11... | collective-permute-start | bytes 786440 | tf_op jit(solution)/shard_map/adjoint_to_core/ppermute | solution.py:407
  46.8 6.4 %collective-permute-start.26 = (f32[8,64,128]{2,1,0:T(8,128)S(1)}, f32[8,64,128]{2,1,0:T(8,128)S(1)}, u32[]{:S(2)}, u32[]{:S(2)}) collective-permute-start(f32[8,64,128]{2,1,0:T(8,128)S(1)} %get-tuple-element.82.own), channel_id=1, source_target_pairs={{0,16},{1,2},{2,1},{3,4},{4,3},{5,6},{6,5},{7,23},{8,24},{9,10},{1... | collective-permute-start | bytes 786440 | tf_op jit(solution)/shard_map/state_to_chip/ppermute | solution.py:411
  47.6 5.7 %collective-permute-start.27 = (f32[8,64,128]{2,1,0:T(8,128)S(1)}, f32[8,64,128]{2,1,0:T(8,128)S(1)}, u32[]{:S(2)}, u32[]{:S(2)}) collective-permute-start(f32[8,64,128]{2,1,0:T(8,128)S(1)} %get-tuple-element.82.own), channel_id=1, source_target_pairs={{0,1},{1,0},{2,3},{3,2},{4,5},{5,4},{6,7},{7,6},{8,9},{9,8},{10,11... | collective-permute-start | bytes 786440 | tf_op jit(solution)/shard_map/state_to_core/ppermute | solution.py:407
  50.1 7.7 %collective-permute-start.24 = (f32[8,64,128]{2,1,0:T(8,128)S(1)}, f32[8,64,128]{2,1,0:T(8,128)S(1)}, u32[]{:S(2)}, u32[]{:S(2)}) collective-permute-start(f32[8,64,128]{2,1,0:T(8,128)S(1)} %get-tuple-element.78.own), channel_id=1, source_target_pairs={{0,16},{1,2},{2,1},{3,4},{4,3},{5,6},{6,5},{7,23},{8,24},{9,10},{1... | collective-permute-start | bytes 786440 | tf_op jit(solution)/shard_map/adjoint_to_chip/ppermute | solution.py:411
  50.9 6.9 %collective-permute-start.25 = (f32[8,64,128]{2,1,0:T(8,128)S(1)}, f32[8,64,128]{2,1,0:T(8,128)S(1)}, u32[]{:S(2)}, u32[]{:S(2)}) collective-permute-start(f32[8,64,128]{2,1,0:T(8,128)S(1)} %get-tuple-element.78.own), channel_id=1, source_target_pairs={{0,1},{1,0},{2,3},{3,2},{4,5},{5,4},{6,7},{7,6},{8,9},{9,8},{10,11... | collective-permute-start | bytes 786440 | tf_op jit(solution)/shard_map/adjoint_to_core/ppermute | solution.py:407
  54.2 5.9 %collective-permute-start.28 = (f32[8,32,128]{2,1,0:T(8,128)S(1)}, f32[8,32,128]{2,1,0:T(8,128)S(1)}, u32[]{:S(2)}, u32[]{:S(2)}) collective-permute-start(f32[8,32,128]{2,1,0:T(8,128)S(1)} %get-tuple-element.85), channel_id=1, source_target_pairs={{0,8},{8,0},{16,24},{24,16},{1,9},{9,1},{17,25},{25,17},{2,10},{10... | collective-permute-start | bytes 393224 | tf_op jit(solution)/shard_map/grad_to_1/ppermute | solution.py:421
  54.7 7.4 %collective-permute-start.29 = (f32[8,32,128]{2,1,0:T(8,128)S(1)}, f32[8,32,128]{2,1,0:T(8,128)S(1)}, u32[]{:S(2)}, u32[]{:S(2)}) collective-permute-start(f32[8,32,128]{2,1,0:T(8,128)S(1)} %get-tuple-element.86), channel_id=1, source_target_pairs={{0,16},{8,24},{16,0},{24,8},{1,17},{9,25},{17,1},{25,9},{2,18},{10... | collective-permute-start | bytes 393224 | tf_op jit(solution)/shard_map/grad_to_2/ppermute | solution.py:421
  55.9 6.3 %collective-permute-start.30 = (f32[8,32,128]{2,1,0:T(8,128)S(1)}, f32[8,32,128]{2,1,0:T(8,128)S(1)}, u32[]{:S(2)}, u32[]{:S(2)}) collective-permute-start(f32[8,32,128]{2,1,0:T(8,128)S(1)} %get-tuple-element.87), channel_id=1, source_target_pairs={{0,24},{8,16},{16,8},{24,0},{1,25},{9,17},{17,9},{25,1},{2,26},{10... | collective-permute-start | bytes 393224 | tf_op jit(solution)/shard_map/grad_to_3/ppermute | solution.py:421

commit v7 on v6

--- a/solution.py
+++ b/solution.py
@@ -181,11 +181,10 @@
         slope[0, i] = stencil(lambda k: wide[i + 4 + k])
 
 
-def inject_kernel(step, sx, sy, sz, wavelet, rx, ry, rz, traces, src, inj):
+def source_kernel(step, sx, sy, sz, wavelet, src):
     rows, width, depth = src.shape[1:]
     start, sx, sy, sz = (ref[...].reshape(1, 1) for ref in (step, sx, sy, sz))
     first = lax.axis_index("blk") * rows
-    shape = (rows, width, depth)
     plane = (width, depth)
     here = (lax.broadcasted_iota(jnp.int32, plane, 0) == sy) & (
         lax.broadcasted_iota(jnp.int32, plane, 1) == sz
@@ -196,6 +195,12 @@
         value = jnp.sum(chosen, axis=1, keepdims=True)
         for r in range(rows):
             src[t, r] = jnp.where(here & (sx == first + r), value, 0.0)
+
+
+def inject_kernel(step, rx, ry, rz, traces, inj):
+    rows, width, depth = inj.shape[1:]
+    start = step[...].reshape(1, 1)
+    first = lax.axis_index("blk") * rows
     receivers = rx.shape[1]
     local = rx[...] - first
     cell = jnp.where((local >= 0) & (local < rows), local * width + ry[...], -1)
@@ -215,7 +220,7 @@
             precision=lax.Precision.HIGHEST,
             preferred_element_type=jnp.float32,
         )
-        inj[t] = added.reshape(shape)
+        inj[t] = added.reshape(rows, width, depth)
 
 
 def relay_kernel(parts, wz_first, own, received, *refs):
@@ -493,14 +498,18 @@
     )
     edges_a = [across_chips(a, "edge") for a in edges[:2]]
     edges_p = [to_partner(a, "edge") for a in edges[2:]]
-    src, inj = call(
+    src = call(
+        "source",
+        source_kernel,
+        f32(STEPS - 1, rows, width, depth),
+        [step_index, source_x, source_y, source_z, wavelet],
+    )
+    inj = call(
         "inject",
         inject_kernel,
-        (f32(STEPS - 1, rows, width, depth), f32(STEPS, rows, width, depth)),
-        [step_index, source_x, source_y, source_z, wavelet, receiver_x, receiver_y, receiver_z]
-        + [residual_traces],
-    )
-
+        f32(STEPS, rows, width, depth),
+        [step_index, receiver_x, receiver_y, receiver_z, residual_traces],
+    )
     speed, operand = call(
         "speed",
         functools.partial(speed_kernel, speed_places, parts),

time: 63 us -> 63.1 us (level)
  starting transfers between devices: 26.2 us -> 27 us
  waiting for transfers between devices: 19.4 us -> 18.6 us
    ppermute x10, waiting for transfers between devices: 10.6 us -> 9.71 us  [across_chips(): return lax.ppermute(array, ('shot', 'blk'), chip_pairs(hop))]
    pallas_call x19 -> x20, Pallas kernels: 13.1 us -> 13.3 us  [call(): pl.pallas_call(body, name=name, out_shape=outs, in_specs=[s for _, s in p...]
  transfers between devices with their start and end apart: 31 -> 31, of which waited for: 14 -> 13; matrix products, arithmetic and copies ran while one was open for 0% -> 0% of each run, Pallas kernels for 17% -> 18%
where the time goes in v7:
time: 63.1 us; the launch traced here: 63 us
  starting transfers between devices  27 us (43%)
  waiting for transfers between devices  18.6 us (29%)
  Pallas kernels  13.3 us (21%)
  between operations  4.1 us (6%)
    ppermute x11, starting transfers between devices, to_owners(): return lax.ppermute(array, 'shot', [(i, i ^ k) for i in range(shots)])  15.6 us
    pallas_call x20, Pallas kernels, call(): pl.pallas_call(body, name=name, out_shape=outs, in_specs=[s for _, s in p...  13.3 us
    ppermute x10, waiting for transfers between devices, across_chips(): return lax.ppermute(array, ('shot', 'blk'), chip_pairs(hop))  9.71 us
    ppermute x11, waiting for transfers between devices, to_owners(): return lax.ppermute(array, 'shot', [(i, i ^ k) for i in range(shots)])  8.83 us
    ppermute x10, starting transfers between devices, across_chips(): return lax.ppermute(array, ('shot', 'blk'), chip_pairs(hop))  8.62 us
    ppermute x10, starting transfers between devices, to_partner(): return lax.ppermute(array, 'blk', core_pairs)  2.74 us
  transfers between devices with their start and end apart: 31, of which 13 were waited for; matrix products, arithmetic and copies ran while one was open for 0% of the time, Pallas kernels for 18%

profile of v7, /device:TPU:0, one launch (start us, length us, event | category | flops | bytes accessed | tf_op | source)
XLA Modules:
  0.0 63.0 jit_solution(16665993840147535169)
XLA Ops:
  1.3 1.4 %owner.1 = (f32[8,32,128]{2,1,0:T(8,128)S(1)}, f32[8,32,128]{2,1,0:T(8,128)S(1)}, f32[8,32,128]{2,1,0:T(8,128)S(1)}, f32[8,32,128]{2,1,0:T(8,128)S(1)}, f32[8,64,128]{2,1,0:T(8,128)S(1)}) custom-call(f32[8,32,128]{2,1,0:T(8,128)} %eps.1, f32[8,32,128]{2,1,0:T(8,128)} %tilt.1, f32[8,32,128]{2,1,0:T(8,128)} %azimuth.1, f32[8,32,128]{2,1,0:T(8,128)} %speed.2, ...), custom_call_target="tpu_custom_call" | custom-call | flops 1048576 | bytes 1048576 | tf_op jit(solution)/shard_map/owner/pallas_call | solution.py:26
  2.7 0.1 first.1
  2.8 2.9 %collective-permute-start.2 = (f32[9,32,128]{2,1,0:T(8,128)S(1)}, f32[9,32,128]{2,1,0:T(8,128)S(1)}, u32[]{:S(2)}, u32[]{:S(2)}) collective-permute-start(f32[9,32,128]{2,1,0:T(8,128)S(1)} %get-tuple-element.47), channel_id=1, source_target_pairs={{0,8},{8,0},{16,24},{24,16},{1,9},{9,1},{17,25},{25,17},{2,10},{10... | collective-permute-start | bytes 442376 | tf_op jit(solution)/shard_map/wz_to_1/ppermute | solution.py:426
  5.7 1.5 %collective-permute-start.3 = (f32[8,32,128]{2,1,0:T(8,128)S(1)}, f32[8,32,128]{2,1,0:T(8,128)S(1)}, u32[]{:S(2)}, u32[]{:S(2)}) collective-permute-start(f32[8,32,128]{2,1,0:T(8,128)S(1)} %get-tuple-element.48.own.refs_0_), channel_id=1, source_target_pairs={{0,16},{8,24},{16,0},{24,8},{1,17},{9,25},{17,1},{25,9},{2,18},{10... | collective-permute-start | bytes 393224 | tf_op jit(solution)/shard_map/wx_to_2/ppermute | solution.py:426
  7.2 0.0 collective-permute-start
  7.2 0.5 collective-permute-start.1
  7.8 0.1 collective-permute-start.9
  7.8 1.7 %collective-permute-done.2.wz_first.received.refs_7_ = f32[9,32,128]{2,1,0:T(8,128)S(1)} collective-permute-done((f32[9,32,128]{2,1,0:T(8,128)S(1)}, f32[9,32,128]{2,1,0:T(8,128)S(1)}, u32[]{:S(2)}, u32[]{:S(2)}) %collective-permute-start.2) | collective-permute-done | bytes 147488 | tf_op jit(solution)/shard_map/wz_to_1/ppermute | solution.py:426
  9.5 1.7 %collective-permute-start.5 = (f32[8,32,128]{2,1,0:T(8,128)S(1)}, f32[8,32,128]{2,1,0:T(8,128)S(1)}, u32[]{:S(2)}, u32[]{:S(2)}) collective-permute-start(f32[8,32,128]{2,1,0:T(8,128)S(1)} %get-tuple-element.49.own.refs_0_), channel_id=1, source_target_pairs={{0,8},{8,0},{16,24},{24,16},{1,9},{9,1},{17,25},{25,17},{2,10},{10... | collective-permute-start | bytes 393224 | tf_op jit(solution)/shard_map/speed_to_1/ppermute | solution.py:426
  11.3 0.0 collective-permute-done.3.received.refs_2_
  11.3 1.6 %collective-permute-start.11 = (f32[2,8,32,128]{3,2,1,0:T(8,128)S(1)}, f32[2,8,32,128]{3,2,1,0:T(8,128)S(1)}, u32[]{:S(2)}, u32[]{:S(2)}) collective-permute-start(f32[2,8,32,128]{3,2,1,0:T(8,128)S(1)} %pair_wz.1), channel_id=1, source_target_pairs={{0,16},{8,24},{16,0},{24,8},{1,17},{9,25},{17,1},{25,9},{2,18},{10... | collective-permute-start | bytes 786440 | tf_op jit(solution)/shard_map/wz_to_2/ppermute | solution.py:426
  12.9 1.0 %collective-permute-done.9.received.refs_5_ = f32[8,32,128]{2,1,0:T(8,128)S(1)} collective-permute-done((f32[8,32,128]{2,1,0:T(8,128)S(1)}, f32[8,32,128]{2,1,0:T(8,128)S(1)}, u32[]{:S(2)}, u32[]{:S(2)}) %collective-permute-start.9) | collective-permute-done | bytes 131104 | tf_op jit(solution)/shard_map/wy_to_2/ppermute | solution.py:426
  13.9 1.6 %collective-permute-start.4 = (f32[8,32,128]{2,1,0:T(8,128)S(1)}, f32[8,32,128]{2,1,0:T(8,128)S(1)}, u32[]{:S(2)}, u32[]{:S(2)}) collective-permute-start(f32[8,32,128]{2,1,0:T(8,128)S(1)} %relay_wx.1.refs_0_), channel_id=1, source_target_pairs={{0,8},{8,0},{16,24},{24,16},{1,9},{9,1},{17,25},{25,17},{2,10},{10... | collective-permute-start | bytes 393224 | tf_op jit(solution)/shard_map/wx_to_1/ppermute | solution.py:426
  15.6 0.8 %collective-permute-done.5.refs_1_.received = f32[8,32,128]{2,1,0:T(8,128)S(1)} collective-permute-done((f32[8,32,128]{2,1,0:T(8,128)S(1)}, f32[8,32,128]{2,1,0:T(8,128)S(1)}, u32[]{:S(2)}, u32[]{:S(2)}) %collective-permute-start.5) | collective-permute-done | bytes 131104 | tf_op jit(solution)/shard_map/speed_to_1/ppermute | solution.py:426
  16.4 0.5 collective-permute-start.10
  17.0 0.0 copy-start
  17.0 0.0 collective-permute-done.partner
  17.0 2.1 %collective-permute-start.6 = (f32[2,8,32,128]{3,2,1,0:T(8,128)S(1)}, f32[2,8,32,128]{3,2,1,0:T(8,128)S(1)}, u32[]{:S(2)}, u32[]{:S(2)}) collective-permute-start(f32[2,8,32,128]{3,2,1,0:T(8,128)S(1)} %pair_speed.1), channel_id=1, source_target_pairs={{0,16},{8,24},{16,0},{24,8},{1,17},{9,25},{17,1},{25,9},{2,18},{10... | collective-permute-start | bytes 786440 | tf_op jit(solution)/shard_map/speed_to_2/ppermute | solution.py:426
  19.0 1.2 %collective-permute-done.4.refs_0_.refs_1_ = f32[8,32,128]{2,1,0:T(8,128)S(1)} collective-permute-done((f32[8,32,128]{2,1,0:T(8,128)S(1)}, f32[8,32,128]{2,1,0:T(8,128)S(1)}, u32[]{:S(2)}, u32[]{:S(2)}) %collective-permute-start.4) | collective-permute-done | bytes 131104 | tf_op jit(solution)/shard_map/wx_to_1/ppermute | solution.py:426
  20.3 0.8 %prepare.1 = (f32[3,16,64,128]{3,2,1,0:T(8,128)S(1)}, f32[8,128]{1,0:T(8,128)S(1)}, bf16[64,128]{1,0:T(8,128)(2,1)S(1)}, bf16[256,128]{1,0:T(8,128)(2,1)S(1)}) custom-call(f32[8,128]{1,0:T(8,128)S(1)} %get-tuple-element.45.first, f32[8,64,128]{2,1,0:T(8,128)S(1)} %get-tuple-element.46.own.previous, f32[8,64,128]{2,1,0:T(8,128)S(1)} %collective-permute-done.partner, ...), custom_call_target="tpu_custom_call" | custom-call | flops 1048576 | bytes 1048576 | tf_op jit(solution)/shard_map/prepare/pallas_call | solution.py:26
  21.1 0.0 copy-start.7
  21.1 1.4 %collective-permute-done.10.refs_4_ = f32[8,32,128]{2,1,0:T(8,128)S(1)} collective-permute-done((f32[8,32,128]{2,1,0:T(8,128)S(1)}, f32[8,32,128]{2,1,0:T(8,128)S(1)}, u32[]{:S(2)}, u32[]{:S(2)}) %collective-permute-start.10) | collective-permute-done | bytes 131104 | tf_op jit(solution)/shard_map/wy_to_1/ppermute | solution.py:426
  22.5 0.0 collective-permute-done.11.refs_8_
  22.5 0.6 flux.1
  23.0 0.1 collective-permute-start.12
  23.1 0.5 collective-permute-start.13
  23.6 0.7 %collective-permute-start.14 = (f32[3,2,64,128]{3,2,1,0:T(8,128)S(1)}, f32[3,2,64,128]{3,2,1,0:T(8,128)S(1)}, u32[]{:S(2)}, u32[]{:S(2)}) collective-permute-start(f32[3,2,64,128]{3,2,1,0:T(8,128)S(1)} %get-tuple-element.59), channel_id=1, source_target_pairs={{0,16},{1,2},{2,1},{3,4},{4,3},{5,6},{6,5},{7,23},{8,24},{9,10},{1... | collective-permute-start | bytes 589832 | tf_op jit(solution)/shard_map/edge_to_chip/ppermute | solution.py:416
  24.3 1.3 %collective-permute-start.15 = (f32[3,2,64,128]{3,2,1,0:T(8,128)S(1)}, f32[3,2,64,128]{3,2,1,0:T(8,128)S(1)}, u32[]{:S(2)}, u32[]{:S(2)}) collective-permute-start(f32[3,2,64,128]{3,2,1,0:T(8,128)S(1)} %get-tuple-element.60), channel_id=1, source_target_pairs={{0,16},{1,2},{2,1},{3,4},{4,3},{5,6},{6,5},{7,23},{8,24},{9,10},{1... | collective-permute-start | bytes 589832 | tf_op jit(solution)/shard_map/edge_to_chip/ppermute | solution.py:416
  25.6 0.1 speed.3
  25.7 0.8 %collective-permute-start.7 = (f32[8,64,128]{2,1,0:T(8,128)S(1)}, f32[8,64,128]{2,1,0:T(8,128)S(1)}, u32[]{:S(2)}, u32[]{:S(2)}) collective-permute-start(f32[8,64,128]{2,1,0:T(8,128)S(1)} %get-tuple-element.51.own), channel_id=1, source_target_pairs={{0,16},{1,2},{2,1},{3,4},{4,3},{5,6},{6,5},{7,23},{8,24},{9,10},{1... | collective-permute-start | bytes 786440 | tf_op jit(solution)/shard_map/adjoint_to_chip/ppermute | solution.py:416
  26.5 0.7 %collective-permute-start.8 = (f32[8,64,128]{2,1,0:T(8,128)S(1)}, f32[8,64,128]{2,1,0:T(8,128)S(1)}, u32[]{:S(2)}, u32[]{:S(2)}) collective-permute-start(f32[8,64,128]{2,1,0:T(8,128)S(1)} %get-tuple-element.51.own), channel_id=1, source_target_pairs={{0,1},{1,0},{2,3},{3,2},{4,5},{5,4},{6,7},{7,6},{8,9},{9,8},{10,11... | collective-permute-start | bytes 786440 | tf_op jit(solution)/shard_map/adjoint_to_core/ppermute | solution.py:412
  29.9 0.2 source.1.src
  30.1 1.3 %collective-permute-done.15.edge_a1 = f32[3,2,64,128]{3,2,1,0:T(8,128)S(1)} collective-permute-done((f32[3,2,64,128]{3,2,1,0:T(8,128)S(1)}, f32[3,2,64,128]{3,2,1,0:T(8,128)S(1)}, u32[]{:S(2)}, u32[]{:S(2)}) %collective-permute-start.15) | collective-permute-done | bytes 196640 | tf_op jit(solution)/shard_map/edge_to_chip/ppermute | solution.py:416
  31.4 0.0 copy-start.6
  31.4 0.0 copy-start.2
  31.4 0.5 forward0.1
  31.9 0.8 %collective-permute-start.20 = (f32[8,64,128]{2,1,0:T(8,128)S(1)}, f32[8,64,128]{2,1,0:T(8,128)S(1)}, u32[]{:S(2)}, u32[]{:S(2)}) collective-permute-start(f32[8,64,128]{2,1,0:T(8,128)S(1)} %get-tuple-element.70.own.previous), channel_id=1, source_target_pairs={{0,16},{1,2},{2,1},{3,4},{4,3},{5,6},{6,5},{7,23},{8,24},{9,10},{1... | collective-permute-start | bytes 786440 | tf_op jit(solution)/shard_map/state_to_chip/ppermute | solution.py:416
  32.7 0.4 collective-permute-start.21
  33.2 1.1 %inject.1.inj = f32[4,8,64,128]{3,2,1,0:T(8,128)S(1)} custom-call(s32[1]{0:T(128)S(6)} %copy.22.step, s32[1,128]{1,0:T(1,128)S(1)} %copy-done.4, s32[1,128]{1,0:T(1,128)S(1)} %copy-done.5, s32[1,128]{1,0:T(1,128)S(1)} %copy-done.6, f32[1,16,128]{2,1,0:T(8,128)S(1)} %copy-done.3), custom_call_target="tpu_custom_call" | custom-call | flops 1048576 | bytes 1048576 | tf_op jit(solution)/shard_map/inject/pallas_call | solution.py:26
  34.3 1.0 %backward0.1 = (f32[8,64,128]{2,1,0:T(8,128)S(1)}, f32[8,64,128]{2,1,0:T(8,128)S(1)}) custom-call(f32[8,64,128]{2,1,0:T(8,128)S(1)} %get-tuple-element.51.own, f32[8,64,128]{2,1,0:T(8,128)S(1)} %collective-permute-done.7.across, f32[8,64,128]{2,1,0:T(8,128)S(1)} %collective-permute-done.8.partner, f32[4,16,64,128]{3,2,1,0:T(8,128)S(1)} %get-tuple-element.64.coef, ...), custom_call_target="tpu_custom_call" | custom-call | flops 13107200 | bytes 1048576 | tf_op jit(solution)/shard_map/backward0/pallas_call | solution.py:26
  35.3 1.0 %collective-permute-start.16 = (f32[8,64,128]{2,1,0:T(8,128)S(1)}, f32[8,64,128]{2,1,0:T(8,128)S(1)}, u32[]{:S(2)}, u32[]{:S(2)}) collective-permute-start(f32[8,64,128]{2,1,0:T(8,128)S(1)} %get-tuple-element.65.own), channel_id=1, source_target_pairs={{0,16},{1,2},{2,1},{3,4},{4,3},{5,6},{6,5},{7,23},{8,24},{9,10},{1... | collective-permute-start | bytes 786440 | tf_op jit(solution)/shard_map/adjoint_to_chip/ppermute | solution.py:416
  36.2 0.8 %collective-permute-start.17 = (f32[8,64,128]{2,1,0:T(8,128)S(1)}, f32[8,64,128]{2,1,0:T(8,128)S(1)}, u32[]{:S(2)}, u32[]{:S(2)}) collective-permute-start(f32[8,64,128]{2,1,0:T(8,128)S(1)} %get-tuple-element.65.own), channel_id=1, source_target_pairs={{0,1},{1,0},{2,3},{3,2},{4,5},{5,4},{6,7},{7,6},{8,9},{9,8},{10,11... | collective-permute-start | bytes 786440 | tf_op jit(solution)/shard_map/adjoint_to_core/ppermute | solution.py:412
  37.0 1.3 %collective-permute-done.20.across = f32[8,64,128]{2,1,0:T(8,128)S(1)} collective-permute-done((f32[8,64,128]{2,1,0:T(8,128)S(1)}, f32[8,64,128]{2,1,0:T(8,128)S(1)}, u32[]{:S(2)}, u32[]{:S(2)}) %collective-permute-start.20) | collective-permute-done | bytes 262176 | tf_op jit(solution)/shard_map/state_to_chip/ppermute | solution.py:416
  38.4 1.0 %forward1.1 = (f32[8,64,128]{2,1,0:T(8,128)S(1)}, f32[8,64,128]{2,1,0:T(8,128)S(1)}) custom-call(f32[8,64,128]{2,1,0:T(8,128)S(1)} %get-tuple-element.70.own.previous, f32[8,64,128]{2,1,0:T(8,128)S(1)} %collective-permute-done.20.across, f32[8,64,128]{2,1,0:T(8,128)S(1)} %collective-permute-done.21.partner, f32[4,16,64,128]{3,2,1,0:T(8,128)S(1)} %get-tuple-element.64.coef, ...), custom_call_target="tpu_custom_call" | custom-call | flops 13107200 | bytes 1048576 | tf_op jit(solution)/shard_map/forward1/pallas_call | solution.py:26
  39.4 0.8 %collective-permute-start.22 = (f32[8,64,128]{2,1,0:T(8,128)S(1)}, f32[8,64,128]{2,1,0:T(8,128)S(1)}, u32[]{:S(2)}, u32[]{:S(2)}) collective-permute-start(f32[8,64,128]{2,1,0:T(8,128)S(1)} %get-tuple-element.72.own), channel_id=1, source_target_pairs={{0,16},{1,2},{2,1},{3,4},{4,3},{5,6},{6,5},{7,23},{8,24},{9,10},{1... | collective-permute-start | bytes 786440 | tf_op jit(solution)/shard_map/state_to_chip/ppermute | solution.py:416
  40.2 1.5 %collective-permute-done.16.across = f32[8,64,128]{2,1,0:T(8,128)S(1)} collective-permute-done((f32[8,64,128]{2,1,0:T(8,128)S(1)}, f32[8,64,128]{2,1,0:T(8,128)S(1)}, u32[]{:S(2)}, u32[]{:S(2)}) %collective-permute-start.16) | collective-permute-done | bytes 262176 | tf_op jit(solution)/shard_map/adjoint_to_chip/ppermute | solution.py:416
  41.7 1.0 %backward1.1 = (f32[8,64,128]{2,1,0:T(8,128)S(1)}, f32[8,64,128]{2,1,0:T(8,128)S(1)}) custom-call(f32[8,64,128]{2,1,0:T(8,128)S(1)} %get-tuple-element.65.own, f32[8,64,128]{2,1,0:T(8,128)S(1)} %collective-permute-done.16.across, f32[8,64,128]{2,1,0:T(8,128)S(1)} %collective-permute-done.17.partner, f32[4,16,64,128]{3,2,1,0:T(8,128)S(1)} %get-tuple-element.64.coef, ...), custom_call_target="tpu_custom_call" | custom-call | flops 13107200 | bytes 1048576 | tf_op jit(solution)/shard_map/backward1/pallas_call | solution.py:26
  42.7 1.0 %collective-permute-start.18 = (f32[8,64,128]{2,1,0:T(8,128)S(1)}, f32[8,64,128]{2,1,0:T(8,128)S(1)}, u32[]{:S(2)}, u32[]{:S(2)}) collective-permute-start(f32[8,64,128]{2,1,0:T(8,128)S(1)} %get-tuple-element.67.own), channel_id=1, source_target_pairs={{0,16},{1,2},{2,1},{3,4},{4,3},{5,6},{6,5},{7,23},{8,24},{9,10},{1... | collective-permute-start | bytes 786440 | tf_op jit(solution)/shard_map/adjoint_to_chip/ppermute | solution.py:416
  43.7 0.2 collective-permute-start.19
  43.9 1.9 %collective-permute-done.22.across = f32[8,64,128]{2,1,0:T(8,128)S(1)} collective-permute-done((f32[8,64,128]{2,1,0:T(8,128)S(1)}, f32[8,64,128]{2,1,0:T(8,128)S(1)}, u32[]{:S(2)}, u32[]{:S(2)}) %collective-permute-start.22) | collective-permute-done | bytes 262176 | tf_op jit(solution)/shard_map/state_to_chip/ppermute | solution.py:416
  45.8 1.0 %forward2.1 = (f32[8,64,128]{2,1,0:T(8,128)S(1)}, f32[8,64,128]{2,1,0:T(8,128)S(1)}) custom-call(f32[8,64,128]{2,1,0:T(8,128)S(1)} %get-tuple-element.72.own, f32[8,64,128]{2,1,0:T(8,128)S(1)} %collective-permute-done.22.across, f32[8,64,128]{2,1,0:T(8,128)S(1)} %collective-permute-done.23.partner, f32[4,16,64,128]{3,2,1,0:T(8,128)S(1)} %get-tuple-element.64.coef, ...), custom_call_target="tpu_custom_call" | custom-call | flops 13107200 | bytes 1048576 | tf_op jit(solution)/shard_map/forward2/pallas_call | solution.py:26
  46.8 0.8 %collective-permute-start.26 = (f32[8,64,128]{2,1,0:T(8,128)S(1)}, f32[8,64,128]{2,1,0:T(8,128)S(1)}, u32[]{:S(2)}, u32[]{:S(2)}) collective-permute-start(f32[8,64,128]{2,1,0:T(8,128)S(1)} %get-tuple-element.78.own), channel_id=1, source_target_pairs={{0,16},{1,2},{2,1},{3,4},{4,3},{5,6},{6,5},{7,23},{8,24},{9,10},{1... | collective-permute-start | bytes 786440 | tf_op jit(solution)/shard_map/state_to_chip/ppermute | solution.py:416
  47.6 1.5 %collective-permute-done.18.across = f32[8,64,128]{2,1,0:T(8,128)S(1)} collective-permute-done((f32[8,64,128]{2,1,0:T(8,128)S(1)}, f32[8,64,128]{2,1,0:T(8,128)S(1)}, u32[]{:S(2)}, u32[]{:S(2)}) %collective-permute-start.18) | collective-permute-done | bytes 262176 | tf_op jit(solution)/shard_map/adjoint_to_chip/ppermute | solution.py:416
  49.1 1.0 %backward2.1 = (f32[8,64,128]{2,1,0:T(8,128)S(1)}, f32[8,64,128]{2,1,0:T(8,128)S(1)}, f32[8,64,128]{2,1,0:T(8,128)S(1)}) custom-call(f32[8,64,128]{2,1,0:T(8,128)S(1)} %get-tuple-element.67.own, f32[8,64,128]{2,1,0:T(8,128)S(1)} %collective-permute-done.18.across, f32[8,64,128]{2,1,0:T(8,128)S(1)} %collective-permute-done.19.partner, ...), custom_call_target="tpu_custom_call" | custom-call | flops 13107200 | bytes 1048576 | tf_op jit(solution)/shard_map/backward2/pallas_call | solution.py:26
  50.2 1.0 %collective-permute-start.24 = (f32[8,64,128]{2,1,0:T(8,128)S(1)}, f32[8,64,128]{2,1,0:T(8,128)S(1)}, u32[]{:S(2)}, u32[]{:S(2)}) collective-permute-start(f32[8,64,128]{2,1,0:T(8,128)S(1)} %get-tuple-element.74.own), channel_id=1, source_target_pairs={{0,16},{1,2},{2,1},{3,4},{4,3},{5,6},{6,5},{7,23},{8,24},{9,10},{1... | collective-permute-start | bytes 786440 | tf_op jit(solution)/shard_map/adjoint_to_chip/ppermute | solution.py:416
  51.2 2.1 %collective-permute-done.26.across = f32[8,64,128]{2,1,0:T(8,128)S(1)} collective-permute-done((f32[8,64,128]{2,1,0:T(8,128)S(1)}, f32[8,64,128]{2,1,0:T(8,128)S(1)}, u32[]{:S(2)}, u32[]{:S(2)}) %collective-permute-start.26) | collective-permute-done | bytes 262176 | tf_op jit(solution)/shard_map/state_to_chip/ppermute | solution.py:416
  53.3 1.0 %forward3.1 = (f32[8,32,128]{2,1,0:T(8,128)S(1)}, f32[8,32,128]{2,1,0:T(8,128)S(1)}, f32[8,32,128]{2,1,0:T(8,128)S(1)}, f32[8,32,128]{2,1,0:T(8,128)S(1)}) custom-call(f32[8,64,128]{2,1,0:T(8,128)S(1)} %get-tuple-element.78.own, f32[8,64,128]{2,1,0:T(8,128)S(1)} %collective-permute-done.26.across, f32[8,64,128]{2,1,0:T(8,128)S(1)} %collective-permute-done.27.partner, ...), custom_call_target="tpu_custom_call" | custom-call | flops 13107200 | bytes 1048576 | tf_op jit(solution)/shard_map/forward3/pallas_call | solution.py:26
  54.3 0.5 collective-permute-start.28
  54.8 1.1 %collective-permute-start.29 = (f32[8,32,128]{2,1,0:T(8,128)S(1)}, f32[8,32,128]{2,1,0:T(8,128)S(1)}, u32[]{:S(2)}, u32[]{:S(2)}) collective-permute-start(f32[8,32,128]{2,1,0:T(8,128)S(1)} %get-tuple-element.82), channel_id=1, source_target_pairs={{0,16},{8,24},{16,0},{24,8},{1,17},{9,25},{17,1},{25,9},{2,18},{10... | collective-permute-start | bytes 393224 | tf_op jit(solution)/shard_map/grad_to_2/ppermute | solution.py:426
  55.9 1.9 %collective-permute-start.30 = (f32[8,32,128]{2,1,0:T(8,128)S(1)}, f32[8,32,128]{2,1,0:T(8,128)S(1)}, u32[]{:S(2)}, u32[]{:S(2)}) collective-permute-start(f32[8,32,128]{2,1,0:T(8,128)S(1)} %get-tuple-element.83), channel_id=1, source_target_pairs={{0,24},{8,16},{16,8},{24,0},{1,25},{9,17},{17,9},{25,1},{2,26},{10... | collective-permute-start | bytes 393224 | tf_op jit(solution)/shard_map/grad_to_3/ppermute | solution.py:426
  57.8 1.7 %backward3.1 = (f32[8,64,128]{2,1,0:T(8,128)}, f32[8,64,128]{2,1,0:T(8,128)}, f32[8,128]{1,0:T(8,128)S(1)}) custom-call(f32[8,64,128]{2,1,0:T(8,128)S(1)} %get-tuple-element.74.own, f32[8,64,128]{2,1,0:T(8,128)S(1)} %collective-permute-done.24.across, f32[8,64,128]{2,1,0:T(8,128)S(1)} %collective-permute-done.25.partner, ...), custom_call_target="tpu_custom_call" | custom-call | flops 13107200 | bytes 1048576 | tf_op jit(solution)/shard_map/backward3/pallas_call | solution.py:26
  59.6 0.5 collective-permute-done.28.refs_1_
  60.1 2.2 %collective-permute-done.29.refs_2_ = f32[8,32,128]{2,1,0:T(8,128)S(1)} collective-permute-done((f32[8,32,128]{2,1,0:T(8,128)S(1)}, f32[8,32,128]{2,1,0:T(8,128)S(1)}, u32[]{:S(2)}, u32[]{:S(2)}) %collective-permute-start.29) | collective-permute-done | bytes 131104 | tf_op jit(solution)/shard_map/grad_to_2/ppermute | solution.py:426
  62.3 0.7 %total.1 = f32[8,32,128]{2,1,0:T(8,128)} custom-call(f32[8,32,128]{2,1,0:T(8,128)S(1)} %get-tuple-element.80.refs_0_, f32[8,32,128]{2,1,0:T(8,128)S(1)} %collective-permute-done.28.refs_1_, f32[8,32,128]{2,1,0:T(8,128)S(1)} %collective-permute-done.29.refs_2_, f32[8,32,128]{2,1,0:T(8,128)S(1)} %collective-permute-done.30.refs_3_, ...), custom_call_target="tpu_custom_call" | custom-call | flops 1048576 | bytes 1048576 | tf_op jit(solution)/shard_map/total/pallas_call | solution.py:26
  (34 shorter events, 0.2 us)
Async XLA Ops:
  2.8 6.8 %collective-permute-start.2 = (f32[9,32,128]{2,1,0:T(8,128)S(1)}, f32[9,32,128]{2,1,0:T(8,128)S(1)}, u32[]{:S(2)}, u32[]{:S(2)}) collective-permute-start(f32[9,32,128]{2,1,0:T(8,128)S(1)} %get-tuple-element.47), channel_id=1, source_target_pairs={{0,8},{8,0},{16,24},{24,16},{1,9},{9,1},{17,25},{25,17},{2,10},{10... | collective-permute-start | bytes 442376 | tf_op jit(solution)/shard_map/wz_to_1/ppermute | solution.py:426
  5.7 5.6 %collective-permute-start.3 = (f32[8,32,128]{2,1,0:T(8,128)S(1)}, f32[8,32,128]{2,1,0:T(8,128)S(1)}, u32[]{:S(2)}, u32[]{:S(2)}) collective-permute-start(f32[8,32,128]{2,1,0:T(8,128)S(1)} %get-tuple-element.48.own.refs_0_), channel_id=1, source_target_pairs={{0,16},{8,24},{16,0},{24,8},{1,17},{9,25},{17,1},{25,9},{2,18},{10... | collective-permute-start | bytes 393224 | tf_op jit(solution)/shard_map/wx_to_2/ppermute | solution.py:426
  7.2 9.8 %collective-permute-start = (f32[8,64,128]{2,1,0:T(8,128)S(1)}, f32[8,64,128]{2,1,0:T(8,128)S(1)}, u32[]{:S(2)}, u32[]{:S(2)}) collective-permute-start(f32[8,64,128]{2,1,0:T(8,128)S(1)} %get-tuple-element.46.own.previous), channel_id=1, source_target_pairs={{0,1},{1,0},{2,3},{3,2},{4,5},{5,4},{6,7},{7,6},{8,9},{9,8},{10,11... | collective-permute-start | bytes 786440 | tf_op jit(solution)/shard_map/state_to_core/ppermute | solution.py:412
  7.2 11.8 %collective-permute-start.1 = (f32[8,64,128]{2,1,0:T(8,128)S(1)}, f32[8,64,128]{2,1,0:T(8,128)S(1)}, u32[]{:S(2)}, u32[]{:S(2)}) collective-permute-start(f32[8,64,128]{2,1,0:T(8,128)S(1)} %get-tuple-element.46.own.previous), channel_id=1, source_target_pairs={{0,8},{1,2},{2,1},{3,4},{4,3},{5,6},{6,5},{7,15},{8,0},{9,10},{10,... | collective-permute-start | bytes 786440 | tf_op jit(solution)/shard_map/state_to_chip/ppermute | solution.py:416
  7.8 6.2 %collective-permute-start.9 = (f32[8,32,128]{2,1,0:T(8,128)S(1)}, f32[8,32,128]{2,1,0:T(8,128)S(1)}, u32[]{:S(2)}, u32[]{:S(2)}) collective-permute-start(f32[8,32,128]{2,1,0:T(8,128)S(1)} %get-tuple-element.55.own.refs_3_), channel_id=1, source_target_pairs={{0,16},{8,24},{16,0},{24,8},{1,17},{9,25},{17,1},{25,9},{2,18},{10... | collective-permute-start | bytes 393224 | tf_op jit(solution)/shard_map/wy_to_2/ppermute | solution.py:426
  9.5 6.9 %collective-permute-start.5 = (f32[8,32,128]{2,1,0:T(8,128)S(1)}, f32[8,32,128]{2,1,0:T(8,128)S(1)}, u32[]{:S(2)}, u32[]{:S(2)}) collective-permute-start(f32[8,32,128]{2,1,0:T(8,128)S(1)} %get-tuple-element.49.own.refs_0_), channel_id=1, source_target_pairs={{0,8},{8,0},{16,24},{24,16},{1,9},{9,1},{17,25},{25,17},{2,10},{10... | collective-permute-start | bytes 393224 | tf_op jit(solution)/shard_map/speed_to_1/ppermute | solution.py:426
  11.3 11.1 %collective-permute-start.11 = (f32[2,8,32,128]{3,2,1,0:T(8,128)S(1)}, f32[2,8,32,128]{3,2,1,0:T(8,128)S(1)}, u32[]{:S(2)}, u32[]{:S(2)}) collective-permute-start(f32[2,8,32,128]{3,2,1,0:T(8,128)S(1)} %pair_wz.1), channel_id=1, source_target_pairs={{0,16},{8,24},{16,0},{24,8},{1,17},{9,25},{17,1},{25,9},{2,18},{10... | collective-permute-start | bytes 786440 | tf_op jit(solution)/shard_map/wz_to_2/ppermute | solution.py:426
  13.9 6.3 %collective-permute-start.4 = (f32[8,32,128]{2,1,0:T(8,128)S(1)}, f32[8,32,128]{2,1,0:T(8,128)S(1)}, u32[]{:S(2)}, u32[]{:S(2)}) collective-permute-start(f32[8,32,128]{2,1,0:T(8,128)S(1)} %relay_wx.1.refs_0_), channel_id=1, source_target_pairs={{0,8},{8,0},{16,24},{24,16},{1,9},{9,1},{17,25},{25,17},{2,10},{10... | collective-permute-start | bytes 393224 | tf_op jit(solution)/shard_map/wx_to_1/ppermute | solution.py:426
  16.4 6.1 %collective-permute-start.10 = (f32[8,32,128]{2,1,0:T(8,128)S(1)}, f32[8,32,128]{2,1,0:T(8,128)S(1)}, u32[]{:S(2)}, u32[]{:S(2)}) collective-permute-start(f32[8,32,128]{2,1,0:T(8,128)S(1)} %relay_wy.1), channel_id=1, source_target_pairs={{0,8},{8,0},{16,24},{24,16},{1,9},{9,1},{17,25},{25,17},{2,10},{10... | collective-permute-start | bytes 393224 | tf_op jit(solution)/shard_map/wy_to_1/ppermute | solution.py:426
  17.0 8.7 %copy-start = (f32[1,8,64,128]{3,2,1,0:T(8,128)S(1)}, f32[1,8,64,128]{3,2,1,0:T(8,128)}, u32[]{:S(2)}) copy-start(f32[1,8,64,128]{3,2,1,0:T(8,128)} %param.21) | copy-start | bytes 786436
  17.0 8.6 %collective-permute-start.6 = (f32[2,8,32,128]{3,2,1,0:T(8,128)S(1)}, f32[2,8,32,128]{3,2,1,0:T(8,128)S(1)}, u32[]{:S(2)}, u32[]{:S(2)}) collective-permute-start(f32[2,8,32,128]{3,2,1,0:T(8,128)S(1)} %pair_speed.1), channel_id=1, source_target_pairs={{0,16},{8,24},{16,0},{24,8},{1,17},{9,25},{17,1},{25,9},{2,18},{10... | collective-permute-start | bytes 786440 | tf_op jit(solution)/shard_map/speed_to_2/ppermute | solution.py:426
  21.1 8.8 %copy-start.7 = (f32[1,16]{1,0:T(1,128)S(1)}, f32[1,16]{1,0:T(1,128)}, u32[]{:S(2)}) copy-start(f32[1,16]{1,0:T(1,128)} %wavelet.1) | copy-start | bytes 196
  22.5 8.9 %copy-start.1 = (f32[1,8,64,128]{3,2,1,0:T(8,128)S(1)}, f32[1,8,64,128]{3,2,1,0:T(8,128)}, u32[]{:S(2)}) copy-start(f32[1,8,64,128]{3,2,1,0:T(8,128)} %param.18) | copy-start | bytes 786436
  23.0 3.5 %collective-permute-start.12 = (f32[3,2,64,128]{3,2,1,0:T(8,128)S(1)}, f32[3,2,64,128]{3,2,1,0:T(8,128)S(1)}, u32[]{:S(2)}, u32[]{:S(2)}) collective-permute-start(f32[3,2,64,128]{3,2,1,0:T(8,128)S(1)} %get-tuple-element.57), channel_id=1, source_target_pairs={{0,1},{1,0},{2,3},{3,2},{4,5},{5,4},{6,7},{7,6},{8,9},{9,8},{10,11... | collective-permute-start | bytes 589832 | tf_op jit(solution)/shard_map/edge_to_core/ppermute | solution.py:412
  23.1 7.0 %collective-permute-start.13 = (f32[3,2,64,128]{3,2,1,0:T(8,128)S(1)}, f32[3,2,64,128]{3,2,1,0:T(8,128)S(1)}, u32[]{:S(2)}, u32[]{:S(2)}) collective-permute-start(f32[3,2,64,128]{3,2,1,0:T(8,128)S(1)} %get-tuple-element.58), channel_id=1, source_target_pairs={{0,1},{1,0},{2,3},{3,2},{4,5},{5,4},{6,7},{7,6},{8,9},{9,8},{10,11... | collective-permute-start | bytes 589832 | tf_op jit(solution)/shard_map/edge_to_core/ppermute | solution.py:412
  23.6 6.5 %collective-permute-start.14 = (f32[3,2,64,128]{3,2,1,0:T(8,128)S(1)}, f32[3,2,64,128]{3,2,1,0:T(8,128)S(1)}, u32[]{:S(2)}, u32[]{:S(2)}) collective-permute-start(f32[3,2,64,128]{3,2,1,0:T(8,128)S(1)} %get-tuple-element.59), channel_id=1, source_target_pairs={{0,16},{1,2},{2,1},{3,4},{4,3},{5,6},{6,5},{7,23},{8,24},{9,10},{1... | collective-permute-start | bytes 589832 | tf_op jit(solution)/shard_map/edge_to_chip/ppermute | solution.py:416
  24.3 7.1 %collective-permute-start.15 = (f32[3,2,64,128]{3,2,1,0:T(8,128)S(1)}, f32[3,2,64,128]{3,2,1,0:T(8,128)S(1)}, u32[]{:S(2)}, u32[]{:S(2)}) collective-permute-start(f32[3,2,64,128]{3,2,1,0:T(8,128)S(1)} %get-tuple-element.60), channel_id=1, source_target_pairs={{0,16},{1,2},{2,1},{3,4},{4,3},{5,6},{6,5},{7,23},{8,24},{9,10},{1... | collective-permute-start | bytes 589832 | tf_op jit(solution)/shard_map/edge_to_chip/ppermute | solution.py:416
  25.7 8.5 %collective-permute-start.7 = (f32[8,64,128]{2,1,0:T(8,128)S(1)}, f32[8,64,128]{2,1,0:T(8,128)S(1)}, u32[]{:S(2)}, u32[]{:S(2)}) collective-permute-start(f32[8,64,128]{2,1,0:T(8,128)S(1)} %get-tuple-element.51.own), channel_id=1, source_target_pairs={{0,16},{1,2},{2,1},{3,4},{4,3},{5,6},{6,5},{7,23},{8,24},{9,10},{1... | collective-permute-start | bytes 786440 | tf_op jit(solution)/shard_map/adjoint_to_chip/ppermute | solution.py:416
  26.5 7.7 %collective-permute-start.8 = (f32[8,64,128]{2,1,0:T(8,128)S(1)}, f32[8,64,128]{2,1,0:T(8,128)S(1)}, u32[]{:S(2)}, u32[]{:S(2)}) collective-permute-start(f32[8,64,128]{2,1,0:T(8,128)S(1)} %get-tuple-element.51.own), channel_id=1, source_target_pairs={{0,1},{1,0},{2,3},{3,2},{4,5},{5,4},{6,7},{7,6},{8,9},{9,8},{10,11... | collective-permute-start | bytes 786440 | tf_op jit(solution)/shard_map/adjoint_to_core/ppermute | solution.py:412
  31.4 1.8 %copy-start.3 = (f32[1,16,128]{2,1,0:T(8,128)S(1)}, f32[1,16,128]{2,1,0:T(8,128)}, u32[]{:S(2)}) copy-start(f32[1,16,128]{2,1,0:T(8,128)} %traces.1) | copy-start | bytes 24580
  31.4 1.8 %copy-start.4 = (s32[1,128]{1,0:T(1,128)S(1)}, s32[1,128]{1,0:T(1,128)}, u32[]{:S(2)}) copy-start(s32[1,128]{1,0:T(1,128)} %rx.1) | copy-start | bytes 1540
  31.4 1.8 %copy-start.5 = (s32[1,128]{1,0:T(1,128)S(1)}, s32[1,128]{1,0:T(1,128)}, u32[]{:S(2)}) copy-start(s32[1,128]{1,0:T(1,128)} %ry.1) | copy-start | bytes 1540
  31.4 1.8 %copy-start.6 = (s32[1,128]{1,0:T(1,128)S(1)}, s32[1,128]{1,0:T(1,128)}, u32[]{:S(2)}) copy-start(s32[1,128]{1,0:T(1,128)} %rz.1) | copy-start | bytes 1540
  31.4 2.9 %copy-start.2 = (f32[1,8,64,128]{3,2,1,0:T(8,128)S(1)}, f32[1,8,64,128]{3,2,1,0:T(8,128)}, u32[]{:S(2)}) copy-start(f32[1,8,64,128]{3,2,1,0:T(8,128)} %param.20) | copy-start | bytes 786436
  31.9 6.4 %collective-permute-start.20 = (f32[8,64,128]{2,1,0:T(8,128)S(1)}, f32[8,64,128]{2,1,0:T(8,128)S(1)}, u32[]{:S(2)}, u32[]{:S(2)}) collective-permute-start(f32[8,64,128]{2,1,0:T(8,128)S(1)} %get-tuple-element.70.own.previous), channel_id=1, source_target_pairs={{0,16},{1,2},{2,1},{3,4},{4,3},{5,6},{6,5},{7,23},{8,24},{9,10},{1... | collective-permute-start | bytes 786440 | tf_op jit(solution)/shard_map/state_to_chip/ppermute | solution.py:416
  32.7 5.7 %collective-permute-start.21 = (f32[8,64,128]{2,1,0:T(8,128)S(1)}, f32[8,64,128]{2,1,0:T(8,128)S(1)}, u32[]{:S(2)}, u32[]{:S(2)}) collective-permute-start(f32[8,64,128]{2,1,0:T(8,128)S(1)} %get-tuple-element.70.own.previous), channel_id=1, source_target_pairs={{0,1},{1,0},{2,3},{3,2},{4,5},{5,4},{6,7},{7,6},{8,9},{9,8},{10,11... | collective-permute-start | bytes 786440 | tf_op jit(solution)/shard_map/state_to_core/ppermute | solution.py:412
  35.3 6.4 %collective-permute-start.16 = (f32[8,64,128]{2,1,0:T(8,128)S(1)}, f32[8,64,128]{2,1,0:T(8,128)S(1)}, u32[]{:S(2)}, u32[]{:S(2)}) collective-permute-start(f32[8,64,128]{2,1,0:T(8,128)S(1)} %get-tuple-element.65.own), channel_id=1, source_target_pairs={{0,16},{1,2},{2,1},{3,4},{4,3},{5,6},{6,5},{7,23},{8,24},{9,10},{1... | collective-permute-start | bytes 786440 | tf_op jit(solution)/shard_map/adjoint_to_chip/ppermute | solution.py:416
  36.2 5.5 %collective-permute-start.17 = (f32[8,64,128]{2,1,0:T(8,128)S(1)}, f32[8,64,128]{2,1,0:T(8,128)S(1)}, u32[]{:S(2)}, u32[]{:S(2)}) collective-permute-start(f32[8,64,128]{2,1,0:T(8,128)S(1)} %get-tuple-element.65.own), channel_id=1, source_target_pairs={{0,1},{1,0},{2,3},{3,2},{4,5},{5,4},{6,7},{7,6},{8,9},{9,8},{10,11... | collective-permute-start | bytes 786440 | tf_op jit(solution)/shard_map/adjoint_to_core/ppermute | solution.py:412
  39.4 6.4 %collective-permute-start.22 = (f32[8,64,128]{2,1,0:T(8,128)S(1)}, f32[8,64,128]{2,1,0:T(8,128)S(1)}, u32[]{:S(2)}, u32[]{:S(2)}) collective-permute-start(f32[8,64,128]{2,1,0:T(8,128)S(1)} %get-tuple-element.72.own), channel_id=1, source_target_pairs={{0,16},{1,2},{2,1},{3,4},{4,3},{5,6},{6,5},{7,23},{8,24},{9,10},{1... | collective-permute-start | bytes 786440 | tf_op jit(solution)/shard_map/state_to_chip/ppermute | solution.py:416
  40.2 5.7 %collective-permute-start.23 = (f32[8,64,128]{2,1,0:T(8,128)S(1)}, f32[8,64,128]{2,1,0:T(8,128)S(1)}, u32[]{:S(2)}, u32[]{:S(2)}) collective-permute-start(f32[8,64,128]{2,1,0:T(8,128)S(1)} %get-tuple-element.72.own), channel_id=1, source_target_pairs={{0,1},{1,0},{2,3},{3,2},{4,5},{5,4},{6,7},{7,6},{8,9},{9,8},{10,11... | collective-permute-start | bytes 786440 | tf_op jit(solution)/shard_map/state_to_core/ppermute | solution.py:412
  42.7 6.4 %collective-permute-start.18 = (f32[8,64,128]{2,1,0:T(8,128)S(1)}, f32[8,64,128]{2,1,0:T(8,128)S(1)}, u32[]{:S(2)}, u32[]{:S(2)}) collective-permute-start(f32[8,64,128]{2,1,0:T(8,128)S(1)} %get-tuple-element.67.own), channel_id=1, source_target_pairs={{0,16},{1,2},{2,1},{3,4},{4,3},{5,6},{6,5},{7,23},{8,24},{9,10},{1... | collective-permute-start | bytes 786440 | tf_op jit(solution)/shard_map/adjoint_to_chip/ppermute | solution.py:416
  43.7 5.5 %collective-permute-start.19 = (f32[8,64,128]{2,1,0:T(8,128)S(1)}, f32[8,64,128]{2,1,0:T(8,128)S(1)}, u32[]{:S(2)}, u32[]{:S(2)}) collective-permute-start(f32[8,64,128]{2,1,0:T(8,128)S(1)} %get-tuple-element.67.own), channel_id=1, source_target_pairs={{0,1},{1,0},{2,3},{3,2},{4,5},{5,4},{6,7},{7,6},{8,9},{9,8},{10,11... | collective-permute-start | bytes 786440 | tf_op jit(solution)/shard_map/adjoint_to_core/ppermute | solution.py:412
  46.8 6.4 %collective-permute-start.26 = (f32[8,64,128]{2,1,0:T(8,128)S(1)}, f32[8,64,128]{2,1,0:T(8,128)S(1)}, u32[]{:S(2)}, u32[]{:S(2)}) collective-permute-start(f32[8,64,128]{2,1,0:T(8,128)S(1)} %get-tuple-element.78.own), channel_id=1, source_target_pairs={{0,16},{1,2},{2,1},{3,4},{4,3},{5,6},{6,5},{7,23},{8,24},{9,10},{1... | collective-permute-start | bytes 786440 | tf_op jit(solution)/shard_map/state_to_chip/ppermute | solution.py:416
  47.6 5.7 %collective-permute-start.27 = (f32[8,64,128]{2,1,0:T(8,128)S(1)}, f32[8,64,128]{2,1,0:T(8,128)S(1)}, u32[]{:S(2)}, u32[]{:S(2)}) collective-permute-start(f32[8,64,128]{2,1,0:T(8,128)S(1)} %get-tuple-element.78.own), channel_id=1, source_target_pairs={{0,1},{1,0},{2,3},{3,2},{4,5},{5,4},{6,7},{7,6},{8,9},{9,8},{10,11... | collective-permute-start | bytes 786440 | tf_op jit(solution)/shard_map/state_to_core/ppermute | solution.py:412
  50.2 7.6 %collective-permute-start.24 = (f32[8,64,128]{2,1,0:T(8,128)S(1)}, f32[8,64,128]{2,1,0:T(8,128)S(1)}, u32[]{:S(2)}, u32[]{:S(2)}) collective-permute-start(f32[8,64,128]{2,1,0:T(8,128)S(1)} %get-tuple-element.74.own), channel_id=1, source_target_pairs={{0,16},{1,2},{2,1},{3,4},{4,3},{5,6},{6,5},{7,23},{8,24},{9,10},{1... | collective-permute-start | bytes 786440 | tf_op jit(solution)/shard_map/adjoint_to_chip/ppermute | solution.py:416
  51.2 6.7 %collective-permute-start.25 = (f32[8,64,128]{2,1,0:T(8,128)S(1)}, f32[8,64,128]{2,1,0:T(8,128)S(1)}, u32[]{:S(2)}, u32[]{:S(2)}) collective-permute-start(f32[8,64,128]{2,1,0:T(8,128)S(1)} %get-tuple-element.74.own), channel_id=1, source_target_pairs={{0,1},{1,0},{2,3},{3,2},{4,5},{5,4},{6,7},{7,6},{8,9},{9,8},{10,11... | collective-permute-start | bytes 786440 | tf_op jit(solution)/shard_map/adjoint_to_core/ppermute | solution.py:412
  54.3 5.8 %collective-permute-start.28 = (f32[8,32,128]{2,1,0:T(8,128)S(1)}, f32[8,32,128]{2,1,0:T(8,128)S(1)}, u32[]{:S(2)}, u32[]{:S(2)}) collective-permute-start(f32[8,32,128]{2,1,0:T(8,128)S(1)} %get-tuple-element.81), channel_id=1, source_target_pairs={{0,8},{8,0},{16,24},{24,16},{1,9},{9,1},{17,25},{25,17},{2,10},{10... | collective-permute-start | bytes 393224 | tf_op jit(solution)/shard_map/grad_to_1/ppermute | solution.py:426
  54.8 7.5 %collective-permute-start.29 = (f32[8,32,128]{2,1,0:T(8,128)S(1)}, f32[8,32,128]{2,1,0:T(8,128)S(1)}, u32[]{:S(2)}, u32[]{:S(2)}) collective-permute-start(f32[8,32,128]{2,1,0:T(8,128)S(1)} %get-tuple-element.82), channel_id=1, source_target_pairs={{0,16},{8,24},{16,0},{24,8},{1,17},{9,25},{17,1},{25,9},{2,18},{10... | collective-permute-start | bytes 393224 | tf_op jit(solution)/shard_map/grad_to_2/ppermute | solution.py:426
  55.9 6.3 %collective-permute-start.30 = (f32[8,32,128]{2,1,0:T(8,128)S(1)}, f32[8,32,128]{2,1,0:T(8,128)S(1)}, u32[]{:S(2)}, u32[]{:S(2)}) collective-permute-start(f32[8,32,128]{2,1,0:T(8,128)S(1)} %get-tuple-element.83), channel_id=1, source_target_pairs={{0,24},{8,16},{16,8},{24,0},{1,25},{9,17},{17,9},{25,1},{2,26},{10... | collective-permute-start | bytes 393224 | tf_op jit(solution)/shard_map/grad_to_3/ppermute | solution.py:426

commit v8 on v6

--- a/solution.py
+++ b/solution.py
@@ -200,19 +200,23 @@
     local = rx[...] - first
     cell = jnp.where((local >= 0) & (local < rows), local * width + ry[...], -1)
     pick = (
-        lax.broadcasted_iota(jnp.int32, (rows * width, receivers), 0) == cell
-    ).astype(jnp.float32)
+        (lax.broadcasted_iota(jnp.int32, (rows * width, receivers), 0) == cell)
+        .astype(jnp.float32)
+        .astype(jnp.bfloat16)
+    )
+    pick = jnp.concatenate([pick, pick, pick], axis=1)
     match = lax.broadcasted_iota(jnp.int32, (depth, receivers), 0) == rz[...]
     moment = lax.broadcasted_iota(jnp.int32, traces.shape[1:], 0)
     for t in range(STEPS):
         chosen = jnp.where(moment == start + t, traces[0], 0.0)
         samples = jnp.sum(chosen, axis=0, keepdims=True)
         spread = jnp.where(match, samples, 0.0)
+        high, low = halves(spread)
+        middle, low = low, spread - high.astype(jnp.float32) - low.astype(jnp.float32)
         added = lax.dot_general(
             pick,
-            spread,
+            jnp.concatenate([high, middle, low.astype(jnp.bfloat16)], axis=1),
             (((1,), (1,)), ((), ())),
-            precision=lax.Precision.HIGHEST,
             preferred_element_type=jnp.float32,
         )
         inj[t] = added.reshape(shape)

time: 63 us -> 63 us (level)
  waiting for transfers between devices: 19.4 us -> 20.1 us
    ppermute x10, waiting for transfers between devices: 10.6 us -> 11.4 us  [across_chips(): return lax.ppermute(array, ('shot', 'blk'), chip_pairs(hop))]
where the time goes in v8:
time: 63 us; the launch traced here: 62.9 us
  starting transfers between devices  25.9 us (41%)
  waiting for transfers between devices  20.1 us (32%)
  Pallas kernels  12.7 us (20%)
  between operations  4.12 us (7%)
    ppermute x11, starting transfers between devices, to_owners(): return lax.ppermute(array, 'shot', [(i, i ^ k) for i in range(shots)])  15.6 us
    pallas_call x19, Pallas kernels, call(): pl.pallas_call(body, name=name, out_shape=outs, in_specs=[s for _, s in p...  12.7 us
    ppermute x10, waiting for transfers between devices, across_chips(): return lax.ppermute(array, ('shot', 'blk'), chip_pairs(hop))  11.4 us
    ppermute x11, waiting for transfers between devices, to_owners(): return lax.ppermute(array, 'shot', [(i, i ^ k) for i in range(shots)])  8.72 us
    ppermute x10, starting transfers between devices, across_chips(): return lax.ppermute(array, ('shot', 'blk'), chip_pairs(hop))  8.06 us
    ppermute x10, starting transfers between devices, to_partner(): return lax.ppermute(array, 'blk', core_pairs)  2.17 us
  transfers between devices with their start and end apart: 31, of which 14 were waited for; matrix products, arithmetic and copies ran while one was open for 0% of the time, Pallas kernels for 17%

profile of v8, /device:TPU:0, one launch (start us, length us, event | category | flops | bytes accessed | tf_op | source)
XLA Modules:
  0.0 62.9 jit_solution(3094979718966197876)
XLA Ops:
  1.3 1.4 %owner.1 = (f32[8,32,128]{2,1,0:T(8,128)S(1)}, f32[8,32,128]{2,1,0:T(8,128)S(1)}, f32[8,32,128]{2,1,0:T(8,128)S(1)}, f32[8,32,128]{2,1,0:T(8,128)S(1)}, f32[8,64,128]{2,1,0:T(8,128)S(1)}) custom-call(f32[8,32,128]{2,1,0:T(8,128)} %eps.1, f32[8,32,128]{2,1,0:T(8,128)} %tilt.1, f32[8,32,128]{2,1,0:T(8,128)} %azimuth.1, f32[8,32,128]{2,1,0:T(8,128)} %speed.2, ...), custom_call_target="tpu_custom_call" | custom-call | flops 1048576 | bytes 1048576 | tf_op jit(solution)/shard_map/owner/pallas_call | solution.py:26
  2.7 0.1 first.1
  2.8 2.9 %collective-permute-start.2 = (f32[9,32,128]{2,1,0:T(8,128)S(1)}, f32[9,32,128]{2,1,0:T(8,128)S(1)}, u32[]{:S(2)}, u32[]{:S(2)}) collective-permute-start(f32[9,32,128]{2,1,0:T(8,128)S(1)} %get-tuple-element.49), channel_id=1, source_target_pairs={{0,8},{8,0},{16,24},{24,16},{1,9},{9,1},{17,25},{25,17},{2,10},{10... | collective-permute-start | bytes 442376 | tf_op jit(solution)/shard_map/wz_to_1/ppermute | solution.py:425
  5.7 1.5 %collective-permute-start.3 = (f32[8,32,128]{2,1,0:T(8,128)S(1)}, f32[8,32,128]{2,1,0:T(8,128)S(1)}, u32[]{:S(2)}, u32[]{:S(2)}) collective-permute-start(f32[8,32,128]{2,1,0:T(8,128)S(1)} %get-tuple-element.50.own.refs_0_), channel_id=1, source_target_pairs={{0,16},{8,24},{16,0},{24,8},{1,17},{9,25},{17,1},{25,9},{2,18},{10... | collective-permute-start | bytes 393224 | tf_op jit(solution)/shard_map/wx_to_2/ppermute | solution.py:425
  7.2 0.5 collective-permute-start.1
  7.8 0.1 collective-permute-start.9
  7.8 1.7 %collective-permute-done.2.wz_first.received.refs_7_ = f32[9,32,128]{2,1,0:T(8,128)S(1)} collective-permute-done((f32[9,32,128]{2,1,0:T(8,128)S(1)}, f32[9,32,128]{2,1,0:T(8,128)S(1)}, u32[]{:S(2)}, u32[]{:S(2)}) %collective-permute-start.2) | collective-permute-done | bytes 147488 | tf_op jit(solution)/shard_map/wz_to_1/ppermute | solution.py:425
  9.5 1.7 %collective-permute-start.5 = (f32[8,32,128]{2,1,0:T(8,128)S(1)}, f32[8,32,128]{2,1,0:T(8,128)S(1)}, u32[]{:S(2)}, u32[]{:S(2)}) collective-permute-start(f32[8,32,128]{2,1,0:T(8,128)S(1)} %get-tuple-element.51.own.refs_0_), channel_id=1, source_target_pairs={{0,8},{8,0},{16,24},{24,16},{1,9},{9,1},{17,25},{25,17},{2,10},{10... | collective-permute-start | bytes 393224 | tf_op jit(solution)/shard_map/speed_to_1/ppermute | solution.py:425
  11.3 1.6 %collective-permute-start.11 = (f32[2,8,32,128]{3,2,1,0:T(8,128)S(1)}, f32[2,8,32,128]{3,2,1,0:T(8,128)S(1)}, u32[]{:S(2)}, u32[]{:S(2)}) collective-permute-start(f32[2,8,32,128]{3,2,1,0:T(8,128)S(1)} %pair_wz.1), channel_id=1, source_target_pairs={{0,16},{8,24},{16,0},{24,8},{1,17},{9,25},{17,1},{25,9},{2,18},{10... | collective-permute-start | bytes 786440 | tf_op jit(solution)/shard_map/wz_to_2/ppermute | solution.py:425
  12.9 1.0 %collective-permute-done.9.received.refs_5_ = f32[8,32,128]{2,1,0:T(8,128)S(1)} collective-permute-done((f32[8,32,128]{2,1,0:T(8,128)S(1)}, f32[8,32,128]{2,1,0:T(8,128)S(1)}, u32[]{:S(2)}, u32[]{:S(2)}) %collective-permute-start.9) | collective-permute-done | bytes 131104 | tf_op jit(solution)/shard_map/wy_to_2/ppermute | solution.py:425
  13.9 1.6 %collective-permute-start.4 = (f32[8,32,128]{2,1,0:T(8,128)S(1)}, f32[8,32,128]{2,1,0:T(8,128)S(1)}, u32[]{:S(2)}, u32[]{:S(2)}) collective-permute-start(f32[8,32,128]{2,1,0:T(8,128)S(1)} %relay_wx.1.refs_0_), channel_id=1, source_target_pairs={{0,8},{8,0},{16,24},{24,16},{1,9},{9,1},{17,25},{25,17},{2,10},{10... | collective-permute-start | bytes 393224 | tf_op jit(solution)/shard_map/wx_to_1/ppermute | solution.py:425
  15.6 0.8 %collective-permute-done.5.refs_1_.received = f32[8,32,128]{2,1,0:T(8,128)S(1)} collective-permute-done((f32[8,32,128]{2,1,0:T(8,128)S(1)}, f32[8,32,128]{2,1,0:T(8,128)S(1)}, u32[]{:S(2)}, u32[]{:S(2)}) %collective-permute-start.5) | collective-permute-done | bytes 131104 | tf_op jit(solution)/shard_map/speed_to_1/ppermute | solution.py:425
  16.4 0.5 collective-permute-start.10
  17.0 0.0 copy-start
  17.0 2.1 %collective-permute-start.6 = (f32[2,8,32,128]{3,2,1,0:T(8,128)S(1)}, f32[2,8,32,128]{3,2,1,0:T(8,128)S(1)}, u32[]{:S(2)}, u32[]{:S(2)}) collective-permute-start(f32[2,8,32,128]{3,2,1,0:T(8,128)S(1)} %pair_speed.1), channel_id=1, source_target_pairs={{0,16},{8,24},{16,0},{24,8},{1,17},{9,25},{17,1},{25,9},{2,18},{10... | collective-permute-start | bytes 786440 | tf_op jit(solution)/shard_map/speed_to_2/ppermute | solution.py:425
  19.0 0.0 collective-permute-done.1.across
  19.0 1.2 %collective-permute-done.4.refs_0_.refs_1_ = f32[8,32,128]{2,1,0:T(8,128)S(1)} collective-permute-done((f32[8,32,128]{2,1,0:T(8,128)S(1)}, f32[8,32,128]{2,1,0:T(8,128)S(1)}, u32[]{:S(2)}, u32[]{:S(2)}) %collective-permute-start.4) | collective-permute-done | bytes 131104 | tf_op jit(solution)/shard_map/wx_to_1/ppermute | solution.py:425
  20.3 0.8 %prepare.1 = (f32[3,16,64,128]{3,2,1,0:T(8,128)S(1)}, f32[8,128]{1,0:T(8,128)S(1)}, bf16[64,128]{1,0:T(8,128)(2,1)S(1)}, bf16[256,128]{1,0:T(8,128)(2,1)S(1)}) custom-call(f32[8,128]{1,0:T(8,128)S(1)} %get-tuple-element.47.first, f32[8,64,128]{2,1,0:T(8,128)S(1)} %get-tuple-element.48.own.previous, f32[8,64,128]{2,1,0:T(8,128)S(1)} %collective-permute-done.partner, ...), custom_call_target="tpu_custom_call" | custom-call | flops 1048576 | bytes 1048576 | tf_op jit(solution)/shard_map/prepare/pallas_call | solution.py:26
  21.1 0.0 copy-start.3
  21.1 0.0 copy-start.4
  21.1 0.0 copy-start.5
  21.1 0.0 copy-start.6
  21.1 0.0 copy-start.7
  21.1 0.0 copy-start.1
  21.1 1.3 %collective-permute-done.10.refs_4_ = f32[8,32,128]{2,1,0:T(8,128)S(1)} collective-permute-done((f32[8,32,128]{2,1,0:T(8,128)S(1)}, f32[8,32,128]{2,1,0:T(8,128)S(1)}, u32[]{:S(2)}, u32[]{:S(2)}) %collective-permute-start.10) | collective-permute-done | bytes 131104 | tf_op jit(solution)/shard_map/wy_to_1/ppermute | solution.py:425
  22.5 0.6 flux.1
  23.0 0.1 collective-permute-start.12
  23.1 0.5 collective-permute-start.13
  23.6 0.7 %collective-permute-start.14 = (f32[3,2,64,128]{3,2,1,0:T(8,128)S(1)}, f32[3,2,64,128]{3,2,1,0:T(8,128)S(1)}, u32[]{:S(2)}, u32[]{:S(2)}) collective-permute-start(f32[3,2,64,128]{3,2,1,0:T(8,128)S(1)} %get-tuple-element.61), channel_id=1, source_target_pairs={{0,16},{1,2},{2,1},{3,4},{4,3},{5,6},{6,5},{7,23},{8,24},{9,10},{1... | collective-permute-start | bytes 589832 | tf_op jit(solution)/shard_map/edge_to_chip/ppermute | solution.py:415
  24.3 1.3 %collective-permute-start.15 = (f32[3,2,64,128]{3,2,1,0:T(8,128)S(1)}, f32[3,2,64,128]{3,2,1,0:T(8,128)S(1)}, u32[]{:S(2)}, u32[]{:S(2)}) collective-permute-start(f32[3,2,64,128]{3,2,1,0:T(8,128)S(1)} %get-tuple-element.62), channel_id=1, source_target_pairs={{0,16},{1,2},{2,1},{3,4},{4,3},{5,6},{6,5},{7,23},{8,24},{9,10},{1... | collective-permute-start | bytes 589832 | tf_op jit(solution)/shard_map/edge_to_chip/ppermute | solution.py:415
  25.6 0.0 collective-permute-done.6.refs_2_
  25.6 0.1 speed.3
  25.7 0.8 %collective-permute-start.7 = (f32[8,64,128]{2,1,0:T(8,128)S(1)}, f32[8,64,128]{2,1,0:T(8,128)S(1)}, u32[]{:S(2)}, u32[]{:S(2)}) collective-permute-start(f32[8,64,128]{2,1,0:T(8,128)S(1)} %get-tuple-element.53.own), channel_id=1, source_target_pairs={{0,16},{1,2},{2,1},{3,4},{4,3},{5,6},{6,5},{7,23},{8,24},{9,10},{1... | collective-permute-start | bytes 786440 | tf_op jit(solution)/shard_map/adjoint_to_chip/ppermute | solution.py:415
  26.5 0.7 %collective-permute-start.8 = (f32[8,64,128]{2,1,0:T(8,128)S(1)}, f32[8,64,128]{2,1,0:T(8,128)S(1)}, u32[]{:S(2)}, u32[]{:S(2)}) collective-permute-start(f32[8,64,128]{2,1,0:T(8,128)S(1)} %get-tuple-element.53.own), channel_id=1, source_target_pairs={{0,1},{1,0},{2,3},{3,2},{4,5},{5,4},{6,7},{7,6},{8,9},{9,8},{10,11... | collective-permute-start | bytes 786440 | tf_op jit(solution)/shard_map/adjoint_to_core/ppermute | solution.py:411
  29.9 0.8 %inject.1 = (f32[3,8,64,128]{3,2,1,0:T(8,128)S(1)}, f32[4,8,64,128]{3,2,1,0:T(8,128)S(1)}) custom-call(s32[1]{0:T(128)S(6)} %copy.22.step, s32[1]{0:T(128)S(6)} %copy.23.sx, s32[1]{0:T(128)S(6)} %copy.24.sy, s32[1]{0:T(128)S(6)} %copy.25.sz, f32[1,16]{1,0:T(1,128)S(1)} %copy-done.4, s32[1,128]{1,0:T(1,128)S(1)} %copy-done.5, s32[1,128]{1,0:T(1,128)S(1)} %copy-done.6, ...), custom_call_target="tpu_custom_call" | custom-call | flops 1048576 | bytes 1048576 | tf_op jit(solution)/shard_map/inject/pallas_call | solution.py:26
  30.7 0.7 %collective-permute-done.15.edge_a1 = f32[3,2,64,128]{3,2,1,0:T(8,128)S(1)} collective-permute-done((f32[3,2,64,128]{3,2,1,0:T(8,128)S(1)}, f32[3,2,64,128]{3,2,1,0:T(8,128)S(1)}, u32[]{:S(2)}, u32[]{:S(2)}) %collective-permute-start.15) | collective-permute-done | bytes 196640 | tf_op jit(solution)/shard_map/edge_to_chip/ppermute | solution.py:415
  31.4 0.5 forward0.1
  31.9 0.8 %collective-permute-start.20 = (f32[8,64,128]{2,1,0:T(8,128)S(1)}, f32[8,64,128]{2,1,0:T(8,128)S(1)}, u32[]{:S(2)}, u32[]{:S(2)}) collective-permute-start(f32[8,64,128]{2,1,0:T(8,128)S(1)} %get-tuple-element.74.own.previous), channel_id=1, source_target_pairs={{0,16},{1,2},{2,1},{3,4},{4,3},{5,6},{6,5},{7,23},{8,24},{9,10},{1... | collective-permute-start | bytes 786440 | tf_op jit(solution)/shard_map/state_to_chip/ppermute | solution.py:415
  32.7 0.4 collective-permute-start.21
  33.1 1.1 %collective-permute-done.7.across = f32[8,64,128]{2,1,0:T(8,128)S(1)} collective-permute-done((f32[8,64,128]{2,1,0:T(8,128)S(1)}, f32[8,64,128]{2,1,0:T(8,128)S(1)}, u32[]{:S(2)}, u32[]{:S(2)}) %collective-permute-start.7) | collective-permute-done | bytes 262176 | tf_op jit(solution)/shard_map/adjoint_to_chip/ppermute | solution.py:415
  34.2 1.0 %backward0.1 = (f32[8,64,128]{2,1,0:T(8,128)S(1)}, f32[8,64,128]{2,1,0:T(8,128)S(1)}) custom-call(f32[8,64,128]{2,1,0:T(8,128)S(1)} %get-tuple-element.53.own, f32[8,64,128]{2,1,0:T(8,128)S(1)} %collective-permute-done.7.across, f32[8,64,128]{2,1,0:T(8,128)S(1)} %collective-permute-done.8.partner, f32[4,16,64,128]{3,2,1,0:T(8,128)S(1)} %get-tuple-element.67.coef, ...), custom_call_target="tpu_custom_call" | custom-call | flops 13107200 | bytes 1048576 | tf_op jit(solution)/shard_map/backward0/pallas_call | solution.py:26
  35.2 0.8 %collective-permute-start.16 = (f32[8,64,128]{2,1,0:T(8,128)S(1)}, f32[8,64,128]{2,1,0:T(8,128)S(1)}, u32[]{:S(2)}, u32[]{:S(2)}) collective-permute-start(f32[8,64,128]{2,1,0:T(8,128)S(1)} %get-tuple-element.69.own), channel_id=1, source_target_pairs={{0,16},{1,2},{2,1},{3,4},{4,3},{5,6},{6,5},{7,23},{8,24},{9,10},{1... | collective-permute-start | bytes 786440 | tf_op jit(solution)/shard_map/adjoint_to_chip/ppermute | solution.py:415
  36.0 0.4 collective-permute-start.17
  36.4 1.9 %collective-permute-done.20.across = f32[8,64,128]{2,1,0:T(8,128)S(1)} collective-permute-done((f32[8,64,128]{2,1,0:T(8,128)S(1)}, f32[8,64,128]{2,1,0:T(8,128)S(1)}, u32[]{:S(2)}, u32[]{:S(2)}) %collective-permute-start.20) | collective-permute-done | bytes 262176 | tf_op jit(solution)/shard_map/state_to_chip/ppermute | solution.py:415
  38.3 1.0 %forward1.1 = (f32[8,64,128]{2,1,0:T(8,128)S(1)}, f32[8,64,128]{2,1,0:T(8,128)S(1)}) custom-call(f32[8,64,128]{2,1,0:T(8,128)S(1)} %get-tuple-element.74.own.previous, f32[8,64,128]{2,1,0:T(8,128)S(1)} %collective-permute-done.20.across, f32[8,64,128]{2,1,0:T(8,128)S(1)} %collective-permute-done.21.partner, f32[4,16,64,128]{3,2,1,0:T(8,128)S(1)} %get-tuple-element.67.coef, ...), custom_call_target="tpu_custom_call" | custom-call | flops 13107200 | bytes 1048576 | tf_op jit(solution)/shard_map/forward1/pallas_call | solution.py:26
  39.3 0.8 %collective-permute-start.22 = (f32[8,64,128]{2,1,0:T(8,128)S(1)}, f32[8,64,128]{2,1,0:T(8,128)S(1)}, u32[]{:S(2)}, u32[]{:S(2)}) collective-permute-start(f32[8,64,128]{2,1,0:T(8,128)S(1)} %get-tuple-element.76.own), channel_id=1, source_target_pairs={{0,16},{1,2},{2,1},{3,4},{4,3},{5,6},{6,5},{7,23},{8,24},{9,10},{1... | collective-permute-start | bytes 786440 | tf_op jit(solution)/shard_map/state_to_chip/ppermute | solution.py:415
  40.1 1.5 %collective-permute-done.16.across = f32[8,64,128]{2,1,0:T(8,128)S(1)} collective-permute-done((f32[8,64,128]{2,1,0:T(8,128)S(1)}, f32[8,64,128]{2,1,0:T(8,128)S(1)}, u32[]{:S(2)}, u32[]{:S(2)}) %collective-permute-start.16) | collective-permute-done | bytes 262176 | tf_op jit(solution)/shard_map/adjoint_to_chip/ppermute | solution.py:415
  41.6 1.0 %backward1.1 = (f32[8,64,128]{2,1,0:T(8,128)S(1)}, f32[8,64,128]{2,1,0:T(8,128)S(1)}) custom-call(f32[8,64,128]{2,1,0:T(8,128)S(1)} %get-tuple-element.69.own, f32[8,64,128]{2,1,0:T(8,128)S(1)} %collective-permute-done.16.across, f32[8,64,128]{2,1,0:T(8,128)S(1)} %collective-permute-done.17.partner, f32[4,16,64,128]{3,2,1,0:T(8,128)S(1)} %get-tuple-element.67.coef, ...), custom_call_target="tpu_custom_call" | custom-call | flops 13107200 | bytes 1048576 | tf_op jit(solution)/shard_map/backward1/pallas_call | solution.py:26
  42.6 0.8 %collective-permute-start.18 = (f32[8,64,128]{2,1,0:T(8,128)S(1)}, f32[8,64,128]{2,1,0:T(8,128)S(1)}, u32[]{:S(2)}, u32[]{:S(2)}) collective-permute-start(f32[8,64,128]{2,1,0:T(8,128)S(1)} %get-tuple-element.71.own), channel_id=1, source_target_pairs={{0,16},{1,2},{2,1},{3,4},{4,3},{5,6},{6,5},{7,23},{8,24},{9,10},{1... | collective-permute-start | bytes 786440 | tf_op jit(solution)/shard_map/adjoint_to_chip/ppermute | solution.py:415
  43.4 2.4 %collective-permute-done.22.across = f32[8,64,128]{2,1,0:T(8,128)S(1)} collective-permute-done((f32[8,64,128]{2,1,0:T(8,128)S(1)}, f32[8,64,128]{2,1,0:T(8,128)S(1)}, u32[]{:S(2)}, u32[]{:S(2)}) %collective-permute-start.22) | collective-permute-done | bytes 262176 | tf_op jit(solution)/shard_map/state_to_chip/ppermute | solution.py:415
  45.8 1.0 %forward2.1 = (f32[8,64,128]{2,1,0:T(8,128)S(1)}, f32[8,64,128]{2,1,0:T(8,128)S(1)}) custom-call(f32[8,64,128]{2,1,0:T(8,128)S(1)} %get-tuple-element.76.own, f32[8,64,128]{2,1,0:T(8,128)S(1)} %collective-permute-done.22.across, f32[8,64,128]{2,1,0:T(8,128)S(1)} %collective-permute-done.23.partner, f32[4,16,64,128]{3,2,1,0:T(8,128)S(1)} %get-tuple-element.67.coef, ...), custom_call_target="tpu_custom_call" | custom-call | flops 13107200 | bytes 1048576 | tf_op jit(solution)/shard_map/forward2/pallas_call | solution.py:26
  46.8 0.8 %collective-permute-start.26 = (f32[8,64,128]{2,1,0:T(8,128)S(1)}, f32[8,64,128]{2,1,0:T(8,128)S(1)}, u32[]{:S(2)}, u32[]{:S(2)}) collective-permute-start(f32[8,64,128]{2,1,0:T(8,128)S(1)} %get-tuple-element.82.own), channel_id=1, source_target_pairs={{0,16},{1,2},{2,1},{3,4},{4,3},{5,6},{6,5},{7,23},{8,24},{9,10},{1... | collective-permute-start | bytes 786440 | tf_op jit(solution)/shard_map/state_to_chip/ppermute | solution.py:415
  47.6 1.5 %collective-permute-done.18.across = f32[8,64,128]{2,1,0:T(8,128)S(1)} collective-permute-done((f32[8,64,128]{2,1,0:T(8,128)S(1)}, f32[8,64,128]{2,1,0:T(8,128)S(1)}, u32[]{:S(2)}, u32[]{:S(2)}) %collective-permute-start.18) | collective-permute-done | bytes 262176 | tf_op jit(solution)/shard_map/adjoint_to_chip/ppermute | solution.py:415
  49.1 1.0 %backward2.1 = (f32[8,64,128]{2,1,0:T(8,128)S(1)}, f32[8,64,128]{2,1,0:T(8,128)S(1)}, f32[8,64,128]{2,1,0:T(8,128)S(1)}) custom-call(f32[8,64,128]{2,1,0:T(8,128)S(1)} %get-tuple-element.71.own, f32[8,64,128]{2,1,0:T(8,128)S(1)} %collective-permute-done.18.across, f32[8,64,128]{2,1,0:T(8,128)S(1)} %collective-permute-done.19.partner, ...), custom_call_target="tpu_custom_call" | custom-call | flops 13107200 | bytes 1048576 | tf_op jit(solution)/shard_map/backward2/pallas_call | solution.py:26
  50.1 0.8 %collective-permute-start.24 = (f32[8,64,128]{2,1,0:T(8,128)S(1)}, f32[8,64,128]{2,1,0:T(8,128)S(1)}, u32[]{:S(2)}, u32[]{:S(2)}) collective-permute-start(f32[8,64,128]{2,1,0:T(8,128)S(1)} %get-tuple-element.78.own), channel_id=1, source_target_pairs={{0,16},{1,2},{2,1},{3,4},{4,3},{5,6},{6,5},{7,23},{8,24},{9,10},{1... | collective-permute-start | bytes 786440 | tf_op jit(solution)/shard_map/adjoint_to_chip/ppermute | solution.py:415
  50.9 2.3 %collective-permute-done.26.across = f32[8,64,128]{2,1,0:T(8,128)S(1)} collective-permute-done((f32[8,64,128]{2,1,0:T(8,128)S(1)}, f32[8,64,128]{2,1,0:T(8,128)S(1)}, u32[]{:S(2)}, u32[]{:S(2)}) %collective-permute-start.26) | collective-permute-done | bytes 262176 | tf_op jit(solution)/shard_map/state_to_chip/ppermute | solution.py:415
  53.2 1.0 %forward3.1 = (f32[8,32,128]{2,1,0:T(8,128)S(1)}, f32[8,32,128]{2,1,0:T(8,128)S(1)}, f32[8,32,128]{2,1,0:T(8,128)S(1)}, f32[8,32,128]{2,1,0:T(8,128)S(1)}) custom-call(f32[8,64,128]{2,1,0:T(8,128)S(1)} %get-tuple-element.82.own, f32[8,64,128]{2,1,0:T(8,128)S(1)} %collective-permute-done.26.across, f32[8,64,128]{2,1,0:T(8,128)S(1)} %collective-permute-done.27.partner, ...), custom_call_target="tpu_custom_call" | custom-call | flops 13107200 | bytes 1048576 | tf_op jit(solution)/shard_map/forward3/pallas_call | solution.py:26
  54.2 0.5 collective-permute-start.28
  54.7 1.1 %collective-permute-start.29 = (f32[8,32,128]{2,1,0:T(8,128)S(1)}, f32[8,32,128]{2,1,0:T(8,128)S(1)}, u32[]{:S(2)}, u32[]{:S(2)}) collective-permute-start(f32[8,32,128]{2,1,0:T(8,128)S(1)} %get-tuple-element.86), channel_id=1, source_target_pairs={{0,16},{8,24},{16,0},{24,8},{1,17},{9,25},{17,1},{25,9},{2,18},{10... | collective-permute-start | bytes 393224 | tf_op jit(solution)/shard_map/grad_to_2/ppermute | solution.py:425
  55.9 1.9 %collective-permute-start.30 = (f32[8,32,128]{2,1,0:T(8,128)S(1)}, f32[8,32,128]{2,1,0:T(8,128)S(1)}, u32[]{:S(2)}, u32[]{:S(2)}) collective-permute-start(f32[8,32,128]{2,1,0:T(8,128)S(1)} %get-tuple-element.87), channel_id=1, source_target_pairs={{0,24},{8,16},{16,8},{24,0},{1,25},{9,17},{17,9},{25,1},{2,26},{10... | collective-permute-start | bytes 393224 | tf_op jit(solution)/shard_map/grad_to_3/ppermute | solution.py:425
  57.8 1.7 %backward3.1 = (f32[8,64,128]{2,1,0:T(8,128)}, f32[8,64,128]{2,1,0:T(8,128)}, f32[8,128]{1,0:T(8,128)S(1)}) custom-call(f32[8,64,128]{2,1,0:T(8,128)S(1)} %get-tuple-element.78.own, f32[8,64,128]{2,1,0:T(8,128)S(1)} %collective-permute-done.24.across, f32[8,64,128]{2,1,0:T(8,128)S(1)} %collective-permute-done.25.partner, ...), custom_call_target="tpu_custom_call" | custom-call | flops 13107200 | bytes 1048576 | tf_op jit(solution)/shard_map/backward3/pallas_call | solution.py:26
  59.5 0.5 collective-permute-done.28.refs_1_
  60.0 2.1 %collective-permute-done.29.refs_2_ = f32[8,32,128]{2,1,0:T(8,128)S(1)} collective-permute-done((f32[8,32,128]{2,1,0:T(8,128)S(1)}, f32[8,32,128]{2,1,0:T(8,128)S(1)}, u32[]{:S(2)}, u32[]{:S(2)}) %collective-permute-start.29) | collective-permute-done | bytes 131104 | tf_op jit(solution)/shard_map/grad_to_2/ppermute | solution.py:425
  62.2 0.7 %total.1 = f32[8,32,128]{2,1,0:T(8,128)} custom-call(f32[8,32,128]{2,1,0:T(8,128)S(1)} %get-tuple-element.84.refs_0_, f32[8,32,128]{2,1,0:T(8,128)S(1)} %collective-permute-done.28.refs_1_, f32[8,32,128]{2,1,0:T(8,128)S(1)} %collective-permute-done.29.refs_2_, f32[8,32,128]{2,1,0:T(8,128)S(1)} %collective-permute-done.30.refs_3_, ...), custom_call_target="tpu_custom_call" | custom-call | flops 1048576 | bytes 1048576 | tf_op jit(solution)/shard_map/total/pallas_call | solution.py:26
  (33 shorter events, 0.2 us)
Async XLA Ops:
  2.8 6.8 %collective-permute-start.2 = (f32[9,32,128]{2,1,0:T(8,128)S(1)}, f32[9,32,128]{2,1,0:T(8,128)S(1)}, u32[]{:S(2)}, u32[]{:S(2)}) collective-permute-start(f32[9,32,128]{2,1,0:T(8,128)S(1)} %get-tuple-element.49), channel_id=1, source_target_pairs={{0,8},{8,0},{16,24},{24,16},{1,9},{9,1},{17,25},{25,17},{2,10},{10... | collective-permute-start | bytes 442376 | tf_op jit(solution)/shard_map/wz_to_1/ppermute | solution.py:425
  5.7 5.6 %collective-permute-start.3 = (f32[8,32,128]{2,1,0:T(8,128)S(1)}, f32[8,32,128]{2,1,0:T(8,128)S(1)}, u32[]{:S(2)}, u32[]{:S(2)}) collective-permute-start(f32[8,32,128]{2,1,0:T(8,128)S(1)} %get-tuple-element.50.own.refs_0_), channel_id=1, source_target_pairs={{0,16},{8,24},{16,0},{24,8},{1,17},{9,25},{17,1},{25,9},{2,18},{10... | collective-permute-start | bytes 393224 | tf_op jit(solution)/shard_map/wx_to_2/ppermute | solution.py:425
  7.2 9.8 %collective-permute-start = (f32[8,64,128]{2,1,0:T(8,128)S(1)}, f32[8,64,128]{2,1,0:T(8,128)S(1)}, u32[]{:S(2)}, u32[]{:S(2)}) collective-permute-start(f32[8,64,128]{2,1,0:T(8,128)S(1)} %get-tuple-element.48.own.previous), channel_id=1, source_target_pairs={{0,1},{1,0},{2,3},{3,2},{4,5},{5,4},{6,7},{7,6},{8,9},{9,8},{10,11... | collective-permute-start | bytes 786440 | tf_op jit(solution)/shard_map/state_to_core/ppermute | solution.py:411
  7.2 11.8 %collective-permute-start.1 = (f32[8,64,128]{2,1,0:T(8,128)S(1)}, f32[8,64,128]{2,1,0:T(8,128)S(1)}, u32[]{:S(2)}, u32[]{:S(2)}) collective-permute-start(f32[8,64,128]{2,1,0:T(8,128)S(1)} %get-tuple-element.48.own.previous), channel_id=1, source_target_pairs={{0,8},{1,2},{2,1},{3,4},{4,3},{5,6},{6,5},{7,15},{8,0},{9,10},{10,... | collective-permute-start | bytes 786440 | tf_op jit(solution)/shard_map/state_to_chip/ppermute | solution.py:415
  7.8 6.2 %collective-permute-start.9 = (f32[8,32,128]{2,1,0:T(8,128)S(1)}, f32[8,32,128]{2,1,0:T(8,128)S(1)}, u32[]{:S(2)}, u32[]{:S(2)}) collective-permute-start(f32[8,32,128]{2,1,0:T(8,128)S(1)} %get-tuple-element.57.own.refs_3_), channel_id=1, source_target_pairs={{0,16},{8,24},{16,0},{24,8},{1,17},{9,25},{17,1},{25,9},{2,18},{10... | collective-permute-start | bytes 393224 | tf_op jit(solution)/shard_map/wy_to_2/ppermute | solution.py:425
  9.5 6.9 %collective-permute-start.5 = (f32[8,32,128]{2,1,0:T(8,128)S(1)}, f32[8,32,128]{2,1,0:T(8,128)S(1)}, u32[]{:S(2)}, u32[]{:S(2)}) collective-permute-start(f32[8,32,128]{2,1,0:T(8,128)S(1)} %get-tuple-element.51.own.refs_0_), channel_id=1, source_target_pairs={{0,8},{8,0},{16,24},{24,16},{1,9},{9,1},{17,25},{25,17},{2,10},{10... | collective-permute-start | bytes 393224 | tf_op jit(solution)/shard_map/speed_to_1/ppermute | solution.py:425
  11.3 11.1 %collective-permute-start.11 = (f32[2,8,32,128]{3,2,1,0:T(8,128)S(1)}, f32[2,8,32,128]{3,2,1,0:T(8,128)S(1)}, u32[]{:S(2)}, u32[]{:S(2)}) collective-permute-start(f32[2,8,32,128]{3,2,1,0:T(8,128)S(1)} %pair_wz.1), channel_id=1, source_target_pairs={{0,16},{8,24},{16,0},{24,8},{1,17},{9,25},{17,1},{25,9},{2,18},{10... | collective-permute-start | bytes 786440 | tf_op jit(solution)/shard_map/wz_to_2/ppermute | solution.py:425
  13.9 6.3 %collective-permute-start.4 = (f32[8,32,128]{2,1,0:T(8,128)S(1)}, f32[8,32,128]{2,1,0:T(8,128)S(1)}, u32[]{:S(2)}, u32[]{:S(2)}) collective-permute-start(f32[8,32,128]{2,1,0:T(8,128)S(1)} %relay_wx.1.refs_0_), channel_id=1, source_target_pairs={{0,8},{8,0},{16,24},{24,16},{1,9},{9,1},{17,25},{25,17},{2,10},{10... | collective-permute-start | bytes 393224 | tf_op jit(solution)/shard_map/wx_to_1/ppermute | solution.py:425
  16.4 6.1 %collective-permute-start.10 = (f32[8,32,128]{2,1,0:T(8,128)S(1)}, f32[8,32,128]{2,1,0:T(8,128)S(1)}, u32[]{:S(2)}, u32[]{:S(2)}) collective-permute-start(f32[8,32,128]{2,1,0:T(8,128)S(1)} %relay_wy.1), channel_id=1, source_target_pairs={{0,8},{8,0},{16,24},{24,16},{1,9},{9,1},{17,25},{25,17},{2,10},{10... | collective-permute-start | bytes 393224 | tf_op jit(solution)/shard_map/wy_to_1/ppermute | solution.py:425
  17.0 8.7 %copy-start = (f32[1,8,64,128]{3,2,1,0:T(8,128)S(1)}, f32[1,8,64,128]{3,2,1,0:T(8,128)}, u32[]{:S(2)}) copy-start(f32[1,8,64,128]{3,2,1,0:T(8,128)} %param.21) | copy-start | bytes 786436
  17.0 8.6 %collective-permute-start.6 = (f32[2,8,32,128]{3,2,1,0:T(8,128)S(1)}, f32[2,8,32,128]{3,2,1,0:T(8,128)S(1)}, u32[]{:S(2)}, u32[]{:S(2)}) collective-permute-start(f32[2,8,32,128]{3,2,1,0:T(8,128)S(1)} %pair_speed.1), channel_id=1, source_target_pairs={{0,16},{8,24},{16,0},{24,8},{1,17},{9,25},{17,1},{25,9},{2,18},{10... | collective-permute-start | bytes 786440 | tf_op jit(solution)/shard_map/speed_to_2/ppermute | solution.py:425
  21.1 8.8 %copy-start.3 = (f32[1,16,128]{2,1,0:T(8,128)S(1)}, f32[1,16,128]{2,1,0:T(8,128)}, u32[]{:S(2)}) copy-start(f32[1,16,128]{2,1,0:T(8,128)} %traces.1) | copy-start | bytes 24580
  21.1 8.8 %copy-start.4 = (f32[1,16]{1,0:T(1,128)S(1)}, f32[1,16]{1,0:T(1,128)}, u32[]{:S(2)}) copy-start(f32[1,16]{1,0:T(1,128)} %wavelet.1) | copy-start | bytes 196
  21.1 8.8 %copy-start.5 = (s32[1,128]{1,0:T(1,128)S(1)}, s32[1,128]{1,0:T(1,128)}, u32[]{:S(2)}) copy-start(s32[1,128]{1,0:T(1,128)} %rx.1) | copy-start | bytes 1540
  21.1 8.8 %copy-start.6 = (s32[1,128]{1,0:T(1,128)S(1)}, s32[1,128]{1,0:T(1,128)}, u32[]{:S(2)}) copy-start(s32[1,128]{1,0:T(1,128)} %ry.1) | copy-start | bytes 1540
  21.1 8.8 %copy-start.7 = (s32[1,128]{1,0:T(1,128)S(1)}, s32[1,128]{1,0:T(1,128)}, u32[]{:S(2)}) copy-start(s32[1,128]{1,0:T(1,128)} %rz.1) | copy-start | bytes 1540
  21.1 10.3 %copy-start.1 = (f32[1,8,64,128]{3,2,1,0:T(8,128)S(1)}, f32[1,8,64,128]{3,2,1,0:T(8,128)}, u32[]{:S(2)}) copy-start(f32[1,8,64,128]{3,2,1,0:T(8,128)} %param.18) | copy-start | bytes 786436
  23.0 3.5 %collective-permute-start.12 = (f32[3,2,64,128]{3,2,1,0:T(8,128)S(1)}, f32[3,2,64,128]{3,2,1,0:T(8,128)S(1)}, u32[]{:S(2)}, u32[]{:S(2)}) collective-permute-start(f32[3,2,64,128]{3,2,1,0:T(8,128)S(1)} %get-tuple-element.59), channel_id=1, source_target_pairs={{0,1},{1,0},{2,3},{3,2},{4,5},{5,4},{6,7},{7,6},{8,9},{9,8},{10,11... | collective-permute-start | bytes 589832 | tf_op jit(solution)/shard_map/edge_to_core/ppermute | solution.py:411
  23.1 7.6 %collective-permute-start.13 = (f32[3,2,64,128]{3,2,1,0:T(8,128)S(1)}, f32[3,2,64,128]{3,2,1,0:T(8,128)S(1)}, u32[]{:S(2)}, u32[]{:S(2)}) collective-permute-start(f32[3,2,64,128]{3,2,1,0:T(8,128)S(1)} %get-tuple-element.60), channel_id=1, source_target_pairs={{0,1},{1,0},{2,3},{3,2},{4,5},{5,4},{6,7},{7,6},{8,9},{9,8},{10,11... | collective-permute-start | bytes 589832 | tf_op jit(solution)/shard_map/edge_to_core/ppermute | solution.py:411
  23.6 7.1 %collective-permute-start.14 = (f32[3,2,64,128]{3,2,1,0:T(8,128)S(1)}, f32[3,2,64,128]{3,2,1,0:T(8,128)S(1)}, u32[]{:S(2)}, u32[]{:S(2)}) collective-permute-start(f32[3,2,64,128]{3,2,1,0:T(8,128)S(1)} %get-tuple-element.61), channel_id=1, source_target_pairs={{0,16},{1,2},{2,1},{3,4},{4,3},{5,6},{6,5},{7,23},{8,24},{9,10},{1... | collective-permute-start | bytes 589832 | tf_op jit(solution)/shard_map/edge_to_chip/ppermute | solution.py:415
  24.3 7.1 %collective-permute-start.15 = (f32[3,2,64,128]{3,2,1,0:T(8,128)S(1)}, f32[3,2,64,128]{3,2,1,0:T(8,128)S(1)}, u32[]{:S(2)}, u32[]{:S(2)}) collective-permute-start(f32[3,2,64,128]{3,2,1,0:T(8,128)S(1)} %get-tuple-element.62), channel_id=1, source_target_pairs={{0,16},{1,2},{2,1},{3,4},{4,3},{5,6},{6,5},{7,23},{8,24},{9,10},{1... | collective-permute-start | bytes 589832 | tf_op jit(solution)/shard_map/edge_to_chip/ppermute | solution.py:415
  25.7 8.5 %collective-permute-start.7 = (f32[8,64,128]{2,1,0:T(8,128)S(1)}, f32[8,64,128]{2,1,0:T(8,128)S(1)}, u32[]{:S(2)}, u32[]{:S(2)}) collective-permute-start(f32[8,64,128]{2,1,0:T(8,128)S(1)} %get-tuple-element.53.own), channel_id=1, source_target_pairs={{0,16},{1,2},{2,1},{3,4},{4,3},{5,6},{6,5},{7,23},{8,24},{9,10},{1... | collective-permute-start | bytes 786440 | tf_op jit(solution)/shard_map/adjoint_to_chip/ppermute | solution.py:415
  26.5 7.7 %collective-permute-start.8 = (f32[8,64,128]{2,1,0:T(8,128)S(1)}, f32[8,64,128]{2,1,0:T(8,128)S(1)}, u32[]{:S(2)}, u32[]{:S(2)}) collective-permute-start(f32[8,64,128]{2,1,0:T(8,128)S(1)} %get-tuple-element.53.own), channel_id=1, source_target_pairs={{0,1},{1,0},{2,3},{3,2},{4,5},{5,4},{6,7},{7,6},{8,9},{9,8},{10,11... | collective-permute-start | bytes 786440 | tf_op jit(solution)/shard_map/adjoint_to_core/ppermute | solution.py:411
  31.4 2.8 %copy-start.2 = (f32[1,8,64,128]{3,2,1,0:T(8,128)S(1)}, f32[1,8,64,128]{3,2,1,0:T(8,128)}, u32[]{:S(2)}) copy-start(f32[1,8,64,128]{3,2,1,0:T(8,128)} %param.20) | copy-start | bytes 786436
  31.9 6.4 %collective-permute-start.20 = (f32[8,64,128]{2,1,0:T(8,128)S(1)}, f32[8,64,128]{2,1,0:T(8,128)S(1)}, u32[]{:S(2)}, u32[]{:S(2)}) collective-permute-start(f32[8,64,128]{2,1,0:T(8,128)S(1)} %get-tuple-element.74.own.previous), channel_id=1, source_target_pairs={{0,16},{1,2},{2,1},{3,4},{4,3},{5,6},{6,5},{7,23},{8,24},{9,10},{1... | collective-permute-start | bytes 786440 | tf_op jit(solution)/shard_map/state_to_chip/ppermute | solution.py:415
  32.7 5.7 %collective-permute-start.21 = (f32[8,64,128]{2,1,0:T(8,128)S(1)}, f32[8,64,128]{2,1,0:T(8,128)S(1)}, u32[]{:S(2)}, u32[]{:S(2)}) collective-permute-start(f32[8,64,128]{2,1,0:T(8,128)S(1)} %get-tuple-element.74.own.previous), channel_id=1, source_target_pairs={{0,1},{1,0},{2,3},{3,2},{4,5},{5,4},{6,7},{7,6},{8,9},{9,8},{10,11... | collective-permute-start | bytes 786440 | tf_op jit(solution)/shard_map/state_to_core/ppermute | solution.py:411
  35.2 6.4 %collective-permute-start.16 = (f32[8,64,128]{2,1,0:T(8,128)S(1)}, f32[8,64,128]{2,1,0:T(8,128)S(1)}, u32[]{:S(2)}, u32[]{:S(2)}) collective-permute-start(f32[8,64,128]{2,1,0:T(8,128)S(1)} %get-tuple-element.69.own), channel_id=1, source_target_pairs={{0,16},{1,2},{2,1},{3,4},{4,3},{5,6},{6,5},{7,23},{8,24},{9,10},{1... | collective-permute-start | bytes 786440 | tf_op jit(solution)/shard_map/adjoint_to_chip/ppermute | solution.py:415
  36.0 5.7 %collective-permute-start.17 = (f32[8,64,128]{2,1,0:T(8,128)S(1)}, f32[8,64,128]{2,1,0:T(8,128)S(1)}, u32[]{:S(2)}, u32[]{:S(2)}) collective-permute-start(f32[8,64,128]{2,1,0:T(8,128)S(1)} %get-tuple-element.69.own), channel_id=1, source_target_pairs={{0,1},{1,0},{2,3},{3,2},{4,5},{5,4},{6,7},{7,6},{8,9},{9,8},{10,11... | collective-permute-start | bytes 786440 | tf_op jit(solution)/shard_map/adjoint_to_core/ppermute | solution.py:411
  39.3 6.4 %collective-permute-start.22 = (f32[8,64,128]{2,1,0:T(8,128)S(1)}, f32[8,64,128]{2,1,0:T(8,128)S(1)}, u32[]{:S(2)}, u32[]{:S(2)}) collective-permute-start(f32[8,64,128]{2,1,0:T(8,128)S(1)} %get-tuple-element.76.own), channel_id=1, source_target_pairs={{0,16},{1,2},{2,1},{3,4},{4,3},{5,6},{6,5},{7,23},{8,24},{9,10},{1... | collective-permute-start | bytes 786440 | tf_op jit(solution)/shard_map/state_to_chip/ppermute | solution.py:415
  40.1 5.7 %collective-permute-start.23 = (f32[8,64,128]{2,1,0:T(8,128)S(1)}, f32[8,64,128]{2,1,0:T(8,128)S(1)}, u32[]{:S(2)}, u32[]{:S(2)}) collective-permute-start(f32[8,64,128]{2,1,0:T(8,128)S(1)} %get-tuple-element.76.own), channel_id=1, source_target_pairs={{0,1},{1,0},{2,3},{3,2},{4,5},{5,4},{6,7},{7,6},{8,9},{9,8},{10,11... | collective-permute-start | bytes 786440 | tf_op jit(solution)/shard_map/state_to_core/ppermute | solution.py:411
  42.6 6.4 %collective-permute-start.18 = (f32[8,64,128]{2,1,0:T(8,128)S(1)}, f32[8,64,128]{2,1,0:T(8,128)S(1)}, u32[]{:S(2)}, u32[]{:S(2)}) collective-permute-start(f32[8,64,128]{2,1,0:T(8,128)S(1)} %get-tuple-element.71.own), channel_id=1, source_target_pairs={{0,16},{1,2},{2,1},{3,4},{4,3},{5,6},{6,5},{7,23},{8,24},{9,10},{1... | collective-permute-start | bytes 786440 | tf_op jit(solution)/shard_map/adjoint_to_chip/ppermute | solution.py:415
  43.4 5.7 %collective-permute-start.19 = (f32[8,64,128]{2,1,0:T(8,128)S(1)}, f32[8,64,128]{2,1,0:T(8,128)S(1)}, u32[]{:S(2)}, u32[]{:S(2)}) collective-permute-start(f32[8,64,128]{2,1,0:T(8,128)S(1)} %get-tuple-element.71.own), channel_id=1, source_target_pairs={{0,1},{1,0},{2,3},{3,2},{4,5},{5,4},{6,7},{7,6},{8,9},{9,8},{10,11... | collective-permute-start | bytes 786440 | tf_op jit(solution)/shard_map/adjoint_to_core/ppermute | solution.py:411
  46.8 6.4 %collective-permute-start.26 = (f32[8,64,128]{2,1,0:T(8,128)S(1)}, f32[8,64,128]{2,1,0:T(8,128)S(1)}, u32[]{:S(2)}, u32[]{:S(2)}) collective-permute-start(f32[8,64,128]{2,1,0:T(8,128)S(1)} %get-tuple-element.82.own), channel_id=1, source_target_pairs={{0,16},{1,2},{2,1},{3,4},{4,3},{5,6},{6,5},{7,23},{8,24},{9,10},{1... | collective-permute-start | bytes 786440 | tf_op jit(solution)/shard_map/state_to_chip/ppermute | solution.py:415
  47.6 5.7 %collective-permute-start.27 = (f32[8,64,128]{2,1,0:T(8,128)S(1)}, f32[8,64,128]{2,1,0:T(8,128)S(1)}, u32[]{:S(2)}, u32[]{:S(2)}) collective-permute-start(f32[8,64,128]{2,1,0:T(8,128)S(1)} %get-tuple-element.82.own), channel_id=1, source_target_pairs={{0,1},{1,0},{2,3},{3,2},{4,5},{5,4},{6,7},{7,6},{8,9},{9,8},{10,11... | collective-permute-start | bytes 786440 | tf_op jit(solution)/shard_map/state_to_core/ppermute | solution.py:411
  50.1 7.7 %collective-permute-start.24 = (f32[8,64,128]{2,1,0:T(8,128)S(1)}, f32[8,64,128]{2,1,0:T(8,128)S(1)}, u32[]{:S(2)}, u32[]{:S(2)}) collective-permute-start(f32[8,64,128]{2,1,0:T(8,128)S(1)} %get-tuple-element.78.own), channel_id=1, source_target_pairs={{0,16},{1,2},{2,1},{3,4},{4,3},{5,6},{6,5},{7,23},{8,24},{9,10},{1... | collective-permute-start | bytes 786440 | tf_op jit(solution)/shard_map/adjoint_to_chip/ppermute | solution.py:415
  50.9 6.9 %collective-permute-start.25 = (f32[8,64,128]{2,1,0:T(8,128)S(1)}, f32[8,64,128]{2,1,0:T(8,128)S(1)}, u32[]{:S(2)}, u32[]{:S(2)}) collective-permute-start(f32[8,64,128]{2,1,0:T(8,128)S(1)} %get-tuple-element.78.own), channel_id=1, source_target_pairs={{0,1},{1,0},{2,3},{3,2},{4,5},{5,4},{6,7},{7,6},{8,9},{9,8},{10,11... | collective-permute-start | bytes 786440 | tf_op jit(solution)/shard_map/adjoint_to_core/ppermute | solution.py:411
  54.2 5.8 %collective-permute-start.28 = (f32[8,32,128]{2,1,0:T(8,128)S(1)}, f32[8,32,128]{2,1,0:T(8,128)S(1)}, u32[]{:S(2)}, u32[]{:S(2)}) collective-permute-start(f32[8,32,128]{2,1,0:T(8,128)S(1)} %get-tuple-element.85), channel_id=1, source_target_pairs={{0,8},{8,0},{16,24},{24,16},{1,9},{9,1},{17,25},{25,17},{2,10},{10... | collective-permute-start | bytes 393224 | tf_op jit(solution)/shard_map/grad_to_1/ppermute | solution.py:425
  54.7 7.4 %collective-permute-start.29 = (f32[8,32,128]{2,1,0:T(8,128)S(1)}, f32[8,32,128]{2,1,0:T(8,128)S(1)}, u32[]{:S(2)}, u32[]{:S(2)}) collective-permute-start(f32[8,32,128]{2,1,0:T(8,128)S(1)} %get-tuple-element.86), channel_id=1, source_target_pairs={{0,16},{8,24},{16,0},{24,8},{1,17},{9,25},{17,1},{25,9},{2,18},{10... | collective-permute-start | bytes 393224 | tf_op jit(solution)/shard_map/grad_to_2/ppermute | solution.py:425
  55.9 6.3 %collective-permute-start.30 = (f32[8,32,128]{2,1,0:T(8,128)S(1)}, f32[8,32,128]{2,1,0:T(8,128)S(1)}, u32[]{:S(2)}, u32[]{:S(2)}) collective-permute-start(f32[8,32,128]{2,1,0:T(8,128)S(1)} %get-tuple-element.87), channel_id=1, source_target_pairs={{0,24},{8,16},{16,8},{24,0},{1,25},{9,17},{17,9},{25,1},{2,26},{10... | collective-permute-start | bytes 393224 | tf_op jit(solution)/shard_map/grad_to_3/ppermute | solution.py:425
